TPU v7x, 32 devices: a whole 2x2x4 slice. The times are simulated.
32 devices in a mesh: scen: 4 (over z), line: 8 (over y, x, core).
Axes of the slice: x: 2, y: 2, z: 4, core: 2. Of those that a mesh axis runs over, the one named last changes fastest.
Arguments:
- shift_factors: bfloat16 [32768, 20480], P('line', 'scen'), may hold values from -0.0390625 to 0.0390625
- gen_bus: int32 [4096], P('scen'), may hold values from 0 to 20479, as said below
- commit: int32 [4096], P('scen'), may hold values 0 or 1
- cost_coef: float32 [2, 4096], P(None, 'scen'), may hold values from 0.2 to 2
- gen_cap: float32 [4096], P('scen'), may hold values from 0.5 to 4
- bus_loads: float32 [48, 20480], P('line', 'scen'), may hold values from 0.04 to 6
- load_shed: float32 [48, 20480], P('line', 'scen'), may hold values from 0 to 0.3
- dispatch: float32 [48, 4096], P('line', 'scen'), may hold values from 0 to 2
- ph_dual: float32 [48, 4096], P('line', 'scen'), may hold values from -3 to 3
- consensus_prev: float32 [4096], P('scen'), may hold values from 0 to 2
- scen_weight: float32 [48], P('line'), may hold values from 1 to 150000
- flow_copy: float32 [48, 32768], P('scen', 'line'), may hold values from -5 to 5
- flow_dual: float32 [48, 32768], P('scen', 'line'), may hold values from -1.75 to 1.75
- balance_dual: float32 [48], P('line'), may hold values from -3 to 3
- flow_limit: float32 [32768], P('line'), may hold values from 0.4 to 2
Outputs:
- dispatch_out: float32 [48, 4096], P('line', 'scen')
- shed_out: float32 [48, 20480], P('line', 'scen')
- flow_copy_out: float32 [48, 32768], P('scen', 'line')
- flow_dual_out: float32 [48, 32768], P('scen', 'line')
- balance_dual_out: float32 [48], P('line')
- consensus: float32 [4096], P('scen')
- ph_dual_out: float32 [48, 4096], P('line', 'scen')
Inputs may be any that keep to these rules, and one draw needn't show every extreme that they name: `gen_bus`: generator j sits at one of the buses j * (5) to (j + 1) * 5 - 1, so no two generators share a bus.
All inputs are finite; a program needn't handle non-finite values. No bound on the sum of `commit` on one device may be relied on, other than what follows from the above.
Results may differ from a plain program's by a relative error of at most 0.0056.
Values may be sent and summed in bfloat16 or wider, within the bound.
No kernel may reach another device: no remote copies, remote signals or barrier semaphores. Data moves between devices by JAX's collectives and lax.ppermute only.
A program may use at most 128 MiB of HBM per device.

v0:
```python
import jax
import jax.numpy as jnp
from jax import lax
from jax.sharding import PartitionSpec as P

BUSES = 20480
ITERS = 2


def backward_term(every_res, shift_factors):
    return jnp.dot(every_res, shift_factors, preferred_element_type=jnp.float32)


def local(
    shift_factors,
    gen_bus,
    commit,
    cost_coef,
    gen_cap,
    bus_loads,
    load_shed,
    dispatch,
    ph_dual,
    consensus_prev,
    scen_weight,
    flow_copy,
    flow_dual,
    balance_dual,
    flow_limit,
):
    bus_block = shift_factors.shape[1]
    panel_rows = flow_copy.shape[0]
    local_bus = gen_bus - lax.axis_index("scen") * bus_block
    columns = lax.broadcasted_iota(jnp.int32, (gen_bus.shape[0], bus_block), 1)
    selector = (local_bus[:, None] == columns).astype(jnp.float32)
    capacity = gen_cap * commit.astype(jnp.float32)
    limits = flow_limit[None, :]
    generation = dispatch
    served = load_shed
    bal_dual = balance_dual
    copy_now, dual_now = (
        lax.all_gather(flow_copy, "scen", axis=0, tiled=True),
        lax.all_gather(flow_dual, "scen", axis=0, tiled=True),
    )
    for iteration in range(ITERS):
        placed = jnp.dot(
            generation,
            selector,
            precision=lax.Precision.HIGHEST,
            preferred_element_type=jnp.float32,
        )
        inject = (placed + served - bus_loads).astype(jnp.bfloat16)
        bal_part = jnp.sum(inject.astype(jnp.float32), axis=1)
        partial_flows = lax.dot_general(
            lax.all_gather(inject, "line", axis=0, tiled=True),
            shift_factors,
            (((1,), (1,)), ((), ())),
            preferred_element_type=jnp.float32,
        )
        flows_now, bal_total = lax.psum((partial_flows, bal_part), "scen")
        balance = bal_total / BUSES
        residual = (flows_now - copy_now + dual_now).astype(jnp.bfloat16)
        bus_sum = lax.psum_scatter(
            backward_term(residual, shift_factors), "line", scatter_dimension=0, tiled=True
        )
        bus_grad = bus_sum + (balance + bal_dual)[:, None]
        picked = lax.dot_general(
            bus_grad,
            selector,
            (((1,), (1,)), ((), ())),
            precision=lax.Precision.HIGHEST,
            preferred_element_type=jnp.float32,
        )
        gen_grad = (
            cost_coef[0]
            + cost_coef[1] * generation
            + ph_dual
            + (generation - consensus_prev)
            + picked
        )
        generation = jnp.minimum(jnp.maximum(generation - 0.4 * gen_grad, 0.0), capacity[None, :])
        served = jnp.minimum(jnp.maximum(served - 0.4 * (1.5 + bus_grad), 0.0), bus_loads)
        copy_next = jnp.minimum(jnp.maximum(flows_now + dual_now, -limits), limits)
        dual_now = dual_now + flows_now - copy_next
        copy_now = copy_next
        bal_dual = bal_dual + balance
    offset = lax.axis_index("scen") * panel_rows
    copy_now = lax.dynamic_slice_in_dim(copy_now, offset, panel_rows, 0)
    dual_now = lax.dynamic_slice_in_dim(dual_now, offset, panel_rows, 0)
    weighted = jnp.sum(scen_weight[:, None] * generation, axis=0)
    weight_total = jnp.sum(scen_weight)
    weighted, weight_total = lax.psum((weighted, weight_total), "line")
    consensus = weighted / weight_total
    return (
        generation,
        served,
        copy_now,
        dual_now,
        bal_dual,
        consensus,
        ph_dual + (generation - consensus),
    )


def solution(mesh):
    return jax.shard_map(
        local,
        mesh=mesh,
        in_specs=(
            P("line", "scen"),
            P("scen"),
            P("scen"),
            P(None, "scen"),
            P("scen"),
            P("line", "scen"),
            P("line", "scen"),
            P("line", "scen"),
            P("line", "scen"),
            P("scen"),
            P("line"),
            P("scen", "line"),
            P("scen", "line"),
            P("line"),
            P("line"),
        ),
        out_specs=(
            P("line", "scen"),
            P("line", "scen"),
            P("scen", "line"),
            P("scen", "line"),
            P("line"),
            P("scen"),
            P("line", "scen"),
        ),
        check_vma=False,
    )
```

profile of v0, /device:TPU:0, one launch (start us, length us, event | category | flops | bytes accessed | tf_op | source)
XLA Modules:
  0.0 349.8 jit_solution(1324997142481188478)
XLA Ops:
  7.2 0.7 broadcast_subtract_fusion
  7.9 7.8 %convert_reduce_fusion.1 = (f32[6]{0:T(128)S(1)}, bf16[6,5120]{1,0:T(8,128)(2,1)S(1)}) fusion(f32[6,5120]{1,0:T(8,128)} %param.20, f32[6,5120]{1,0:T(8,128)} %param.21, f32[6,1024]{1,0:T(8,128)} %param.22, s32[1024]{0:T(1024)S(1)} %broadcast_subtract_fusion), kind=kOutput, calls=%fused_computation.44 | convolution fusion | flops 382883840 | bytes 335896 | tf_op jit(solution)/shard_map/dot_general | solution.py:46
  15.7 11.6 %all-gather = bf16[8,6,5120]{2,1,0:T(8,128)(2,1)S(1)} all-gather(bf16[1,6,5120]{2,1,0:T(8,128)(2,1)S(1)} %bitcast.29), channel_id=1, replica_groups=mesh['scen'=4,'line'=8] {'line'}, dimensions={0}, use_global_device_ids=true | all-gather | bytes 552960 | tf_op jit(solution)/shard_map/all_gather | solution.py:55
  27.5 19.4 %fusion.40 = f32[48,4096]{1,0:T(8,128)} fusion(bf16[48,5120]{1,0:T(8,128)(2,1)S(1)} %reshape.25, bf16[4096,5120]{1,0:T(8,128)(2,1)} %param.15), kind=kOutput, calls=%fused_computation.58 | convolution fusion | flops 2013265920 | bytes 43220992 | tf_op jit(solution)/shard_map/dot_general | solution.py:54
  47.1 34.7 %all-gather.2 = f32[4,12,4096]{2,1,0:T(8,128)S(1)} all-gather(f32[1,12,4096]{2,1,0:T(8,128)S(1)} %bitcast.27), channel_id=1, replica_groups=mesh['scen'=4,'line'=8] {'scen'}, dimensions={0}, use_global_device_ids=true | all-gather | bytes 983040 | tf_op jit(solution)/shard_map/all_gather | solution.py:43
  81.7 12.2 %psum.43 = f32[6]{0:T(128)S(1)} all-reduce(f32[6]{0:T(128)S(1)} %get-tuple-element.15), channel_id=1, replica_groups=mesh['scen'=4,'line'=8] {'scen'}, use_global_device_ids=true, to_apply=%region_3.0 | all-reduce | flops 6 | bytes 48 | tf_op jit(solution)/shard_map/psum | solution.py:60
  94.1 30.3 %all-gather.1 = f32[4,12,4096]{2,1,0:T(8,128)S(1)} all-gather(f32[1,12,4096]{2,1,0:T(8,128)S(1)} %bitcast.28), channel_id=1, replica_groups=mesh['scen'=4,'line'=8] {'scen'}, dimensions={0}, use_global_device_ids=true | all-gather | bytes 983040 | tf_op jit(solution)/shard_map/all_gather | solution.py:42
  124.5 0.6 dynamic-slice.6
  125.9 17.0 %fusion.29 = f32[48,5120]{1,0:T(8,128)S(1)} fusion(bf16[4096,5120]{1,0:T(8,128)(2,1)} %param.15, f32[48,4096]{1,0:T(8,128)S(1)} %reshape.29, f32[48,4096]{1,0:T(8,128)} %all-reduce.8.cloned.1.call-done, f32[48,4096]{1,0:T(8,128)S(1)} %reshape.27), kind=kOutput, calls=%fused_computation.32 | convolution fusion | flops 2013855744 | bytes 45285376 | tf_op jit(solution)/shard_map/dot_general | solution.py:11
  142.9 20.2 %fusion = f32[8,5120]{1,0:T(8,128)S(1)} fusion(f32[48,5120]{1,0:T(8,128)S(1)} %fusion.29), kind=kCustom, calls=%all-reduce-scatter | all-reduce-scatter fusion | flops 327681 | bytes 1147392
  163.1 1.3 collective-permute-start
  164.4 1.4 collective-permute-start.1
  165.9 2.8 collective-permute-done.1
  169.2 9.5 %fusion.21 = f32[6,1024]{1,0:T(8,128)S(1)} fusion(f32[6,1024]{1,0:T(8,128)S(1)} %copy-done.16, s32[1024]{0:T(1024)S(1)} %broadcast_subtract_fusion, f32[22,5120]{1,0:T(8,128)S(1)} %concatenate, u32[]{:S(6)} %subtract, f32[6]{0:T(128)S(1)} %multiply_add_fusion.1, f32[6,1024]{1,0:T(8,128)S(1)} %copy-done.8, f32[1024]{0:T(1024)S(1)} %convert_multiply_fusion, ...), kind=kOutput, calls=%fused_computation.20 | convolution fusion | flops 382822400 | bytes 274948 | tf_op jit(solution)/shard_map/dot_general | solution.py:67
  178.7 7.0 %convert_reduce_fusion = (f32[6]{0:T(128)S(1)}, bf16[6,5120]{1,0:T(8,128)(2,1)S(1)}) fusion(f32[6,5120]{1,0:T(8,128)S(1)} %copy-done.6, f32[6,5120]{1,0:T(8,128)S(1)} %copy-done.7, f32[6]{0:T(128)S(1)} %multiply_add_fusion.1, f32[22,5120]{1,0:T(8,128)S(1)} %concatenate, u32[]{:S(6)} %subtract, f32[6,1024]{1,0:T(8,128)S(1)} %fusion.21, ...), kind=kOutput, calls=%fused_computation.41 | convolution fusion | flops 383068160 | bytes 458804 | tf_op jit(solution)/shard_map/dot_general | solution.py:46
  185.7 14.8 %all-gather.3 = bf16[8,6,5120]{2,1,0:T(8,128)(2,1)S(1)} all-gather(bf16[1,6,5120]{2,1,0:T(8,128)(2,1)S(1)} %bitcast.30), channel_id=1, replica_groups=mesh['scen'=4,'line'=8] {'line'}, dimensions={0}, use_global_device_ids=true | all-gather | bytes 552960 | tf_op jit(solution)/shard_map/all_gather | solution.py:55
  200.8 19.5 %fusion.41 = f32[48,4096]{1,0:T(8,128)} fusion(bf16[48,5120]{1,0:T(8,128)(2,1)S(1)} %reshape.31, bf16[4096,5120]{1,0:T(8,128)(2,1)} %param.15), kind=kOutput, calls=%fused_computation.59 | convolution fusion | flops 2013265920 | bytes 43220992 | tf_op jit(solution)/shard_map/dot_general | solution.py:54
  220.3 0.6 reduce_sum.39
  220.9 11.3 %psum.45 = f32[6]{0:T(128)S(1)} all-reduce(f32[6]{0:T(128)S(1)} %get-tuple-element.17), channel_id=1, replica_groups=mesh['scen'=4,'line'=8] {'scen'}, use_global_device_ids=true, to_apply=%region_7.0 | all-reduce | flops 6 | bytes 48 | tf_op jit(solution)/shard_map/psum | solution.py:60
  232.7 31.0 %all-reduce.10.cloned.1.call-done = f32[48,4096]{1,0:T(8,128)} async-done(((f32[48,4096]{1,0:T(8,128)}), f32[48,4096]{1,0:T(8,128)}) %all-reduce.10.cloned.1.call-update) | async-done | bytes 786448 | tf_op jit(solution)/shard_map/psum | solution.py:60
  263.8 20.6 %fusion.30 = f32[48,5120]{1,0:T(8,128)S(1)} fusion(bf16[4096,5120]{1,0:T(8,128)(2,1)} %param.15, f32[48,4096]{1,0:T(8,128)} %all-reduce.10.cloned.1.call-done, f32[4096]{0:T(1024)S(1)} %copy-done.5, f32[4096]{0:T(1024)S(1)} %neg.5, f32[48,4096]{1,0:T(8,128)S(1)} %copy-done, f32[48,4096]{1,0:T(8,128)S(1)} %reshape.29), kind=kOutput, calls=%fused_computation.33 | convolution fusion | flops 2014642176 | bytes 45318144 | tf_op jit(solution)/shard_map/dot_general | solution.py:11
  284.4 21.3 %fusion.1 = f32[8,5120]{1,0:T(8,128)S(1)} fusion(f32[48,5120]{1,0:T(8,128)S(1)} %fusion.30), kind=kCustom, calls=%all-reduce-scatter.1 | all-reduce-scatter fusion | flops 327681 | bytes 1147392
  305.7 1.3 collective-permute-start.2
  307.0 1.7 collective-permute-start.3
  309.0 0.8 dynamic-slice_subtract_fusion
  309.8 1.7 collective-permute-done.3
  311.6 0.8 concatenate.1
  312.4 10.3 %multiply_reduce_fusion = (f32[1024]{0:T(1024)S(1)}, f32[6,1024]{1,0:T(8,128)S(1)}) fusion(f32[6]{0:T(128)} %param.25, f32[1024]{0:T(1024)S(1)} %convert_multiply_fusion, f32[6,1024]{1,0:T(8,128)} %copy-done.20, s32[1024]{0:T(1024)S(1)} %broadcast_subtract_fusion, f32[22,5120]{1,0:T(8,128)S(1)} %concatenate.1, u32[]{:S(6)} %subtract, ...), kind=kOutput, calls=%fused_computation.48 | convolution fusion | flops 382833664 | bytes 262196 | tf_op jit(solution)/shard_map/dot_general | solution.py:67
  322.7 2.0 maximum_minimum_fusion.2
  324.7 15.8 %all-reduce.4 = (f32[1024]{0:T(1024)S(1)}, f32[]{:T(128)}) all-reduce(f32[1024]{0:T(1024)S(1)} %get-tuple-element.19, f32[]{:T(128)} %reduce_sum.39), channel_id=1, replica_groups=mesh['scen'=4,'line'=8] {'line'}, use_global_device_ids=true, to_apply=%region_9.0 | all-reduce | flops 1025 | bytes 8200 | tf_op jit(solution)/shard_map/psum | solution.py:92
  340.4 0.6 broadcast_divide_fusion
  341.1 1.4 subtract_add_fusion
  (62 shorter events, 2.1 us)
Async XLA Ops:
  7.2 118.7 %all-reduce.8.cloned.1.call-start = ((), (), s32[]{:S(2)}) async-start(), calls=%async_computation | async-start | bytes 1572864 | tf_op jit(solution)/shard_map/psum | solution.py:60
  27.5 19.6 %copy-start.3 = (f32[12,4096]{1,0:T(8,128)S(1)}, f32[12,4096]{1,0:T(8,128)}, u32[]{:S(2)}) copy-start(f32[12,4096]{1,0:T(8,128)} %param.27) | copy-start | bytes 589828
  27.5 66.6 %copy-start.4 = (f32[12,4096]{1,0:T(8,128)S(1)}, f32[12,4096]{1,0:T(8,128)}, u32[]{:S(2)}) copy-start(f32[12,4096]{1,0:T(8,128)} %param.26) | copy-start | bytes 589828
  27.5 97.0 %copy-start.15 = (u32[32]{0:T(128)S(1)}, u32[32]{0:T(128)}, u32[]{:S(2)}) copy-start(u32[32]{0:T(128)} %constant.34) | copy-start | bytes 388
  27.5 98.3 %copy-start.12 = (f32[1024]{0:T(1024)S(1)}, f32[1024]{0:T(1024)}, u32[]{:S(2)}) copy-start(f32[1024]{0:T(1024)} %param.19) | copy-start | bytes 12292
  27.5 98.3 %copy-start.13 = (s32[1024]{0:T(1024)S(1)}, s32[1024]{0:T(1024)}, u32[]{:S(2)}) copy-start(s32[1024]{0:T(1024)} %param.17) | copy-start | bytes 12292
  27.5 98.3 %copy-start.11 = (f32[2,1024]{1,0:T(2,128)S(1)}, f32[2,1024]{1,0:T(2,128)}, u32[]{:S(2)}) copy-start(f32[2,1024]{1,0:T(2,128)} %param.18) | copy-start | bytes 24580
  47.0 216.8 %all-reduce.10.cloned.1.call-start = ((), (), s32[]{:S(2)}) async-start(), calls=%async_computation.1 | async-start | bytes 1572864 | tf_op jit(solution)/shard_map/psum | solution.py:60
  125.8 40.0 %copy-start.18 = (f32[6]{0:T(128)S(1)}, f32[6]{0:T(128)}, u32[]{:S(2)}) copy-start(f32[6]{0:T(128)} %param.28) | copy-start | bytes 76
  125.8 43.4 %copy-start.8 = (f32[6,1024]{1,0:T(8,128)S(1)}, f32[6,1024]{1,0:T(8,128)}, u32[]{:S(2)}) copy-start(f32[6,1024]{1,0:T(8,128)} %param.23) | copy-start | bytes 73732
  125.8 43.4 %copy-start.16 = (f32[6,1024]{1,0:T(8,128)S(1)}, f32[6,1024]{1,0:T(8,128)}, u32[]{:S(2)}) copy-start(f32[6,1024]{1,0:T(8,128)} %param.22) | copy-start | bytes 73732
  125.8 43.4 %copy-start.17 = (f32[1024]{0:T(1024)S(1)}, f32[1024]{0:T(1024)}, u32[]{:S(2)}) copy-start(f32[1024]{0:T(1024)} %param.24) | copy-start | bytes 12292
  125.9 52.8 %copy-start.6 = (f32[6,5120]{1,0:T(8,128)S(1)}, f32[6,5120]{1,0:T(8,128)}, u32[]{:S(2)}) copy-start(f32[6,5120]{1,0:T(8,128)} %param.20) | copy-start | bytes 368644
  125.9 52.8 %copy-start.7 = (f32[6,5120]{1,0:T(8,128)S(1)}, f32[6,5120]{1,0:T(8,128)}, u32[]{:S(2)}) copy-start(f32[6,5120]{1,0:T(8,128)} %param.21) | copy-start | bytes 368644
  163.1 5.6 %collective-permute-start = (f32[8,5120]{1,0:T(8,128)S(1)}, f32[8,5120]{1,0:T(8,128)S(1)}, u32[]{:S(2)}, u32[]{:S(2)}) collective-permute-start(f32[8,5120]{1,0:T(8,128)S(1)} %fusion), channel_id=1, source_target_pairs={{0,1},{1,2},{2,3},{3,4},{4,5},{5,6},{6,7},{8,9},{9,10},{10,11},{11... | collective-permute-start | bytes 491528
  164.4 4.2 %collective-permute-start.1 = (f32[6,5120]{1,0:T(8,128)S(1)}, f32[6,5120]{1,0:T(8,128)S(1)}, u32[]{:S(2)}, u32[]{:S(2)}) collective-permute-start(f32[6,5120]{1,0:T(8,128)S(1)} %slice.10), channel_id=1, source_target_pairs={{0,2},{1,3},{2,4},{3,5},{4,6},{5,7},{8,10},{9,11},{10,12},{11,13},... | collective-permute-start | bytes 368648
  165.9 66.3 %copy-start.14 = (f32[6]{0:T(128)}, f32[6]{0:T(128)S(1)}, u32[]{:S(2)}) copy-start(f32[6]{0:T(128)S(1)} %multiply_add_fusion.1) | copy-start | bytes 76
  169.2 16.5 %copy-start.2 = (f32[22,5120]{1,0:T(8,128)}, f32[22,5120]{1,0:T(8,128)S(1)}, u32[]{:S(2)}) copy-start(f32[22,5120]{1,0:T(8,128)S(1)} %concatenate) | copy-start | bytes 1351684
  178.7 7.0 %copy-start.20 = (f32[6,1024]{1,0:T(8,128)}, f32[6,1024]{1,0:T(8,128)S(1)}, u32[]{:S(2)}) copy-start(f32[6,1024]{1,0:T(8,128)S(1)} %fusion.21) | copy-start | bytes 73732
  200.7 19.5 %copy-start.5 = (f32[4096]{0:T(1024)S(1)}, f32[4096]{0:T(1024)}, u32[]{:S(2)}) copy-start(f32[4096]{0:T(1024)} %param.29) | copy-start | bytes 49156
  200.7 19.6 %copy-start.19 = (f32[6]{0:T(128)S(1)}, f32[6]{0:T(128)}, u32[]{:S(2)}) copy-start(f32[6]{0:T(128)} %param.25) | copy-start | bytes 76
  200.8 63.0 %copy-start = (f32[48,4096]{1,0:T(8,128)S(1)}, f32[48,4096]{1,0:T(8,128)}, u32[]{:S(2)}) copy-start(f32[48,4096]{1,0:T(8,128)} %all-reduce.8.cloned.1.call-done) | copy-start | bytes 2359300
  263.8 45.0 %copy-start.1 = (f32[48,4096]{1,0:T(8,128)S(1)}, f32[48,4096]{1,0:T(8,128)}, u32[]{:S(2)}) copy-start(f32[48,4096]{1,0:T(8,128)} %all-reduce.10.cloned.1.call-done) | copy-start | bytes 2359300
  305.7 5.9 %collective-permute-start.2 = (f32[8,5120]{1,0:T(8,128)S(1)}, f32[8,5120]{1,0:T(8,128)S(1)}, u32[]{:S(2)}, u32[]{:S(2)}) collective-permute-start(f32[8,5120]{1,0:T(8,128)S(1)} %fusion.1), channel_id=1, source_target_pairs={{0,1},{1,2},{2,3},{3,4},{4,5},{5,6},{6,7},{8,9},{9,10},{10,11},{11... | collective-permute-start | bytes 491528
  307.0 4.5 %collective-permute-start.3 = (f32[6,5120]{1,0:T(8,128)S(1)}, f32[6,5120]{1,0:T(8,128)S(1)}, u32[]{:S(2)}, u32[]{:S(2)}) collective-permute-start(f32[6,5120]{1,0:T(8,128)S(1)} %slice.11), channel_id=1, source_target_pairs={{0,2},{1,3},{2,4},{3,5},{4,6},{5,7},{8,10},{9,11},{10,12},{11,13},... | collective-permute-start | bytes 368648
  322.7 19.8 %copy-start.9 = (f32[6,1024]{1,0:T(8,128)}, f32[6,1024]{1,0:T(8,128)S(1)}, u32[]{:S(2)}) copy-start(f32[6,1024]{1,0:T(8,128)S(1)} %get-tuple-element.20) | copy-start | bytes 73732
  341.1 1.4 copy-start.10
Sparse Core Ops, SparseCore 0:
  47.1 55.8 all-reduce.7
  220.4 43.3 all-reduce.9
where the time goes:
time: 355 us; the launch traced here: 350 us
  blocking collectives  172 us (48%)
  matrix products  111 us (31%)
  waiting for transfers between devices  35.6 us (10%)
  between operations  15.6 us (4%)
  other arithmetic  6.88 us (2%)
  starting transfers between devices  5.83 us (2%)
    unnamed x2, blocking collectives  41.4 us
    dot_general x2, matrix products, local(): lax.dot_general(lax.all_gather(inject, 'line', axis=0, tiled=True), shift...  38.9 us
    dot_general x2, matrix products, backward_term(): return jnp.dot(every_res, shift_factors, preferred_element_type=jnp.float32)  37.6 us
    all_gather x1, blocking collectives, local(): lax.all_gather(flow_dual, 'scen', axis=0, tiled=True)  34.7 us
    psum x2, waiting for transfers between devices, local(): flows_now, bal_total = lax.psum((partial_flows, bal_part), 'scen')  31.1 us
    all_gather x1, blocking collectives, local(): lax.all_gather(flow_copy, 'scen', axis=0, tiled=True)  30.3 us
    all_gather x2, blocking collectives, local(): lax.all_gather(inject, 'line', axis=0, tiled=True)  26.4 us
    psum x2, blocking collectives, local(): flows_now, bal_total = lax.psum((partial_flows, bal_part), 'scen')  23.5 us
  transfers between devices with their start and end apart: 6, of which 3 were waited for; matrix products, arithmetic and copies ran while one was open for 1% of the time, Pallas kernels for 0%

commit v1 on v0

v1 whole, which is shorter than its diff:
```python
import functools

import jax
import jax.numpy as jnp
from jax import lax
from jax.experimental import pallas as pl
from jax.experimental.pallas import tpu as pltpu
from jax.sharding import PartitionSpec as P

BUSES = 20480
ITERS = 2
CHUNKS = 1
LANES = 128
BF = jnp.bfloat16
F32 = jnp.float32
WHOLE = pl.BlockSpec(memory_space=pltpu.VMEM)


def call(kernel, args, outs, scratch=(), flops=0):
    size = sum(a.size * a.dtype.itemsize for a in args)
    return pl.pallas_call(
        kernel,
        in_specs=[WHOLE] * len(args),
        out_specs=[WHOLE] * len(outs),
        out_shape=[jax.ShapeDtypeStruct(shape, kind) for shape, kind in outs],
        scratch_shapes=[pltpu.VMEM(shape, kind) for shape, kind in scratch],
        compiler_params=pltpu.CompilerParams(vmem_limit_bytes=10 << 20),
        cost_estimate=pl.CostEstimate(flops=flops, bytes_accessed=size, transcendentals=0),
    )(*args)


def pieces(value):
    high = value.astype(BF)
    rest = value - high.astype(F32)
    middle = rest.astype(BF)
    low = (rest - middle.astype(F32)).astype(BF)
    return high, middle, low


def dot_t(a, b):
    return lax.dot_general(a, b, (((1,), (1,)), ((), ())), preferred_element_type=F32)


class Sizes:
    def __init__(self, mesh, lines, buses, gens, rows):
        self.scen = mesh.shape["scen"]
        self.line = mesh.shape["line"]
        self.chips = self.line // 2
        assert self.chips == self.scen
        self.lines, self.buses, self.gens, self.rows = lines, buses, gens, rows
        self.pair = 2 * rows
        self.total = rows * self.line
        self.stretch = buses // gens
        self.width = self.stretch * LANES
        self.fold = next(f for f in (4, 2, 1) if buses % (f * self.width) == 0)
        self.part = buses // self.fold
        self.chunk = lines // CHUNKS
        self.half = self.chunk // 2


def where_am_i():
    line = lax.axis_index("line")
    return lax.axis_index("scen"), lax.div(line, 2), lax.rem(line, 2)


def place(sz, gens, select, block):
    spread = select[block]
    high, middle, low = pieces(gens)
    return (dot_t(low, spread) + dot_t(middle, spread)) + dot_t(high, spread)


def blocks_of(sz):
    per = sz.part // sz.width
    for block in range(sz.gens // LANES):
        fold, inner = divmod(block, per)
        yield block, slice(fold * sz.rows, (fold + 1) * sz.rows), slice(inner * sz.width, (inner + 1) * sz.width)


def start_kernel(sz, dispatch, shed, loads, gen_bus, inject, shed_p, loads_p, select):
    first = lax.axis_index("scen") * sz.buses
    bus = lax.broadcasted_iota(jnp.int32, (sz.width, LANES), 0)
    for block, rows, cols in blocks_of(sz):
        lanes = slice(block * LANES, (block + 1) * LANES)
        buses = slice(block * sz.width, (block + 1) * sz.width)
        local = gen_bus[:, lanes] - (first + block * sz.width)
        select[block] = (bus == local).astype(F32).astype(BF)
        here, load = shed[:, buses], loads[:, buses]
        inject[rows, cols] = (place(sz, dispatch[:, lanes], select, block) + here - load).astype(BF)
        shed_p[rows, cols] = here
        loads_p[rows, cols] = load


def forward_kernel(sz, chunk, step, *refs):
    chips = sz.chips
    own, other = refs[:chips], refs[chips : 2 * chips]
    factors = refs[2 * chips]
    outs = refs[2 * chips + 1 : 3 * chips + 1]
    inject, flows = refs[3 * chips + 1 :]
    scen, chip, core = where_am_i()
    extra = LANES if chunk == 0 else 0

    def gather(first, second):
        for slot in range(chips):
            for fold in range(sz.fold):
                rows = slice(fold * sz.rows, (fold + 1) * sz.rows)
                cols = slice(fold * sz.part, (fold + 1) * sz.part)
                base = slot * sz.pair
                inject[base : base + sz.rows, cols] = first[slot][rows, :]
                inject[base + sz.rows : base + sz.pair, cols] = second[slot][rows, :]

    @pl.when(core == 0)
    def _():
        gather(own, other)

    @pl.when(core == 1)
    def _():
        gather(other, own)

    if extra:
        total = jnp.sum(inject[...].astype(F32), axis=1, keepdims=True)
        high, middle, low = (piece.astype(F32) for piece in pieces(total))
        lane = lax.broadcasted_iota(jnp.int32, (sz.total, LANES), 1)
        tile = jnp.where(lane == 0, high, jnp.where(lane == 1, middle, jnp.where(lane == 2, low, 0.0)))
        for slot in range(chips):
            flows[slot, :, sz.half :] = jnp.zeros((2 * sz.pair, LANES), F32)
            flows[slot, : sz.pair, sz.half :] = tile[slot * sz.pair : (slot + 1) * sz.pair]
    for side in range(2):

        def body(i, _, side=side):
            source = pl.ds(pl.multiple_of(chunk * sz.chunk + side * sz.half + i * step, step), step)
            target = pl.ds(pl.multiple_of(i * step, step), step)
            product = dot_t(inject[...], factors[source, :])
            for slot in range(chips):
                flows[slot, side * sz.pair : (side + 1) * sz.pair, target] = product[
                    slot * sz.pair : (slot + 1) * sz.pair
                ]
            return 0

        lax.fori_loop(0, sz.half // step, body, 0)
    for away in range(chips):
        found = flows[chip ^ scen ^ away]
        outs[away][...] = found.astype(outs[away].dtype)


def residual_kernel(sz, chunk, join, *refs):
    scen = sz.scen
    parts = refs[:scen]
    copies, duals, limits = refs[scen : scen + 3]
    old = refs[scen + 3 : scen + 5] if join else None
    residual, copy_out, dual_out = refs[-3:]
    total = parts[0][...]
    for part in parts[1:]:
        total = total + part[...].astype(F32)
    for side in range(2):
        rows = slice(side * sz.pair, (side + 1) * sz.pair)
        start = chunk * sz.chunk + side * sz.half
        base = chunk * sz.chunk if copies.shape[1] == sz.lines else 0
        cols = slice(base + side * sz.half, base + (side + 1) * sz.half)
        to = slice(start, start + sz.half) if join else slice(side * sz.half, (side + 1) * sz.half)
        now, copy, dual = total[rows, : sz.half], copies[:, cols], duals[:, cols]
        limit = limits[:, start : start + sz.half]
        residual[rows, : sz.half] = (now - copy + dual).astype(BF)
        copy_next = jnp.minimum(jnp.maximum(now + dual, -limit), limit)
        copy_out[:, to] = copy_next
        dual_out[:, to] = dual + now - copy_next
    if join:
        copy_out[:, : chunk * sz.chunk] = old[0][...]
        dual_out[:, : chunk * sz.chunk] = old[1][...]
    if chunk == 0:
        balance = jnp.sum(total[:, sz.half :], axis=1, keepdims=True) / BUSES
        high, middle, low = (piece.astype(F32) for piece in pieces(balance))
        lane = lax.broadcasted_iota(jnp.int32, (2 * sz.pair, LANES), 1)
        tile = jnp.where(lane == 0, high, jnp.where(lane == 1, middle, jnp.where(lane == 2, low, 0.0)))
        residual[:, sz.half :] = tile.astype(BF)


def backward_kernel(sz, chunk, step, *refs):
    scen = sz.scen
    parts, factors = refs[:scen], refs[scen]
    before = refs[scen + 1] if chunk else None
    last = chunk == CHUNKS - 1
    residual = refs[-1]
    outs = refs[scen + 1 + (chunk > 0) : -1]
    me, chip, core = where_am_i()
    if chunk == 0:
        balances = outs[-1]
        for slot in range(scen):

            @pl.when(chip == (me ^ slot))
            def _(slot=slot):
                tile = parts[slot][: sz.pair, sz.half :].astype(F32)
                found = jnp.sum(tile, axis=1, keepdims=True)
                balances[...] = jnp.broadcast_to(found, (sz.pair, LANES))

    for slot in range(scen):
        for side in range(2):
            residual[slot * sz.pair : (slot + 1) * sz.pair, side * sz.half : (side + 1) * sz.half] = parts[slot][
                side * sz.pair : (side + 1) * sz.pair, : sz.half
            ]

    def body(i, _):
        cols = pl.ds(pl.multiple_of(i * step, step), step)
        product = jnp.dot(
            residual[...],
            factors[chunk * sz.chunk : (chunk + 1) * sz.chunk, cols],
            preferred_element_type=F32,
        )
        if chunk:
            product = before[:, cols] + product
        if not last:
            outs[0][:, cols] = product
            return 0
        kept, sent = outs[:2]
        even = [product[slot * sz.pair : slot * sz.pair + sz.rows] for slot in range(scen)]
        odd = [product[slot * sz.pair + sz.rows : (slot + 1) * sz.pair] for slot in range(scen)]
        even, odd = jnp.concatenate(even, 0), jnp.concatenate(odd, 0)
        kept[:, cols] = jnp.where(core == 0, even, odd)
        sent[:, cols] = jnp.where(core == 0, odd, even).astype(BF)
        return 0

    lax.fori_loop(0, sz.buses // step, body, 0)


def chip_kernel(sz, *refs):
    kept, received = refs[:2]
    outs, packed = refs[2:-1], refs[-1]
    scen, chip, core = where_am_i()
    total = kept[...] + received[...].astype(F32)
    for slot in range(sz.scen):
        for fold in range(sz.fold):
            packed[slot, fold * sz.rows : (fold + 1) * sz.rows, :] = total[
                slot * sz.rows : (slot + 1) * sz.rows, fold * sz.part : (fold + 1) * sz.part
            ]
    for away in range(sz.chips):
        found = packed[scen ^ chip ^ away]
        outs[away][...] = found.astype(outs[away].dtype)


def update_kernel(sz, last, *refs):
    parts = refs[: sz.chips]
    balances, lam, shed, loads, gens, select, costs, dual, previous, cap, commit = refs[sz.chips : sz.chips + 11]
    rest = refs[sz.chips + 11 :]
    core = where_am_i()[2]
    balance = jnp.where(core == 0, balances[: sz.rows, :1], balances[sz.rows :, :1])
    lam_now = lam[:, :1]
    shift = balance + lam_now
    shift = jnp.concatenate([shift] * sz.fold, 0)
    total = parts[0][...]
    for part in parts[1:]:
        total = total + part[...].astype(F32)
    grad = total + shift
    shed_next = jnp.minimum(jnp.maximum(shed[...] - 0.4 * (1.5 + grad), 0.0), loads[...])
    capacity = cap[...] * commit[...].astype(F32)
    if last:
        weights, gens_out, shed_out, lam_out, weighted_out = rest
    else:
        gens_out, shed_out, lam_out, inject = rest
        shed_out[...] = shed_next
    lam_out[...] = jnp.broadcast_to(lam_now + balance, lam_out.shape)
    for block, rows, cols in blocks_of(sz):
        lanes = slice(block * LANES, (block + 1) * LANES)
        spread = select[block]
        high, middle, low = (
            jnp.dot(piece, spread, preferred_element_type=F32) for piece in pieces(grad[rows, cols])
        )
        picked = (low + middle) + high
        now = gens[:, lanes]
        gen_grad = costs[:1, lanes] + costs[1:, lanes] * now + dual[:, lanes] + (now - previous[:, lanes]) + picked
        now = jnp.minimum(jnp.maximum(now - 0.4 * gen_grad, 0.0), capacity[:, lanes])
        gens_out[:, lanes] = now
        if last:
            shed_out[:, block * sz.width : (block + 1) * sz.width] = shed_next[rows, cols]
            weighted_out[:1, lanes] = jnp.sum(weights[:, :1] * now, axis=0, keepdims=True)
            all_weights = jnp.sum(weights[:, :1], axis=0, keepdims=True)
            weighted_out[1:, lanes] = jnp.broadcast_to(all_weights, (7, LANES))
        else:
            inject[rows, cols] = (
                place(sz, now, select, block) + shed_next[rows, cols] - loads[rows, cols]
            ).astype(BF)


def add_kernel(first, second, out):
    out[...] = first[...] + second[...]


def finish_kernel(sz, *refs):
    parts = refs[: sz.chips]
    dual, gens, consensus, dual_out = refs[sz.chips :]
    total = parts[0][...]
    for part in parts[1:]:
        total = total + part[...]
    mean = total[:1] / total[1:2]
    consensus[...] = mean
    dual_out[...] = dual[...] + (gens[...] - mean)


def to_scen(n, away, value):
    return lax.ppermute(value, "scen", [(i, i ^ away) for i in range(n)])


def to_chip(n, away, value):
    return lax.ppermute(value, "line", [(i, i ^ (2 * away)) for i in range(n)])


def to_core(n, value):
    return lax.ppermute(value, "line", [(i, i ^ 1) for i in range(n)])


def local(
    mesh,
    shift_factors,
    gen_bus,
    commit,
    cost_coef,
    gen_cap,
    bus_loads,
    load_shed,
    dispatch,
    ph_dual,
    consensus_prev,
    scen_weight,
    flow_copy,
    flow_dual,
    balance_dual,
    flow_limit,
):
    lines, buses = shift_factors.shape
    rows, gens = dispatch.shape
    sz = Sizes(mesh, lines, buses, gens, rows)
    n_scen, n_line, chips = sz.scen, sz.line, sz.chips
    row = lambda v: v.reshape(1, -1)
    column = lambda v: jnp.broadcast_to(v[:, None], (rows, LANES))
    capacity, on, previous, limits = row(gen_cap), row(commit), row(consensus_prev), row(flow_limit)
    lam, weights = column(balance_dual), column(scen_weight)
    packed = (sz.fold * rows, sz.part)
    step_f = min(512, sz.half)
    step_b = next(s for s in (1024, 640, 512, 256, 128) if buses % s == 0)
    macs = sz.total * sz.chunk * buses

    generation, copies, duals = dispatch, flow_copy, flow_dual
    inject, shed, loads, select = call(
        functools.partial(start_kernel, sz),
        (dispatch, load_shed, bus_loads, row(gen_bus)),
        (
            (packed, BF),
            (packed, F32),
            (packed, F32),
            ((gens // LANES, sz.width, LANES), BF),
        ),
    )
    for iteration in range(ITERS):
        own = [inject] + [to_chip(n_line, away, inject) for away in range(1, chips)]
        other = [to_core(n_line, value) for value in own]
        residuals, new_copies, new_duals = [], [], []
        final = iteration == ITERS - 1
        for chunk in range(CHUNKS):
            block = (2 * sz.pair, sz.half + (LANES if chunk == 0 else 0))
            flows = call(
                functools.partial(forward_kernel, sz, chunk, step_f),
                (*own, *other, shift_factors),
                [(block, F32)] + [(block, BF)] * (chips - 1),
                [((sz.total, buses), BF), ((chips, *block), F32)],
                flops=2 * macs,
            )
            parts = [flows[0]] + [to_scen(n_scen, away, flows[away]) for away in range(1, n_scen)]
            join = final and chunk == CHUNKS - 1 and CHUNKS > 1
            width = lines if join else sz.chunk
            whole = iteration == 0
            residual, copy_next, dual_next = call(
                functools.partial(residual_kernel, sz, chunk, join),
                (
                    *parts,
                    flow_copy if whole else copies[chunk],
                    flow_dual if whole else duals[chunk],
                    limits,
                    *((new_copies[0], new_duals[0]) if join else ()),
                ),
                [(block, BF), ((sz.pair, width), F32), ((sz.pair, width), F32)],
            )
            new_copies.append(copy_next)
            new_duals.append(dual_next)
            residuals.append([residual] + [to_scen(n_scen, away, residual) for away in range(1, n_scen)])
        copies, duals = new_copies, new_duals
        before, balances = (), None
        for chunk in range(CHUNKS):
            last = chunk == CHUNKS - 1
            half = (sz.total // 2, buses)
            outs = [(half, F32), (half, BF)] if last else [((sz.total, buses), F32)]
            if chunk == 0:
                outs.append(((sz.pair, LANES), F32))
            found = call(
                functools.partial(backward_kernel, sz, chunk, step_b),
                (*residuals[chunk], shift_factors, *before),
                outs,
                [((sz.total, sz.chunk), BF)],
                flops=2 * macs,
            )
            if chunk == 0:
                balances = found[-1]
            before = found[:1]
        kept, sent = found[:2]
        sums = call(
            functools.partial(chip_kernel, sz),
            (kept, to_core(n_line, sent)),
            [(packed, F32)] + [(packed, BF)] * (chips - 1),
            [((chips, *packed), F32)],
        )
        parts = [sums[0]] + [to_chip(n_line, away, sums[away]) for away in range(1, chips)]
        args = (*parts, balances, lam, shed, loads, generation, select, cost_coef, ph_dual, previous, capacity, on)
        if not final:
            generation, shed, lam, inject = call(
                functools.partial(update_kernel, sz, False),
                args,
                [((rows, gens), F32), (packed, F32), ((rows, LANES), F32), (packed, BF)],
            )
        else:
            generation, shed, lam, weighted = call(
                functools.partial(update_kernel, sz, True),
                (*args, weights),
                [((rows, gens), F32), ((rows, buses), F32), ((rows, LANES), F32), ((8, gens), F32)],
            )
    (weighted,) = call(add_kernel, (weighted, to_core(n_line, weighted)), [((8, gens), F32)])
    parts = [weighted] + [to_chip(n_line, away, weighted) for away in range(1, chips)]
    consensus, dual_out = call(
        functools.partial(finish_kernel, sz),
        (*parts, ph_dual, generation),
        [((1, gens), F32), ((rows, gens), F32)],
    )
    return generation, shed, copies[-1], duals[-1], lam[:, 0], consensus.reshape(-1), dual_out


def solution(mesh):
    return jax.shard_map(
        functools.partial(local, mesh),
        mesh=mesh,
        in_specs=(
            P("line", "scen"),
            P("scen"),
            P("scen"),
            P(None, "scen"),
            P("scen"),
            P("line", "scen"),
            P("line", "scen"),
            P("line", "scen"),
            P("line", "scen"),
            P("scen"),
            P("line"),
            P("scen", "line"),
            P("scen", "line"),
            P("line"),
            P("line"),
        ),
        out_specs=(
            P("line", "scen"),
            P("line", "scen"),
            P("scen", "line"),
            P("scen", "line"),
            P("line"),
            P("scen"),
            P("line", "scen"),
        ),
        check_vma=False,
    )
```

time: 355 us -> 203 us (0.57); the launches traced: 350 us -> 203 us
  blocking collectives: 172 us -> 0 us
  matrix products: 111 us -> 0 us
  local copies, waits for them, and re-layouts: 2.61 us -> 56.6 us
  Pallas kernels: 0 us -> 51.3 us
  starting transfers between devices: 5.83 us -> 36.6 us
  waiting for transfers between devices: 35.6 us -> 57.2 us
  between operations: 15.6 us -> 0.88 us
  other arithmetic: 6.88 us -> 0 us
    dot_general x8 -> x0, matrix products: 111 us -> none  [the longest x2 38.9 us: local(): lax.dot_general(lax.all_gather(inject, 'line', axis=0, tiled=True), shift...]
    all_gather x4 -> x0, blocking collectives: 91.4 us -> none  [the longest x1 34.7 us: local(): lax.all_gather(flow_dual, 'scen', axis=0, tiled=True)]
    ppermute x0 -> x38, waiting for transfers between devices: none -> 57.2 us  [the longest x12 31.8 us: to_scen(): return lax.ppermute(value, 'scen', [(i, i ^ away) for i in range(n)])]
    unnamed x51 -> x40, local copies, waits for them, and re-layouts: 2.6 us -> 55.8 us
    pallas_call x0 -> x13, Pallas kernels: none -> 51.3 us  [call(): pl.pallas_call(kernel, in_specs=[WHOLE] * len(args), out_specs=[WHOLE] *...]
    unnamed x2 -> x0, blocking collectives: 41.4 us -> none
    psum x3 -> x0, blocking collectives: 39.3 us -> none  [the longest x2 23.5 us: local(): flows_now, bal_total = lax.psum((partial_flows, bal_part), 'scen')]
    ppermute x0 -> x38, starting transfers between devices: none -> 36.6 us  [the longest x15 18.7 us: to_chip(): return lax.ppermute(value, 'line', [(i, i ^ 2 * away) for i in range(n)])]
  transfers between devices with their start and end apart: 6 -> 38, of which waited for: 3 -> 27; matrix products, arithmetic and copies ran while one was open for 1% -> 0% of each run, Pallas kernels for 0% -> 0%
where the time goes in v1:
time: 203 us
  waiting for transfers between devices  57.2 us (28%)
  local copies, waits for them, and re-layouts  56.6 us (28%)
  Pallas kernels  51.3 us (25%)
  starting transfers between devices  36.6 us (18%)
    unnamed x40, local copies, waits for them, and re-layouts  55.8 us
    pallas_call x13, Pallas kernels, call(): pl.pallas_call(kernel, in_specs=[WHOLE] * len(args), out_specs=[WHOLE] *...  51.3 us
    ppermute x12, waiting for transfers between devices, to_scen(): return lax.ppermute(value, 'scen', [(i, i ^ away) for i in range(n)])  31.8 us
    ppermute x15, waiting for transfers between devices, to_chip(): return lax.ppermute(value, 'line', [(i, i ^ 2 * away) for i in range(n)])  18.8 us
    ppermute x15, starting transfers between devices, to_chip(): return lax.ppermute(value, 'line', [(i, i ^ 2 * away) for i in range(n)])  18.7 us
    ppermute x12, starting transfers between devices, to_scen(): return lax.ppermute(value, 'scen', [(i, i ^ away) for i in range(n)])  17.7 us
    ppermute x11, waiting for transfers between devices, to_core(): return lax.ppermute(value, 'line', [(i, i ^ 1) for i in range(n)])  6.67 us
  transfers between devices with their start and end apart: 38, of which 27 were waited for; matrix products, arithmetic and copies ran while one was open for 0% of the time, Pallas kernels for 0%

profile of v1, /device:TPU:0, one launch (start us, length us, event | category | flops | bytes accessed | tf_op | source)
XLA Modules:
  0.0 202.6 jit_solution(17627330077462211705)
XLA Ops:
  5.4 3.0 %collective-permute-start = (bf16[24,1280]{1,0:T(8,128)(2,1)S(1)}, bf16[24,1280]{1,0:T(8,128)(2,1)S(1)}, u32[]{:S(2)}, u32[]{:S(2)}) collective-permute-start(bf16[24,1280]{1,0:T(8,128)(2,1)S(1)} %get-tuple-element.49.refs_0_), channel_id=1, source_target_pairs={{0,2},{1,3},{2,0},{3,1},{4,6},{5,7},{6,4},{7,5},{8,10},{9,11},{10,... | collective-permute-start | bytes 184328 | tf_op jit(solution)/shard_map/ppermute | solution.py:302
  8.4 1.5 collective-permute-start.1
  10.7 2.0 collective-permute-done.1.refs_2_
  12.6 2.4 %collective-permute-done.2.refs_3_ = bf16[24,1280]{1,0:T(8,128)(2,1)S(1)} collective-permute-done((bf16[24,1280]{1,0:T(8,128)(2,1)S(1)}, bf16[24,1280]{1,0:T(8,128)(2,1)S(1)}, u32[]{:S(2)}, u32[]{:S(2)}) %collective-permute-start.2) | collective-permute-done | bytes 61472 | tf_op jit(solution)/shard_map/ppermute | solution.py:302
  16.3 12.9 %copy-done = bf16[4096,5120]{1,0:T(8,128)(2,1)S(1)} copy-done((bf16[4096,5120]{1,0:T(8,128)(2,1)S(1)}, bf16[4096,5120]{1,0:T(8,128)(2,1)}, u32[]{:S(2)}) %copy-start) | copy-done | bytes 41943064
  29.2 13.8 %shard_map.199 = (f32[24,2176]{1,0:T(8,128)S(1)}, bf16[24,2176]{1,0:T(8,128)(2,1)S(1)}, bf16[24,2176]{1,0:T(8,128)(2,1)S(1)}, bf16[24,2176]{1,0:T(8,128)(2,1)S(1)}) custom-call(bf16[24,1280]{1,0:T(8,128)(2,1)S(1)} %get-tuple-element.49.refs_0_, bf16[24,1280]{1,0:T(8,128)(2,1)S(1)} %collective-permute-done.refs_1_, ...), custom_call_target="tpu_custom_call" | custom-call | flops 2013265920 | bytes 42434560 | tf_op jit(solution)/shard_map/pallas_call | solution.py:21
  43.0 1.6 collective-permute-start.7
  44.7 2.6 %collective-permute-start.8 = (bf16[24,2176]{1,0:T(8,128)(2,1)S(1)}, bf16[24,2176]{1,0:T(8,128)(2,1)S(1)}, u32[]{:S(2)}, u32[]{:S(2)}) collective-permute-start(bf16[24,2176]{1,0:T(8,128)(2,1)S(1)} %get-tuple-element.52), channel_id=1, source_target_pairs={{0,16},{8,24},{16,0},{24,8},{1,17},{9,25},{17,1},{25,9},{2,18},{10... | collective-permute-start | bytes 313352 | tf_op jit(solution)/shard_map/ppermute | solution.py:298
  48.1 7.6 %collective-permute-done.8.refs_2_ = bf16[24,2176]{1,0:T(8,128)(2,1)S(1)} collective-permute-done((bf16[24,2176]{1,0:T(8,128)(2,1)S(1)}, bf16[24,2176]{1,0:T(8,128)(2,1)S(1)}, u32[]{:S(2)}, u32[]{:S(2)}) %collective-permute-start.8) | collective-permute-done | bytes 104480 | tf_op jit(solution)/shard_map/ppermute | solution.py:298
  55.9 1.9 collective-permute-start.10
  61.7 6.4 %collective-permute-done.11.refs_2_ = bf16[24,2176]{1,0:T(8,128)(2,1)S(1)} collective-permute-done((bf16[24,2176]{1,0:T(8,128)(2,1)S(1)}, bf16[24,2176]{1,0:T(8,128)(2,1)S(1)}, u32[]{:S(2)}, u32[]{:S(2)}) %collective-permute-start.11) | collective-permute-done | bytes 104480 | tf_op jit(solution)/shard_map/ppermute | solution.py:298
  68.0 12.9 %copy-done.1 = bf16[4096,5120]{1,0:T(8,128)(2,1)S(1)} copy-done((bf16[4096,5120]{1,0:T(8,128)(2,1)S(1)}, bf16[4096,5120]{1,0:T(8,128)(2,1)}, u32[]{:S(2)}) %copy-start.1) | copy-done | bytes 41943064
  81.0 8.0 %shard_map.201 = (f32[24,5120]{1,0:T(8,128)S(1)}, bf16[24,5120]{1,0:T(8,128)(2,1)S(1)}, f32[12,128]{1,0:T(8,128)S(1)}) custom-call(bf16[24,2176]{1,0:T(8,128)(2,1)S(1)} %get-tuple-element.54.refs_0_, bf16[24,2176]{1,0:T(8,128)(2,1)S(1)} %collective-permute-done.10.refs_1_, bf16[24,2176]{1,0:T(8,128)(2,1)S(1)} %collective-permute-done.11.refs_2_, ...), custom_call_target="tpu_custom_call" | custom-call | flops 2013265920 | bytes 42360832 | tf_op jit(solution)/shard_map/pallas_call | solution.py:21
  89.1 1.5 collective-permute-done.13.refs_1_
  91.8 2.5 %collective-permute-start.16 = (bf16[24,1280]{1,0:T(8,128)(2,1)S(1)}, bf16[24,1280]{1,0:T(8,128)(2,1)S(1)}, u32[]{:S(2)}, u32[]{:S(2)}) collective-permute-start(bf16[24,1280]{1,0:T(8,128)(2,1)S(1)} %get-tuple-element.60), channel_id=1, source_target_pairs={{0,6},{1,7},{2,4},{3,5},{4,2},{5,3},{6,0},{7,1},{8,14},{9,15},{10,... | collective-permute-start | bytes 184328 | tf_op jit(solution)/shard_map/ppermute | solution.py:302
  97.0 2.8 %shard_map.203 = (f32[6,1024]{1,0:T(8,128)S(1)}, f32[24,1280]{1,0:T(8,128)S(1)}, f32[6,128]{1,0:T(8,128)S(1)}, bf16[24,1280]{1,0:T(8,128)(2,1)S(1)}) custom-call(f32[24,1280]{1,0:T(8,128)S(1)} %get-tuple-element.57.refs_0_, bf16[24,1280]{1,0:T(8,128)(2,1)S(1)} %collective-permute-done.14.refs_1_, bf16[24,1280]{1,0:T(8,128)(2,1)S(1)} %collective-permute-done.15.refs_2_, ...), custom_call_target="tpu_custom_call" | custom-call | bytes 1942528 | tf_op jit(solution)/shard_map/pallas_call | solution.py:21
  99.9 1.6 collective-permute-start.17
  101.4 1.5 collective-permute-start.18
  105.9 2.2 %collective-permute-done.19.refs_3_ = bf16[24,1280]{1,0:T(8,128)(2,1)S(1)} collective-permute-done((bf16[24,1280]{1,0:T(8,128)(2,1)S(1)}, bf16[24,1280]{1,0:T(8,128)(2,1)S(1)}, u32[]{:S(2)}, u32[]{:S(2)}) %collective-permute-start.19) | collective-permute-done | bytes 61472 | tf_op jit(solution)/shard_map/ppermute | solution.py:302
  109.3 12.9 %copy-done.2 = bf16[4096,5120]{1,0:T(8,128)(2,1)S(1)} copy-done((bf16[4096,5120]{1,0:T(8,128)(2,1)S(1)}, bf16[4096,5120]{1,0:T(8,128)(2,1)}, u32[]{:S(2)}) %copy-start.2) | copy-done | bytes 41943064
  122.3 13.8 %shard_map.204 = (f32[24,2176]{1,0:T(8,128)S(1)}, bf16[24,2176]{1,0:T(8,128)(2,1)S(1)}, bf16[24,2176]{1,0:T(8,128)(2,1)S(1)}, bf16[24,2176]{1,0:T(8,128)(2,1)S(1)}) custom-call(bf16[24,1280]{1,0:T(8,128)(2,1)S(1)} %get-tuple-element.65.refs_0_, bf16[24,1280]{1,0:T(8,128)(2,1)S(1)} %collective-permute-done.17.refs_1_, ...), custom_call_target="tpu_custom_call" | custom-call | flops 2013265920 | bytes 42434560 | tf_op jit(solution)/shard_map/pallas_call | solution.py:21
  136.1 1.7 collective-permute-start.24
  138.7 1.8 collective-permute-start.26
  141.1 7.9 %collective-permute-done.25.refs_2_ = bf16[24,2176]{1,0:T(8,128)(2,1)S(1)} collective-permute-done((bf16[24,2176]{1,0:T(8,128)(2,1)S(1)}, bf16[24,2176]{1,0:T(8,128)(2,1)S(1)}, u32[]{:S(2)}, u32[]{:S(2)}) %collective-permute-start.25) | collective-permute-done | bytes 104480 | tf_op jit(solution)/shard_map/ppermute | solution.py:298
  150.0 1.7 collective-permute-start.27
  152.5 1.9 collective-permute-start.29
  155.8 6.0 %collective-permute-done.28.refs_2_ = bf16[24,2176]{1,0:T(8,128)(2,1)S(1)} collective-permute-done((bf16[24,2176]{1,0:T(8,128)(2,1)S(1)}, bf16[24,2176]{1,0:T(8,128)(2,1)S(1)}, u32[]{:S(2)}, u32[]{:S(2)}) %collective-permute-start.28) | collective-permute-done | bytes 104480 | tf_op jit(solution)/shard_map/ppermute | solution.py:298
  161.8 12.9 %copy-done.3 = bf16[4096,5120]{1,0:T(8,128)(2,1)S(1)} copy-done((bf16[4096,5120]{1,0:T(8,128)(2,1)S(1)}, bf16[4096,5120]{1,0:T(8,128)(2,1)}, u32[]{:S(2)}) %copy-start.3) | copy-done | bytes 41943064
  174.7 8.0 %shard_map.206 = (f32[24,5120]{1,0:T(8,128)S(1)}, bf16[24,5120]{1,0:T(8,128)(2,1)S(1)}, f32[12,128]{1,0:T(8,128)S(1)}) custom-call(bf16[24,2176]{1,0:T(8,128)(2,1)S(1)} %get-tuple-element.72.refs_0_, bf16[24,2176]{1,0:T(8,128)(2,1)S(1)} %collective-permute-done.27.refs_1_, bf16[24,2176]{1,0:T(8,128)(2,1)S(1)} %collective-permute-done.28.refs_2_, ...), custom_call_target="tpu_custom_call" | custom-call | flops 2013265920 | bytes 42360832 | tf_op jit(solution)/shard_map/pallas_call | solution.py:21
  185.5 2.5 %collective-permute-start.33 = (bf16[24,1280]{1,0:T(8,128)(2,1)S(1)}, bf16[24,1280]{1,0:T(8,128)(2,1)S(1)}, u32[]{:S(2)}, u32[]{:S(2)}) collective-permute-start(bf16[24,1280]{1,0:T(8,128)(2,1)S(1)} %get-tuple-element.78), channel_id=1, source_target_pairs={{0,6},{1,7},{2,4},{3,5},{4,2},{5,3},{6,0},{7,1},{8,14},{9,15},{10,... | collective-permute-start | bytes 184328 | tf_op jit(solution)/shard_map/ppermute | solution.py:302
  194.9 1.5 collective-permute-start.36
  198.8 2.4 %collective-permute-done.37.refs_3_ = f32[8,1024]{1,0:T(8,128)S(1)} collective-permute-done((f32[8,1024]{1,0:T(8,128)S(1)}, f32[8,1024]{1,0:T(8,128)S(1)}, u32[]{:S(2)}, u32[]{:S(2)}) %collective-permute-start.37) | collective-permute-done | bytes 32800 | tf_op jit(solution)/shard_map/ppermute | solution.py:302
  (100 shorter events, 38.0 us)
Async XLA Ops:
  5.4 5.3 %collective-permute-start = (bf16[24,1280]{1,0:T(8,128)(2,1)S(1)}, bf16[24,1280]{1,0:T(8,128)(2,1)S(1)}, u32[]{:S(2)}, u32[]{:S(2)}) collective-permute-start(bf16[24,1280]{1,0:T(8,128)(2,1)S(1)} %get-tuple-element.49.refs_0_), channel_id=1, source_target_pairs={{0,2},{1,3},{2,0},{3,1},{4,6},{5,7},{6,4},{7,5},{8,10},{9,11},{10,... | collective-permute-start | bytes 184328 | tf_op jit(solution)/shard_map/ppermute | solution.py:302
  8.4 4.2 %collective-permute-start.1 = (bf16[24,1280]{1,0:T(8,128)(2,1)S(1)}, bf16[24,1280]{1,0:T(8,128)(2,1)S(1)}, u32[]{:S(2)}, u32[]{:S(2)}) collective-permute-start(bf16[24,1280]{1,0:T(8,128)(2,1)S(1)} %get-tuple-element.49.refs_0_), channel_id=1, source_target_pairs={{0,4},{1,5},{2,6},{3,7},{4,0},{5,1},{6,2},{7,3},{8,12},{9,13},{10,... | collective-permute-start | bytes 184328 | tf_op jit(solution)/shard_map/ppermute | solution.py:302
  9.9 5.1 %collective-permute-start.2 = (bf16[24,1280]{1,0:T(8,128)(2,1)S(1)}, bf16[24,1280]{1,0:T(8,128)(2,1)S(1)}, u32[]{:S(2)}, u32[]{:S(2)}) collective-permute-start(bf16[24,1280]{1,0:T(8,128)(2,1)S(1)} %get-tuple-element.49.refs_0_), channel_id=1, source_target_pairs={{0,6},{1,7},{2,4},{3,5},{4,2},{5,3},{6,0},{7,1},{8,14},{9,15},{10,... | collective-permute-start | bytes 184328 | tf_op jit(solution)/shard_map/ppermute | solution.py:302
  9.9 5.1 %collective-permute-start.3 = (bf16[24,1280]{1,0:T(8,128)(2,1)S(1)}, bf16[24,1280]{1,0:T(8,128)(2,1)S(1)}, u32[]{:S(2)}, u32[]{:S(2)}) collective-permute-start(bf16[24,1280]{1,0:T(8,128)(2,1)S(1)} %get-tuple-element.49.refs_0_), channel_id=1, source_target_pairs={{0,1},{1,0},{2,3},{3,2},{4,5},{5,4},{6,7},{7,6},{8,9},{9,8},{10,11... | collective-permute-start | bytes 184328 | tf_op jit(solution)/shard_map/ppermute | solution.py:306
  10.7 4.4 %collective-permute-start.4 = (bf16[24,1280]{1,0:T(8,128)(2,1)S(1)}, bf16[24,1280]{1,0:T(8,128)(2,1)S(1)}, u32[]{:S(2)}, u32[]{:S(2)}) collective-permute-start(bf16[24,1280]{1,0:T(8,128)(2,1)S(1)} %collective-permute-done.refs_1_), channel_id=1, source_target_pairs={{0,1},{1,0},{2,3},{3,2},{4,5},{5,4},{6,7},{7,6},{8,9},{9,8},{10,11... | collective-permute-start | bytes 184328 | tf_op jit(solution)/shard_map/ppermute | solution.py:306
  12.6 2.4 %collective-permute-start.5 = (bf16[24,1280]{1,0:T(8,128)(2,1)S(1)}, bf16[24,1280]{1,0:T(8,128)(2,1)S(1)}, u32[]{:S(2)}, u32[]{:S(2)}) collective-permute-start(bf16[24,1280]{1,0:T(8,128)(2,1)S(1)} %collective-permute-done.1.refs_2_), channel_id=1, source_target_pairs={{0,1},{1,0},{2,3},{3,2},{4,5},{5,4},{6,7},{7,6},{8,9},{9,8},{10,11... | collective-permute-start | bytes 184328 | tf_op jit(solution)/shard_map/ppermute | solution.py:306
  43.0 5.1 %collective-permute-start.7 = (bf16[24,2176]{1,0:T(8,128)(2,1)S(1)}, bf16[24,2176]{1,0:T(8,128)(2,1)S(1)}, u32[]{:S(2)}, u32[]{:S(2)}) collective-permute-start(bf16[24,2176]{1,0:T(8,128)(2,1)S(1)} %get-tuple-element.51), channel_id=1, source_target_pairs={{0,8},{8,0},{16,24},{24,16},{1,9},{9,1},{17,25},{25,17},{2,10},{10... | collective-permute-start | bytes 313352 | tf_op jit(solution)/shard_map/ppermute | solution.py:298
  44.7 11.0 %collective-permute-start.8 = (bf16[24,2176]{1,0:T(8,128)(2,1)S(1)}, bf16[24,2176]{1,0:T(8,128)(2,1)S(1)}, u32[]{:S(2)}, u32[]{:S(2)}) collective-permute-start(bf16[24,2176]{1,0:T(8,128)(2,1)S(1)} %get-tuple-element.52), channel_id=1, source_target_pairs={{0,16},{8,24},{16,0},{24,8},{1,17},{9,25},{17,1},{25,9},{2,18},{10... | collective-permute-start | bytes 313352 | tf_op jit(solution)/shard_map/ppermute | solution.py:298
  47.3 8.4 %collective-permute-start.9 = (bf16[24,2176]{1,0:T(8,128)(2,1)S(1)}, bf16[24,2176]{1,0:T(8,128)(2,1)S(1)}, u32[]{:S(2)}, u32[]{:S(2)}) collective-permute-start(bf16[24,2176]{1,0:T(8,128)(2,1)S(1)} %get-tuple-element.53), channel_id=1, source_target_pairs={{0,24},{8,16},{16,8},{24,0},{1,25},{9,17},{17,9},{25,1},{2,26},{10... | collective-permute-start | bytes 313352 | tf_op jit(solution)/shard_map/ppermute | solution.py:298
  55.9 5.7 %collective-permute-start.10 = (bf16[24,2176]{1,0:T(8,128)(2,1)S(1)}, bf16[24,2176]{1,0:T(8,128)(2,1)S(1)}, u32[]{:S(2)}, u32[]{:S(2)}) collective-permute-start(bf16[24,2176]{1,0:T(8,128)(2,1)S(1)} %get-tuple-element.54.refs_0_), channel_id=1, source_target_pairs={{0,8},{8,0},{16,24},{24,16},{1,9},{9,1},{17,25},{25,17},{2,10},{10... | collective-permute-start | bytes 313352 | tf_op jit(solution)/shard_map/ppermute | solution.py:298
  57.8 10.2 %collective-permute-start.11 = (bf16[24,2176]{1,0:T(8,128)(2,1)S(1)}, bf16[24,2176]{1,0:T(8,128)(2,1)S(1)}, u32[]{:S(2)}, u32[]{:S(2)}) collective-permute-start(bf16[24,2176]{1,0:T(8,128)(2,1)S(1)} %get-tuple-element.54.refs_0_), channel_id=1, source_target_pairs={{0,16},{8,24},{16,0},{24,8},{1,17},{9,25},{17,1},{25,9},{2,18},{10... | collective-permute-start | bytes 313352 | tf_op jit(solution)/shard_map/ppermute | solution.py:298
  59.2 8.9 %collective-permute-start.12 = (bf16[24,2176]{1,0:T(8,128)(2,1)S(1)}, bf16[24,2176]{1,0:T(8,128)(2,1)S(1)}, u32[]{:S(2)}, u32[]{:S(2)}) collective-permute-start(bf16[24,2176]{1,0:T(8,128)(2,1)S(1)} %get-tuple-element.54.refs_0_), channel_id=1, source_target_pairs={{0,24},{8,16},{16,8},{24,0},{1,25},{9,17},{17,9},{25,1},{2,26},{10... | collective-permute-start | bytes 313352 | tf_op jit(solution)/shard_map/ppermute | solution.py:298
  90.7 4.4 %collective-permute-start.14 = (bf16[24,1280]{1,0:T(8,128)(2,1)S(1)}, bf16[24,1280]{1,0:T(8,128)(2,1)S(1)}, u32[]{:S(2)}, u32[]{:S(2)}) collective-permute-start(bf16[24,1280]{1,0:T(8,128)(2,1)S(1)} %get-tuple-element.58), channel_id=1, source_target_pairs={{0,2},{1,3},{2,0},{3,1},{4,6},{5,7},{6,4},{7,5},{8,10},{9,11},{10,... | collective-permute-start | bytes 184328 | tf_op jit(solution)/shard_map/ppermute | solution.py:302
  91.3 4.9 %collective-permute-start.15 = (bf16[24,1280]{1,0:T(8,128)(2,1)S(1)}, bf16[24,1280]{1,0:T(8,128)(2,1)S(1)}, u32[]{:S(2)}, u32[]{:S(2)}) collective-permute-start(bf16[24,1280]{1,0:T(8,128)(2,1)S(1)} %get-tuple-element.59), channel_id=1, source_target_pairs={{0,4},{1,5},{2,6},{3,7},{4,0},{5,1},{6,2},{7,3},{8,12},{9,13},{10,... | collective-permute-start | bytes 184328 | tf_op jit(solution)/shard_map/ppermute | solution.py:302
  91.8 5.1 %collective-permute-start.16 = (bf16[24,1280]{1,0:T(8,128)(2,1)S(1)}, bf16[24,1280]{1,0:T(8,128)(2,1)S(1)}, u32[]{:S(2)}, u32[]{:S(2)}) collective-permute-start(bf16[24,1280]{1,0:T(8,128)(2,1)S(1)} %get-tuple-element.60), channel_id=1, source_target_pairs={{0,6},{1,7},{2,4},{3,5},{4,2},{5,3},{6,0},{7,1},{8,14},{9,15},{10,... | collective-permute-start | bytes 184328 | tf_op jit(solution)/shard_map/ppermute | solution.py:302
  99.9 4.9 %collective-permute-start.17 = (bf16[24,1280]{1,0:T(8,128)(2,1)S(1)}, bf16[24,1280]{1,0:T(8,128)(2,1)S(1)}, u32[]{:S(2)}, u32[]{:S(2)}) collective-permute-start(bf16[24,1280]{1,0:T(8,128)(2,1)S(1)} %get-tuple-element.65.refs_0_), channel_id=1, source_target_pairs={{0,2},{1,3},{2,0},{3,1},{4,6},{5,7},{6,4},{7,5},{8,10},{9,11},{10,... | collective-permute-start | bytes 184328 | tf_op jit(solution)/shard_map/ppermute | solution.py:302
  101.4 4.5 %collective-permute-start.18 = (bf16[24,1280]{1,0:T(8,128)(2,1)S(1)}, bf16[24,1280]{1,0:T(8,128)(2,1)S(1)}, u32[]{:S(2)}, u32[]{:S(2)}) collective-permute-start(bf16[24,1280]{1,0:T(8,128)(2,1)S(1)} %get-tuple-element.65.refs_0_), channel_id=1, source_target_pairs={{0,4},{1,5},{2,6},{3,7},{4,0},{5,1},{6,2},{7,3},{8,12},{9,13},{10,... | collective-permute-start | bytes 184328 | tf_op jit(solution)/shard_map/ppermute | solution.py:302
  103.0 5.1 %collective-permute-start.19 = (bf16[24,1280]{1,0:T(8,128)(2,1)S(1)}, bf16[24,1280]{1,0:T(8,128)(2,1)S(1)}, u32[]{:S(2)}, u32[]{:S(2)}) collective-permute-start(bf16[24,1280]{1,0:T(8,128)(2,1)S(1)} %get-tuple-element.65.refs_0_), channel_id=1, source_target_pairs={{0,6},{1,7},{2,4},{3,5},{4,2},{5,3},{6,0},{7,1},{8,14},{9,15},{10,... | collective-permute-start | bytes 184328 | tf_op jit(solution)/shard_map/ppermute | solution.py:302
  103.4 4.7 %collective-permute-start.20 = (bf16[24,1280]{1,0:T(8,128)(2,1)S(1)}, bf16[24,1280]{1,0:T(8,128)(2,1)S(1)}, u32[]{:S(2)}, u32[]{:S(2)}) collective-permute-start(bf16[24,1280]{1,0:T(8,128)(2,1)S(1)} %get-tuple-element.65.refs_0_), channel_id=1, source_target_pairs={{0,1},{1,0},{2,3},{3,2},{4,5},{5,4},{6,7},{7,6},{8,9},{9,8},{10,11... | collective-permute-start | bytes 184328 | tf_op jit(solution)/shard_map/ppermute | solution.py:306
  104.8 3.3 %collective-permute-start.21 = (bf16[24,1280]{1,0:T(8,128)(2,1)S(1)}, bf16[24,1280]{1,0:T(8,128)(2,1)S(1)}, u32[]{:S(2)}, u32[]{:S(2)}) collective-permute-start(bf16[24,1280]{1,0:T(8,128)(2,1)S(1)} %collective-permute-done.17.refs_1_), channel_id=1, source_target_pairs={{0,1},{1,0},{2,3},{3,2},{4,5},{5,4},{6,7},{7,6},{8,9},{9,8},{10,11... | collective-permute-start | bytes 184328 | tf_op jit(solution)/shard_map/ppermute | solution.py:306
  136.1 5.1 %collective-permute-start.24 = (bf16[24,2176]{1,0:T(8,128)(2,1)S(1)}, bf16[24,2176]{1,0:T(8,128)(2,1)S(1)}, u32[]{:S(2)}, u32[]{:S(2)}) collective-permute-start(bf16[24,2176]{1,0:T(8,128)(2,1)S(1)} %get-tuple-element.67), channel_id=1, source_target_pairs={{0,8},{8,0},{16,24},{24,16},{1,9},{9,1},{17,25},{25,17},{2,10},{10... | collective-permute-start | bytes 313352 | tf_op jit(solution)/shard_map/ppermute | solution.py:298
  137.8 11.2 %collective-permute-start.25 = (bf16[24,2176]{1,0:T(8,128)(2,1)S(1)}, bf16[24,2176]{1,0:T(8,128)(2,1)S(1)}, u32[]{:S(2)}, u32[]{:S(2)}) collective-permute-start(bf16[24,2176]{1,0:T(8,128)(2,1)S(1)} %get-tuple-element.68), channel_id=1, source_target_pairs={{0,16},{8,24},{16,0},{24,8},{1,17},{9,25},{17,1},{25,9},{2,18},{10... | collective-permute-start | bytes 313352 | tf_op jit(solution)/shard_map/ppermute | solution.py:298
  138.7 10.3 %collective-permute-start.26 = (bf16[24,2176]{1,0:T(8,128)(2,1)S(1)}, bf16[24,2176]{1,0:T(8,128)(2,1)S(1)}, u32[]{:S(2)}, u32[]{:S(2)}) collective-permute-start(bf16[24,2176]{1,0:T(8,128)(2,1)S(1)} %get-tuple-element.69), channel_id=1, source_target_pairs={{0,24},{8,16},{16,8},{24,0},{1,25},{9,17},{17,9},{25,1},{2,26},{10... | collective-permute-start | bytes 313352 | tf_op jit(solution)/shard_map/ppermute | solution.py:298
  150.0 5.8 %collective-permute-start.27 = (bf16[24,2176]{1,0:T(8,128)(2,1)S(1)}, bf16[24,2176]{1,0:T(8,128)(2,1)S(1)}, u32[]{:S(2)}, u32[]{:S(2)}) collective-permute-start(bf16[24,2176]{1,0:T(8,128)(2,1)S(1)} %get-tuple-element.72.refs_0_), channel_id=1, source_target_pairs={{0,8},{8,0},{16,24},{24,16},{1,9},{9,1},{17,25},{25,17},{2,10},{10... | collective-permute-start | bytes 313352 | tf_op jit(solution)/shard_map/ppermute | solution.py:298
  151.7 10.1 %collective-permute-start.28 = (bf16[24,2176]{1,0:T(8,128)(2,1)S(1)}, bf16[24,2176]{1,0:T(8,128)(2,1)S(1)}, u32[]{:S(2)}, u32[]{:S(2)}) collective-permute-start(bf16[24,2176]{1,0:T(8,128)(2,1)S(1)} %get-tuple-element.72.refs_0_), channel_id=1, source_target_pairs={{0,16},{8,24},{16,0},{24,8},{1,17},{9,25},{17,1},{25,9},{2,18},{10... | collective-permute-start | bytes 313352 | tf_op jit(solution)/shard_map/ppermute | solution.py:298
  152.5 9.3 %collective-permute-start.29 = (bf16[24,2176]{1,0:T(8,128)(2,1)S(1)}, bf16[24,2176]{1,0:T(8,128)(2,1)S(1)}, u32[]{:S(2)}, u32[]{:S(2)}) collective-permute-start(bf16[24,2176]{1,0:T(8,128)(2,1)S(1)} %get-tuple-element.72.refs_0_), channel_id=1, source_target_pairs={{0,24},{8,16},{16,8},{24,0},{1,25},{9,17},{17,9},{25,1},{2,26},{10... | collective-permute-start | bytes 313352 | tf_op jit(solution)/shard_map/ppermute | solution.py:298
  184.4 4.4 %collective-permute-start.31 = (bf16[24,1280]{1,0:T(8,128)(2,1)S(1)}, bf16[24,1280]{1,0:T(8,128)(2,1)S(1)}, u32[]{:S(2)}, u32[]{:S(2)}) collective-permute-start(bf16[24,1280]{1,0:T(8,128)(2,1)S(1)} %get-tuple-element.76), channel_id=1, source_target_pairs={{0,2},{1,3},{2,0},{3,1},{4,6},{5,7},{6,4},{7,5},{8,10},{9,11},{10,... | collective-permute-start | bytes 184328 | tf_op jit(solution)/shard_map/ppermute | solution.py:302
  185.0 4.9 %collective-permute-start.32 = (bf16[24,1280]{1,0:T(8,128)(2,1)S(1)}, bf16[24,1280]{1,0:T(8,128)(2,1)S(1)}, u32[]{:S(2)}, u32[]{:S(2)}) collective-permute-start(bf16[24,1280]{1,0:T(8,128)(2,1)S(1)} %get-tuple-element.77), channel_id=1, source_target_pairs={{0,4},{1,5},{2,6},{3,7},{4,0},{5,1},{6,2},{7,3},{8,12},{9,13},{10,... | collective-permute-start | bytes 184328 | tf_op jit(solution)/shard_map/ppermute | solution.py:302
  185.5 5.1 %collective-permute-start.33 = (bf16[24,1280]{1,0:T(8,128)(2,1)S(1)}, bf16[24,1280]{1,0:T(8,128)(2,1)S(1)}, u32[]{:S(2)}, u32[]{:S(2)}) collective-permute-start(bf16[24,1280]{1,0:T(8,128)(2,1)S(1)} %get-tuple-element.78), channel_id=1, source_target_pairs={{0,6},{1,7},{2,4},{3,5},{4,2},{5,3},{6,0},{7,1},{8,14},{9,15},{10,... | collective-permute-start | bytes 184328 | tf_op jit(solution)/shard_map/ppermute | solution.py:302
  193.4 4.1 %collective-permute-start.35 = (f32[8,1024]{1,0:T(8,128)S(1)}, f32[8,1024]{1,0:T(8,128)S(1)}, u32[]{:S(2)}, u32[]{:S(2)}) collective-permute-start(f32[8,1024]{1,0:T(8,128)S(1)} %shard_map.209.refs_0_), channel_id=1, source_target_pairs={{0,2},{1,3},{2,0},{3,1},{4,6},{5,7},{6,4},{7,5},{8,10},{9,11},{10,... | collective-permute-start | bytes 98312 | tf_op jit(solution)/shard_map/ppermute | solution.py:302
  194.9 3.9 %collective-permute-start.36 = (f32[8,1024]{1,0:T(8,128)S(1)}, f32[8,1024]{1,0:T(8,128)S(1)}, u32[]{:S(2)}, u32[]{:S(2)}) collective-permute-start(f32[8,1024]{1,0:T(8,128)S(1)} %shard_map.209.refs_0_), channel_id=1, source_target_pairs={{0,4},{1,5},{2,6},{3,7},{4,0},{5,1},{6,2},{7,3},{8,12},{9,13},{10,... | collective-permute-start | bytes 98312 | tf_op jit(solution)/shard_map/ppermute | solution.py:302
  196.4 4.8 %collective-permute-start.37 = (f32[8,1024]{1,0:T(8,128)S(1)}, f32[8,1024]{1,0:T(8,128)S(1)}, u32[]{:S(2)}, u32[]{:S(2)}) collective-permute-start(f32[8,1024]{1,0:T(8,128)S(1)} %shard_map.209.refs_0_), channel_id=1, source_target_pairs={{0,6},{1,7},{2,4},{3,5},{4,2},{5,3},{6,0},{7,1},{8,14},{9,15},{10,... | collective-permute-start | bytes 98312 | tf_op jit(solution)/shard_map/ppermute | solution.py:302
  (26 other events, 938.7 us)

commit v2 on v1

--- a/solution.py
+++ b/solution.py
@@ -1,4 +1,5 @@
 import functools
+import math
 
 import jax
 import jax.numpy as jnp
@@ -11,22 +12,31 @@
 ITERS = 2
 CHUNKS = 1
 LANES = 128
+GRANT = 11 << 20
 BF = jnp.bfloat16
 F32 = jnp.float32
 WHOLE = pl.BlockSpec(memory_space=pltpu.VMEM)
 
 
-def call(kernel, args, outs, scratch=(), flops=0):
+def call(kernel, args, outs, scratch=(), flops=0, keep=None, limit=GRANT):
     size = sum(a.size * a.dtype.itemsize for a in args)
+    if keep is not None:
+        inner, args = kernel, (keep, *args)
+        kernel = lambda kept, *refs: inner(*refs)
     return pl.pallas_call(
         kernel,
         in_specs=[WHOLE] * len(args),
         out_specs=[WHOLE] * len(outs),
         out_shape=[jax.ShapeDtypeStruct(shape, kind) for shape, kind in outs],
         scratch_shapes=[pltpu.VMEM(shape, kind) for shape, kind in scratch],
-        compiler_params=pltpu.CompilerParams(vmem_limit_bytes=10 << 20),
+        compiler_params=pltpu.CompilerParams(vmem_limit_bytes=limit),
         cost_estimate=pl.CostEstimate(flops=flops, bytes_accessed=size, transcendentals=0),
     )(*args)
+
+
+def nbytes(arrays):
+    size = lambda a: math.prod(a.shape[:-2]) * -(-a.shape[-2] // 8) * 8 * a.shape[-1] * a.dtype.itemsize
+    return sum(size(a) for a in arrays)
 
 
 def pieces(value):
@@ -347,6 +357,7 @@
             (packed, F32),
             ((gens // LANES, sz.width, LANES), BF),
         ),
+        limit=GRANT + lines * buses * 2,
     )
     for iteration in range(ITERS):
         own = [inject] + [to_chip(n_line, away, inject) for away in range(1, chips)]
@@ -361,6 +372,7 @@
                 [(block, F32)] + [(block, BF)] * (chips - 1),
                 [((sz.total, buses), BF), ((chips, *block), F32)],
                 flops=2 * macs,
+                limit=GRANT - (nbytes(own + other) if iteration == 0 else 0),
             )
             parts = [flows[0]] + [to_scen(n_scen, away, flows[away]) for away in range(1, n_scen)]
             join = final and chunk == CHUNKS - 1 and CHUNKS > 1
@@ -376,6 +388,7 @@
                     *((new_copies[0], new_duals[0]) if join else ()),
                 ),
                 [(block, BF), ((sz.pair, width), F32), ((sz.pair, width), F32)],
+                keep=shift_factors,
             )
             new_copies.append(copy_next)
             new_duals.append(dual_next)
@@ -404,6 +417,7 @@
             (kept, to_core(n_line, sent)),
             [(packed, F32)] + [(packed, BF)] * (chips - 1),
             [((chips, *packed), F32)],
+            keep=None if final else shift_factors,
         )
         parts = [sums[0]] + [to_chip(n_line, away, sums[away]) for away in range(1, chips)]
         args = (*parts, balances, lam, shed, loads, generation, select, cost_coef, ph_dual, previous, capacity, on)
@@ -412,6 +426,8 @@
                 functools.partial(update_kernel, sz, False),
                 args,
                 [((rows, gens), F32), (packed, F32), ((rows, LANES), F32), (packed, BF)],
+                keep=shift_factors,
+                limit=GRANT - nbytes((dispatch, shed, loads, select)),
             )
         else:
             generation, shed, lam, weighted = call(

time: 203 us -> 164 us (0.81)
  local copies, waits for them, and re-layouts: 56.6 us -> 17.8 us
    unnamed x40 -> x34, local copies, waits for them, and re-layouts: 55.8 us -> 17.1 us
where the time goes in v2:
time: 164 us
  waiting for transfers between devices  57.2 us (35%)
  Pallas kernels  51.4 us (31%)
  starting transfers between devices  36.6 us (22%)
  local copies, waits for them, and re-layouts  17.8 us (11%)
    pallas_call x13, Pallas kernels, call(): pl.pallas_call(kernel, in_specs=[WHOLE] * len(args), out_specs=[WHOLE] *...  51.4 us
    ppermute x12, waiting for transfers between devices, to_scen(): return lax.ppermute(value, 'scen', [(i, i ^ away) for i in range(n)])  31.8 us
    ppermute x15, waiting for transfers between devices, to_chip(): return lax.ppermute(value, 'line', [(i, i ^ 2 * away) for i in range(n)])  18.8 us
    ppermute x15, starting transfers between devices, to_chip(): return lax.ppermute(value, 'line', [(i, i ^ 2 * away) for i in range(n)])  18.7 us
    ppermute x12, starting transfers between devices, to_scen(): return lax.ppermute(value, 'scen', [(i, i ^ away) for i in range(n)])  17.7 us
    unnamed x34, local copies, waits for them, and re-layouts  17.1 us
    ppermute x11, waiting for transfers between devices, to_core(): return lax.ppermute(value, 'line', [(i, i ^ 1) for i in range(n)])  6.67 us
  transfers between devices with their start and end apart: 38, of which 27 were waited for; matrix products, arithmetic and copies ran while one was open for 0% of the time, Pallas kernels for 0%

profile of v2, /device:TPU:0, one launch (start us, length us, event | category | flops | bytes accessed | tf_op | source)
XLA Modules:
  0.0 163.9 jit_solution(10154683715488532430)
XLA Ops:
  5.3 3.0 %collective-permute-start = (bf16[24,1280]{1,0:T(8,128)(2,1)S(1)}, bf16[24,1280]{1,0:T(8,128)(2,1)S(1)}, u32[]{:S(2)}, u32[]{:S(2)}) collective-permute-start(bf16[24,1280]{1,0:T(8,128)(2,1)S(1)} %get-tuple-element.49.refs_0_), channel_id=1, source_target_pairs={{0,2},{1,3},{2,0},{3,1},{4,6},{5,7},{6,4},{7,5},{8,10},{9,11},{10,... | collective-permute-start | bytes 184328 | tf_op jit(solution)/shard_map/ppermute | solution.py:312
  8.3 1.5 collective-permute-start.1
  10.6 2.0 %collective-permute-done.1.refs_2_ = bf16[24,1280]{1,0:T(8,128)(2,1)S(1)} collective-permute-done((bf16[24,1280]{1,0:T(8,128)(2,1)S(1)}, bf16[24,1280]{1,0:T(8,128)(2,1)S(1)}, u32[]{:S(2)}, u32[]{:S(2)}) %collective-permute-start.1) | collective-permute-done | bytes 61472 | tf_op jit(solution)/shard_map/ppermute | solution.py:312
  12.6 2.4 %collective-permute-done.2.refs_3_ = bf16[24,1280]{1,0:T(8,128)(2,1)S(1)} collective-permute-done((bf16[24,1280]{1,0:T(8,128)(2,1)S(1)}, bf16[24,1280]{1,0:T(8,128)(2,1)S(1)}, u32[]{:S(2)}, u32[]{:S(2)}) %collective-permute-start.2) | collective-permute-done | bytes 61472 | tf_op jit(solution)/shard_map/ppermute | solution.py:312
  16.2 12.9 %copy-done = bf16[4096,5120]{1,0:T(8,128)(2,1)S(1)} copy-done((bf16[4096,5120]{1,0:T(8,128)(2,1)S(1)}, bf16[4096,5120]{1,0:T(8,128)(2,1)}, u32[]{:S(2)}) %copy-start) | copy-done | bytes 41943064
  29.2 13.8 %shard_map.199 = (f32[24,2176]{1,0:T(8,128)S(1)}, bf16[24,2176]{1,0:T(8,128)(2,1)S(1)}, bf16[24,2176]{1,0:T(8,128)(2,1)S(1)}, bf16[24,2176]{1,0:T(8,128)(2,1)S(1)}) custom-call(bf16[24,1280]{1,0:T(8,128)(2,1)S(1)} %get-tuple-element.49.refs_0_, bf16[24,1280]{1,0:T(8,128)(2,1)S(1)} %collective-permute-done.refs_1_, ...), custom_call_target="tpu_custom_call" | custom-call | flops 2013265920 | bytes 42434560 | tf_op jit(solution)/shard_map/pallas_call | solution.py:26
  43.0 1.6 %collective-permute-start.7 = (bf16[24,2176]{1,0:T(8,128)(2,1)S(1)}, bf16[24,2176]{1,0:T(8,128)(2,1)S(1)}, u32[]{:S(2)}, u32[]{:S(2)}) collective-permute-start(bf16[24,2176]{1,0:T(8,128)(2,1)S(1)} %get-tuple-element.51), channel_id=1, source_target_pairs={{0,8},{8,0},{16,24},{24,16},{1,9},{9,1},{17,25},{25,17},{2,10},{10... | collective-permute-start | bytes 313352 | tf_op jit(solution)/shard_map/ppermute | solution.py:308
  44.6 2.6 %collective-permute-start.8 = (bf16[24,2176]{1,0:T(8,128)(2,1)S(1)}, bf16[24,2176]{1,0:T(8,128)(2,1)S(1)}, u32[]{:S(2)}, u32[]{:S(2)}) collective-permute-start(bf16[24,2176]{1,0:T(8,128)(2,1)S(1)} %get-tuple-element.52), channel_id=1, source_target_pairs={{0,16},{8,24},{16,0},{24,8},{1,17},{9,25},{17,1},{25,9},{2,18},{10... | collective-permute-start | bytes 313352 | tf_op jit(solution)/shard_map/ppermute | solution.py:308
  48.0 7.6 %collective-permute-done.8.refs_2_ = bf16[24,2176]{1,0:T(8,128)(2,1)S(1)} collective-permute-done((bf16[24,2176]{1,0:T(8,128)(2,1)S(1)}, bf16[24,2176]{1,0:T(8,128)(2,1)S(1)}, u32[]{:S(2)}, u32[]{:S(2)}) %collective-permute-start.8) | collective-permute-done | bytes 104480 | tf_op jit(solution)/shard_map/ppermute | solution.py:308
  55.9 1.9 %collective-permute-start.10 = (bf16[24,2176]{1,0:T(8,128)(2,1)S(1)}, bf16[24,2176]{1,0:T(8,128)(2,1)S(1)}, u32[]{:S(2)}, u32[]{:S(2)}) collective-permute-start(bf16[24,2176]{1,0:T(8,128)(2,1)S(1)} %get-tuple-element.54.refs_0_), channel_id=1, source_target_pairs={{0,8},{8,0},{16,24},{24,16},{1,9},{9,1},{17,25},{25,17},{2,10},{10... | collective-permute-start | bytes 313352 | tf_op jit(solution)/shard_map/ppermute | solution.py:308
  61.7 6.4 %collective-permute-done.11.refs_2_ = bf16[24,2176]{1,0:T(8,128)(2,1)S(1)} collective-permute-done((bf16[24,2176]{1,0:T(8,128)(2,1)S(1)}, bf16[24,2176]{1,0:T(8,128)(2,1)S(1)}, u32[]{:S(2)}, u32[]{:S(2)}) %collective-permute-start.11) | collective-permute-done | bytes 104480 | tf_op jit(solution)/shard_map/ppermute | solution.py:308
  68.1 8.0 %shard_map.201 = (f32[24,5120]{1,0:T(8,128)S(1)}, bf16[24,5120]{1,0:T(8,128)(2,1)S(1)}, f32[12,128]{1,0:T(8,128)S(1)}) custom-call(bf16[24,2176]{1,0:T(8,128)(2,1)S(1)} %get-tuple-element.54.refs_0_, bf16[24,2176]{1,0:T(8,128)(2,1)S(1)} %collective-permute-done.10.refs_1_, bf16[24,2176]{1,0:T(8,128)(2,1)S(1)} %collective-permute-done.11.refs_2_, ...), custom_call_target="tpu_custom_call" | custom-call | flops 2013265920 | bytes 42360832 | tf_op jit(solution)/shard_map/pallas_call | solution.py:26
  76.1 1.5 collective-permute-done.13.refs_1_
  78.9 2.4 %collective-permute-start.16 = (bf16[24,1280]{1,0:T(8,128)(2,1)S(1)}, bf16[24,1280]{1,0:T(8,128)(2,1)S(1)}, u32[]{:S(2)}, u32[]{:S(2)}) collective-permute-start(bf16[24,1280]{1,0:T(8,128)(2,1)S(1)} %get-tuple-element.60), channel_id=1, source_target_pairs={{0,6},{1,7},{2,4},{3,5},{4,2},{5,3},{6,0},{7,1},{8,14},{9,15},{10,... | collective-permute-start | bytes 184328 | tf_op jit(solution)/shard_map/ppermute | solution.py:312
  84.1 2.8 %shard_map.203 = (f32[6,1024]{1,0:T(8,128)S(1)}, f32[24,1280]{1,0:T(8,128)S(1)}, f32[6,128]{1,0:T(8,128)S(1)}, bf16[24,1280]{1,0:T(8,128)(2,1)S(1)}) custom-call(bf16[4096,5120]{1,0:T(8,128)(2,1)S(1)} %copy-done, f32[24,1280]{1,0:T(8,128)S(1)} %get-tuple-element.57.refs_0_, bf16[24,1280]{1,0:T(8,128)(2,1)S(1)} %collective-permute-done.14.refs_1_, ...), custom_call_target="tpu_custom_call" | custom-call | bytes 1942528 | tf_op jit(solution)/shard_map/pallas_call | solution.py:26
  87.0 1.6 collective-permute-start.17
  88.5 1.5 collective-permute-start.18
  93.0 2.2 %collective-permute-done.19.refs_3_ = bf16[24,1280]{1,0:T(8,128)(2,1)S(1)} collective-permute-done((bf16[24,1280]{1,0:T(8,128)(2,1)S(1)}, bf16[24,1280]{1,0:T(8,128)(2,1)S(1)}, u32[]{:S(2)}, u32[]{:S(2)}) %collective-permute-start.19) | collective-permute-done | bytes 61472 | tf_op jit(solution)/shard_map/ppermute | solution.py:312
  96.4 13.8 %shard_map.204 = (f32[24,2176]{1,0:T(8,128)S(1)}, bf16[24,2176]{1,0:T(8,128)(2,1)S(1)}, bf16[24,2176]{1,0:T(8,128)(2,1)S(1)}, bf16[24,2176]{1,0:T(8,128)(2,1)S(1)}) custom-call(bf16[24,1280]{1,0:T(8,128)(2,1)S(1)} %get-tuple-element.65.refs_0_, bf16[24,1280]{1,0:T(8,128)(2,1)S(1)} %collective-permute-done.17.refs_1_, ...), custom_call_target="tpu_custom_call" | custom-call | flops 2013265920 | bytes 42434560 | tf_op jit(solution)/shard_map/pallas_call | solution.py:26
  110.2 1.7 %collective-permute-start.24 = (bf16[24,2176]{1,0:T(8,128)(2,1)S(1)}, bf16[24,2176]{1,0:T(8,128)(2,1)S(1)}, u32[]{:S(2)}, u32[]{:S(2)}) collective-permute-start(bf16[24,2176]{1,0:T(8,128)(2,1)S(1)} %get-tuple-element.67), channel_id=1, source_target_pairs={{0,8},{8,0},{16,24},{24,16},{1,9},{9,1},{17,25},{25,17},{2,10},{10... | collective-permute-start | bytes 313352 | tf_op jit(solution)/shard_map/ppermute | solution.py:308
  112.9 1.8 %collective-permute-start.26 = (bf16[24,2176]{1,0:T(8,128)(2,1)S(1)}, bf16[24,2176]{1,0:T(8,128)(2,1)S(1)}, u32[]{:S(2)}, u32[]{:S(2)}) collective-permute-start(bf16[24,2176]{1,0:T(8,128)(2,1)S(1)} %get-tuple-element.69), channel_id=1, source_target_pairs={{0,24},{8,16},{16,8},{24,0},{1,25},{9,17},{17,9},{25,1},{2,26},{10... | collective-permute-start | bytes 313352 | tf_op jit(solution)/shard_map/ppermute | solution.py:308
  115.3 7.9 %collective-permute-done.25.refs_2_ = bf16[24,2176]{1,0:T(8,128)(2,1)S(1)} collective-permute-done((bf16[24,2176]{1,0:T(8,128)(2,1)S(1)}, bf16[24,2176]{1,0:T(8,128)(2,1)S(1)}, u32[]{:S(2)}, u32[]{:S(2)}) %collective-permute-start.25) | collective-permute-done | bytes 104480 | tf_op jit(solution)/shard_map/ppermute | solution.py:308
  124.1 1.7 %collective-permute-start.27 = (bf16[24,2176]{1,0:T(8,128)(2,1)S(1)}, bf16[24,2176]{1,0:T(8,128)(2,1)S(1)}, u32[]{:S(2)}, u32[]{:S(2)}) collective-permute-start(bf16[24,2176]{1,0:T(8,128)(2,1)S(1)} %get-tuple-element.72.refs_0_), channel_id=1, source_target_pairs={{0,8},{8,0},{16,24},{24,16},{1,9},{9,1},{17,25},{25,17},{2,10},{10... | collective-permute-start | bytes 313352 | tf_op jit(solution)/shard_map/ppermute | solution.py:308
  126.6 1.9 %collective-permute-start.29 = (bf16[24,2176]{1,0:T(8,128)(2,1)S(1)}, bf16[24,2176]{1,0:T(8,128)(2,1)S(1)}, u32[]{:S(2)}, u32[]{:S(2)}) collective-permute-start(bf16[24,2176]{1,0:T(8,128)(2,1)S(1)} %get-tuple-element.72.refs_0_), channel_id=1, source_target_pairs={{0,24},{8,16},{16,8},{24,0},{1,25},{9,17},{17,9},{25,1},{2,26},{10... | collective-permute-start | bytes 313352 | tf_op jit(solution)/shard_map/ppermute | solution.py:308
  129.9 6.0 %collective-permute-done.28.refs_2_ = bf16[24,2176]{1,0:T(8,128)(2,1)S(1)} collective-permute-done((bf16[24,2176]{1,0:T(8,128)(2,1)S(1)}, bf16[24,2176]{1,0:T(8,128)(2,1)S(1)}, u32[]{:S(2)}, u32[]{:S(2)}) %collective-permute-start.28) | collective-permute-done | bytes 104480 | tf_op jit(solution)/shard_map/ppermute | solution.py:308
  135.9 8.1 %shard_map.206 = (f32[24,5120]{1,0:T(8,128)S(1)}, bf16[24,5120]{1,0:T(8,128)(2,1)S(1)}, f32[12,128]{1,0:T(8,128)S(1)}) custom-call(bf16[24,2176]{1,0:T(8,128)(2,1)S(1)} %get-tuple-element.72.refs_0_, bf16[24,2176]{1,0:T(8,128)(2,1)S(1)} %collective-permute-done.27.refs_1_, bf16[24,2176]{1,0:T(8,128)(2,1)S(1)} %collective-permute-done.28.refs_2_, ...), custom_call_target="tpu_custom_call" | custom-call | flops 2013265920 | bytes 42360832 | tf_op jit(solution)/shard_map/pallas_call | solution.py:26
  144.1 1.5 collective-permute-done.30.refs_1_
  146.9 2.5 %collective-permute-start.33 = (bf16[24,1280]{1,0:T(8,128)(2,1)S(1)}, bf16[24,1280]{1,0:T(8,128)(2,1)S(1)}, u32[]{:S(2)}, u32[]{:S(2)}) collective-permute-start(bf16[24,1280]{1,0:T(8,128)(2,1)S(1)} %get-tuple-element.78), channel_id=1, source_target_pairs={{0,6},{1,7},{2,4},{3,5},{4,2},{5,3},{6,0},{7,1},{8,14},{9,15},{10,... | collective-permute-start | bytes 184328 | tf_op jit(solution)/shard_map/ppermute | solution.py:312
  152.0 1.4 shard_map.208
  154.7 1.5 collective-permute-start.35
  156.2 1.5 collective-permute-start.36
  160.1 2.4 %collective-permute-done.37.refs_3_ = f32[8,1024]{1,0:T(8,128)S(1)} collective-permute-done((f32[8,1024]{1,0:T(8,128)S(1)}, f32[8,1024]{1,0:T(8,128)S(1)}, u32[]{:S(2)}, u32[]{:S(2)}) %collective-permute-start.37) | collective-permute-done | bytes 32800 | tf_op jit(solution)/shard_map/ppermute | solution.py:312
  (94 shorter events, 33.6 us)
Async XLA Ops:
  5.3 5.3 %collective-permute-start = (bf16[24,1280]{1,0:T(8,128)(2,1)S(1)}, bf16[24,1280]{1,0:T(8,128)(2,1)S(1)}, u32[]{:S(2)}, u32[]{:S(2)}) collective-permute-start(bf16[24,1280]{1,0:T(8,128)(2,1)S(1)} %get-tuple-element.49.refs_0_), channel_id=1, source_target_pairs={{0,2},{1,3},{2,0},{3,1},{4,6},{5,7},{6,4},{7,5},{8,10},{9,11},{10,... | collective-permute-start | bytes 184328 | tf_op jit(solution)/shard_map/ppermute | solution.py:312
  8.3 4.2 %collective-permute-start.1 = (bf16[24,1280]{1,0:T(8,128)(2,1)S(1)}, bf16[24,1280]{1,0:T(8,128)(2,1)S(1)}, u32[]{:S(2)}, u32[]{:S(2)}) collective-permute-start(bf16[24,1280]{1,0:T(8,128)(2,1)S(1)} %get-tuple-element.49.refs_0_), channel_id=1, source_target_pairs={{0,4},{1,5},{2,6},{3,7},{4,0},{5,1},{6,2},{7,3},{8,12},{9,13},{10,... | collective-permute-start | bytes 184328 | tf_op jit(solution)/shard_map/ppermute | solution.py:312
  9.9 5.1 %collective-permute-start.2 = (bf16[24,1280]{1,0:T(8,128)(2,1)S(1)}, bf16[24,1280]{1,0:T(8,128)(2,1)S(1)}, u32[]{:S(2)}, u32[]{:S(2)}) collective-permute-start(bf16[24,1280]{1,0:T(8,128)(2,1)S(1)} %get-tuple-element.49.refs_0_), channel_id=1, source_target_pairs={{0,6},{1,7},{2,4},{3,5},{4,2},{5,3},{6,0},{7,1},{8,14},{9,15},{10,... | collective-permute-start | bytes 184328 | tf_op jit(solution)/shard_map/ppermute | solution.py:312
  9.9 5.1 %collective-permute-start.3 = (bf16[24,1280]{1,0:T(8,128)(2,1)S(1)}, bf16[24,1280]{1,0:T(8,128)(2,1)S(1)}, u32[]{:S(2)}, u32[]{:S(2)}) collective-permute-start(bf16[24,1280]{1,0:T(8,128)(2,1)S(1)} %get-tuple-element.49.refs_0_), channel_id=1, source_target_pairs={{0,1},{1,0},{2,3},{3,2},{4,5},{5,4},{6,7},{7,6},{8,9},{9,8},{10,11... | collective-permute-start | bytes 184328 | tf_op jit(solution)/shard_map/ppermute | solution.py:316
  10.6 4.4 %collective-permute-start.4 = (bf16[24,1280]{1,0:T(8,128)(2,1)S(1)}, bf16[24,1280]{1,0:T(8,128)(2,1)S(1)}, u32[]{:S(2)}, u32[]{:S(2)}) collective-permute-start(bf16[24,1280]{1,0:T(8,128)(2,1)S(1)} %collective-permute-done.refs_1_), channel_id=1, source_target_pairs={{0,1},{1,0},{2,3},{3,2},{4,5},{5,4},{6,7},{7,6},{8,9},{9,8},{10,11... | collective-permute-start | bytes 184328 | tf_op jit(solution)/shard_map/ppermute | solution.py:316
  12.6 2.4 %collective-permute-start.5 = (bf16[24,1280]{1,0:T(8,128)(2,1)S(1)}, bf16[24,1280]{1,0:T(8,128)(2,1)S(1)}, u32[]{:S(2)}, u32[]{:S(2)}) collective-permute-start(bf16[24,1280]{1,0:T(8,128)(2,1)S(1)} %collective-permute-done.1.refs_2_), channel_id=1, source_target_pairs={{0,1},{1,0},{2,3},{3,2},{4,5},{5,4},{6,7},{7,6},{8,9},{9,8},{10,11... | collective-permute-start | bytes 184328 | tf_op jit(solution)/shard_map/ppermute | solution.py:316
  43.0 5.1 %collective-permute-start.7 = (bf16[24,2176]{1,0:T(8,128)(2,1)S(1)}, bf16[24,2176]{1,0:T(8,128)(2,1)S(1)}, u32[]{:S(2)}, u32[]{:S(2)}) collective-permute-start(bf16[24,2176]{1,0:T(8,128)(2,1)S(1)} %get-tuple-element.51), channel_id=1, source_target_pairs={{0,8},{8,0},{16,24},{24,16},{1,9},{9,1},{17,25},{25,17},{2,10},{10... | collective-permute-start | bytes 313352 | tf_op jit(solution)/shard_map/ppermute | solution.py:308
  44.6 11.0 %collective-permute-start.8 = (bf16[24,2176]{1,0:T(8,128)(2,1)S(1)}, bf16[24,2176]{1,0:T(8,128)(2,1)S(1)}, u32[]{:S(2)}, u32[]{:S(2)}) collective-permute-start(bf16[24,2176]{1,0:T(8,128)(2,1)S(1)} %get-tuple-element.52), channel_id=1, source_target_pairs={{0,16},{8,24},{16,0},{24,8},{1,17},{9,25},{17,1},{25,9},{2,18},{10... | collective-permute-start | bytes 313352 | tf_op jit(solution)/shard_map/ppermute | solution.py:308
  47.2 8.4 %collective-permute-start.9 = (bf16[24,2176]{1,0:T(8,128)(2,1)S(1)}, bf16[24,2176]{1,0:T(8,128)(2,1)S(1)}, u32[]{:S(2)}, u32[]{:S(2)}) collective-permute-start(bf16[24,2176]{1,0:T(8,128)(2,1)S(1)} %get-tuple-element.53), channel_id=1, source_target_pairs={{0,24},{8,16},{16,8},{24,0},{1,25},{9,17},{17,9},{25,1},{2,26},{10... | collective-permute-start | bytes 313352 | tf_op jit(solution)/shard_map/ppermute | solution.py:308
  55.9 5.8 %collective-permute-start.10 = (bf16[24,2176]{1,0:T(8,128)(2,1)S(1)}, bf16[24,2176]{1,0:T(8,128)(2,1)S(1)}, u32[]{:S(2)}, u32[]{:S(2)}) collective-permute-start(bf16[24,2176]{1,0:T(8,128)(2,1)S(1)} %get-tuple-element.54.refs_0_), channel_id=1, source_target_pairs={{0,8},{8,0},{16,24},{24,16},{1,9},{9,1},{17,25},{25,17},{2,10},{10... | collective-permute-start | bytes 313352 | tf_op jit(solution)/shard_map/ppermute | solution.py:308
  57.9 10.2 %collective-permute-start.11 = (bf16[24,2176]{1,0:T(8,128)(2,1)S(1)}, bf16[24,2176]{1,0:T(8,128)(2,1)S(1)}, u32[]{:S(2)}, u32[]{:S(2)}) collective-permute-start(bf16[24,2176]{1,0:T(8,128)(2,1)S(1)} %get-tuple-element.54.refs_0_), channel_id=1, source_target_pairs={{0,16},{8,24},{16,0},{24,8},{1,17},{9,25},{17,1},{25,9},{2,18},{10... | collective-permute-start | bytes 313352 | tf_op jit(solution)/shard_map/ppermute | solution.py:308
  59.2 8.9 %collective-permute-start.12 = (bf16[24,2176]{1,0:T(8,128)(2,1)S(1)}, bf16[24,2176]{1,0:T(8,128)(2,1)S(1)}, u32[]{:S(2)}, u32[]{:S(2)}) collective-permute-start(bf16[24,2176]{1,0:T(8,128)(2,1)S(1)} %get-tuple-element.54.refs_0_), channel_id=1, source_target_pairs={{0,24},{8,16},{16,8},{24,0},{1,25},{9,17},{17,9},{25,1},{2,26},{10... | collective-permute-start | bytes 313352 | tf_op jit(solution)/shard_map/ppermute | solution.py:308
  77.8 4.4 %collective-permute-start.14 = (bf16[24,1280]{1,0:T(8,128)(2,1)S(1)}, bf16[24,1280]{1,0:T(8,128)(2,1)S(1)}, u32[]{:S(2)}, u32[]{:S(2)}) collective-permute-start(bf16[24,1280]{1,0:T(8,128)(2,1)S(1)} %get-tuple-element.58), channel_id=1, source_target_pairs={{0,2},{1,3},{2,0},{3,1},{4,6},{5,7},{6,4},{7,5},{8,10},{9,11},{10,... | collective-permute-start | bytes 184328 | tf_op jit(solution)/shard_map/ppermute | solution.py:312
  78.4 4.9 %collective-permute-start.15 = (bf16[24,1280]{1,0:T(8,128)(2,1)S(1)}, bf16[24,1280]{1,0:T(8,128)(2,1)S(1)}, u32[]{:S(2)}, u32[]{:S(2)}) collective-permute-start(bf16[24,1280]{1,0:T(8,128)(2,1)S(1)} %get-tuple-element.59), channel_id=1, source_target_pairs={{0,4},{1,5},{2,6},{3,7},{4,0},{5,1},{6,2},{7,3},{8,12},{9,13},{10,... | collective-permute-start | bytes 184328 | tf_op jit(solution)/shard_map/ppermute | solution.py:312
  78.9 5.1 %collective-permute-start.16 = (bf16[24,1280]{1,0:T(8,128)(2,1)S(1)}, bf16[24,1280]{1,0:T(8,128)(2,1)S(1)}, u32[]{:S(2)}, u32[]{:S(2)}) collective-permute-start(bf16[24,1280]{1,0:T(8,128)(2,1)S(1)} %get-tuple-element.60), channel_id=1, source_target_pairs={{0,6},{1,7},{2,4},{3,5},{4,2},{5,3},{6,0},{7,1},{8,14},{9,15},{10,... | collective-permute-start | bytes 184328 | tf_op jit(solution)/shard_map/ppermute | solution.py:312
  87.0 4.9 %collective-permute-start.17 = (bf16[24,1280]{1,0:T(8,128)(2,1)S(1)}, bf16[24,1280]{1,0:T(8,128)(2,1)S(1)}, u32[]{:S(2)}, u32[]{:S(2)}) collective-permute-start(bf16[24,1280]{1,0:T(8,128)(2,1)S(1)} %get-tuple-element.65.refs_0_), channel_id=1, source_target_pairs={{0,2},{1,3},{2,0},{3,1},{4,6},{5,7},{6,4},{7,5},{8,10},{9,11},{10,... | collective-permute-start | bytes 184328 | tf_op jit(solution)/shard_map/ppermute | solution.py:312
  88.5 4.5 %collective-permute-start.18 = (bf16[24,1280]{1,0:T(8,128)(2,1)S(1)}, bf16[24,1280]{1,0:T(8,128)(2,1)S(1)}, u32[]{:S(2)}, u32[]{:S(2)}) collective-permute-start(bf16[24,1280]{1,0:T(8,128)(2,1)S(1)} %get-tuple-element.65.refs_0_), channel_id=1, source_target_pairs={{0,4},{1,5},{2,6},{3,7},{4,0},{5,1},{6,2},{7,3},{8,12},{9,13},{10,... | collective-permute-start | bytes 184328 | tf_op jit(solution)/shard_map/ppermute | solution.py:312
  90.0 5.1 %collective-permute-start.19 = (bf16[24,1280]{1,0:T(8,128)(2,1)S(1)}, bf16[24,1280]{1,0:T(8,128)(2,1)S(1)}, u32[]{:S(2)}, u32[]{:S(2)}) collective-permute-start(bf16[24,1280]{1,0:T(8,128)(2,1)S(1)} %get-tuple-element.65.refs_0_), channel_id=1, source_target_pairs={{0,6},{1,7},{2,4},{3,5},{4,2},{5,3},{6,0},{7,1},{8,14},{9,15},{10,... | collective-permute-start | bytes 184328 | tf_op jit(solution)/shard_map/ppermute | solution.py:312
  90.5 4.6 %collective-permute-start.20 = (bf16[24,1280]{1,0:T(8,128)(2,1)S(1)}, bf16[24,1280]{1,0:T(8,128)(2,1)S(1)}, u32[]{:S(2)}, u32[]{:S(2)}) collective-permute-start(bf16[24,1280]{1,0:T(8,128)(2,1)S(1)} %get-tuple-element.65.refs_0_), channel_id=1, source_target_pairs={{0,1},{1,0},{2,3},{3,2},{4,5},{5,4},{6,7},{7,6},{8,9},{9,8},{10,11... | collective-permute-start | bytes 184328 | tf_op jit(solution)/shard_map/ppermute | solution.py:316
  91.9 3.3 %collective-permute-start.21 = (bf16[24,1280]{1,0:T(8,128)(2,1)S(1)}, bf16[24,1280]{1,0:T(8,128)(2,1)S(1)}, u32[]{:S(2)}, u32[]{:S(2)}) collective-permute-start(bf16[24,1280]{1,0:T(8,128)(2,1)S(1)} %collective-permute-done.17.refs_1_), channel_id=1, source_target_pairs={{0,1},{1,0},{2,3},{3,2},{4,5},{5,4},{6,7},{7,6},{8,9},{9,8},{10,11... | collective-permute-start | bytes 184328 | tf_op jit(solution)/shard_map/ppermute | solution.py:316
  110.2 5.1 %collective-permute-start.24 = (bf16[24,2176]{1,0:T(8,128)(2,1)S(1)}, bf16[24,2176]{1,0:T(8,128)(2,1)S(1)}, u32[]{:S(2)}, u32[]{:S(2)}) collective-permute-start(bf16[24,2176]{1,0:T(8,128)(2,1)S(1)} %get-tuple-element.67), channel_id=1, source_target_pairs={{0,8},{8,0},{16,24},{24,16},{1,9},{9,1},{17,25},{25,17},{2,10},{10... | collective-permute-start | bytes 313352 | tf_op jit(solution)/shard_map/ppermute | solution.py:308
  112.0 11.2 %collective-permute-start.25 = (bf16[24,2176]{1,0:T(8,128)(2,1)S(1)}, bf16[24,2176]{1,0:T(8,128)(2,1)S(1)}, u32[]{:S(2)}, u32[]{:S(2)}) collective-permute-start(bf16[24,2176]{1,0:T(8,128)(2,1)S(1)} %get-tuple-element.68), channel_id=1, source_target_pairs={{0,16},{8,24},{16,0},{24,8},{1,17},{9,25},{17,1},{25,9},{2,18},{10... | collective-permute-start | bytes 313352 | tf_op jit(solution)/shard_map/ppermute | solution.py:308
  112.9 10.3 %collective-permute-start.26 = (bf16[24,2176]{1,0:T(8,128)(2,1)S(1)}, bf16[24,2176]{1,0:T(8,128)(2,1)S(1)}, u32[]{:S(2)}, u32[]{:S(2)}) collective-permute-start(bf16[24,2176]{1,0:T(8,128)(2,1)S(1)} %get-tuple-element.69), channel_id=1, source_target_pairs={{0,24},{8,16},{16,8},{24,0},{1,25},{9,17},{17,9},{25,1},{2,26},{10... | collective-permute-start | bytes 313352 | tf_op jit(solution)/shard_map/ppermute | solution.py:308
  124.1 5.8 %collective-permute-start.27 = (bf16[24,2176]{1,0:T(8,128)(2,1)S(1)}, bf16[24,2176]{1,0:T(8,128)(2,1)S(1)}, u32[]{:S(2)}, u32[]{:S(2)}) collective-permute-start(bf16[24,2176]{1,0:T(8,128)(2,1)S(1)} %get-tuple-element.72.refs_0_), channel_id=1, source_target_pairs={{0,8},{8,0},{16,24},{24,16},{1,9},{9,1},{17,25},{25,17},{2,10},{10... | collective-permute-start | bytes 313352 | tf_op jit(solution)/shard_map/ppermute | solution.py:308
  125.8 10.1 %collective-permute-start.28 = (bf16[24,2176]{1,0:T(8,128)(2,1)S(1)}, bf16[24,2176]{1,0:T(8,128)(2,1)S(1)}, u32[]{:S(2)}, u32[]{:S(2)}) collective-permute-start(bf16[24,2176]{1,0:T(8,128)(2,1)S(1)} %get-tuple-element.72.refs_0_), channel_id=1, source_target_pairs={{0,16},{8,24},{16,0},{24,8},{1,17},{9,25},{17,1},{25,9},{2,18},{10... | collective-permute-start | bytes 313352 | tf_op jit(solution)/shard_map/ppermute | solution.py:308
  126.6 9.3 %collective-permute-start.29 = (bf16[24,2176]{1,0:T(8,128)(2,1)S(1)}, bf16[24,2176]{1,0:T(8,128)(2,1)S(1)}, u32[]{:S(2)}, u32[]{:S(2)}) collective-permute-start(bf16[24,2176]{1,0:T(8,128)(2,1)S(1)} %get-tuple-element.72.refs_0_), channel_id=1, source_target_pairs={{0,24},{8,16},{16,8},{24,0},{1,25},{9,17},{17,9},{25,1},{2,26},{10... | collective-permute-start | bytes 313352 | tf_op jit(solution)/shard_map/ppermute | solution.py:308
  145.7 4.4 %collective-permute-start.31 = (bf16[24,1280]{1,0:T(8,128)(2,1)S(1)}, bf16[24,1280]{1,0:T(8,128)(2,1)S(1)}, u32[]{:S(2)}, u32[]{:S(2)}) collective-permute-start(bf16[24,1280]{1,0:T(8,128)(2,1)S(1)} %get-tuple-element.76), channel_id=1, source_target_pairs={{0,2},{1,3},{2,0},{3,1},{4,6},{5,7},{6,4},{7,5},{8,10},{9,11},{10,... | collective-permute-start | bytes 184328 | tf_op jit(solution)/shard_map/ppermute | solution.py:312
  146.4 4.9 %collective-permute-start.32 = (bf16[24,1280]{1,0:T(8,128)(2,1)S(1)}, bf16[24,1280]{1,0:T(8,128)(2,1)S(1)}, u32[]{:S(2)}, u32[]{:S(2)}) collective-permute-start(bf16[24,1280]{1,0:T(8,128)(2,1)S(1)} %get-tuple-element.77), channel_id=1, source_target_pairs={{0,4},{1,5},{2,6},{3,7},{4,0},{5,1},{6,2},{7,3},{8,12},{9,13},{10,... | collective-permute-start | bytes 184328 | tf_op jit(solution)/shard_map/ppermute | solution.py:312
  146.9 5.1 %collective-permute-start.33 = (bf16[24,1280]{1,0:T(8,128)(2,1)S(1)}, bf16[24,1280]{1,0:T(8,128)(2,1)S(1)}, u32[]{:S(2)}, u32[]{:S(2)}) collective-permute-start(bf16[24,1280]{1,0:T(8,128)(2,1)S(1)} %get-tuple-element.78), channel_id=1, source_target_pairs={{0,6},{1,7},{2,4},{3,5},{4,2},{5,3},{6,0},{7,1},{8,14},{9,15},{10,... | collective-permute-start | bytes 184328 | tf_op jit(solution)/shard_map/ppermute | solution.py:312
  154.7 4.1 %collective-permute-start.35 = (f32[8,1024]{1,0:T(8,128)S(1)}, f32[8,1024]{1,0:T(8,128)S(1)}, u32[]{:S(2)}, u32[]{:S(2)}) collective-permute-start(f32[8,1024]{1,0:T(8,128)S(1)} %shard_map.209.refs_0_), channel_id=1, source_target_pairs={{0,2},{1,3},{2,0},{3,1},{4,6},{5,7},{6,4},{7,5},{8,10},{9,11},{10,... | collective-permute-start | bytes 98312 | tf_op jit(solution)/shard_map/ppermute | solution.py:312
  156.2 3.9 %collective-permute-start.36 = (f32[8,1024]{1,0:T(8,128)S(1)}, f32[8,1024]{1,0:T(8,128)S(1)}, u32[]{:S(2)}, u32[]{:S(2)}) collective-permute-start(f32[8,1024]{1,0:T(8,128)S(1)} %shard_map.209.refs_0_), channel_id=1, source_target_pairs={{0,4},{1,5},{2,6},{3,7},{4,0},{5,1},{6,2},{7,3},{8,12},{9,13},{10,... | collective-permute-start | bytes 98312 | tf_op jit(solution)/shard_map/ppermute | solution.py:312
  157.7 4.8 %collective-permute-start.37 = (f32[8,1024]{1,0:T(8,128)S(1)}, f32[8,1024]{1,0:T(8,128)S(1)}, u32[]{:S(2)}, u32[]{:S(2)}) collective-permute-start(f32[8,1024]{1,0:T(8,128)S(1)} %shard_map.209.refs_0_), channel_id=1, source_target_pairs={{0,6},{1,7},{2,4},{3,5},{4,2},{5,3},{6,0},{7,1},{8,14},{9,15},{10,... | collective-permute-start | bytes 98312 | tf_op jit(solution)/shard_map/ppermute | solution.py:312
  (23 other events, 385.6 us)

commit v3 on v2

--- a/solution.py
+++ b/solution.py
@@ -348,16 +348,14 @@
     macs = sz.total * sz.chunk * buses
 
     generation, copies, duals = dispatch, flow_copy, flow_dual
+    first = (dispatch, load_shed, bus_loads, row(gen_bus))
+    made = ((packed, BF), (packed, F32), (packed, F32), ((gens // LANES, sz.width, LANES), BF))
     inject, shed, loads, select = call(
         functools.partial(start_kernel, sz),
-        (dispatch, load_shed, bus_loads, row(gen_bus)),
-        (
-            (packed, BF),
-            (packed, F32),
-            (packed, F32),
-            ((gens // LANES, sz.width, LANES), BF),
-        ),
-        limit=GRANT + lines * buses * 2,
+        first,
+        made,
+        flops=1000 * lines * buses,
+        limit=GRANT - nbytes(first + tuple(jax.ShapeDtypeStruct(*each) for each in made)) - (1 << 16),
     )
     for iteration in range(ITERS):
         own = [inject] + [to_chip(n_line, away, inject) for away in range(1, chips)]

time: 164 us -> 152 us (0.927)
  local copies, waits for them, and re-layouts: 17.8 us -> 5.26 us
    unnamed x34 -> x52, local copies, waits for them, and re-layouts: 17.1 us -> 4.5 us
where the time goes in v3:
time: 152 us
  waiting for transfers between devices  56.6 us (37%)
  Pallas kernels  51.4 us (34%)
  starting transfers between devices  37.2 us (24%)
  local copies, waits for them, and re-layouts  5.26 us (3%)
    pallas_call x13, Pallas kernels, call(): pl.pallas_call(kernel, in_specs=[WHOLE] * len(args), out_specs=[WHOLE] *...  51.4 us
    ppermute x12, waiting for transfers between devices, to_scen(): return lax.ppermute(value, 'scen', [(i, i ^ away) for i in range(n)])  31.2 us
    ppermute x15, waiting for transfers between devices, to_chip(): return lax.ppermute(value, 'line', [(i, i ^ 2 * away) for i in range(n)])  18.8 us
    ppermute x15, starting transfers between devices, to_chip(): return lax.ppermute(value, 'line', [(i, i ^ 2 * away) for i in range(n)])  18.7 us
    ppermute x12, starting transfers between devices, to_scen(): return lax.ppermute(value, 'scen', [(i, i ^ away) for i in range(n)])  18.3 us
    ppermute x11, waiting for transfers between devices, to_core(): return lax.ppermute(value, 'line', [(i, i ^ 1) for i in range(n)])  6.67 us
    unnamed x52, local copies, waits for them, and re-layouts  4.5 us
  transfers between devices with their start and end apart: 38, of which 27 were waited for; matrix products, arithmetic and copies ran while one was open for 0% of the time, Pallas kernels for 0%

profile of v3, /device:TPU:0, one launch (start us, length us, event | category | flops | bytes accessed | tf_op | source)
XLA Modules:
  0.0 151.5 jit_solution(16889064250970695320)
XLA Ops:
  5.8 3.0 %collective-permute-start = (bf16[24,1280]{1,0:T(8,128)(2,1)S(1)}, bf16[24,1280]{1,0:T(8,128)(2,1)S(1)}, u32[]{:S(2)}, u32[]{:S(2)}) collective-permute-start(bf16[24,1280]{1,0:T(8,128)(2,1)S(1)} %get-tuple-element.49.refs_0_), channel_id=1, source_target_pairs={{0,2},{1,3},{2,0},{3,1},{4,6},{5,7},{6,4},{7,5},{8,10},{9,11},{10,... | collective-permute-start | bytes 184328 | tf_op jit(solution)/shard_map/ppermute | solution.py:312
  8.8 1.5 %collective-permute-start.1 = (bf16[24,1280]{1,0:T(8,128)(2,1)S(1)}, bf16[24,1280]{1,0:T(8,128)(2,1)S(1)}, u32[]{:S(2)}, u32[]{:S(2)}) collective-permute-start(bf16[24,1280]{1,0:T(8,128)(2,1)S(1)} %get-tuple-element.49.refs_0_), channel_id=1, source_target_pairs={{0,4},{1,5},{2,6},{3,7},{4,0},{5,1},{6,2},{7,3},{8,12},{9,13},{10,... | collective-permute-start | bytes 184328 | tf_op jit(solution)/shard_map/ppermute | solution.py:312
  11.0 2.0 %collective-permute-done.1.refs_2_ = bf16[24,1280]{1,0:T(8,128)(2,1)S(1)} collective-permute-done((bf16[24,1280]{1,0:T(8,128)(2,1)S(1)}, bf16[24,1280]{1,0:T(8,128)(2,1)S(1)}, u32[]{:S(2)}, u32[]{:S(2)}) %collective-permute-start.1) | collective-permute-done | bytes 61472 | tf_op jit(solution)/shard_map/ppermute | solution.py:312
  13.0 2.4 %collective-permute-done.2.refs_3_ = bf16[24,1280]{1,0:T(8,128)(2,1)S(1)} collective-permute-done((bf16[24,1280]{1,0:T(8,128)(2,1)S(1)}, bf16[24,1280]{1,0:T(8,128)(2,1)S(1)}, u32[]{:S(2)}, u32[]{:S(2)}) %collective-permute-start.2) | collective-permute-done | bytes 61472 | tf_op jit(solution)/shard_map/ppermute | solution.py:312
  16.7 13.8 %shard_map.199 = (f32[24,2176]{1,0:T(8,128)S(1)}, bf16[24,2176]{1,0:T(8,128)(2,1)S(1)}, bf16[24,2176]{1,0:T(8,128)(2,1)S(1)}, bf16[24,2176]{1,0:T(8,128)(2,1)S(1)}) custom-call(bf16[24,1280]{1,0:T(8,128)(2,1)S(1)} %get-tuple-element.49.refs_0_, bf16[24,1280]{1,0:T(8,128)(2,1)S(1)} %collective-permute-done.refs_1_, ...), custom_call_target="tpu_custom_call" | custom-call | flops 2013265920 | bytes 42434560 | tf_op jit(solution)/shard_map/pallas_call | solution.py:26
  30.6 2.5 %collective-permute-start.7 = (bf16[24,2176]{1,0:T(8,128)(2,1)S(1)}, bf16[24,2176]{1,0:T(8,128)(2,1)S(1)}, u32[]{:S(2)}, u32[]{:S(2)}) collective-permute-start(bf16[24,2176]{1,0:T(8,128)(2,1)S(1)} %get-tuple-element.51), channel_id=1, source_target_pairs={{0,8},{8,0},{16,24},{24,16},{1,9},{9,1},{17,25},{25,17},{2,10},{10... | collective-permute-start | bytes 313352 | tf_op jit(solution)/shard_map/ppermute | solution.py:308
  33.0 2.6 %collective-permute-start.8 = (bf16[24,2176]{1,0:T(8,128)(2,1)S(1)}, bf16[24,2176]{1,0:T(8,128)(2,1)S(1)}, u32[]{:S(2)}, u32[]{:S(2)}) collective-permute-start(bf16[24,2176]{1,0:T(8,128)(2,1)S(1)} %get-tuple-element.52), channel_id=1, source_target_pairs={{0,16},{8,24},{16,0},{24,8},{1,17},{9,25},{17,1},{25,9},{2,18},{10... | collective-permute-start | bytes 313352 | tf_op jit(solution)/shard_map/ppermute | solution.py:308
  35.9 8.0 %collective-permute-done.8.refs_2_ = bf16[24,2176]{1,0:T(8,128)(2,1)S(1)} collective-permute-done((bf16[24,2176]{1,0:T(8,128)(2,1)S(1)}, bf16[24,2176]{1,0:T(8,128)(2,1)S(1)}, u32[]{:S(2)}, u32[]{:S(2)}) %collective-permute-start.8) | collective-permute-done | bytes 104480 | tf_op jit(solution)/shard_map/ppermute | solution.py:308
  44.2 1.7 %collective-permute-start.10 = (bf16[24,2176]{1,0:T(8,128)(2,1)S(1)}, bf16[24,2176]{1,0:T(8,128)(2,1)S(1)}, u32[]{:S(2)}, u32[]{:S(2)}) collective-permute-start(bf16[24,2176]{1,0:T(8,128)(2,1)S(1)} %get-tuple-element.54.refs_0_), channel_id=1, source_target_pairs={{0,8},{8,0},{16,24},{24,16},{1,9},{9,1},{17,25},{25,17},{2,10},{10... | collective-permute-start | bytes 313352 | tf_op jit(solution)/shard_map/ppermute | solution.py:308
  50.0 5.6 %collective-permute-done.11.refs_2_ = bf16[24,2176]{1,0:T(8,128)(2,1)S(1)} collective-permute-done((bf16[24,2176]{1,0:T(8,128)(2,1)S(1)}, bf16[24,2176]{1,0:T(8,128)(2,1)S(1)}, u32[]{:S(2)}, u32[]{:S(2)}) %collective-permute-start.11) | collective-permute-done | bytes 104480 | tf_op jit(solution)/shard_map/ppermute | solution.py:308
  55.6 8.0 %shard_map.201 = (f32[24,5120]{1,0:T(8,128)S(1)}, bf16[24,5120]{1,0:T(8,128)(2,1)S(1)}, f32[12,128]{1,0:T(8,128)S(1)}) custom-call(bf16[24,2176]{1,0:T(8,128)(2,1)S(1)} %get-tuple-element.54.refs_0_, bf16[24,2176]{1,0:T(8,128)(2,1)S(1)} %collective-permute-done.10.refs_1_, bf16[24,2176]{1,0:T(8,128)(2,1)S(1)} %collective-permute-done.11.refs_2_, ...), custom_call_target="tpu_custom_call" | custom-call | flops 2013265920 | bytes 42360832 | tf_op jit(solution)/shard_map/pallas_call | solution.py:26
  63.7 1.5 collective-permute-done.13.refs_1_
  65.3 1.6 %collective-permute-start.14 = (bf16[24,1280]{1,0:T(8,128)(2,1)S(1)}, bf16[24,1280]{1,0:T(8,128)(2,1)S(1)}, u32[]{:S(2)}, u32[]{:S(2)}) collective-permute-start(bf16[24,1280]{1,0:T(8,128)(2,1)S(1)} %get-tuple-element.58), channel_id=1, source_target_pairs={{0,2},{1,3},{2,0},{3,1},{4,6},{5,7},{6,4},{7,5},{8,10},{9,11},{10,... | collective-permute-start | bytes 184328 | tf_op jit(solution)/shard_map/ppermute | solution.py:312
  66.9 1.5 %collective-permute-start.15 = (bf16[24,1280]{1,0:T(8,128)(2,1)S(1)}, bf16[24,1280]{1,0:T(8,128)(2,1)S(1)}, u32[]{:S(2)}, u32[]{:S(2)}) collective-permute-start(bf16[24,1280]{1,0:T(8,128)(2,1)S(1)} %get-tuple-element.59), channel_id=1, source_target_pairs={{0,4},{1,5},{2,6},{3,7},{4,0},{5,1},{6,2},{7,3},{8,12},{9,13},{10,... | collective-permute-start | bytes 184328 | tf_op jit(solution)/shard_map/ppermute | solution.py:312
  69.6 1.5 collective-permute-done.15.refs_2_
  71.1 2.4 %collective-permute-done.16.refs_3_ = bf16[24,1280]{1,0:T(8,128)(2,1)S(1)} collective-permute-done((bf16[24,1280]{1,0:T(8,128)(2,1)S(1)}, bf16[24,1280]{1,0:T(8,128)(2,1)S(1)}, u32[]{:S(2)}, u32[]{:S(2)}) %collective-permute-start.16) | collective-permute-done | bytes 61472 | tf_op jit(solution)/shard_map/ppermute | solution.py:312
  73.6 2.8 %shard_map.203 = (f32[6,1024]{1,0:T(8,128)S(1)}, f32[24,1280]{1,0:T(8,128)S(1)}, f32[6,128]{1,0:T(8,128)S(1)}, bf16[24,1280]{1,0:T(8,128)(2,1)S(1)}) custom-call(bf16[4096,5120]{1,0:T(8,128)(2,1)S(1)} %bitcast.7, f32[24,1280]{1,0:T(8,128)S(1)} %get-tuple-element.57.refs_0_, bf16[24,1280]{1,0:T(8,128)(2,1)S(1)} %collective-permute-done.14.refs_1_, ...), custom_call_target="tpu_custom_call" | custom-call | bytes 1942528 | tf_op jit(solution)/shard_map/pallas_call | solution.py:26
  77.6 2.4 %collective-permute-start.19 = (bf16[24,1280]{1,0:T(8,128)(2,1)S(1)}, bf16[24,1280]{1,0:T(8,128)(2,1)S(1)}, u32[]{:S(2)}, u32[]{:S(2)}) collective-permute-start(bf16[24,1280]{1,0:T(8,128)(2,1)S(1)} %get-tuple-element.65.refs_0_), channel_id=1, source_target_pairs={{0,6},{1,7},{2,4},{3,5},{4,2},{5,3},{6,0},{7,1},{8,14},{9,15},{10,... | collective-permute-start | bytes 184328 | tf_op jit(solution)/shard_map/ppermute | solution.py:312
  83.9 13.8 %shard_map.204 = (f32[24,2176]{1,0:T(8,128)S(1)}, bf16[24,2176]{1,0:T(8,128)(2,1)S(1)}, bf16[24,2176]{1,0:T(8,128)(2,1)S(1)}, bf16[24,2176]{1,0:T(8,128)(2,1)S(1)}) custom-call(bf16[24,1280]{1,0:T(8,128)(2,1)S(1)} %get-tuple-element.65.refs_0_, bf16[24,1280]{1,0:T(8,128)(2,1)S(1)} %collective-permute-done.17.refs_1_, ...), custom_call_target="tpu_custom_call" | custom-call | flops 2013265920 | bytes 42434560 | tf_op jit(solution)/shard_map/pallas_call | solution.py:26
  97.7 1.7 %collective-permute-start.24 = (bf16[24,2176]{1,0:T(8,128)(2,1)S(1)}, bf16[24,2176]{1,0:T(8,128)(2,1)S(1)}, u32[]{:S(2)}, u32[]{:S(2)}) collective-permute-start(bf16[24,2176]{1,0:T(8,128)(2,1)S(1)} %get-tuple-element.67), channel_id=1, source_target_pairs={{0,8},{8,0},{16,24},{24,16},{1,9},{9,1},{17,25},{25,17},{2,10},{10... | collective-permute-start | bytes 313352 | tf_op jit(solution)/shard_map/ppermute | solution.py:308
  100.5 1.7 %collective-permute-start.26 = (bf16[24,2176]{1,0:T(8,128)(2,1)S(1)}, bf16[24,2176]{1,0:T(8,128)(2,1)S(1)}, u32[]{:S(2)}, u32[]{:S(2)}) collective-permute-start(bf16[24,2176]{1,0:T(8,128)(2,1)S(1)} %get-tuple-element.69), channel_id=1, source_target_pairs={{0,24},{8,16},{16,8},{24,0},{1,25},{9,17},{17,9},{25,1},{2,26},{10... | collective-permute-start | bytes 313352 | tf_op jit(solution)/shard_map/ppermute | solution.py:308
  102.8 7.8 %collective-permute-done.25.refs_2_ = bf16[24,2176]{1,0:T(8,128)(2,1)S(1)} collective-permute-done((bf16[24,2176]{1,0:T(8,128)(2,1)S(1)}, bf16[24,2176]{1,0:T(8,128)(2,1)S(1)}, u32[]{:S(2)}, u32[]{:S(2)}) %collective-permute-start.25) | collective-permute-done | bytes 104480 | tf_op jit(solution)/shard_map/ppermute | solution.py:308
  111.6 1.7 %collective-permute-start.27 = (bf16[24,2176]{1,0:T(8,128)(2,1)S(1)}, bf16[24,2176]{1,0:T(8,128)(2,1)S(1)}, u32[]{:S(2)}, u32[]{:S(2)}) collective-permute-start(bf16[24,2176]{1,0:T(8,128)(2,1)S(1)} %get-tuple-element.72.refs_0_), channel_id=1, source_target_pairs={{0,8},{8,0},{16,24},{24,16},{1,9},{9,1},{17,25},{25,17},{2,10},{10... | collective-permute-start | bytes 313352 | tf_op jit(solution)/shard_map/ppermute | solution.py:308
  114.2 1.7 %collective-permute-start.29 = (bf16[24,2176]{1,0:T(8,128)(2,1)S(1)}, bf16[24,2176]{1,0:T(8,128)(2,1)S(1)}, u32[]{:S(2)}, u32[]{:S(2)}) collective-permute-start(bf16[24,2176]{1,0:T(8,128)(2,1)S(1)} %get-tuple-element.72.refs_0_), channel_id=1, source_target_pairs={{0,24},{8,16},{16,8},{24,0},{1,25},{9,17},{17,9},{25,1},{2,26},{10... | collective-permute-start | bytes 313352 | tf_op jit(solution)/shard_map/ppermute | solution.py:308
  117.4 6.1 %collective-permute-done.28.refs_2_ = bf16[24,2176]{1,0:T(8,128)(2,1)S(1)} collective-permute-done((bf16[24,2176]{1,0:T(8,128)(2,1)S(1)}, bf16[24,2176]{1,0:T(8,128)(2,1)S(1)}, u32[]{:S(2)}, u32[]{:S(2)}) %collective-permute-start.28) | collective-permute-done | bytes 104480 | tf_op jit(solution)/shard_map/ppermute | solution.py:308
  123.5 8.1 %shard_map.206 = (f32[24,5120]{1,0:T(8,128)S(1)}, bf16[24,5120]{1,0:T(8,128)(2,1)S(1)}, f32[12,128]{1,0:T(8,128)S(1)}) custom-call(bf16[24,2176]{1,0:T(8,128)(2,1)S(1)} %get-tuple-element.72.refs_0_, bf16[24,2176]{1,0:T(8,128)(2,1)S(1)} %collective-permute-done.27.refs_1_, bf16[24,2176]{1,0:T(8,128)(2,1)S(1)} %collective-permute-done.28.refs_2_, ...), custom_call_target="tpu_custom_call" | custom-call | flops 2013265920 | bytes 42360832 | tf_op jit(solution)/shard_map/pallas_call | solution.py:26
  131.7 1.5 collective-permute-done.30.refs_1_
  133.4 1.5 %collective-permute-start.31 = (bf16[24,1280]{1,0:T(8,128)(2,1)S(1)}, bf16[24,1280]{1,0:T(8,128)(2,1)S(1)}, u32[]{:S(2)}, u32[]{:S(2)}) collective-permute-start(bf16[24,1280]{1,0:T(8,128)(2,1)S(1)} %get-tuple-element.76), channel_id=1, source_target_pairs={{0,2},{1,3},{2,0},{3,1},{4,6},{5,7},{6,4},{7,5},{8,10},{9,11},{10,... | collective-permute-start | bytes 184328 | tf_op jit(solution)/shard_map/ppermute | solution.py:312
  134.9 1.5 %collective-permute-start.32 = (bf16[24,1280]{1,0:T(8,128)(2,1)S(1)}, bf16[24,1280]{1,0:T(8,128)(2,1)S(1)}, u32[]{:S(2)}, u32[]{:S(2)}) collective-permute-start(bf16[24,1280]{1,0:T(8,128)(2,1)S(1)} %get-tuple-element.77), channel_id=1, source_target_pairs={{0,4},{1,5},{2,6},{3,7},{4,0},{5,1},{6,2},{7,3},{8,12},{9,13},{10,... | collective-permute-start | bytes 184328 | tf_op jit(solution)/shard_map/ppermute | solution.py:312
  137.6 1.5 collective-permute-done.32.refs_2_
  139.1 2.4 %collective-permute-done.33.refs_3_ = bf16[24,1280]{1,0:T(8,128)(2,1)S(1)} collective-permute-done((bf16[24,1280]{1,0:T(8,128)(2,1)S(1)}, bf16[24,1280]{1,0:T(8,128)(2,1)S(1)}, u32[]{:S(2)}, u32[]{:S(2)}) %collective-permute-start.33) | collective-permute-done | bytes 61472 | tf_op jit(solution)/shard_map/ppermute | solution.py:312
  145.3 2.4 %collective-permute-start.37 = (f32[8,1024]{1,0:T(8,128)S(1)}, f32[8,1024]{1,0:T(8,128)S(1)}, u32[]{:S(2)}, u32[]{:S(2)}) collective-permute-start(f32[8,1024]{1,0:T(8,128)S(1)} %shard_map.209.refs_0_), channel_id=1, source_target_pairs={{0,6},{1,7},{2,4},{3,5},{4,2},{5,3},{6,0},{7,1},{8,14},{9,15},{10,... | collective-permute-start | bytes 98312 | tf_op jit(solution)/shard_map/ppermute | solution.py:312
  (113 shorter events, 32.0 us)
Async XLA Ops:
  5.8 5.3 %collective-permute-start = (bf16[24,1280]{1,0:T(8,128)(2,1)S(1)}, bf16[24,1280]{1,0:T(8,128)(2,1)S(1)}, u32[]{:S(2)}, u32[]{:S(2)}) collective-permute-start(bf16[24,1280]{1,0:T(8,128)(2,1)S(1)} %get-tuple-element.49.refs_0_), channel_id=1, source_target_pairs={{0,2},{1,3},{2,0},{3,1},{4,6},{5,7},{6,4},{7,5},{8,10},{9,11},{10,... | collective-permute-start | bytes 184328 | tf_op jit(solution)/shard_map/ppermute | solution.py:312
  8.8 4.2 %collective-permute-start.1 = (bf16[24,1280]{1,0:T(8,128)(2,1)S(1)}, bf16[24,1280]{1,0:T(8,128)(2,1)S(1)}, u32[]{:S(2)}, u32[]{:S(2)}) collective-permute-start(bf16[24,1280]{1,0:T(8,128)(2,1)S(1)} %get-tuple-element.49.refs_0_), channel_id=1, source_target_pairs={{0,4},{1,5},{2,6},{3,7},{4,0},{5,1},{6,2},{7,3},{8,12},{9,13},{10,... | collective-permute-start | bytes 184328 | tf_op jit(solution)/shard_map/ppermute | solution.py:312
  10.3 5.1 %collective-permute-start.2 = (bf16[24,1280]{1,0:T(8,128)(2,1)S(1)}, bf16[24,1280]{1,0:T(8,128)(2,1)S(1)}, u32[]{:S(2)}, u32[]{:S(2)}) collective-permute-start(bf16[24,1280]{1,0:T(8,128)(2,1)S(1)} %get-tuple-element.49.refs_0_), channel_id=1, source_target_pairs={{0,6},{1,7},{2,4},{3,5},{4,2},{5,3},{6,0},{7,1},{8,14},{9,15},{10,... | collective-permute-start | bytes 184328 | tf_op jit(solution)/shard_map/ppermute | solution.py:312
  10.3 5.1 %collective-permute-start.3 = (bf16[24,1280]{1,0:T(8,128)(2,1)S(1)}, bf16[24,1280]{1,0:T(8,128)(2,1)S(1)}, u32[]{:S(2)}, u32[]{:S(2)}) collective-permute-start(bf16[24,1280]{1,0:T(8,128)(2,1)S(1)} %get-tuple-element.49.refs_0_), channel_id=1, source_target_pairs={{0,1},{1,0},{2,3},{3,2},{4,5},{5,4},{6,7},{7,6},{8,9},{9,8},{10,11... | collective-permute-start | bytes 184328 | tf_op jit(solution)/shard_map/ppermute | solution.py:316
  11.0 4.4 %collective-permute-start.4 = (bf16[24,1280]{1,0:T(8,128)(2,1)S(1)}, bf16[24,1280]{1,0:T(8,128)(2,1)S(1)}, u32[]{:S(2)}, u32[]{:S(2)}) collective-permute-start(bf16[24,1280]{1,0:T(8,128)(2,1)S(1)} %collective-permute-done.refs_1_), channel_id=1, source_target_pairs={{0,1},{1,0},{2,3},{3,2},{4,5},{5,4},{6,7},{7,6},{8,9},{9,8},{10,11... | collective-permute-start | bytes 184328 | tf_op jit(solution)/shard_map/ppermute | solution.py:316
  13.0 2.4 %collective-permute-start.5 = (bf16[24,1280]{1,0:T(8,128)(2,1)S(1)}, bf16[24,1280]{1,0:T(8,128)(2,1)S(1)}, u32[]{:S(2)}, u32[]{:S(2)}) collective-permute-start(bf16[24,1280]{1,0:T(8,128)(2,1)S(1)} %collective-permute-done.1.refs_2_), channel_id=1, source_target_pairs={{0,1},{1,0},{2,3},{3,2},{4,5},{5,4},{6,7},{7,6},{8,9},{9,8},{10,11... | collective-permute-start | bytes 184328 | tf_op jit(solution)/shard_map/ppermute | solution.py:316
  30.6 5.4 %collective-permute-start.7 = (bf16[24,2176]{1,0:T(8,128)(2,1)S(1)}, bf16[24,2176]{1,0:T(8,128)(2,1)S(1)}, u32[]{:S(2)}, u32[]{:S(2)}) collective-permute-start(bf16[24,2176]{1,0:T(8,128)(2,1)S(1)} %get-tuple-element.51), channel_id=1, source_target_pairs={{0,8},{8,0},{16,24},{24,16},{1,9},{9,1},{17,25},{25,17},{2,10},{10... | collective-permute-start | bytes 313352 | tf_op jit(solution)/shard_map/ppermute | solution.py:308
  33.0 10.9 %collective-permute-start.8 = (bf16[24,2176]{1,0:T(8,128)(2,1)S(1)}, bf16[24,2176]{1,0:T(8,128)(2,1)S(1)}, u32[]{:S(2)}, u32[]{:S(2)}) collective-permute-start(bf16[24,2176]{1,0:T(8,128)(2,1)S(1)} %get-tuple-element.52), channel_id=1, source_target_pairs={{0,16},{8,24},{16,0},{24,8},{1,17},{9,25},{17,1},{25,9},{2,18},{10... | collective-permute-start | bytes 313352 | tf_op jit(solution)/shard_map/ppermute | solution.py:308
  35.6 8.3 %collective-permute-start.9 = (bf16[24,2176]{1,0:T(8,128)(2,1)S(1)}, bf16[24,2176]{1,0:T(8,128)(2,1)S(1)}, u32[]{:S(2)}, u32[]{:S(2)}) collective-permute-start(bf16[24,2176]{1,0:T(8,128)(2,1)S(1)} %get-tuple-element.53), channel_id=1, source_target_pairs={{0,24},{8,16},{16,8},{24,0},{1,25},{9,17},{17,9},{25,1},{2,26},{10... | collective-permute-start | bytes 313352 | tf_op jit(solution)/shard_map/ppermute | solution.py:308
  44.2 5.8 %collective-permute-start.10 = (bf16[24,2176]{1,0:T(8,128)(2,1)S(1)}, bf16[24,2176]{1,0:T(8,128)(2,1)S(1)}, u32[]{:S(2)}, u32[]{:S(2)}) collective-permute-start(bf16[24,2176]{1,0:T(8,128)(2,1)S(1)} %get-tuple-element.54.refs_0_), channel_id=1, source_target_pairs={{0,8},{8,0},{16,24},{24,16},{1,9},{9,1},{17,25},{25,17},{2,10},{10... | collective-permute-start | bytes 313352 | tf_op jit(solution)/shard_map/ppermute | solution.py:308
  45.9 9.6 %collective-permute-start.11 = (bf16[24,2176]{1,0:T(8,128)(2,1)S(1)}, bf16[24,2176]{1,0:T(8,128)(2,1)S(1)}, u32[]{:S(2)}, u32[]{:S(2)}) collective-permute-start(bf16[24,2176]{1,0:T(8,128)(2,1)S(1)} %get-tuple-element.54.refs_0_), channel_id=1, source_target_pairs={{0,16},{8,24},{16,0},{24,8},{1,17},{9,25},{17,1},{25,9},{2,18},{10... | collective-permute-start | bytes 313352 | tf_op jit(solution)/shard_map/ppermute | solution.py:308
  47.3 8.3 %collective-permute-start.12 = (bf16[24,2176]{1,0:T(8,128)(2,1)S(1)}, bf16[24,2176]{1,0:T(8,128)(2,1)S(1)}, u32[]{:S(2)}, u32[]{:S(2)}) collective-permute-start(bf16[24,2176]{1,0:T(8,128)(2,1)S(1)} %get-tuple-element.54.refs_0_), channel_id=1, source_target_pairs={{0,24},{8,16},{16,8},{24,0},{1,25},{9,17},{17,9},{25,1},{2,26},{10... | collective-permute-start | bytes 313352 | tf_op jit(solution)/shard_map/ppermute | solution.py:308
  65.3 4.3 %collective-permute-start.14 = (bf16[24,1280]{1,0:T(8,128)(2,1)S(1)}, bf16[24,1280]{1,0:T(8,128)(2,1)S(1)}, u32[]{:S(2)}, u32[]{:S(2)}) collective-permute-start(bf16[24,1280]{1,0:T(8,128)(2,1)S(1)} %get-tuple-element.58), channel_id=1, source_target_pairs={{0,2},{1,3},{2,0},{3,1},{4,6},{5,7},{6,4},{7,5},{8,10},{9,11},{10,... | collective-permute-start | bytes 184328 | tf_op jit(solution)/shard_map/ppermute | solution.py:312
  66.9 4.2 %collective-permute-start.15 = (bf16[24,1280]{1,0:T(8,128)(2,1)S(1)}, bf16[24,1280]{1,0:T(8,128)(2,1)S(1)}, u32[]{:S(2)}, u32[]{:S(2)}) collective-permute-start(bf16[24,1280]{1,0:T(8,128)(2,1)S(1)} %get-tuple-element.59), channel_id=1, source_target_pairs={{0,4},{1,5},{2,6},{3,7},{4,0},{5,1},{6,2},{7,3},{8,12},{9,13},{10,... | collective-permute-start | bytes 184328 | tf_op jit(solution)/shard_map/ppermute | solution.py:312
  68.4 5.1 %collective-permute-start.16 = (bf16[24,1280]{1,0:T(8,128)(2,1)S(1)}, bf16[24,1280]{1,0:T(8,128)(2,1)S(1)}, u32[]{:S(2)}, u32[]{:S(2)}) collective-permute-start(bf16[24,1280]{1,0:T(8,128)(2,1)S(1)} %get-tuple-element.60), channel_id=1, source_target_pairs={{0,6},{1,7},{2,4},{3,5},{4,2},{5,3},{6,0},{7,1},{8,14},{9,15},{10,... | collective-permute-start | bytes 184328 | tf_op jit(solution)/shard_map/ppermute | solution.py:312
  76.4 4.3 %collective-permute-start.17 = (bf16[24,1280]{1,0:T(8,128)(2,1)S(1)}, bf16[24,1280]{1,0:T(8,128)(2,1)S(1)}, u32[]{:S(2)}, u32[]{:S(2)}) collective-permute-start(bf16[24,1280]{1,0:T(8,128)(2,1)S(1)} %get-tuple-element.65.refs_0_), channel_id=1, source_target_pairs={{0,2},{1,3},{2,0},{3,1},{4,6},{5,7},{6,4},{7,5},{8,10},{9,11},{10,... | collective-permute-start | bytes 184328 | tf_op jit(solution)/shard_map/ppermute | solution.py:312
  77.0 4.2 %collective-permute-start.18 = (bf16[24,1280]{1,0:T(8,128)(2,1)S(1)}, bf16[24,1280]{1,0:T(8,128)(2,1)S(1)}, u32[]{:S(2)}, u32[]{:S(2)}) collective-permute-start(bf16[24,1280]{1,0:T(8,128)(2,1)S(1)} %get-tuple-element.65.refs_0_), channel_id=1, source_target_pairs={{0,4},{1,5},{2,6},{3,7},{4,0},{5,1},{6,2},{7,3},{8,12},{9,13},{10,... | collective-permute-start | bytes 184328 | tf_op jit(solution)/shard_map/ppermute | solution.py:312
  77.6 5.1 %collective-permute-start.19 = (bf16[24,1280]{1,0:T(8,128)(2,1)S(1)}, bf16[24,1280]{1,0:T(8,128)(2,1)S(1)}, u32[]{:S(2)}, u32[]{:S(2)}) collective-permute-start(bf16[24,1280]{1,0:T(8,128)(2,1)S(1)} %get-tuple-element.65.refs_0_), channel_id=1, source_target_pairs={{0,6},{1,7},{2,4},{3,5},{4,2},{5,3},{6,0},{7,1},{8,14},{9,15},{10,... | collective-permute-start | bytes 184328 | tf_op jit(solution)/shard_map/ppermute | solution.py:312
  80.0 2.7 %collective-permute-start.20 = (bf16[24,1280]{1,0:T(8,128)(2,1)S(1)}, bf16[24,1280]{1,0:T(8,128)(2,1)S(1)}, u32[]{:S(2)}, u32[]{:S(2)}) collective-permute-start(bf16[24,1280]{1,0:T(8,128)(2,1)S(1)} %get-tuple-element.65.refs_0_), channel_id=1, source_target_pairs={{0,1},{1,0},{2,3},{3,2},{4,5},{5,4},{6,7},{7,6},{8,9},{9,8},{10,11... | collective-permute-start | bytes 184328 | tf_op jit(solution)/shard_map/ppermute | solution.py:316
  80.7 2.0 %collective-permute-start.21 = (bf16[24,1280]{1,0:T(8,128)(2,1)S(1)}, bf16[24,1280]{1,0:T(8,128)(2,1)S(1)}, u32[]{:S(2)}, u32[]{:S(2)}) collective-permute-start(bf16[24,1280]{1,0:T(8,128)(2,1)S(1)} %collective-permute-done.17.refs_1_), channel_id=1, source_target_pairs={{0,1},{1,0},{2,3},{3,2},{4,5},{5,4},{6,7},{7,6},{8,9},{9,8},{10,11... | collective-permute-start | bytes 184328 | tf_op jit(solution)/shard_map/ppermute | solution.py:316
  97.7 5.1 %collective-permute-start.24 = (bf16[24,2176]{1,0:T(8,128)(2,1)S(1)}, bf16[24,2176]{1,0:T(8,128)(2,1)S(1)}, u32[]{:S(2)}, u32[]{:S(2)}) collective-permute-start(bf16[24,2176]{1,0:T(8,128)(2,1)S(1)} %get-tuple-element.67), channel_id=1, source_target_pairs={{0,8},{8,0},{16,24},{24,16},{1,9},{9,1},{17,25},{25,17},{2,10},{10... | collective-permute-start | bytes 313352 | tf_op jit(solution)/shard_map/ppermute | solution.py:308
  99.5 11.1 %collective-permute-start.25 = (bf16[24,2176]{1,0:T(8,128)(2,1)S(1)}, bf16[24,2176]{1,0:T(8,128)(2,1)S(1)}, u32[]{:S(2)}, u32[]{:S(2)}) collective-permute-start(bf16[24,2176]{1,0:T(8,128)(2,1)S(1)} %get-tuple-element.68), channel_id=1, source_target_pairs={{0,16},{8,24},{16,0},{24,8},{1,17},{9,25},{17,1},{25,9},{2,18},{10... | collective-permute-start | bytes 313352 | tf_op jit(solution)/shard_map/ppermute | solution.py:308
  100.5 10.2 %collective-permute-start.26 = (bf16[24,2176]{1,0:T(8,128)(2,1)S(1)}, bf16[24,2176]{1,0:T(8,128)(2,1)S(1)}, u32[]{:S(2)}, u32[]{:S(2)}) collective-permute-start(bf16[24,2176]{1,0:T(8,128)(2,1)S(1)} %get-tuple-element.69), channel_id=1, source_target_pairs={{0,24},{8,16},{16,8},{24,0},{1,25},{9,17},{17,9},{25,1},{2,26},{10... | collective-permute-start | bytes 313352 | tf_op jit(solution)/shard_map/ppermute | solution.py:308
  111.6 5.8 %collective-permute-start.27 = (bf16[24,2176]{1,0:T(8,128)(2,1)S(1)}, bf16[24,2176]{1,0:T(8,128)(2,1)S(1)}, u32[]{:S(2)}, u32[]{:S(2)}) collective-permute-start(bf16[24,2176]{1,0:T(8,128)(2,1)S(1)} %get-tuple-element.72.refs_0_), channel_id=1, source_target_pairs={{0,8},{8,0},{16,24},{24,16},{1,9},{9,1},{17,25},{25,17},{2,10},{10... | collective-permute-start | bytes 313352 | tf_op jit(solution)/shard_map/ppermute | solution.py:308
  113.3 10.2 %collective-permute-start.28 = (bf16[24,2176]{1,0:T(8,128)(2,1)S(1)}, bf16[24,2176]{1,0:T(8,128)(2,1)S(1)}, u32[]{:S(2)}, u32[]{:S(2)}) collective-permute-start(bf16[24,2176]{1,0:T(8,128)(2,1)S(1)} %get-tuple-element.72.refs_0_), channel_id=1, source_target_pairs={{0,16},{8,24},{16,0},{24,8},{1,17},{9,25},{17,1},{25,9},{2,18},{10... | collective-permute-start | bytes 313352 | tf_op jit(solution)/shard_map/ppermute | solution.py:308
  114.2 9.3 %collective-permute-start.29 = (bf16[24,2176]{1,0:T(8,128)(2,1)S(1)}, bf16[24,2176]{1,0:T(8,128)(2,1)S(1)}, u32[]{:S(2)}, u32[]{:S(2)}) collective-permute-start(bf16[24,2176]{1,0:T(8,128)(2,1)S(1)} %get-tuple-element.72.refs_0_), channel_id=1, source_target_pairs={{0,24},{8,16},{16,8},{24,0},{1,25},{9,17},{17,9},{25,1},{2,26},{10... | collective-permute-start | bytes 313352 | tf_op jit(solution)/shard_map/ppermute | solution.py:308
  133.4 4.3 %collective-permute-start.31 = (bf16[24,1280]{1,0:T(8,128)(2,1)S(1)}, bf16[24,1280]{1,0:T(8,128)(2,1)S(1)}, u32[]{:S(2)}, u32[]{:S(2)}) collective-permute-start(bf16[24,1280]{1,0:T(8,128)(2,1)S(1)} %get-tuple-element.76), channel_id=1, source_target_pairs={{0,2},{1,3},{2,0},{3,1},{4,6},{5,7},{6,4},{7,5},{8,10},{9,11},{10,... | collective-permute-start | bytes 184328 | tf_op jit(solution)/shard_map/ppermute | solution.py:312
  134.9 4.2 %collective-permute-start.32 = (bf16[24,1280]{1,0:T(8,128)(2,1)S(1)}, bf16[24,1280]{1,0:T(8,128)(2,1)S(1)}, u32[]{:S(2)}, u32[]{:S(2)}) collective-permute-start(bf16[24,1280]{1,0:T(8,128)(2,1)S(1)} %get-tuple-element.77), channel_id=1, source_target_pairs={{0,4},{1,5},{2,6},{3,7},{4,0},{5,1},{6,2},{7,3},{8,12},{9,13},{10,... | collective-permute-start | bytes 184328 | tf_op jit(solution)/shard_map/ppermute | solution.py:312
  136.4 5.1 %collective-permute-start.33 = (bf16[24,1280]{1,0:T(8,128)(2,1)S(1)}, bf16[24,1280]{1,0:T(8,128)(2,1)S(1)}, u32[]{:S(2)}, u32[]{:S(2)}) collective-permute-start(bf16[24,1280]{1,0:T(8,128)(2,1)S(1)} %get-tuple-element.78), channel_id=1, source_target_pairs={{0,6},{1,7},{2,4},{3,5},{4,2},{5,3},{6,0},{7,1},{8,14},{9,15},{10,... | collective-permute-start | bytes 184328 | tf_op jit(solution)/shard_map/ppermute | solution.py:312
  144.3 4.1 %collective-permute-start.35 = (f32[8,1024]{1,0:T(8,128)S(1)}, f32[8,1024]{1,0:T(8,128)S(1)}, u32[]{:S(2)}, u32[]{:S(2)}) collective-permute-start(f32[8,1024]{1,0:T(8,128)S(1)} %shard_map.209.refs_0_), channel_id=1, source_target_pairs={{0,2},{1,3},{2,0},{3,1},{4,6},{5,7},{6,4},{7,5},{8,10},{9,11},{10,... | collective-permute-start | bytes 98312 | tf_op jit(solution)/shard_map/ppermute | solution.py:312
  144.8 4.3 %collective-permute-start.36 = (f32[8,1024]{1,0:T(8,128)S(1)}, f32[8,1024]{1,0:T(8,128)S(1)}, u32[]{:S(2)}, u32[]{:S(2)}) collective-permute-start(f32[8,1024]{1,0:T(8,128)S(1)} %shard_map.209.refs_0_), channel_id=1, source_target_pairs={{0,4},{1,5},{2,6},{3,7},{4,0},{5,1},{6,2},{7,3},{8,12},{9,13},{10,... | collective-permute-start | bytes 98312 | tf_op jit(solution)/shard_map/ppermute | solution.py:312
  145.3 4.8 %collective-permute-start.37 = (f32[8,1024]{1,0:T(8,128)S(1)}, f32[8,1024]{1,0:T(8,128)S(1)}, u32[]{:S(2)}, u32[]{:S(2)}) collective-permute-start(f32[8,1024]{1,0:T(8,128)S(1)} %shard_map.209.refs_0_), channel_id=1, source_target_pairs={{0,6},{1,7},{2,4},{3,5},{4,2},{5,3},{6,0},{7,1},{8,14},{9,15},{10,... | collective-permute-start | bytes 98312 | tf_op jit(solution)/shard_map/ppermute | solution.py:312
  (32 other events, 495.7 us)

commit v4 on v3

--- a/solution.py
+++ b/solution.py
@@ -10,7 +10,7 @@
 
 BUSES = 20480
 ITERS = 2
-CHUNKS = 1
+CHUNKS = 2
 LANES = 128
 GRANT = 11 << 20
 BF = jnp.bfloat16
@@ -45,6 +45,19 @@
     middle = rest.astype(BF)
     low = (rest - middle.astype(F32)).astype(BF)
     return high, middle, low
+
+
+def stacked(value):
+    rows, columns = value.shape
+    below = [jnp.zeros((8 - rows, columns), F32)] if rows < 8 else []
+    parts = []
+    for piece in pieces(value):
+        parts += [piece.astype(F32)] + below
+    return jnp.concatenate(parts, 0).astype(BF)
+
+
+def unstacked(product, rows):
+    return (product[16 : 16 + rows] + product[8 : 8 + rows]) + product[:rows]
 
 
 def dot_t(a, b):
@@ -74,9 +87,7 @@
 
 
 def place(sz, gens, select, block):
-    spread = select[block]
-    high, middle, low = pieces(gens)
-    return (dot_t(low, spread) + dot_t(middle, spread)) + dot_t(high, spread)
+    return unstacked(dot_t(stacked(gens), select[block]), sz.rows)
 
 
 def blocks_of(sz):
@@ -94,9 +105,9 @@
         buses = slice(block * sz.width, (block + 1) * sz.width)
         local = gen_bus[:, lanes] - (first + block * sz.width)
         select[block] = (bus == local).astype(F32).astype(BF)
-        here, load = shed[:, buses], loads[:, buses]
-        inject[rows, cols] = (place(sz, dispatch[:, lanes], select, block) + here - load).astype(BF)
-        shed_p[rows, cols] = here
+        served, load = shed[:, buses], loads[:, buses]
+        inject[rows, cols] = (place(sz, dispatch[:, lanes], select, block) + served - load).astype(BF)
+        shed_p[rows, cols] = served
         loads_p[rows, cols] = load
 
 
@@ -139,7 +150,7 @@
         def body(i, _, side=side):
             source = pl.ds(pl.multiple_of(chunk * sz.chunk + side * sz.half + i * step, step), step)
             target = pl.ds(pl.multiple_of(i * step, step), step)
-            product = dot_t(inject[...], factors[source, :])
+            product = dot_t(factors[source, :], inject[...]).T
             for slot in range(chips):
                 flows[slot, side * sz.pair : (side + 1) * sz.pair, target] = product[
                     slot * sz.pair : (slot + 1) * sz.pair
@@ -156,11 +167,17 @@
     scen = sz.scen
     parts = refs[:scen]
     copies, duals, limits = refs[scen : scen + 3]
-    old = refs[scen + 3 : scen + 5] if join else None
-    residual, copy_out, dual_out = refs[-3:]
+    wide = sz.half + LANES
+    if chunk == 0:
+        flows = refs[scen + 3 : 2 * scen + 2]
+        residual, copy_out, dual_out = refs[2 * scen + 2 : 2 * scen + 5]
+        messages = refs[2 * scen + 5 :]
+    else:
+        old = refs[scen + 3 : scen + 5] if join else None
+        residual, copy_out, dual_out = refs[-3:]
     total = parts[0][...]
     for part in parts[1:]:
-        total = total + part[...].astype(F32)
+        total = total + part[:, wide if chunk else 0 :].astype(F32)
     for side in range(2):
         rows = slice(side * sz.pair, (side + 1) * sz.pair)
         start = chunk * sz.chunk + side * sz.half
@@ -173,15 +190,18 @@
         copy_next = jnp.minimum(jnp.maximum(now + dual, -limit), limit)
         copy_out[:, to] = copy_next
         dual_out[:, to] = dual + now - copy_next
-    if join:
-        copy_out[:, : chunk * sz.chunk] = old[0][...]
-        dual_out[:, : chunk * sz.chunk] = old[1][...]
     if chunk == 0:
         balance = jnp.sum(total[:, sz.half :], axis=1, keepdims=True) / BUSES
         high, middle, low = (piece.astype(F32) for piece in pieces(balance))
         lane = lax.broadcasted_iota(jnp.int32, (2 * sz.pair, LANES), 1)
         tile = jnp.where(lane == 0, high, jnp.where(lane == 1, middle, jnp.where(lane == 2, low, 0.0)))
         residual[:, sz.half :] = tile.astype(BF)
+        for message, flow in zip(messages, flows):
+            message[:, :wide] = residual[...]
+            message[:, wide:] = flow[...]
+    elif join:
+        copy_out[:, : chunk * sz.chunk] = old[0][...]
+        dual_out[:, : chunk * sz.chunk] = old[1][...]
 
 
 def backward_kernel(sz, chunk, step, *refs):
@@ -198,7 +218,7 @@
 
             @pl.when(chip == (me ^ slot))
             def _(slot=slot):
-                tile = parts[slot][: sz.pair, sz.half :].astype(F32)
+                tile = parts[slot][: sz.pair, sz.half : sz.half + LANES].astype(F32)
                 found = jnp.sum(tile, axis=1, keepdims=True)
                 balances[...] = jnp.broadcast_to(found, (sz.pair, LANES))
 
@@ -262,23 +282,21 @@
     shed_next = jnp.minimum(jnp.maximum(shed[...] - 0.4 * (1.5 + grad), 0.0), loads[...])
     capacity = cap[...] * commit[...].astype(F32)
     if last:
-        weights, gens_out, shed_out, lam_out, weighted_out = rest
+        weights, gens_out, shed_out, lam_out, weighted_out, dual_out = rest
     else:
         gens_out, shed_out, lam_out, inject = rest
         shed_out[...] = shed_next
     lam_out[...] = jnp.broadcast_to(lam_now + balance, lam_out.shape)
     for block, rows, cols in blocks_of(sz):
         lanes = slice(block * LANES, (block + 1) * LANES)
-        spread = select[block]
-        high, middle, low = (
-            jnp.dot(piece, spread, preferred_element_type=F32) for piece in pieces(grad[rows, cols])
-        )
-        picked = (low + middle) + high
+        picked = jnp.dot(stacked(grad[rows, cols]), select[block], preferred_element_type=F32)
+        picked = unstacked(picked, sz.rows)
         now = gens[:, lanes]
         gen_grad = costs[:1, lanes] + costs[1:, lanes] * now + dual[:, lanes] + (now - previous[:, lanes]) + picked
         now = jnp.minimum(jnp.maximum(now - 0.4 * gen_grad, 0.0), capacity[:, lanes])
         gens_out[:, lanes] = now
         if last:
+            dual_out[:, lanes] = dual[:, lanes] + now
             shed_out[:, block * sz.width : (block + 1) * sz.width] = shed_next[rows, cols]
             weighted_out[:1, lanes] = jnp.sum(weights[:, :1] * now, axis=0, keepdims=True)
             all_weights = jnp.sum(weights[:, :1], axis=0, keepdims=True)
@@ -295,13 +313,13 @@
 
 def finish_kernel(sz, *refs):
     parts = refs[: sz.chips]
-    dual, gens, consensus, dual_out = refs[sz.chips :]
+    dual, consensus, dual_out = refs[sz.chips :]
     total = parts[0][...]
     for part in parts[1:]:
         total = total + part[...]
     mean = total[:1] / total[1:2]
     consensus[...] = mean
-    dual_out[...] = dual[...] + (gens[...] - mean)
+    dual_out[...] = dual[...] - mean
 
 
 def to_scen(n, away, value):
@@ -343,7 +361,7 @@
     capacity, on, previous, limits = row(gen_cap), row(commit), row(consensus_prev), row(flow_limit)
     lam, weights = column(balance_dual), column(scen_weight)
     packed = (sz.fold * rows, sz.part)
-    step_f = min(512, sz.half)
+    step_f = min(1024, sz.half)
     step_b = next(s for s in (1024, 640, 512, 256, 128) if buses % s == 0)
     macs = sz.total * sz.chunk * buses
 
@@ -360,37 +378,50 @@
     for iteration in range(ITERS):
         own = [inject] + [to_chip(n_line, away, inject) for away in range(1, chips)]
         other = [to_core(n_line, value) for value in own]
-        residuals, new_copies, new_duals = [], [], []
         final = iteration == ITERS - 1
+        tall = 2 * sz.pair
+        widths = (sz.half + LANES, sz.half)
+        flows = []
         for chunk in range(CHUNKS):
-            block = (2 * sz.pair, sz.half + (LANES if chunk == 0 else 0))
-            flows = call(
-                functools.partial(forward_kernel, sz, chunk, step_f),
-                (*own, *other, shift_factors),
-                [(block, F32)] + [(block, BF)] * (chips - 1),
-                [((sz.total, buses), BF), ((chips, *block), F32)],
-                flops=2 * macs,
-                limit=GRANT - (nbytes(own + other) if iteration == 0 else 0),
+            block = (tall, widths[chunk])
+            flows.append(
+                call(
+                    functools.partial(forward_kernel, sz, chunk, step_f),
+                    (*own, *other, shift_factors),
+                    [(block, F32)] + [(block, BF)] * (n_scen - 1),
+                    [((sz.total, buses), BF), ((chips, *block), F32)],
+                    flops=2 * macs,
+                    limit=GRANT - (nbytes(own + other) if iteration == 0 else 0),
+                )
             )
-            parts = [flows[0]] + [to_scen(n_scen, away, flows[away]) for away in range(1, n_scen)]
-            join = final and chunk == CHUNKS - 1 and CHUNKS > 1
-            width = lines if join else sz.chunk
-            whole = iteration == 0
-            residual, copy_next, dual_next = call(
-                functools.partial(residual_kernel, sz, chunk, join),
-                (
-                    *parts,
-                    flow_copy if whole else copies[chunk],
-                    flow_dual if whole else duals[chunk],
-                    limits,
-                    *((new_copies[0], new_duals[0]) if join else ()),
-                ),
-                [(block, BF), ((sz.pair, width), F32), ((sz.pair, width), F32)],
-                keep=shift_factors,
-            )
-            new_copies.append(copy_next)
-            new_duals.append(dual_next)
-            residuals.append([residual] + [to_scen(n_scen, away, residual) for away in range(1, n_scen)])
+            if chunk == 0:
+                parts = [flows[0][0]] + [to_scen(n_scen, away, flows[0][away]) for away in range(1, n_scen)]
+        state = lambda width: [((sz.pair, width), F32)] * 2
+        old = (flow_copy, flow_dual) if iteration == 0 else None
+        first_res, first_copy, first_dual, *messages = call(
+            functools.partial(residual_kernel, sz, 0, False),
+            (*parts, *(old or (copies[0], duals[0])), limits, *flows[1][1:]),
+            [((tall, widths[0]), BF), *state(sz.chunk)] + [((tall, sum(widths)), BF)] * (n_scen - 1),
+            keep=shift_factors,
+        )
+        got = [to_scen(n_scen, away, message) for away, message in enumerate(messages, 1)]
+        second_res, second_copy, second_dual = call(
+            functools.partial(residual_kernel, sz, 1, final),
+            (
+                flows[1][0],
+                *got,
+                *(old or (copies[1], duals[1])),
+                limits,
+                *((first_copy, first_dual) if final else ()),
+            ),
+            [((tall, widths[1]), BF), *state(lines if final else sz.chunk)],
+            keep=shift_factors,
+        )
+        residuals = [
+            [first_res, *got],
+            [second_res] + [to_scen(n_scen, away, second_res) for away in range(1, n_scen)],
+        ]
+        new_copies, new_duals = [first_copy, second_copy], [first_dual, second_dual]
         copies, duals = new_copies, new_duals
         before, balances = (), None
         for chunk in range(CHUNKS):
@@ -428,16 +459,16 @@
                 limit=GRANT - nbytes((dispatch, shed, loads, select)),
             )
         else:
-            generation, shed, lam, weighted = call(
+            generation, shed, lam, weighted, dual_sum = call(
                 functools.partial(update_kernel, sz, True),
                 (*args, weights),
-                [((rows, gens), F32), ((rows, buses), F32), ((rows, LANES), F32), ((8, gens), F32)],
+                [((rows, gens), F32), ((rows, buses), F32), ((rows, LANES), F32), ((8, gens), F32), ((rows, gens), F32)],
             )
     (weighted,) = call(add_kernel, (weighted, to_core(n_line, weighted)), [((8, gens), F32)])
     parts = [weighted] + [to_chip(n_line, away, weighted) for away in range(1, chips)]
     consensus, dual_out = call(
         functools.partial(finish_kernel, sz),
-        (*parts, ph_dual, generation),
+        (*parts, dual_sum),
         [((1, gens), F32), ((rows, gens), F32)],
     )
     return generation, shed, copies[-1], duals[-1], lam[:, 0], consensus.reshape(-1), dual_out

time: 152 us -> 138 us (0.908)
  waiting for transfers between devices: 56.6 us -> 39.6 us
  starting transfers between devices: 37.2 us -> 46.7 us
  Pallas kernels: 51.4 us -> 45.6 us
    ppermute x12 -> x18, waiting for transfers between devices: 31.2 us -> 14.1 us  [to_scen(): return lax.ppermute(value, 'scen', [(i, i ^ away) for i in range(n)])]
    ppermute x12 -> x18, starting transfers between devices: 18.3 us -> 27.9 us  [to_scen(): return lax.ppermute(value, 'scen', [(i, i ^ away) for i in range(n)])]
    pallas_call x13 -> x19, Pallas kernels: 51.4 us -> 45.6 us  [call(): pl.pallas_call(kernel, in_specs=[WHOLE] * len(args), out_specs=[WHOLE] *...]
    unnamed x52 -> x50, local copies, waits for them, and re-layouts: 4.5 us -> 3.89 us
  transfers between devices with their start and end apart: 38 -> 44, of which waited for: 27 -> 25; matrix products, arithmetic and copies ran while one was open for 0% -> 0% of each run, Pallas kernels for 0% -> 15%
where the time goes in v4:
time: 138 us
  starting transfers between devices  46.7 us (34%)
  Pallas kernels  45.6 us (33%)
  waiting for transfers between devices  39.6 us (29%)
  local copies, waits for them, and re-layouts  4.65 us (3%)
    pallas_call x19, Pallas kernels, call(): pl.pallas_call(kernel, in_specs=[WHOLE] * len(args), out_specs=[WHOLE] *...  45.6 us
    ppermute x18, starting transfers between devices, to_scen(): return lax.ppermute(value, 'scen', [(i, i ^ away) for i in range(n)])  27.9 us
    ppermute x15, waiting for transfers between devices, to_chip(): return lax.ppermute(value, 'line', [(i, i ^ 2 * away) for i in range(n)])  18.8 us
    ppermute x15, starting transfers between devices, to_chip(): return lax.ppermute(value, 'line', [(i, i ^ 2 * away) for i in range(n)])  18.7 us
    ppermute x18, waiting for transfers between devices, to_scen(): return lax.ppermute(value, 'scen', [(i, i ^ away) for i in range(n)])  14.1 us
    ppermute x11, waiting for transfers between devices, to_core(): return lax.ppermute(value, 'line', [(i, i ^ 1) for i in range(n)])  6.67 us
    unnamed x50, local copies, waits for them, and re-layouts  3.89 us
  transfers between devices with their start and end apart: 44, of which 25 were waited for; matrix products, arithmetic and copies ran while one was open for 0% of the time, Pallas kernels for 15%

profile of v4, /device:TPU:0, one launch (start us, length us, event | category | flops | bytes accessed | tf_op | source)
XLA Modules:
  0.0 137.7 jit_solution(13529548731765155181)
XLA Ops:
  5.0 3.0 %collective-permute-start = (bf16[24,1280]{1,0:T(8,128)(2,1)S(1)}, bf16[24,1280]{1,0:T(8,128)(2,1)S(1)}, u32[]{:S(2)}, u32[]{:S(2)}) collective-permute-start(bf16[24,1280]{1,0:T(8,128)(2,1)S(1)} %get-tuple-element.72.refs_0_), channel_id=1, source_target_pairs={{0,2},{1,3},{2,0},{3,1},{4,6},{5,7},{6,4},{7,5},{8,10},{9,11},{10,... | collective-permute-start | bytes 184328 | tf_op jit(solution)/shard_map/ppermute | solution.py:330
  8.0 1.5 %collective-permute-start.1 = (bf16[24,1280]{1,0:T(8,128)(2,1)S(1)}, bf16[24,1280]{1,0:T(8,128)(2,1)S(1)}, u32[]{:S(2)}, u32[]{:S(2)}) collective-permute-start(bf16[24,1280]{1,0:T(8,128)(2,1)S(1)} %get-tuple-element.72.refs_0_), channel_id=1, source_target_pairs={{0,4},{1,5},{2,6},{3,7},{4,0},{5,1},{6,2},{7,3},{8,12},{9,13},{10,... | collective-permute-start | bytes 184328 | tf_op jit(solution)/shard_map/ppermute | solution.py:330
  10.3 2.0 %collective-permute-done.1.refs_2_ = bf16[24,1280]{1,0:T(8,128)(2,1)S(1)} collective-permute-done((bf16[24,1280]{1,0:T(8,128)(2,1)S(1)}, bf16[24,1280]{1,0:T(8,128)(2,1)S(1)}, u32[]{:S(2)}, u32[]{:S(2)}) %collective-permute-start.1) | collective-permute-done | bytes 61472 | tf_op jit(solution)/shard_map/ppermute | solution.py:330
  12.2 2.4 %collective-permute-done.2.refs_3_ = bf16[24,1280]{1,0:T(8,128)(2,1)S(1)} collective-permute-done((bf16[24,1280]{1,0:T(8,128)(2,1)S(1)}, bf16[24,1280]{1,0:T(8,128)(2,1)S(1)}, u32[]{:S(2)}, u32[]{:S(2)}) %collective-permute-start.2) | collective-permute-done | bytes 61472 | tf_op jit(solution)/shard_map/ppermute | solution.py:330
  16.1 5.8 %shard_map.200 = (f32[24,1152]{1,0:T(8,128)S(1)}, bf16[24,1152]{1,0:T(8,128)(2,1)S(1)}, bf16[24,1152]{1,0:T(8,128)(2,1)S(1)}, bf16[24,1152]{1,0:T(8,128)(2,1)S(1)}) custom-call(bf16[24,1280]{1,0:T(8,128)(2,1)S(1)} %get-tuple-element.72.refs_0_, bf16[24,1280]{1,0:T(8,128)(2,1)S(1)} %collective-permute-done.refs_1_, ...), custom_call_target="tpu_custom_call" | custom-call | flops 1006632960 | bytes 42434560 | tf_op jit(solution)/shard_map/pallas_call | solution.py:26
  21.9 3.1 %collective-permute-start.7 = (bf16[24,1152]{1,0:T(8,128)(2,1)S(1)}, bf16[24,1152]{1,0:T(8,128)(2,1)S(1)}, u32[]{:S(2)}, u32[]{:S(2)}) collective-permute-start(bf16[24,1152]{1,0:T(8,128)(2,1)S(1)} %get-tuple-element.75), channel_id=1, source_target_pairs={{0,8},{8,0},{16,24},{24,16},{1,9},{9,1},{17,25},{25,17},{2,10},{10... | collective-permute-start | bytes 165896 | tf_op jit(solution)/shard_map/ppermute | solution.py:326
  25.0 2.6 %collective-permute-start.8 = (bf16[24,1152]{1,0:T(8,128)(2,1)S(1)}, bf16[24,1152]{1,0:T(8,128)(2,1)S(1)}, u32[]{:S(2)}, u32[]{:S(2)}) collective-permute-start(bf16[24,1152]{1,0:T(8,128)(2,1)S(1)} %get-tuple-element.76), channel_id=1, source_target_pairs={{0,16},{8,24},{16,0},{24,8},{1,17},{9,25},{17,1},{25,9},{2,18},{10... | collective-permute-start | bytes 165896 | tf_op jit(solution)/shard_map/ppermute | solution.py:326
  27.6 5.8 %shard_map.199 = (f32[24,1024]{1,0:T(8,128)S(1)}, bf16[24,1024]{1,0:T(8,128)(2,1)S(1)}, bf16[24,1024]{1,0:T(8,128)(2,1)S(1)}, bf16[24,1024]{1,0:T(8,128)(2,1)S(1)}) custom-call(bf16[24,1280]{1,0:T(8,128)(2,1)S(1)} %get-tuple-element.72.refs_0_, bf16[24,1280]{1,0:T(8,128)(2,1)S(1)} %collective-permute-done.refs_1_, ...), custom_call_target="tpu_custom_call" | custom-call | flops 1006632960 | bytes 42434560 | tf_op jit(solution)/shard_map/pallas_call | solution.py:26
  34.5 3.5 %collective-permute-start.11 = (bf16[24,2176]{1,0:T(8,128)(2,1)S(1)}, bf16[24,2176]{1,0:T(8,128)(2,1)S(1)}, u32[]{:S(2)}, u32[]{:S(2)}) collective-permute-start(bf16[24,2176]{1,0:T(8,128)(2,1)S(1)} %get-tuple-element.82), channel_id=1, source_target_pairs={{0,16},{8,24},{16,0},{24,8},{1,17},{9,25},{17,1},{25,9},{2,18},{10... | collective-permute-start | bytes 313352 | tf_op jit(solution)/shard_map/ppermute | solution.py:326
  39.4 5.9 %collective-permute-done.11.refs_2_ = bf16[24,2176]{1,0:T(8,128)(2,1)S(1)} collective-permute-done((bf16[24,2176]{1,0:T(8,128)(2,1)S(1)}, bf16[24,2176]{1,0:T(8,128)(2,1)S(1)}, u32[]{:S(2)}, u32[]{:S(2)}) %collective-permute-start.11) | collective-permute-done | bytes 104480 | tf_op jit(solution)/shard_map/ppermute | solution.py:326
  45.4 1.7 %collective-permute-start.13 = (bf16[24,1024]{1,0:T(8,128)(2,1)S(1)}, bf16[24,1024]{1,0:T(8,128)(2,1)S(1)}, u32[]{:S(2)}, u32[]{:S(2)}) collective-permute-start(bf16[24,1024]{1,0:T(8,128)(2,1)S(1)} %get-tuple-element.84.refs_0_), channel_id=1, source_target_pairs={{0,8},{8,0},{16,24},{24,16},{1,9},{9,1},{17,25},{25,17},{2,10},{10... | collective-permute-start | bytes 147464 | tf_op jit(solution)/shard_map/ppermute | solution.py:326
  49.9 4.3 %shard_map.203 = (f32[48,5120]{1,0:T(8,128)S(1)}, f32[12,128]{1,0:T(8,128)S(1)}) custom-call(bf16[24,1152]{1,0:T(8,128)(2,1)S(1)} %get-tuple-element.85.refs_0_, bf16[24,2176]{1,0:T(8,128)(2,1)S(1)} %collective-permute-done.10.refs_1_, bf16[24,2176]{1,0:T(8,128)(2,1)S(1)} %collective-permute-done.11.refs_2_, ...), custom_call_target="tpu_custom_call" | custom-call | flops 1006632960 | bytes 42311680 | tf_op jit(solution)/shard_map/pallas_call | solution.py:26
  54.5 4.3 %shard_map.204 = (f32[24,5120]{1,0:T(8,128)S(1)}, bf16[24,5120]{1,0:T(8,128)(2,1)S(1)}) custom-call(bf16[24,1024]{1,0:T(8,128)(2,1)S(1)} %get-tuple-element.84.refs_0_, bf16[24,1024]{1,0:T(8,128)(2,1)S(1)} %collective-permute-done.13.refs_1_, bf16[24,1024]{1,0:T(8,128)(2,1)S(1)} %collective-permute-done.14.refs_2_, ...), custom_call_target="tpu_custom_call" | custom-call | flops 1006632960 | bytes 43122688 | tf_op jit(solution)/shard_map/pallas_call | solution.py:26
  60.5 1.6 %collective-permute-start.17 = (bf16[24,1280]{1,0:T(8,128)(2,1)S(1)}, bf16[24,1280]{1,0:T(8,128)(2,1)S(1)}, u32[]{:S(2)}, u32[]{:S(2)}) collective-permute-start(bf16[24,1280]{1,0:T(8,128)(2,1)S(1)} %get-tuple-element.90), channel_id=1, source_target_pairs={{0,2},{1,3},{2,0},{3,1},{4,6},{5,7},{6,4},{7,5},{8,10},{9,11},{10,... | collective-permute-start | bytes 184328 | tf_op jit(solution)/shard_map/ppermute | solution.py:330
  62.1 1.5 %collective-permute-start.18 = (bf16[24,1280]{1,0:T(8,128)(2,1)S(1)}, bf16[24,1280]{1,0:T(8,128)(2,1)S(1)}, u32[]{:S(2)}, u32[]{:S(2)}) collective-permute-start(bf16[24,1280]{1,0:T(8,128)(2,1)S(1)} %get-tuple-element.91), channel_id=1, source_target_pairs={{0,4},{1,5},{2,6},{3,7},{4,0},{5,1},{6,2},{7,3},{8,12},{9,13},{10,... | collective-permute-start | bytes 184328 | tf_op jit(solution)/shard_map/ppermute | solution.py:330
  66.3 2.4 %collective-permute-done.19.refs_3_ = bf16[24,1280]{1,0:T(8,128)(2,1)S(1)} collective-permute-done((bf16[24,1280]{1,0:T(8,128)(2,1)S(1)}, bf16[24,1280]{1,0:T(8,128)(2,1)S(1)}, u32[]{:S(2)}, u32[]{:S(2)}) %collective-permute-start.19) | collective-permute-done | bytes 61472 | tf_op jit(solution)/shard_map/ppermute | solution.py:330
  68.8 1.7 %shard_map.206 = (f32[6,1024]{1,0:T(8,128)S(1)}, f32[24,1280]{1,0:T(8,128)S(1)}, f32[6,128]{1,0:T(8,128)S(1)}, bf16[24,1280]{1,0:T(8,128)(2,1)S(1)}) custom-call(bf16[4096,5120]{1,0:T(8,128)(2,1)S(1)} %bitcast.7, f32[24,1280]{1,0:T(8,128)S(1)} %get-tuple-element.89.refs_0_, bf16[24,1280]{1,0:T(8,128)(2,1)S(1)} %collective-permute-done.17.refs_1_, ...), custom_call_target="tpu_custom_call" | custom-call | bytes 1942528 | tf_op jit(solution)/shard_map/pallas_call | solution.py:26
  71.6 2.4 %collective-permute-start.22 = (bf16[24,1280]{1,0:T(8,128)(2,1)S(1)}, bf16[24,1280]{1,0:T(8,128)(2,1)S(1)}, u32[]{:S(2)}, u32[]{:S(2)}) collective-permute-start(bf16[24,1280]{1,0:T(8,128)(2,1)S(1)} %get-tuple-element.97.refs_0_), channel_id=1, source_target_pairs={{0,6},{1,7},{2,4},{3,5},{4,2},{5,3},{6,0},{7,1},{8,14},{9,15},{10,... | collective-permute-start | bytes 184328 | tf_op jit(solution)/shard_map/ppermute | solution.py:330
  78.0 5.8 %shard_map.208 = (f32[24,1152]{1,0:T(8,128)S(1)}, bf16[24,1152]{1,0:T(8,128)(2,1)S(1)}, bf16[24,1152]{1,0:T(8,128)(2,1)S(1)}, bf16[24,1152]{1,0:T(8,128)(2,1)S(1)}) custom-call(bf16[24,1280]{1,0:T(8,128)(2,1)S(1)} %get-tuple-element.97.refs_0_, bf16[24,1280]{1,0:T(8,128)(2,1)S(1)} %collective-permute-done.20.refs_1_, ...), custom_call_target="tpu_custom_call" | custom-call | flops 1006632960 | bytes 42434560 | tf_op jit(solution)/shard_map/pallas_call | solution.py:26
  84.4 2.3 %collective-permute-start.28 = (bf16[24,1152]{1,0:T(8,128)(2,1)S(1)}, bf16[24,1152]{1,0:T(8,128)(2,1)S(1)}, u32[]{:S(2)}, u32[]{:S(2)}) collective-permute-start(bf16[24,1152]{1,0:T(8,128)(2,1)S(1)} %get-tuple-element.101), channel_id=1, source_target_pairs={{0,16},{8,24},{16,0},{24,8},{1,17},{9,25},{17,1},{25,9},{2,18},{10... | collective-permute-start | bytes 165896 | tf_op jit(solution)/shard_map/ppermute | solution.py:326
  86.7 1.5 %collective-permute-start.29 = (bf16[24,1152]{1,0:T(8,128)(2,1)S(1)}, bf16[24,1152]{1,0:T(8,128)(2,1)S(1)}, u32[]{:S(2)}, u32[]{:S(2)}) collective-permute-start(bf16[24,1152]{1,0:T(8,128)(2,1)S(1)} %get-tuple-element.102), channel_id=1, source_target_pairs={{0,24},{8,16},{16,8},{24,0},{1,25},{9,17},{17,9},{25,1},{2,26},{10... | collective-permute-start | bytes 165896 | tf_op jit(solution)/shard_map/ppermute | solution.py:326
  88.2 5.8 %shard_map.207 = (f32[24,1024]{1,0:T(8,128)S(1)}, bf16[24,1024]{1,0:T(8,128)(2,1)S(1)}, bf16[24,1024]{1,0:T(8,128)(2,1)S(1)}, bf16[24,1024]{1,0:T(8,128)(2,1)S(1)}) custom-call(bf16[24,1280]{1,0:T(8,128)(2,1)S(1)} %get-tuple-element.97.refs_0_, bf16[24,1280]{1,0:T(8,128)(2,1)S(1)} %collective-permute-done.20.refs_1_, ...), custom_call_target="tpu_custom_call" | custom-call | flops 1006632960 | bytes 42434560 | tf_op jit(solution)/shard_map/pallas_call | solution.py:26
  94.2 2.9 %collective-permute-start.31 = (bf16[24,2176]{1,0:T(8,128)(2,1)S(1)}, bf16[24,2176]{1,0:T(8,128)(2,1)S(1)}, u32[]{:S(2)}, u32[]{:S(2)}) collective-permute-start(bf16[24,2176]{1,0:T(8,128)(2,1)S(1)} %get-tuple-element.109), channel_id=1, source_target_pairs={{0,16},{8,24},{16,0},{24,8},{1,17},{9,25},{17,1},{25,9},{2,18},{10... | collective-permute-start | bytes 313352 | tf_op jit(solution)/shard_map/ppermute | solution.py:326
  97.1 1.5 %collective-permute-start.32 = (bf16[24,2176]{1,0:T(8,128)(2,1)S(1)}, bf16[24,2176]{1,0:T(8,128)(2,1)S(1)}, u32[]{:S(2)}, u32[]{:S(2)}) collective-permute-start(bf16[24,2176]{1,0:T(8,128)(2,1)S(1)} %get-tuple-element.110), channel_id=1, source_target_pairs={{0,24},{8,16},{16,8},{24,0},{1,25},{9,17},{17,9},{25,1},{2,26},{10... | collective-permute-start | bytes 313352 | tf_op jit(solution)/shard_map/ppermute | solution.py:326
  99.7 5.3 %collective-permute-done.31.refs_2_ = bf16[24,2176]{1,0:T(8,128)(2,1)S(1)} collective-permute-done((bf16[24,2176]{1,0:T(8,128)(2,1)S(1)}, bf16[24,2176]{1,0:T(8,128)(2,1)S(1)}, u32[]{:S(2)}, u32[]{:S(2)}) %collective-permute-start.31) | collective-permute-done | bytes 104480 | tf_op jit(solution)/shard_map/ppermute | solution.py:326
  105.8 1.7 %collective-permute-start.33 = (bf16[24,1024]{1,0:T(8,128)(2,1)S(1)}, bf16[24,1024]{1,0:T(8,128)(2,1)S(1)}, u32[]{:S(2)}, u32[]{:S(2)}) collective-permute-start(bf16[24,1024]{1,0:T(8,128)(2,1)S(1)} %get-tuple-element.115.refs_0_), channel_id=1, source_target_pairs={{0,8},{8,0},{16,24},{24,16},{1,9},{9,1},{17,25},{25,17},{2,10},{10... | collective-permute-start | bytes 147464 | tf_op jit(solution)/shard_map/ppermute | solution.py:326
  108.7 1.5 %collective-permute-start.35 = (bf16[24,1024]{1,0:T(8,128)(2,1)S(1)}, bf16[24,1024]{1,0:T(8,128)(2,1)S(1)}, u32[]{:S(2)}, u32[]{:S(2)}) collective-permute-start(bf16[24,1024]{1,0:T(8,128)(2,1)S(1)} %get-tuple-element.115.refs_0_), channel_id=1, source_target_pairs={{0,24},{8,16},{16,8},{24,0},{1,25},{9,17},{17,9},{25,1},{2,26},{10... | collective-permute-start | bytes 147464 | tf_op jit(solution)/shard_map/ppermute | solution.py:326
  110.2 4.3 %shard_map.211 = (f32[48,5120]{1,0:T(8,128)S(1)}, f32[12,128]{1,0:T(8,128)S(1)}) custom-call(bf16[24,1152]{1,0:T(8,128)(2,1)S(1)} %get-tuple-element.116.refs_0_, bf16[24,2176]{1,0:T(8,128)(2,1)S(1)} %collective-permute-done.30.refs_1_, bf16[24,2176]{1,0:T(8,128)(2,1)S(1)} %collective-permute-done.31.refs_2_, ...), custom_call_target="tpu_custom_call" | custom-call | flops 1006632960 | bytes 42311680 | tf_op jit(solution)/shard_map/pallas_call | solution.py:26
  114.6 4.3 %shard_map.212 = (f32[24,5120]{1,0:T(8,128)S(1)}, bf16[24,5120]{1,0:T(8,128)(2,1)S(1)}) custom-call(bf16[24,1024]{1,0:T(8,128)(2,1)S(1)} %get-tuple-element.115.refs_0_, bf16[24,1024]{1,0:T(8,128)(2,1)S(1)} %collective-permute-done.33.refs_1_, bf16[24,1024]{1,0:T(8,128)(2,1)S(1)} %collective-permute-done.34.refs_2_, ...), custom_call_target="tpu_custom_call" | custom-call | flops 1006632960 | bytes 43122688 | tf_op jit(solution)/shard_map/pallas_call | solution.py:26
  120.6 1.6 %collective-permute-start.37 = (bf16[24,1280]{1,0:T(8,128)(2,1)S(1)}, bf16[24,1280]{1,0:T(8,128)(2,1)S(1)}, u32[]{:S(2)}, u32[]{:S(2)}) collective-permute-start(bf16[24,1280]{1,0:T(8,128)(2,1)S(1)} %get-tuple-element.121), channel_id=1, source_target_pairs={{0,2},{1,3},{2,0},{3,1},{4,6},{5,7},{6,4},{7,5},{8,10},{9,11},{10,... | collective-permute-start | bytes 184328 | tf_op jit(solution)/shard_map/ppermute | solution.py:330
  126.4 2.4 %collective-permute-done.39.refs_3_ = bf16[24,1280]{1,0:T(8,128)(2,1)S(1)} collective-permute-done((bf16[24,1280]{1,0:T(8,128)(2,1)S(1)}, bf16[24,1280]{1,0:T(8,128)(2,1)S(1)}, u32[]{:S(2)}, u32[]{:S(2)}) %collective-permute-start.39) | collective-permute-done | bytes 61472 | tf_op jit(solution)/shard_map/ppermute | solution.py:330
  132.2 2.4 %collective-permute-start.43 = (f32[8,1024]{1,0:T(8,128)S(1)}, f32[8,1024]{1,0:T(8,128)S(1)}, u32[]{:S(2)}, u32[]{:S(2)}) collective-permute-start(f32[8,1024]{1,0:T(8,128)S(1)} %shard_map.215.refs_0_), channel_id=1, source_target_pairs={{0,6},{1,7},{2,4},{3,5},{4,2},{5,3},{6,0},{7,1},{8,14},{9,15},{10,... | collective-permute-start | bytes 98312 | tf_op jit(solution)/shard_map/ppermute | solution.py:330
  (129 shorter events, 38.0 us)
Async XLA Ops:
  5.0 5.3 %collective-permute-start = (bf16[24,1280]{1,0:T(8,128)(2,1)S(1)}, bf16[24,1280]{1,0:T(8,128)(2,1)S(1)}, u32[]{:S(2)}, u32[]{:S(2)}) collective-permute-start(bf16[24,1280]{1,0:T(8,128)(2,1)S(1)} %get-tuple-element.72.refs_0_), channel_id=1, source_target_pairs={{0,2},{1,3},{2,0},{3,1},{4,6},{5,7},{6,4},{7,5},{8,10},{9,11},{10,... | collective-permute-start | bytes 184328 | tf_op jit(solution)/shard_map/ppermute | solution.py:330
  8.0 4.2 %collective-permute-start.1 = (bf16[24,1280]{1,0:T(8,128)(2,1)S(1)}, bf16[24,1280]{1,0:T(8,128)(2,1)S(1)}, u32[]{:S(2)}, u32[]{:S(2)}) collective-permute-start(bf16[24,1280]{1,0:T(8,128)(2,1)S(1)} %get-tuple-element.72.refs_0_), channel_id=1, source_target_pairs={{0,4},{1,5},{2,6},{3,7},{4,0},{5,1},{6,2},{7,3},{8,12},{9,13},{10,... | collective-permute-start | bytes 184328 | tf_op jit(solution)/shard_map/ppermute | solution.py:330
  9.5 5.1 %collective-permute-start.2 = (bf16[24,1280]{1,0:T(8,128)(2,1)S(1)}, bf16[24,1280]{1,0:T(8,128)(2,1)S(1)}, u32[]{:S(2)}, u32[]{:S(2)}) collective-permute-start(bf16[24,1280]{1,0:T(8,128)(2,1)S(1)} %get-tuple-element.72.refs_0_), channel_id=1, source_target_pairs={{0,6},{1,7},{2,4},{3,5},{4,2},{5,3},{6,0},{7,1},{8,14},{9,15},{10,... | collective-permute-start | bytes 184328 | tf_op jit(solution)/shard_map/ppermute | solution.py:330
  9.6 5.1 %collective-permute-start.3 = (bf16[24,1280]{1,0:T(8,128)(2,1)S(1)}, bf16[24,1280]{1,0:T(8,128)(2,1)S(1)}, u32[]{:S(2)}, u32[]{:S(2)}) collective-permute-start(bf16[24,1280]{1,0:T(8,128)(2,1)S(1)} %get-tuple-element.72.refs_0_), channel_id=1, source_target_pairs={{0,1},{1,0},{2,3},{3,2},{4,5},{5,4},{6,7},{7,6},{8,9},{9,8},{10,11... | collective-permute-start | bytes 184328 | tf_op jit(solution)/shard_map/ppermute | solution.py:334
  10.3 4.4 %collective-permute-start.4 = (bf16[24,1280]{1,0:T(8,128)(2,1)S(1)}, bf16[24,1280]{1,0:T(8,128)(2,1)S(1)}, u32[]{:S(2)}, u32[]{:S(2)}) collective-permute-start(bf16[24,1280]{1,0:T(8,128)(2,1)S(1)} %collective-permute-done.refs_1_), channel_id=1, source_target_pairs={{0,1},{1,0},{2,3},{3,2},{4,5},{5,4},{6,7},{7,6},{8,9},{9,8},{10,11... | collective-permute-start | bytes 184328 | tf_op jit(solution)/shard_map/ppermute | solution.py:334
  21.9 11.5 %collective-permute-start.7 = (bf16[24,1152]{1,0:T(8,128)(2,1)S(1)}, bf16[24,1152]{1,0:T(8,128)(2,1)S(1)}, u32[]{:S(2)}, u32[]{:S(2)}) collective-permute-start(bf16[24,1152]{1,0:T(8,128)(2,1)S(1)} %get-tuple-element.75), channel_id=1, source_target_pairs={{0,8},{8,0},{16,24},{24,16},{1,9},{9,1},{17,25},{25,17},{2,10},{10... | collective-permute-start | bytes 165896 | tf_op jit(solution)/shard_map/ppermute | solution.py:326
  25.0 8.4 %collective-permute-start.8 = (bf16[24,1152]{1,0:T(8,128)(2,1)S(1)}, bf16[24,1152]{1,0:T(8,128)(2,1)S(1)}, u32[]{:S(2)}, u32[]{:S(2)}) collective-permute-start(bf16[24,1152]{1,0:T(8,128)(2,1)S(1)} %get-tuple-element.76), channel_id=1, source_target_pairs={{0,16},{8,24},{16,0},{24,8},{1,17},{9,25},{17,1},{25,9},{2,18},{10... | collective-permute-start | bytes 165896 | tf_op jit(solution)/shard_map/ppermute | solution.py:326
  27.6 6.0 %collective-permute-start.9 = (bf16[24,1152]{1,0:T(8,128)(2,1)S(1)}, bf16[24,1152]{1,0:T(8,128)(2,1)S(1)}, u32[]{:S(2)}, u32[]{:S(2)}) collective-permute-start(bf16[24,1152]{1,0:T(8,128)(2,1)S(1)} %get-tuple-element.77), channel_id=1, source_target_pairs={{0,24},{8,16},{16,8},{24,0},{1,25},{9,17},{17,9},{25,1},{2,26},{10... | collective-permute-start | bytes 165896 | tf_op jit(solution)/shard_map/ppermute | solution.py:326
  33.6 5.8 %collective-permute-start.10 = (bf16[24,2176]{1,0:T(8,128)(2,1)S(1)}, bf16[24,2176]{1,0:T(8,128)(2,1)S(1)}, u32[]{:S(2)}, u32[]{:S(2)}) collective-permute-start(bf16[24,2176]{1,0:T(8,128)(2,1)S(1)} %get-tuple-element.81), channel_id=1, source_target_pairs={{0,8},{8,0},{16,24},{24,16},{1,9},{9,1},{17,25},{25,17},{2,10},{10... | collective-permute-start | bytes 313352 | tf_op jit(solution)/shard_map/ppermute | solution.py:326
  34.5 10.9 %collective-permute-start.11 = (bf16[24,2176]{1,0:T(8,128)(2,1)S(1)}, bf16[24,2176]{1,0:T(8,128)(2,1)S(1)}, u32[]{:S(2)}, u32[]{:S(2)}) collective-permute-start(bf16[24,2176]{1,0:T(8,128)(2,1)S(1)} %get-tuple-element.82), channel_id=1, source_target_pairs={{0,16},{8,24},{16,0},{24,8},{1,17},{9,25},{17,1},{25,9},{2,18},{10... | collective-permute-start | bytes 313352 | tf_op jit(solution)/shard_map/ppermute | solution.py:326
  38.0 7.4 %collective-permute-start.12 = (bf16[24,2176]{1,0:T(8,128)(2,1)S(1)}, bf16[24,2176]{1,0:T(8,128)(2,1)S(1)}, u32[]{:S(2)}, u32[]{:S(2)}) collective-permute-start(bf16[24,2176]{1,0:T(8,128)(2,1)S(1)} %get-tuple-element.83), channel_id=1, source_target_pairs={{0,24},{8,16},{16,8},{24,0},{1,25},{9,17},{17,9},{25,1},{2,26},{10... | collective-permute-start | bytes 313352 | tf_op jit(solution)/shard_map/ppermute | solution.py:326
  45.4 8.7 %collective-permute-start.13 = (bf16[24,1024]{1,0:T(8,128)(2,1)S(1)}, bf16[24,1024]{1,0:T(8,128)(2,1)S(1)}, u32[]{:S(2)}, u32[]{:S(2)}) collective-permute-start(bf16[24,1024]{1,0:T(8,128)(2,1)S(1)} %get-tuple-element.84.refs_0_), channel_id=1, source_target_pairs={{0,8},{8,0},{16,24},{24,16},{1,9},{9,1},{17,25},{25,17},{2,10},{10... | collective-permute-start | bytes 147464 | tf_op jit(solution)/shard_map/ppermute | solution.py:326
  47.2 7.0 %collective-permute-start.14 = (bf16[24,1024]{1,0:T(8,128)(2,1)S(1)}, bf16[24,1024]{1,0:T(8,128)(2,1)S(1)}, u32[]{:S(2)}, u32[]{:S(2)}) collective-permute-start(bf16[24,1024]{1,0:T(8,128)(2,1)S(1)} %get-tuple-element.84.refs_0_), channel_id=1, source_target_pairs={{0,16},{8,24},{16,0},{24,8},{1,17},{9,25},{17,1},{25,9},{2,18},{10... | collective-permute-start | bytes 147464 | tf_op jit(solution)/shard_map/ppermute | solution.py:326
  48.6 5.9 %collective-permute-start.15 = (bf16[24,1024]{1,0:T(8,128)(2,1)S(1)}, bf16[24,1024]{1,0:T(8,128)(2,1)S(1)}, u32[]{:S(2)}, u32[]{:S(2)}) collective-permute-start(bf16[24,1024]{1,0:T(8,128)(2,1)S(1)} %get-tuple-element.84.refs_0_), channel_id=1, source_target_pairs={{0,24},{8,16},{16,8},{24,0},{1,25},{9,17},{17,9},{25,1},{2,26},{10... | collective-permute-start | bytes 147464 | tf_op jit(solution)/shard_map/ppermute | solution.py:326
  60.5 4.3 %collective-permute-start.17 = (bf16[24,1280]{1,0:T(8,128)(2,1)S(1)}, bf16[24,1280]{1,0:T(8,128)(2,1)S(1)}, u32[]{:S(2)}, u32[]{:S(2)}) collective-permute-start(bf16[24,1280]{1,0:T(8,128)(2,1)S(1)} %get-tuple-element.90), channel_id=1, source_target_pairs={{0,2},{1,3},{2,0},{3,1},{4,6},{5,7},{6,4},{7,5},{8,10},{9,11},{10,... | collective-permute-start | bytes 184328 | tf_op jit(solution)/shard_map/ppermute | solution.py:330
  62.1 4.2 %collective-permute-start.18 = (bf16[24,1280]{1,0:T(8,128)(2,1)S(1)}, bf16[24,1280]{1,0:T(8,128)(2,1)S(1)}, u32[]{:S(2)}, u32[]{:S(2)}) collective-permute-start(bf16[24,1280]{1,0:T(8,128)(2,1)S(1)} %get-tuple-element.91), channel_id=1, source_target_pairs={{0,4},{1,5},{2,6},{3,7},{4,0},{5,1},{6,2},{7,3},{8,12},{9,13},{10,... | collective-permute-start | bytes 184328 | tf_op jit(solution)/shard_map/ppermute | solution.py:330
  63.6 5.1 %collective-permute-start.19 = (bf16[24,1280]{1,0:T(8,128)(2,1)S(1)}, bf16[24,1280]{1,0:T(8,128)(2,1)S(1)}, u32[]{:S(2)}, u32[]{:S(2)}) collective-permute-start(bf16[24,1280]{1,0:T(8,128)(2,1)S(1)} %get-tuple-element.92), channel_id=1, source_target_pairs={{0,6},{1,7},{2,4},{3,5},{4,2},{5,3},{6,0},{7,1},{8,14},{9,15},{10,... | collective-permute-start | bytes 184328 | tf_op jit(solution)/shard_map/ppermute | solution.py:330
  70.5 4.3 %collective-permute-start.20 = (bf16[24,1280]{1,0:T(8,128)(2,1)S(1)}, bf16[24,1280]{1,0:T(8,128)(2,1)S(1)}, u32[]{:S(2)}, u32[]{:S(2)}) collective-permute-start(bf16[24,1280]{1,0:T(8,128)(2,1)S(1)} %get-tuple-element.97.refs_0_), channel_id=1, source_target_pairs={{0,2},{1,3},{2,0},{3,1},{4,6},{5,7},{6,4},{7,5},{8,10},{9,11},{10,... | collective-permute-start | bytes 184328 | tf_op jit(solution)/shard_map/ppermute | solution.py:330
  71.6 5.1 %collective-permute-start.22 = (bf16[24,1280]{1,0:T(8,128)(2,1)S(1)}, bf16[24,1280]{1,0:T(8,128)(2,1)S(1)}, u32[]{:S(2)}, u32[]{:S(2)}) collective-permute-start(bf16[24,1280]{1,0:T(8,128)(2,1)S(1)} %get-tuple-element.97.refs_0_), channel_id=1, source_target_pairs={{0,6},{1,7},{2,4},{3,5},{4,2},{5,3},{6,0},{7,1},{8,14},{9,15},{10,... | collective-permute-start | bytes 184328 | tf_op jit(solution)/shard_map/ppermute | solution.py:330
  83.8 10.2 %collective-permute-start.27 = (bf16[24,1152]{1,0:T(8,128)(2,1)S(1)}, bf16[24,1152]{1,0:T(8,128)(2,1)S(1)}, u32[]{:S(2)}, u32[]{:S(2)}) collective-permute-start(bf16[24,1152]{1,0:T(8,128)(2,1)S(1)} %get-tuple-element.100), channel_id=1, source_target_pairs={{0,8},{8,0},{16,24},{24,16},{1,9},{9,1},{17,25},{25,17},{2,10},{10... | collective-permute-start | bytes 165896 | tf_op jit(solution)/shard_map/ppermute | solution.py:326
  84.4 9.6 %collective-permute-start.28 = (bf16[24,1152]{1,0:T(8,128)(2,1)S(1)}, bf16[24,1152]{1,0:T(8,128)(2,1)S(1)}, u32[]{:S(2)}, u32[]{:S(2)}) collective-permute-start(bf16[24,1152]{1,0:T(8,128)(2,1)S(1)} %get-tuple-element.101), channel_id=1, source_target_pairs={{0,16},{8,24},{16,0},{24,8},{1,17},{9,25},{17,1},{25,9},{2,18},{10... | collective-permute-start | bytes 165896 | tf_op jit(solution)/shard_map/ppermute | solution.py:326
  86.7 7.3 %collective-permute-start.29 = (bf16[24,1152]{1,0:T(8,128)(2,1)S(1)}, bf16[24,1152]{1,0:T(8,128)(2,1)S(1)}, u32[]{:S(2)}, u32[]{:S(2)}) collective-permute-start(bf16[24,1152]{1,0:T(8,128)(2,1)S(1)} %get-tuple-element.102), channel_id=1, source_target_pairs={{0,24},{8,16},{16,8},{24,0},{1,25},{9,17},{17,9},{25,1},{2,26},{10... | collective-permute-start | bytes 165896 | tf_op jit(solution)/shard_map/ppermute | solution.py:326
  94.1 5.5 %collective-permute-start.30 = (bf16[24,2176]{1,0:T(8,128)(2,1)S(1)}, bf16[24,2176]{1,0:T(8,128)(2,1)S(1)}, u32[]{:S(2)}, u32[]{:S(2)}) collective-permute-start(bf16[24,2176]{1,0:T(8,128)(2,1)S(1)} %get-tuple-element.108), channel_id=1, source_target_pairs={{0,8},{8,0},{16,24},{24,16},{1,9},{9,1},{17,25},{25,17},{2,10},{10... | collective-permute-start | bytes 313352 | tf_op jit(solution)/shard_map/ppermute | solution.py:326
  94.2 10.8 %collective-permute-start.31 = (bf16[24,2176]{1,0:T(8,128)(2,1)S(1)}, bf16[24,2176]{1,0:T(8,128)(2,1)S(1)}, u32[]{:S(2)}, u32[]{:S(2)}) collective-permute-start(bf16[24,2176]{1,0:T(8,128)(2,1)S(1)} %get-tuple-element.109), channel_id=1, source_target_pairs={{0,16},{8,24},{16,0},{24,8},{1,17},{9,25},{17,1},{25,9},{2,18},{10... | collective-permute-start | bytes 313352 | tf_op jit(solution)/shard_map/ppermute | solution.py:326
  97.1 7.9 %collective-permute-start.32 = (bf16[24,2176]{1,0:T(8,128)(2,1)S(1)}, bf16[24,2176]{1,0:T(8,128)(2,1)S(1)}, u32[]{:S(2)}, u32[]{:S(2)}) collective-permute-start(bf16[24,2176]{1,0:T(8,128)(2,1)S(1)} %get-tuple-element.110), channel_id=1, source_target_pairs={{0,24},{8,16},{16,8},{24,0},{1,25},{9,17},{17,9},{25,1},{2,26},{10... | collective-permute-start | bytes 313352 | tf_op jit(solution)/shard_map/ppermute | solution.py:326
  105.8 8.7 %collective-permute-start.33 = (bf16[24,1024]{1,0:T(8,128)(2,1)S(1)}, bf16[24,1024]{1,0:T(8,128)(2,1)S(1)}, u32[]{:S(2)}, u32[]{:S(2)}) collective-permute-start(bf16[24,1024]{1,0:T(8,128)(2,1)S(1)} %get-tuple-element.115.refs_0_), channel_id=1, source_target_pairs={{0,8},{8,0},{16,24},{24,16},{1,9},{9,1},{17,25},{25,17},{2,10},{10... | collective-permute-start | bytes 147464 | tf_op jit(solution)/shard_map/ppermute | solution.py:326
  107.5 7.0 %collective-permute-start.34 = (bf16[24,1024]{1,0:T(8,128)(2,1)S(1)}, bf16[24,1024]{1,0:T(8,128)(2,1)S(1)}, u32[]{:S(2)}, u32[]{:S(2)}) collective-permute-start(bf16[24,1024]{1,0:T(8,128)(2,1)S(1)} %get-tuple-element.115.refs_0_), channel_id=1, source_target_pairs={{0,16},{8,24},{16,0},{24,8},{1,17},{9,25},{17,1},{25,9},{2,18},{10... | collective-permute-start | bytes 147464 | tf_op jit(solution)/shard_map/ppermute | solution.py:326
  108.7 5.9 %collective-permute-start.35 = (bf16[24,1024]{1,0:T(8,128)(2,1)S(1)}, bf16[24,1024]{1,0:T(8,128)(2,1)S(1)}, u32[]{:S(2)}, u32[]{:S(2)}) collective-permute-start(bf16[24,1024]{1,0:T(8,128)(2,1)S(1)} %get-tuple-element.115.refs_0_), channel_id=1, source_target_pairs={{0,24},{8,16},{16,8},{24,0},{1,25},{9,17},{17,9},{25,1},{2,26},{10... | collective-permute-start | bytes 147464 | tf_op jit(solution)/shard_map/ppermute | solution.py:326
  120.6 4.3 %collective-permute-start.37 = (bf16[24,1280]{1,0:T(8,128)(2,1)S(1)}, bf16[24,1280]{1,0:T(8,128)(2,1)S(1)}, u32[]{:S(2)}, u32[]{:S(2)}) collective-permute-start(bf16[24,1280]{1,0:T(8,128)(2,1)S(1)} %get-tuple-element.121), channel_id=1, source_target_pairs={{0,2},{1,3},{2,0},{3,1},{4,6},{5,7},{6,4},{7,5},{8,10},{9,11},{10,... | collective-permute-start | bytes 184328 | tf_op jit(solution)/shard_map/ppermute | solution.py:330
  123.7 5.1 %collective-permute-start.39 = (bf16[24,1280]{1,0:T(8,128)(2,1)S(1)}, bf16[24,1280]{1,0:T(8,128)(2,1)S(1)}, u32[]{:S(2)}, u32[]{:S(2)}) collective-permute-start(bf16[24,1280]{1,0:T(8,128)(2,1)S(1)} %get-tuple-element.123), channel_id=1, source_target_pairs={{0,6},{1,7},{2,4},{3,5},{4,2},{5,3},{6,0},{7,1},{8,14},{9,15},{10,... | collective-permute-start | bytes 184328 | tf_op jit(solution)/shard_map/ppermute | solution.py:330
  131.7 4.3 %collective-permute-start.42 = (f32[8,1024]{1,0:T(8,128)S(1)}, f32[8,1024]{1,0:T(8,128)S(1)}, u32[]{:S(2)}, u32[]{:S(2)}) collective-permute-start(f32[8,1024]{1,0:T(8,128)S(1)} %shard_map.215.refs_0_), channel_id=1, source_target_pairs={{0,4},{1,5},{2,6},{3,7},{4,0},{5,1},{6,2},{7,3},{8,12},{9,13},{10,... | collective-permute-start | bytes 98312 | tf_op jit(solution)/shard_map/ppermute | solution.py:330
  132.2 4.8 %collective-permute-start.43 = (f32[8,1024]{1,0:T(8,128)S(1)}, f32[8,1024]{1,0:T(8,128)S(1)}, u32[]{:S(2)}, u32[]{:S(2)}) collective-permute-start(f32[8,1024]{1,0:T(8,128)S(1)} %shard_map.215.refs_0_), channel_id=1, source_target_pairs={{0,6},{1,7},{2,4},{3,5},{4,2},{5,3},{6,0},{7,1},{8,14},{9,15},{10,... | collective-permute-start | bytes 98312 | tf_op jit(solution)/shard_map/ppermute | solution.py:330
  (37 other events, 356.2 us)

commit v5 on v4

--- a/solution.py
+++ b/solution.py
@@ -11,6 +11,8 @@
 BUSES = 20480
 ITERS = 2
 CHUNKS = 2
+FIRST_SHARE = 0.5625
+EARLY_SHARE = 0.4375
 LANES = 128
 GRANT = 11 << 20
 BF = jnp.bfloat16
@@ -77,8 +79,12 @@
         self.width = self.stretch * LANES
         self.fold = next(f for f in (4, 2, 1) if buses % (f * self.width) == 0)
         self.part = buses // self.fold
-        self.chunk = lines // CHUNKS
-        self.half = self.chunk // 2
+        tiles = lambda share, least, most: min(max(round(share * lines / 2 / LANES), least), most) * LANES
+        first = tiles(FIRST_SHARE, 2, lines // 2 // LANES - 1)
+        self.halves = (first, lines // 2 - first)
+        self.early = tiles(EARLY_SHARE, 1, first // LANES - 1)
+        self.starts = (0, 2 * first)
+        self.ranges = (((0, self.early), (first, first + self.early)), ((self.early, first), (first + self.early, lines)))
 
 
 def where_am_i():
@@ -97,7 +103,7 @@
         yield block, slice(fold * sz.rows, (fold + 1) * sz.rows), slice(inner * sz.width, (inner + 1) * sz.width)
 
 
-def start_kernel(sz, dispatch, shed, loads, gen_bus, inject, shed_p, loads_p, select):
+def start_kernel(sz, dispatch, net, gen_bus, inject, select):
     first = lax.axis_index("scen") * sz.buses
     bus = lax.broadcasted_iota(jnp.int32, (sz.width, LANES), 0)
     for block, rows, cols in blocks_of(sz):
@@ -105,20 +111,17 @@
         buses = slice(block * sz.width, (block + 1) * sz.width)
         local = gen_bus[:, lanes] - (first + block * sz.width)
         select[block] = (bus == local).astype(F32).astype(BF)
-        served, load = shed[:, buses], loads[:, buses]
-        inject[rows, cols] = (place(sz, dispatch[:, lanes], select, block) + served - load).astype(BF)
-        shed_p[rows, cols] = served
-        loads_p[rows, cols] = load
-
-
-def forward_kernel(sz, chunk, step, *refs):
+        inject[rows, cols] = (place(sz, dispatch[:, lanes], select, block) + net[:, buses]).astype(BF)
+
+
+def forward_kernel(sz, chunk, *refs):
     chips = sz.chips
     own, other = refs[:chips], refs[chips : 2 * chips]
     factors = refs[2 * chips]
     outs = refs[2 * chips + 1 : 3 * chips + 1]
     inject, flows = refs[3 * chips + 1 :]
     scen, chip, core = where_am_i()
-    extra = LANES if chunk == 0 else 0
+    half = sz.halves[chunk]
 
     def gather(first, second):
         for slot in range(chips):
@@ -137,71 +140,67 @@
     def _():
         gather(other, own)
 
-    if extra:
+    if chunk == 0:
         total = jnp.sum(inject[...].astype(F32), axis=1, keepdims=True)
         high, middle, low = (piece.astype(F32) for piece in pieces(total))
         lane = lax.broadcasted_iota(jnp.int32, (sz.total, LANES), 1)
         tile = jnp.where(lane == 0, high, jnp.where(lane == 1, middle, jnp.where(lane == 2, low, 0.0)))
         for slot in range(chips):
-            flows[slot, :, sz.half :] = jnp.zeros((2 * sz.pair, LANES), F32)
-            flows[slot, : sz.pair, sz.half :] = tile[slot * sz.pair : (slot + 1) * sz.pair]
+            flows[slot, :, half:] = jnp.zeros((2 * sz.pair, LANES), F32)
+            flows[slot, : sz.pair, half:] = tile[slot * sz.pair : (slot + 1) * sz.pair]
     for side in range(2):
-
-        def body(i, _, side=side):
-            source = pl.ds(pl.multiple_of(chunk * sz.chunk + side * sz.half + i * step, step), step)
-            target = pl.ds(pl.multiple_of(i * step, step), step)
-            product = dot_t(factors[source, :], inject[...]).T
-            for slot in range(chips):
-                flows[slot, side * sz.pair : (side + 1) * sz.pair, target] = product[
-                    slot * sz.pair : (slot + 1) * sz.pair
-                ]
-            return 0
-
-        lax.fori_loop(0, sz.half // step, body, 0)
+        start = sz.starts[chunk] + side * half
+        product = dot_t(factors[start : start + half, :], inject[...]).T
+        for slot in range(chips):
+            flows[slot, side * sz.pair : (side + 1) * sz.pair, :half] = product[slot * sz.pair : (slot + 1) * sz.pair]
     for away in range(chips):
         found = flows[chip ^ scen ^ away]
         outs[away][...] = found.astype(outs[away].dtype)
 
 
-def residual_kernel(sz, chunk, join, *refs):
+def residual_kernel(sz, chunk, *refs):
     scen = sz.scen
+    half, early, start = sz.halves[chunk], sz.early, sz.starts[chunk]
     parts = refs[:scen]
     copies, duals, limits = refs[scen : scen + 3]
-    wide = sz.half + LANES
     if chunk == 0:
         flows = refs[scen + 3 : 2 * scen + 2]
-        residual, copy_out, dual_out = refs[2 * scen + 2 : 2 * scen + 5]
-        messages = refs[2 * scen + 5 :]
+        residual, rest, copy_out, dual_out = refs[2 * scen + 2 : 2 * scen + 6]
+        messages = refs[2 * scen + 6 :]
+        skip = 0
     else:
-        old = refs[scen + 3 : scen + 5] if join else None
-        residual, copy_out, dual_out = refs[-3:]
+        rest, residual, copy_out, dual_out = refs[scen + 3 :]
+        before = rest.shape[1]
+        residual[:, :before] = rest[...]
+        skip = early + LANES
     total = parts[0][...]
     for part in parts[1:]:
-        total = total + part[:, wide if chunk else 0 :].astype(F32)
+        total = total + part[:, skip:].astype(F32)
     for side in range(2):
         rows = slice(side * sz.pair, (side + 1) * sz.pair)
-        start = chunk * sz.chunk + side * sz.half
-        base = chunk * sz.chunk if copies.shape[1] == sz.lines else 0
-        cols = slice(base + side * sz.half, base + (side + 1) * sz.half)
-        to = slice(start, start + sz.half) if join else slice(side * sz.half, (side + 1) * sz.half)
-        now, copy, dual = total[rows, : sz.half], copies[:, cols], duals[:, cols]
-        limit = limits[:, start : start + sz.half]
-        residual[rows, : sz.half] = (now - copy + dual).astype(BF)
+        base = start if copies.shape[1] == sz.lines else 0
+        cols = slice(base + side * half, base + (side + 1) * half)
+        to = slice(side * half, (side + 1) * half)
+        now, copy, dual = total[rows, :half], copies[:, cols], duals[:, cols]
+        limit = limits[:, start + side * half : start + (side + 1) * half]
+        found = (now - copy + dual).astype(BF)
+        if chunk == 0:
+            residual[rows, :early] = found[:, :early]
+            rest[rows, :] = found[:, early:]
+        else:
+            residual[rows, before:] = found
         copy_next = jnp.minimum(jnp.maximum(now + dual, -limit), limit)
         copy_out[:, to] = copy_next
         dual_out[:, to] = dual + now - copy_next
     if chunk == 0:
-        balance = jnp.sum(total[:, sz.half :], axis=1, keepdims=True) / BUSES
+        balance = jnp.sum(total[:, half:], axis=1, keepdims=True) / BUSES
         high, middle, low = (piece.astype(F32) for piece in pieces(balance))
         lane = lax.broadcasted_iota(jnp.int32, (2 * sz.pair, LANES), 1)
         tile = jnp.where(lane == 0, high, jnp.where(lane == 1, middle, jnp.where(lane == 2, low, 0.0)))
-        residual[:, sz.half :] = tile.astype(BF)
+        residual[:, early:] = tile.astype(BF)
         for message, flow in zip(messages, flows):
-            message[:, :wide] = residual[...]
-            message[:, wide:] = flow[...]
-    elif join:
-        copy_out[:, : chunk * sz.chunk] = old[0][...]
-        dual_out[:, : chunk * sz.chunk] = old[1][...]
+            message[:, : early + LANES] = residual[...]
+            message[:, early + LANES :] = flow[...]
 
 
 def backward_kernel(sz, chunk, step, *refs):
@@ -218,23 +217,30 @@
 
             @pl.when(chip == (me ^ slot))
             def _(slot=slot):
-                tile = parts[slot][: sz.pair, sz.half : sz.half + LANES].astype(F32)
+                tile = parts[slot][: sz.pair, sz.early : sz.early + LANES].astype(F32)
                 found = jnp.sum(tile, axis=1, keepdims=True)
                 balances[...] = jnp.broadcast_to(found, (sz.pair, LANES))
 
+    widths = (sz.early,) if chunk == 0 else (sz.halves[0] - sz.early, sz.halves[1])
     for slot in range(scen):
-        for side in range(2):
-            residual[slot * sz.pair : (slot + 1) * sz.pair, side * sz.half : (side + 1) * sz.half] = parts[slot][
-                side * sz.pair : (side + 1) * sz.pair, : sz.half
-            ]
+        source = target = 0
+        for width in widths:
+            for side in range(2):
+                residual[slot * sz.pair : (slot + 1) * sz.pair, target : target + width] = parts[slot][
+                    side * sz.pair : (side + 1) * sz.pair, source : source + width
+                ]
+                target += width
+            source += width
 
     def body(i, _):
         cols = pl.ds(pl.multiple_of(i * step, step), step)
-        product = jnp.dot(
-            residual[...],
-            factors[chunk * sz.chunk : (chunk + 1) * sz.chunk, cols],
-            preferred_element_type=F32,
-        )
+        product, at = None, 0
+        for low, high in sz.ranges[chunk]:
+            term = jnp.dot(
+                residual[:, at : at + high - low], factors[low:high, cols], preferred_element_type=F32
+            )
+            product = term if product is None else product + term
+            at += high - low
         if chunk:
             product = before[:, cols] + product
         if not last:
@@ -279,16 +285,18 @@
     for part in parts[1:]:
         total = total + part[...].astype(F32)
     grad = total + shift
-    shed_next = jnp.minimum(jnp.maximum(shed[...] - 0.4 * (1.5 + grad), 0.0), loads[...])
     capacity = cap[...] * commit[...].astype(F32)
     if last:
         weights, gens_out, shed_out, lam_out, weighted_out, dual_out = rest
     else:
         gens_out, shed_out, lam_out, inject = rest
-        shed_out[...] = shed_next
     lam_out[...] = jnp.broadcast_to(lam_now + balance, lam_out.shape)
     for block, rows, cols in blocks_of(sz):
         lanes = slice(block * LANES, (block + 1) * LANES)
+        buses = slice(block * sz.width, (block + 1) * sz.width)
+        load = loads[:, buses]
+        shed_next = jnp.minimum(jnp.maximum(shed[:, buses] - 0.4 * (1.5 + grad[rows, cols]), 0.0), load)
+        shed_out[:, buses] = shed_next
         picked = jnp.dot(stacked(grad[rows, cols]), select[block], preferred_element_type=F32)
         picked = unstacked(picked, sz.rows)
         now = gens[:, lanes]
@@ -297,14 +305,11 @@
         gens_out[:, lanes] = now
         if last:
             dual_out[:, lanes] = dual[:, lanes] + now
-            shed_out[:, block * sz.width : (block + 1) * sz.width] = shed_next[rows, cols]
             weighted_out[:1, lanes] = jnp.sum(weights[:, :1] * now, axis=0, keepdims=True)
             all_weights = jnp.sum(weights[:, :1], axis=0, keepdims=True)
             weighted_out[1:, lanes] = jnp.broadcast_to(all_weights, (7, LANES))
         else:
-            inject[rows, cols] = (
-                place(sz, now, select, block) + shed_next[rows, cols] - loads[rows, cols]
-            ).astype(BF)
+            inject[rows, cols] = (place(sz, now, select, block) + shed_next - load).astype(BF)
 
 
 def add_kernel(first, second, out):
@@ -328,6 +333,11 @@
 
 def to_chip(n, away, value):
     return lax.ppermute(value, "line", [(i, i ^ (2 * away)) for i in range(n)])
+
+
+def spread(move, n, values):
+    found = {away: move(n, away, values[away - 1]) for away in range(1, len(values) + 1)}
+    return [found[away] for away in range(1, len(values) + 1)]
 
 
 def to_core(n, value):
@@ -361,14 +371,14 @@
     capacity, on, previous, limits = row(gen_cap), row(commit), row(consensus_prev), row(flow_limit)
     lam, weights = column(balance_dual), column(scen_weight)
     packed = (sz.fold * rows, sz.part)
-    step_f = min(1024, sz.half)
     step_b = next(s for s in (1024, 640, 512, 256, 128) if buses % s == 0)
-    macs = sz.total * sz.chunk * buses
+    macs = [sz.total * 2 * half * buses for half in sz.halves]
 
     generation, copies, duals = dispatch, flow_copy, flow_dual
-    first = (dispatch, load_shed, bus_loads, row(gen_bus))
-    made = ((packed, BF), (packed, F32), (packed, F32), ((gens // LANES, sz.width, LANES), BF))
-    inject, shed, loads, select = call(
+    first = (dispatch, load_shed - bus_loads, row(gen_bus))
+    made = ((packed, BF), ((gens // LANES, sz.width, LANES), BF))
+    shed = load_shed
+    inject, select = call(
         functools.partial(start_kernel, sz),
         first,
         made,
@@ -376,50 +386,55 @@
         limit=GRANT - nbytes(first + tuple(jax.ShapeDtypeStruct(*each) for each in made)) - (1 << 16),
     )
     for iteration in range(ITERS):
-        own = [inject] + [to_chip(n_line, away, inject) for away in range(1, chips)]
+        own = [inject] + spread(to_chip, n_line, [inject] * (chips - 1))
         other = [to_core(n_line, value) for value in own]
         final = iteration == ITERS - 1
         tall = 2 * sz.pair
-        widths = (sz.half + LANES, sz.half)
+        widths = (sz.halves[0] + LANES, sz.halves[1])
         flows = []
         for chunk in range(CHUNKS):
             block = (tall, widths[chunk])
             flows.append(
                 call(
-                    functools.partial(forward_kernel, sz, chunk, step_f),
+                    functools.partial(forward_kernel, sz, chunk),
                     (*own, *other, shift_factors),
                     [(block, F32)] + [(block, BF)] * (n_scen - 1),
                     [((sz.total, buses), BF), ((chips, *block), F32)],
-                    flops=2 * macs,
+                    flops=2 * macs[chunk],
                     limit=GRANT - (nbytes(own + other) if iteration == 0 else 0),
                 )
             )
             if chunk == 0:
-                parts = [flows[0][0]] + [to_scen(n_scen, away, flows[0][away]) for away in range(1, n_scen)]
+                parts = [flows[0][0]] + spread(to_scen, n_scen, flows[0][1:])
         state = lambda width: [((sz.pair, width), F32)] * 2
         old = (flow_copy, flow_dual) if iteration == 0 else None
-        first_res, first_copy, first_dual, *messages = call(
-            functools.partial(residual_kernel, sz, 0, False),
+        first_res, rest, first_copy, first_dual, *messages = call(
+            functools.partial(residual_kernel, sz, 0),
             (*parts, *(old or (copies[0], duals[0])), limits, *flows[1][1:]),
-            [((tall, widths[0]), BF), *state(sz.chunk)] + [((tall, sum(widths)), BF)] * (n_scen - 1),
+            [
+                ((tall, sz.early + LANES), BF),
+                ((tall, sz.halves[0] - sz.early), BF),
+                *state(2 * sz.halves[0]),
+                *[((tall, sz.early + LANES + sz.halves[1]), BF)] * (n_scen - 1),
+            ],
             keep=shift_factors,
         )
-        got = [to_scen(n_scen, away, message) for away, message in enumerate(messages, 1)]
+        got = spread(to_scen, n_scen, messages)
         second_res, second_copy, second_dual = call(
-            functools.partial(residual_kernel, sz, 1, final),
+            functools.partial(residual_kernel, sz, 1),
             (
                 flows[1][0],
                 *got,
                 *(old or (copies[1], duals[1])),
                 limits,
-                *((first_copy, first_dual) if final else ()),
+                rest,
             ),
-            [((tall, widths[1]), BF), *state(lines if final else sz.chunk)],
+            [((tall, lines // 2 - sz.early), BF), *state(2 * sz.halves[1])],
             keep=shift_factors,
         )
         residuals = [
             [first_res, *got],
-            [second_res] + [to_scen(n_scen, away, second_res) for away in range(1, n_scen)],
+            [second_res] + spread(to_scen, n_scen, [second_res] * (n_scen - 1)),
         ]
         new_copies, new_duals = [first_copy, second_copy], [first_dual, second_dual]
         copies, duals = new_copies, new_duals
@@ -434,8 +449,8 @@
                 functools.partial(backward_kernel, sz, chunk, step_b),
                 (*residuals[chunk], shift_factors, *before),
                 outs,
-                [((sz.total, sz.chunk), BF)],
-                flops=2 * macs,
+                [((sz.total, sum(high - low for low, high in sz.ranges[chunk])), BF)],
+                flops=sum(macs),
             )
             if chunk == 0:
                 balances = found[-1]
@@ -448,15 +463,15 @@
             [((chips, *packed), F32)],
             keep=None if final else shift_factors,
         )
-        parts = [sums[0]] + [to_chip(n_line, away, sums[away]) for away in range(1, chips)]
-        args = (*parts, balances, lam, shed, loads, generation, select, cost_coef, ph_dual, previous, capacity, on)
+        parts = [sums[0]] + spread(to_chip, n_line, sums[1:])
+        args = (*parts, balances, lam, shed, bus_loads, generation, select, cost_coef, ph_dual, previous, capacity, on)
         if not final:
             generation, shed, lam, inject = call(
                 functools.partial(update_kernel, sz, False),
                 args,
-                [((rows, gens), F32), (packed, F32), ((rows, LANES), F32), (packed, BF)],
+                [((rows, gens), F32), ((rows, buses), F32), ((rows, LANES), F32), (packed, BF)],
                 keep=shift_factors,
-                limit=GRANT - nbytes((dispatch, shed, loads, select)),
+                limit=GRANT - nbytes((dispatch, select)),
             )
         else:
             generation, shed, lam, weighted, dual_sum = call(
@@ -465,13 +480,13 @@
                 [((rows, gens), F32), ((rows, buses), F32), ((rows, LANES), F32), ((8, gens), F32), ((rows, gens), F32)],
             )
     (weighted,) = call(add_kernel, (weighted, to_core(n_line, weighted)), [((8, gens), F32)])
-    parts = [weighted] + [to_chip(n_line, away, weighted) for away in range(1, chips)]
+    parts = [weighted] + spread(to_chip, n_line, [weighted] * (chips - 1))
     consensus, dual_out = call(
         functools.partial(finish_kernel, sz),
         (*parts, dual_sum),
         [((1, gens), F32), ((rows, gens), F32)],
     )
-    return generation, shed, copies[-1], duals[-1], lam[:, 0], consensus.reshape(-1), dual_out
+    return generation, shed, jnp.concatenate(copies, 1), jnp.concatenate(duals, 1), lam[:, 0], consensus.reshape(-1), dual_out
 
 
 def solution(mesh):

time: 138 us -> 135 us (0.978)
  waiting for transfers between devices: 39.6 us -> 37.3 us
  other arithmetic: 0.01 us -> 1.99 us
  local copies, waits for them, and re-layouts: 4.65 us -> 2.71 us
    unnamed x50, local copies, waits for them, and re-layouts: 3.89 us -> 1.94 us
    ppermute x18, waiting for transfers between devices: 14.1 us -> 12.7 us  [to_scen(): return lax.ppermute(value, 'scen', [(i, i ^ away) for i in range(n)])]
  transfers between devices with their start and end apart: 44 -> 44, of which waited for: 25 -> 25; matrix products, arithmetic and copies ran while one was open for 0% -> 1% of each run, Pallas kernels for 15% -> 13%
where the time goes in v5:
time: 135 us
  starting transfers between devices  46.8 us (35%)
  Pallas kernels  44.9 us (33%)
  waiting for transfers between devices  37.3 us (28%)
  local copies, waits for them, and re-layouts  2.71 us (2%)
  other arithmetic  1.99 us (1%)
    pallas_call x19, Pallas kernels, call(): pl.pallas_call(kernel, in_specs=[WHOLE] * len(args), out_specs=[WHOLE] *...  44.9 us
    ppermute x18, starting transfers between devices, to_scen(): return lax.ppermute(value, 'scen', [(i, i ^ away) for i in range(n)])  27.9 us
    ppermute x15, waiting for transfers between devices, to_chip(): return lax.ppermute(value, 'line', [(i, i ^ 2 * away) for i in range(n)])  18.8 us
    ppermute x15, starting transfers between devices, to_chip(): return lax.ppermute(value, 'line', [(i, i ^ 2 * away) for i in range(n)])  18.7 us
    ppermute x18, waiting for transfers between devices, to_scen(): return lax.ppermute(value, 'scen', [(i, i ^ away) for i in range(n)])  12.7 us
    ppermute x11, waiting for transfers between devices, to_core(): return lax.ppermute(value, 'line', [(i, i ^ 1) for i in range(n)])  5.84 us
  transfers between devices with their start and end apart: 44, of which 25 were waited for; matrix products, arithmetic and copies ran while one was open for 1% of the time, Pallas kernels for 13%

profile of v5, /device:TPU:0, one launch (start us, length us, event | category | flops | bytes accessed | tf_op | source)
XLA Modules:
  0.0 134.8 jit_solution(18236652990933696269)
XLA Ops:
  4.2 3.0 %collective-permute-start = (bf16[24,1280]{1,0:T(8,128)(2,1)S(1)}, bf16[24,1280]{1,0:T(8,128)(2,1)S(1)}, u32[]{:S(2)}, u32[]{:S(2)}) collective-permute-start(bf16[24,1280]{1,0:T(8,128)(2,1)S(1)} %get-tuple-element.72.refs_0_), channel_id=1, source_target_pairs={{0,2},{1,3},{2,0},{3,1},{4,6},{5,7},{6,4},{7,5},{8,10},{9,11},{10,... | collective-permute-start | bytes 184328 | tf_op jit(solution)/shard_map/ppermute | solution.py:335
  7.2 1.5 %collective-permute-start.1 = (bf16[24,1280]{1,0:T(8,128)(2,1)S(1)}, bf16[24,1280]{1,0:T(8,128)(2,1)S(1)}, u32[]{:S(2)}, u32[]{:S(2)}) collective-permute-start(bf16[24,1280]{1,0:T(8,128)(2,1)S(1)} %get-tuple-element.72.refs_0_), channel_id=1, source_target_pairs={{0,4},{1,5},{2,6},{3,7},{4,0},{5,1},{6,2},{7,3},{8,12},{9,13},{10,... | collective-permute-start | bytes 184328 | tf_op jit(solution)/shard_map/ppermute | solution.py:335
  9.5 1.9 %collective-permute-done.1.refs_2_ = bf16[24,1280]{1,0:T(8,128)(2,1)S(1)} collective-permute-done((bf16[24,1280]{1,0:T(8,128)(2,1)S(1)}, bf16[24,1280]{1,0:T(8,128)(2,1)S(1)}, u32[]{:S(2)}, u32[]{:S(2)}) %collective-permute-start.1) | collective-permute-done | bytes 61472 | tf_op jit(solution)/shard_map/ppermute | solution.py:335
  11.4 2.4 %collective-permute-done.2.refs_3_ = bf16[24,1280]{1,0:T(8,128)(2,1)S(1)} collective-permute-done((bf16[24,1280]{1,0:T(8,128)(2,1)S(1)}, bf16[24,1280]{1,0:T(8,128)(2,1)S(1)}, u32[]{:S(2)}, u32[]{:S(2)}) %collective-permute-start.2) | collective-permute-done | bytes 61472 | tf_op jit(solution)/shard_map/ppermute | solution.py:335
  15.3 6.5 %shard_map.200 = (f32[24,1280]{1,0:T(8,128)S(1)}, bf16[24,1280]{1,0:T(8,128)(2,1)S(1)}, bf16[24,1280]{1,0:T(8,128)(2,1)S(1)}, bf16[24,1280]{1,0:T(8,128)(2,1)S(1)}) custom-call(bf16[24,1280]{1,0:T(8,128)(2,1)S(1)} %get-tuple-element.72.refs_0_, bf16[24,1280]{1,0:T(8,128)(2,1)S(1)} %collective-permute-done.refs_1_, ...), custom_call_target="tpu_custom_call" | custom-call | flops 1132462080 | bytes 42434560 | tf_op jit(solution)/shard_map/pallas_call | solution.py:28
  21.8 3.1 %collective-permute-start.7 = (bf16[24,1280]{1,0:T(8,128)(2,1)S(1)}, bf16[24,1280]{1,0:T(8,128)(2,1)S(1)}, u32[]{:S(2)}, u32[]{:S(2)}) collective-permute-start(bf16[24,1280]{1,0:T(8,128)(2,1)S(1)} %get-tuple-element.75), channel_id=1, source_target_pairs={{0,8},{8,0},{16,24},{24,16},{1,9},{9,1},{17,25},{25,17},{2,10},{10... | collective-permute-start | bytes 184328 | tf_op jit(solution)/shard_map/ppermute | solution.py:331
  24.9 2.6 %collective-permute-start.8 = (bf16[24,1280]{1,0:T(8,128)(2,1)S(1)}, bf16[24,1280]{1,0:T(8,128)(2,1)S(1)}, u32[]{:S(2)}, u32[]{:S(2)}) collective-permute-start(bf16[24,1280]{1,0:T(8,128)(2,1)S(1)} %get-tuple-element.76), channel_id=1, source_target_pairs={{0,16},{8,24},{16,0},{24,8},{1,17},{9,25},{17,1},{25,9},{2,18},{10... | collective-permute-start | bytes 184328 | tf_op jit(solution)/shard_map/ppermute | solution.py:331
  27.5 5.1 %shard_map.199 = (f32[24,896]{1,0:T(8,128)S(1)}, bf16[24,896]{1,0:T(8,128)(2,1)S(1)}, bf16[24,896]{1,0:T(8,128)(2,1)S(1)}, bf16[24,896]{1,0:T(8,128)(2,1)S(1)}) custom-call(bf16[24,1280]{1,0:T(8,128)(2,1)S(1)} %get-tuple-element.72.refs_0_, bf16[24,1280]{1,0:T(8,128)(2,1)S(1)} %collective-permute-done.refs_1_, ...), custom_call_target="tpu_custom_call" | custom-call | flops 880803840 | bytes 42434560 | tf_op jit(solution)/shard_map/pallas_call | solution.py:28
  33.7 3.5 %collective-permute-start.11 = (bf16[24,1920]{1,0:T(8,128)(2,1)S(1)}, bf16[24,1920]{1,0:T(8,128)(2,1)S(1)}, u32[]{:S(2)}, u32[]{:S(2)}) collective-permute-start(bf16[24,1920]{1,0:T(8,128)(2,1)S(1)} %get-tuple-element.82), channel_id=1, source_target_pairs={{0,16},{8,24},{16,0},{24,8},{1,17},{9,25},{17,1},{25,9},{2,18},{10... | collective-permute-start | bytes 276488 | tf_op jit(solution)/shard_map/ppermute | solution.py:331
  38.7 5.0 %collective-permute-done.11.refs_2_ = bf16[24,1920]{1,0:T(8,128)(2,1)S(1)} collective-permute-done((bf16[24,1920]{1,0:T(8,128)(2,1)S(1)}, bf16[24,1920]{1,0:T(8,128)(2,1)S(1)}, u32[]{:S(2)}, u32[]{:S(2)}) %collective-permute-start.11) | collective-permute-done | bytes 92192 | tf_op jit(solution)/shard_map/ppermute | solution.py:331
  43.8 1.6 %collective-permute-start.13 = (bf16[24,1152]{1,0:T(8,128)(2,1)S(1)}, bf16[24,1152]{1,0:T(8,128)(2,1)S(1)}, u32[]{:S(2)}, u32[]{:S(2)}) collective-permute-start(bf16[24,1152]{1,0:T(8,128)(2,1)S(1)} %get-tuple-element.85.refs_0_), channel_id=1, source_target_pairs={{0,8},{8,0},{16,24},{24,16},{1,9},{9,1},{17,25},{25,17},{2,10},{10... | collective-permute-start | bytes 165896 | tf_op jit(solution)/shard_map/ppermute | solution.py:331
  48.2 3.9 %shard_map.203 = (f32[48,5120]{1,0:T(8,128)S(1)}, f32[12,128]{1,0:T(8,128)S(1)}) custom-call(bf16[24,1024]{1,0:T(8,128)(2,1)S(1)} %get-tuple-element.86.refs_0_, bf16[24,1920]{1,0:T(8,128)(2,1)S(1)} %collective-permute-done.10.refs_1_, bf16[24,1920]{1,0:T(8,128)(2,1)S(1)} %collective-permute-done.11.refs_2_, ...), custom_call_target="tpu_custom_call" | custom-call | flops 1006632960 | bytes 42268672 | tf_op jit(solution)/shard_map/pallas_call | solution.py:28
  52.9 4.7 %shard_map.204 = (f32[24,5120]{1,0:T(8,128)S(1)}, bf16[24,5120]{1,0:T(8,128)(2,1)S(1)}) custom-call(bf16[24,1152]{1,0:T(8,128)(2,1)S(1)} %get-tuple-element.85.refs_0_, bf16[24,1152]{1,0:T(8,128)(2,1)S(1)} %collective-permute-done.13.refs_1_, bf16[24,1152]{1,0:T(8,128)(2,1)S(1)} %collective-permute-done.14.refs_2_, ...), custom_call_target="tpu_custom_call" | custom-call | flops 1006632960 | bytes 43147264 | tf_op jit(solution)/shard_map/pallas_call | solution.py:28
  59.3 1.6 %collective-permute-start.17 = (bf16[24,1280]{1,0:T(8,128)(2,1)S(1)}, bf16[24,1280]{1,0:T(8,128)(2,1)S(1)}, u32[]{:S(2)}, u32[]{:S(2)}) collective-permute-start(bf16[24,1280]{1,0:T(8,128)(2,1)S(1)} %get-tuple-element.91), channel_id=1, source_target_pairs={{0,2},{1,3},{2,0},{3,1},{4,6},{5,7},{6,4},{7,5},{8,10},{9,11},{10,... | collective-permute-start | bytes 184328 | tf_op jit(solution)/shard_map/ppermute | solution.py:335
  60.8 1.5 %collective-permute-start.18 = (bf16[24,1280]{1,0:T(8,128)(2,1)S(1)}, bf16[24,1280]{1,0:T(8,128)(2,1)S(1)}, u32[]{:S(2)}, u32[]{:S(2)}) collective-permute-start(bf16[24,1280]{1,0:T(8,128)(2,1)S(1)} %get-tuple-element.92), channel_id=1, source_target_pairs={{0,4},{1,5},{2,6},{3,7},{4,0},{5,1},{6,2},{7,3},{8,12},{9,13},{10,... | collective-permute-start | bytes 184328 | tf_op jit(solution)/shard_map/ppermute | solution.py:335
  65.1 2.4 %collective-permute-done.19.refs_3_ = bf16[24,1280]{1,0:T(8,128)(2,1)S(1)} collective-permute-done((bf16[24,1280]{1,0:T(8,128)(2,1)S(1)}, bf16[24,1280]{1,0:T(8,128)(2,1)S(1)}, u32[]{:S(2)}, u32[]{:S(2)}) %collective-permute-start.19) | collective-permute-done | bytes 61472 | tf_op jit(solution)/shard_map/ppermute | solution.py:335
  67.6 1.7 %shard_map.206 = (f32[6,1024]{1,0:T(8,128)S(1)}, f32[6,5120]{1,0:T(8,128)S(1)}, f32[6,128]{1,0:T(8,128)S(1)}, bf16[24,1280]{1,0:T(8,128)(2,1)S(1)}) custom-call(bf16[4096,5120]{1,0:T(8,128)(2,1)S(1)} %bitcast.7, f32[24,1280]{1,0:T(8,128)S(1)} %get-tuple-element.90.refs_0_, bf16[24,1280]{1,0:T(8,128)(2,1)S(1)} %collective-permute-done.17.refs_1_, ...), custom_call_target="tpu_custom_call" | custom-call | bytes 1942528 | tf_op jit(solution)/shard_map/pallas_call | solution.py:28
  70.4 2.5 %collective-permute-start.22 = (bf16[24,1280]{1,0:T(8,128)(2,1)S(1)}, bf16[24,1280]{1,0:T(8,128)(2,1)S(1)}, u32[]{:S(2)}, u32[]{:S(2)}) collective-permute-start(bf16[24,1280]{1,0:T(8,128)(2,1)S(1)} %get-tuple-element.96.refs_0_), channel_id=1, source_target_pairs={{0,6},{1,7},{2,4},{3,5},{4,2},{5,3},{6,0},{7,1},{8,14},{9,15},{10,... | collective-permute-start | bytes 184328 | tf_op jit(solution)/shard_map/ppermute | solution.py:335
  76.8 6.5 %shard_map.208 = (f32[24,1280]{1,0:T(8,128)S(1)}, bf16[24,1280]{1,0:T(8,128)(2,1)S(1)}, bf16[24,1280]{1,0:T(8,128)(2,1)S(1)}, bf16[24,1280]{1,0:T(8,128)(2,1)S(1)}) custom-call(bf16[24,1280]{1,0:T(8,128)(2,1)S(1)} %get-tuple-element.96.refs_0_, bf16[24,1280]{1,0:T(8,128)(2,1)S(1)} %collective-permute-done.20.refs_1_, ...), custom_call_target="tpu_custom_call" | custom-call | flops 1132462080 | bytes 42434560 | tf_op jit(solution)/shard_map/pallas_call | solution.py:28
  83.4 2.4 %collective-permute-start.28 = (bf16[24,1280]{1,0:T(8,128)(2,1)S(1)}, bf16[24,1280]{1,0:T(8,128)(2,1)S(1)}, u32[]{:S(2)}, u32[]{:S(2)}) collective-permute-start(bf16[24,1280]{1,0:T(8,128)(2,1)S(1)} %get-tuple-element.100), channel_id=1, source_target_pairs={{0,16},{8,24},{16,0},{24,8},{1,17},{9,25},{17,1},{25,9},{2,18},{10... | collective-permute-start | bytes 184328 | tf_op jit(solution)/shard_map/ppermute | solution.py:331
  85.7 2.0 %collective-permute-start.29 = (bf16[24,1280]{1,0:T(8,128)(2,1)S(1)}, bf16[24,1280]{1,0:T(8,128)(2,1)S(1)}, u32[]{:S(2)}, u32[]{:S(2)}) collective-permute-start(bf16[24,1280]{1,0:T(8,128)(2,1)S(1)} %get-tuple-element.101), channel_id=1, source_target_pairs={{0,24},{8,16},{16,8},{24,0},{1,25},{9,17},{17,9},{25,1},{2,26},{10... | collective-permute-start | bytes 184328 | tf_op jit(solution)/shard_map/ppermute | solution.py:331
  87.7 5.1 %shard_map.207 = (f32[24,896]{1,0:T(8,128)S(1)}, bf16[24,896]{1,0:T(8,128)(2,1)S(1)}, bf16[24,896]{1,0:T(8,128)(2,1)S(1)}, bf16[24,896]{1,0:T(8,128)(2,1)S(1)}) custom-call(bf16[24,1280]{1,0:T(8,128)(2,1)S(1)} %get-tuple-element.96.refs_0_, bf16[24,1280]{1,0:T(8,128)(2,1)S(1)} %collective-permute-done.20.refs_1_, ...), custom_call_target="tpu_custom_call" | custom-call | flops 880803840 | bytes 42434560 | tf_op jit(solution)/shard_map/pallas_call | solution.py:28
  93.2 2.2 %collective-permute-start.31 = (bf16[24,1920]{1,0:T(8,128)(2,1)S(1)}, bf16[24,1920]{1,0:T(8,128)(2,1)S(1)}, u32[]{:S(2)}, u32[]{:S(2)}) collective-permute-start(bf16[24,1920]{1,0:T(8,128)(2,1)S(1)} %get-tuple-element.108), channel_id=1, source_target_pairs={{0,16},{8,24},{16,0},{24,8},{1,17},{9,25},{17,1},{25,9},{2,18},{10... | collective-permute-start | bytes 276488 | tf_op jit(solution)/shard_map/ppermute | solution.py:331
  95.4 2.0 %collective-permute-start.32 = (bf16[24,1920]{1,0:T(8,128)(2,1)S(1)}, bf16[24,1920]{1,0:T(8,128)(2,1)S(1)}, u32[]{:S(2)}, u32[]{:S(2)}) collective-permute-start(bf16[24,1920]{1,0:T(8,128)(2,1)S(1)} %get-tuple-element.109), channel_id=1, source_target_pairs={{0,24},{8,16},{16,8},{24,0},{1,25},{9,17},{17,9},{25,1},{2,26},{10... | collective-permute-start | bytes 276488 | tf_op jit(solution)/shard_map/ppermute | solution.py:331
  98.0 4.9 %collective-permute-done.31.refs_2_ = bf16[24,1920]{1,0:T(8,128)(2,1)S(1)} collective-permute-done((bf16[24,1920]{1,0:T(8,128)(2,1)S(1)}, bf16[24,1920]{1,0:T(8,128)(2,1)S(1)}, u32[]{:S(2)}, u32[]{:S(2)}) %collective-permute-start.31) | collective-permute-done | bytes 92192 | tf_op jit(solution)/shard_map/ppermute | solution.py:331
  103.0 1.6 %collective-permute-start.33 = (bf16[24,1152]{1,0:T(8,128)(2,1)S(1)}, bf16[24,1152]{1,0:T(8,128)(2,1)S(1)}, u32[]{:S(2)}, u32[]{:S(2)}) collective-permute-start(bf16[24,1152]{1,0:T(8,128)(2,1)S(1)} %get-tuple-element.113.refs_0_), channel_id=1, source_target_pairs={{0,8},{8,0},{16,24},{24,16},{1,9},{9,1},{17,25},{25,17},{2,10},{10... | collective-permute-start | bytes 165896 | tf_op jit(solution)/shard_map/ppermute | solution.py:331
  105.3 2.1 %collective-permute-start.35 = (bf16[24,1152]{1,0:T(8,128)(2,1)S(1)}, bf16[24,1152]{1,0:T(8,128)(2,1)S(1)}, u32[]{:S(2)}, u32[]{:S(2)}) collective-permute-start(bf16[24,1152]{1,0:T(8,128)(2,1)S(1)} %get-tuple-element.113.refs_0_), channel_id=1, source_target_pairs={{0,24},{8,16},{16,8},{24,0},{1,25},{9,17},{17,9},{25,1},{2,26},{10... | collective-permute-start | bytes 165896 | tf_op jit(solution)/shard_map/ppermute | solution.py:331
  107.4 3.9 %shard_map.211 = (f32[48,5120]{1,0:T(8,128)S(1)}, f32[12,128]{1,0:T(8,128)S(1)}) custom-call(bf16[24,1024]{1,0:T(8,128)(2,1)S(1)} %get-tuple-element.114.refs_0_, bf16[24,1920]{1,0:T(8,128)(2,1)S(1)} %collective-permute-done.30.refs_1_, bf16[24,1920]{1,0:T(8,128)(2,1)S(1)} %collective-permute-done.31.refs_2_, ...), custom_call_target="tpu_custom_call" | custom-call | flops 1006632960 | bytes 42268672 | tf_op jit(solution)/shard_map/pallas_call | solution.py:28
  111.3 4.7 %shard_map.212 = (f32[24,5120]{1,0:T(8,128)S(1)}, bf16[24,5120]{1,0:T(8,128)(2,1)S(1)}) custom-call(bf16[24,1152]{1,0:T(8,128)(2,1)S(1)} %get-tuple-element.113.refs_0_, bf16[24,1152]{1,0:T(8,128)(2,1)S(1)} %collective-permute-done.33.refs_1_, bf16[24,1152]{1,0:T(8,128)(2,1)S(1)} %collective-permute-done.34.refs_2_, ...), custom_call_target="tpu_custom_call" | custom-call | flops 1006632960 | bytes 43147264 | tf_op jit(solution)/shard_map/pallas_call | solution.py:28
  117.7 1.6 %collective-permute-start.37 = (bf16[24,1280]{1,0:T(8,128)(2,1)S(1)}, bf16[24,1280]{1,0:T(8,128)(2,1)S(1)}, u32[]{:S(2)}, u32[]{:S(2)}) collective-permute-start(bf16[24,1280]{1,0:T(8,128)(2,1)S(1)} %get-tuple-element.119), channel_id=1, source_target_pairs={{0,2},{1,3},{2,0},{3,1},{4,6},{5,7},{6,4},{7,5},{8,10},{9,11},{10,... | collective-permute-start | bytes 184328 | tf_op jit(solution)/shard_map/ppermute | solution.py:335
  123.5 2.4 %collective-permute-done.39.refs_3_ = bf16[24,1280]{1,0:T(8,128)(2,1)S(1)} collective-permute-done((bf16[24,1280]{1,0:T(8,128)(2,1)S(1)}, bf16[24,1280]{1,0:T(8,128)(2,1)S(1)}, u32[]{:S(2)}, u32[]{:S(2)}) %collective-permute-start.39) | collective-permute-done | bytes 61472 | tf_op jit(solution)/shard_map/ppermute | solution.py:335
  129.3 2.5 %collective-permute-start.43 = (f32[8,1024]{1,0:T(8,128)S(1)}, f32[8,1024]{1,0:T(8,128)S(1)}, u32[]{:S(2)}, u32[]{:S(2)}) collective-permute-start(f32[8,1024]{1,0:T(8,128)S(1)} %shard_map.215.refs_0_), channel_id=1, source_target_pairs={{0,6},{1,7},{2,4},{3,5},{4,2},{5,3},{6,0},{7,1},{8,14},{9,15},{10,... | collective-permute-start | bytes 98312 | tf_op jit(solution)/shard_map/ppermute | solution.py:335
  (131 shorter events, 35.6 us)
Async XLA Ops:
  4.2 5.3 %collective-permute-start = (bf16[24,1280]{1,0:T(8,128)(2,1)S(1)}, bf16[24,1280]{1,0:T(8,128)(2,1)S(1)}, u32[]{:S(2)}, u32[]{:S(2)}) collective-permute-start(bf16[24,1280]{1,0:T(8,128)(2,1)S(1)} %get-tuple-element.72.refs_0_), channel_id=1, source_target_pairs={{0,2},{1,3},{2,0},{3,1},{4,6},{5,7},{6,4},{7,5},{8,10},{9,11},{10,... | collective-permute-start | bytes 184328 | tf_op jit(solution)/shard_map/ppermute | solution.py:335
  8.7 5.1 %collective-permute-start.2 = (bf16[24,1280]{1,0:T(8,128)(2,1)S(1)}, bf16[24,1280]{1,0:T(8,128)(2,1)S(1)}, u32[]{:S(2)}, u32[]{:S(2)}) collective-permute-start(bf16[24,1280]{1,0:T(8,128)(2,1)S(1)} %get-tuple-element.72.refs_0_), channel_id=1, source_target_pairs={{0,6},{1,7},{2,4},{3,5},{4,2},{5,3},{6,0},{7,1},{8,14},{9,15},{10,... | collective-permute-start | bytes 184328 | tf_op jit(solution)/shard_map/ppermute | solution.py:335
  8.8 5.1 %collective-permute-start.3 = (bf16[24,1280]{1,0:T(8,128)(2,1)S(1)}, bf16[24,1280]{1,0:T(8,128)(2,1)S(1)}, u32[]{:S(2)}, u32[]{:S(2)}) collective-permute-start(bf16[24,1280]{1,0:T(8,128)(2,1)S(1)} %get-tuple-element.72.refs_0_), channel_id=1, source_target_pairs={{0,1},{1,0},{2,3},{3,2},{4,5},{5,4},{6,7},{7,6},{8,9},{9,8},{10,11... | collective-permute-start | bytes 184328 | tf_op jit(solution)/shard_map/ppermute | solution.py:344
  9.5 4.4 %collective-permute-start.4 = (bf16[24,1280]{1,0:T(8,128)(2,1)S(1)}, bf16[24,1280]{1,0:T(8,128)(2,1)S(1)}, u32[]{:S(2)}, u32[]{:S(2)}) collective-permute-start(bf16[24,1280]{1,0:T(8,128)(2,1)S(1)} %collective-permute-done.refs_1_), channel_id=1, source_target_pairs={{0,1},{1,0},{2,3},{3,2},{4,5},{5,4},{6,7},{7,6},{8,9},{9,8},{10,11... | collective-permute-start | bytes 184328 | tf_op jit(solution)/shard_map/ppermute | solution.py:344
  21.8 10.8 %collective-permute-start.7 = (bf16[24,1280]{1,0:T(8,128)(2,1)S(1)}, bf16[24,1280]{1,0:T(8,128)(2,1)S(1)}, u32[]{:S(2)}, u32[]{:S(2)}) collective-permute-start(bf16[24,1280]{1,0:T(8,128)(2,1)S(1)} %get-tuple-element.75), channel_id=1, source_target_pairs={{0,8},{8,0},{16,24},{24,16},{1,9},{9,1},{17,25},{25,17},{2,10},{10... | collective-permute-start | bytes 184328 | tf_op jit(solution)/shard_map/ppermute | solution.py:331
  24.9 7.7 %collective-permute-start.8 = (bf16[24,1280]{1,0:T(8,128)(2,1)S(1)}, bf16[24,1280]{1,0:T(8,128)(2,1)S(1)}, u32[]{:S(2)}, u32[]{:S(2)}) collective-permute-start(bf16[24,1280]{1,0:T(8,128)(2,1)S(1)} %get-tuple-element.76), channel_id=1, source_target_pairs={{0,16},{8,24},{16,0},{24,8},{1,17},{9,25},{17,1},{25,9},{2,18},{10... | collective-permute-start | bytes 184328 | tf_op jit(solution)/shard_map/ppermute | solution.py:331
  27.5 6.0 %collective-permute-start.9 = (bf16[24,1280]{1,0:T(8,128)(2,1)S(1)}, bf16[24,1280]{1,0:T(8,128)(2,1)S(1)}, u32[]{:S(2)}, u32[]{:S(2)}) collective-permute-start(bf16[24,1280]{1,0:T(8,128)(2,1)S(1)} %get-tuple-element.77), channel_id=1, source_target_pairs={{0,24},{8,16},{16,8},{24,0},{1,25},{9,17},{17,9},{25,1},{2,26},{10... | collective-permute-start | bytes 184328 | tf_op jit(solution)/shard_map/ppermute | solution.py:331
  33.6 5.0 %collective-permute-start.10 = (bf16[24,1920]{1,0:T(8,128)(2,1)S(1)}, bf16[24,1920]{1,0:T(8,128)(2,1)S(1)}, u32[]{:S(2)}, u32[]{:S(2)}) collective-permute-start(bf16[24,1920]{1,0:T(8,128)(2,1)S(1)} %get-tuple-element.81), channel_id=1, source_target_pairs={{0,8},{8,0},{16,24},{24,16},{1,9},{9,1},{17,25},{25,17},{2,10},{10... | collective-permute-start | bytes 276488 | tf_op jit(solution)/shard_map/ppermute | solution.py:331
  33.7 10.0 %collective-permute-start.11 = (bf16[24,1920]{1,0:T(8,128)(2,1)S(1)}, bf16[24,1920]{1,0:T(8,128)(2,1)S(1)}, u32[]{:S(2)}, u32[]{:S(2)}) collective-permute-start(bf16[24,1920]{1,0:T(8,128)(2,1)S(1)} %get-tuple-element.82), channel_id=1, source_target_pairs={{0,16},{8,24},{16,0},{24,8},{1,17},{9,25},{17,1},{25,9},{2,18},{10... | collective-permute-start | bytes 276488 | tf_op jit(solution)/shard_map/ppermute | solution.py:331
  37.2 6.5 %collective-permute-start.12 = (bf16[24,1920]{1,0:T(8,128)(2,1)S(1)}, bf16[24,1920]{1,0:T(8,128)(2,1)S(1)}, u32[]{:S(2)}, u32[]{:S(2)}) collective-permute-start(bf16[24,1920]{1,0:T(8,128)(2,1)S(1)} %get-tuple-element.83), channel_id=1, source_target_pairs={{0,24},{8,16},{16,8},{24,0},{1,25},{9,17},{17,9},{25,1},{2,26},{10... | collective-permute-start | bytes 276488 | tf_op jit(solution)/shard_map/ppermute | solution.py:331
  43.8 8.3 %collective-permute-start.13 = (bf16[24,1152]{1,0:T(8,128)(2,1)S(1)}, bf16[24,1152]{1,0:T(8,128)(2,1)S(1)}, u32[]{:S(2)}, u32[]{:S(2)}) collective-permute-start(bf16[24,1152]{1,0:T(8,128)(2,1)S(1)} %get-tuple-element.85.refs_0_), channel_id=1, source_target_pairs={{0,8},{8,0},{16,24},{24,16},{1,9},{9,1},{17,25},{25,17},{2,10},{10... | collective-permute-start | bytes 165896 | tf_op jit(solution)/shard_map/ppermute | solution.py:331
  45.4 6.7 %collective-permute-start.14 = (bf16[24,1152]{1,0:T(8,128)(2,1)S(1)}, bf16[24,1152]{1,0:T(8,128)(2,1)S(1)}, u32[]{:S(2)}, u32[]{:S(2)}) collective-permute-start(bf16[24,1152]{1,0:T(8,128)(2,1)S(1)} %get-tuple-element.85.refs_0_), channel_id=1, source_target_pairs={{0,16},{8,24},{16,0},{24,8},{1,17},{9,25},{17,1},{25,9},{2,18},{10... | collective-permute-start | bytes 165896 | tf_op jit(solution)/shard_map/ppermute | solution.py:331
  46.8 6.0 %collective-permute-start.15 = (bf16[24,1152]{1,0:T(8,128)(2,1)S(1)}, bf16[24,1152]{1,0:T(8,128)(2,1)S(1)}, u32[]{:S(2)}, u32[]{:S(2)}) collective-permute-start(bf16[24,1152]{1,0:T(8,128)(2,1)S(1)} %get-tuple-element.85.refs_0_), channel_id=1, source_target_pairs={{0,24},{8,16},{16,8},{24,0},{1,25},{9,17},{17,9},{25,1},{2,26},{10... | collective-permute-start | bytes 165896 | tf_op jit(solution)/shard_map/ppermute | solution.py:331
  59.3 4.3 %collective-permute-start.17 = (bf16[24,1280]{1,0:T(8,128)(2,1)S(1)}, bf16[24,1280]{1,0:T(8,128)(2,1)S(1)}, u32[]{:S(2)}, u32[]{:S(2)}) collective-permute-start(bf16[24,1280]{1,0:T(8,128)(2,1)S(1)} %get-tuple-element.91), channel_id=1, source_target_pairs={{0,2},{1,3},{2,0},{3,1},{4,6},{5,7},{6,4},{7,5},{8,10},{9,11},{10,... | collective-permute-start | bytes 184328 | tf_op jit(solution)/shard_map/ppermute | solution.py:335
  60.8 4.2 %collective-permute-start.18 = (bf16[24,1280]{1,0:T(8,128)(2,1)S(1)}, bf16[24,1280]{1,0:T(8,128)(2,1)S(1)}, u32[]{:S(2)}, u32[]{:S(2)}) collective-permute-start(bf16[24,1280]{1,0:T(8,128)(2,1)S(1)} %get-tuple-element.92), channel_id=1, source_target_pairs={{0,4},{1,5},{2,6},{3,7},{4,0},{5,1},{6,2},{7,3},{8,12},{9,13},{10,... | collective-permute-start | bytes 184328 | tf_op jit(solution)/shard_map/ppermute | solution.py:335
  62.4 5.1 %collective-permute-start.19 = (bf16[24,1280]{1,0:T(8,128)(2,1)S(1)}, bf16[24,1280]{1,0:T(8,128)(2,1)S(1)}, u32[]{:S(2)}, u32[]{:S(2)}) collective-permute-start(bf16[24,1280]{1,0:T(8,128)(2,1)S(1)} %get-tuple-element.93), channel_id=1, source_target_pairs={{0,6},{1,7},{2,4},{3,5},{4,2},{5,3},{6,0},{7,1},{8,14},{9,15},{10,... | collective-permute-start | bytes 184328 | tf_op jit(solution)/shard_map/ppermute | solution.py:335
  69.3 4.3 %collective-permute-start.20 = (bf16[24,1280]{1,0:T(8,128)(2,1)S(1)}, bf16[24,1280]{1,0:T(8,128)(2,1)S(1)}, u32[]{:S(2)}, u32[]{:S(2)}) collective-permute-start(bf16[24,1280]{1,0:T(8,128)(2,1)S(1)} %get-tuple-element.96.refs_0_), channel_id=1, source_target_pairs={{0,2},{1,3},{2,0},{3,1},{4,6},{5,7},{6,4},{7,5},{8,10},{9,11},{10,... | collective-permute-start | bytes 184328 | tf_op jit(solution)/shard_map/ppermute | solution.py:335
  69.9 4.2 %collective-permute-start.21 = (bf16[24,1280]{1,0:T(8,128)(2,1)S(1)}, bf16[24,1280]{1,0:T(8,128)(2,1)S(1)}, u32[]{:S(2)}, u32[]{:S(2)}) collective-permute-start(bf16[24,1280]{1,0:T(8,128)(2,1)S(1)} %get-tuple-element.96.refs_0_), channel_id=1, source_target_pairs={{0,4},{1,5},{2,6},{3,7},{4,0},{5,1},{6,2},{7,3},{8,12},{9,13},{10,... | collective-permute-start | bytes 184328 | tf_op jit(solution)/shard_map/ppermute | solution.py:335
  70.4 5.1 %collective-permute-start.22 = (bf16[24,1280]{1,0:T(8,128)(2,1)S(1)}, bf16[24,1280]{1,0:T(8,128)(2,1)S(1)}, u32[]{:S(2)}, u32[]{:S(2)}) collective-permute-start(bf16[24,1280]{1,0:T(8,128)(2,1)S(1)} %get-tuple-element.96.refs_0_), channel_id=1, source_target_pairs={{0,6},{1,7},{2,4},{3,5},{4,2},{5,3},{6,0},{7,1},{8,14},{9,15},{10,... | collective-permute-start | bytes 184328 | tf_op jit(solution)/shard_map/ppermute | solution.py:335
  83.3 9.5 %collective-permute-start.27 = (bf16[24,1280]{1,0:T(8,128)(2,1)S(1)}, bf16[24,1280]{1,0:T(8,128)(2,1)S(1)}, u32[]{:S(2)}, u32[]{:S(2)}) collective-permute-start(bf16[24,1280]{1,0:T(8,128)(2,1)S(1)} %get-tuple-element.99), channel_id=1, source_target_pairs={{0,8},{8,0},{16,24},{24,16},{1,9},{9,1},{17,25},{25,17},{2,10},{10... | collective-permute-start | bytes 184328 | tf_op jit(solution)/shard_map/ppermute | solution.py:331
  83.4 9.5 %collective-permute-start.28 = (bf16[24,1280]{1,0:T(8,128)(2,1)S(1)}, bf16[24,1280]{1,0:T(8,128)(2,1)S(1)}, u32[]{:S(2)}, u32[]{:S(2)}) collective-permute-start(bf16[24,1280]{1,0:T(8,128)(2,1)S(1)} %get-tuple-element.100), channel_id=1, source_target_pairs={{0,16},{8,24},{16,0},{24,8},{1,17},{9,25},{17,1},{25,9},{2,18},{10... | collective-permute-start | bytes 184328 | tf_op jit(solution)/shard_map/ppermute | solution.py:331
  85.7 7.1 %collective-permute-start.29 = (bf16[24,1280]{1,0:T(8,128)(2,1)S(1)}, bf16[24,1280]{1,0:T(8,128)(2,1)S(1)}, u32[]{:S(2)}, u32[]{:S(2)}) collective-permute-start(bf16[24,1280]{1,0:T(8,128)(2,1)S(1)} %get-tuple-element.101), channel_id=1, source_target_pairs={{0,24},{8,16},{16,8},{24,0},{1,25},{9,17},{17,9},{25,1},{2,26},{10... | collective-permute-start | bytes 184328 | tf_op jit(solution)/shard_map/ppermute | solution.py:331
  93.0 5.1 %collective-permute-start.30 = (bf16[24,1920]{1,0:T(8,128)(2,1)S(1)}, bf16[24,1920]{1,0:T(8,128)(2,1)S(1)}, u32[]{:S(2)}, u32[]{:S(2)}) collective-permute-start(bf16[24,1920]{1,0:T(8,128)(2,1)S(1)} %get-tuple-element.107), channel_id=1, source_target_pairs={{0,8},{8,0},{16,24},{24,16},{1,9},{9,1},{17,25},{25,17},{2,10},{10... | collective-permute-start | bytes 276488 | tf_op jit(solution)/shard_map/ppermute | solution.py:331
  93.2 9.7 %collective-permute-start.31 = (bf16[24,1920]{1,0:T(8,128)(2,1)S(1)}, bf16[24,1920]{1,0:T(8,128)(2,1)S(1)}, u32[]{:S(2)}, u32[]{:S(2)}) collective-permute-start(bf16[24,1920]{1,0:T(8,128)(2,1)S(1)} %get-tuple-element.108), channel_id=1, source_target_pairs={{0,16},{8,24},{16,0},{24,8},{1,17},{9,25},{17,1},{25,9},{2,18},{10... | collective-permute-start | bytes 276488 | tf_op jit(solution)/shard_map/ppermute | solution.py:331
  95.4 7.5 %collective-permute-start.32 = (bf16[24,1920]{1,0:T(8,128)(2,1)S(1)}, bf16[24,1920]{1,0:T(8,128)(2,1)S(1)}, u32[]{:S(2)}, u32[]{:S(2)}) collective-permute-start(bf16[24,1920]{1,0:T(8,128)(2,1)S(1)} %get-tuple-element.109), channel_id=1, source_target_pairs={{0,24},{8,16},{16,8},{24,0},{1,25},{9,17},{17,9},{25,1},{2,26},{10... | collective-permute-start | bytes 276488 | tf_op jit(solution)/shard_map/ppermute | solution.py:331
  103.0 8.3 %collective-permute-start.33 = (bf16[24,1152]{1,0:T(8,128)(2,1)S(1)}, bf16[24,1152]{1,0:T(8,128)(2,1)S(1)}, u32[]{:S(2)}, u32[]{:S(2)}) collective-permute-start(bf16[24,1152]{1,0:T(8,128)(2,1)S(1)} %get-tuple-element.113.refs_0_), channel_id=1, source_target_pairs={{0,8},{8,0},{16,24},{24,16},{1,9},{9,1},{17,25},{25,17},{2,10},{10... | collective-permute-start | bytes 165896 | tf_op jit(solution)/shard_map/ppermute | solution.py:331
  104.6 6.7 %collective-permute-start.34 = (bf16[24,1152]{1,0:T(8,128)(2,1)S(1)}, bf16[24,1152]{1,0:T(8,128)(2,1)S(1)}, u32[]{:S(2)}, u32[]{:S(2)}) collective-permute-start(bf16[24,1152]{1,0:T(8,128)(2,1)S(1)} %get-tuple-element.113.refs_0_), channel_id=1, source_target_pairs={{0,16},{8,24},{16,0},{24,8},{1,17},{9,25},{17,1},{25,9},{2,18},{10... | collective-permute-start | bytes 165896 | tf_op jit(solution)/shard_map/ppermute | solution.py:331
  105.3 6.0 %collective-permute-start.35 = (bf16[24,1152]{1,0:T(8,128)(2,1)S(1)}, bf16[24,1152]{1,0:T(8,128)(2,1)S(1)}, u32[]{:S(2)}, u32[]{:S(2)}) collective-permute-start(bf16[24,1152]{1,0:T(8,128)(2,1)S(1)} %get-tuple-element.113.refs_0_), channel_id=1, source_target_pairs={{0,24},{8,16},{16,8},{24,0},{1,25},{9,17},{17,9},{25,1},{2,26},{10... | collective-permute-start | bytes 165896 | tf_op jit(solution)/shard_map/ppermute | solution.py:331
  117.7 4.3 %collective-permute-start.37 = (bf16[24,1280]{1,0:T(8,128)(2,1)S(1)}, bf16[24,1280]{1,0:T(8,128)(2,1)S(1)}, u32[]{:S(2)}, u32[]{:S(2)}) collective-permute-start(bf16[24,1280]{1,0:T(8,128)(2,1)S(1)} %get-tuple-element.119), channel_id=1, source_target_pairs={{0,2},{1,3},{2,0},{3,1},{4,6},{5,7},{6,4},{7,5},{8,10},{9,11},{10,... | collective-permute-start | bytes 184328 | tf_op jit(solution)/shard_map/ppermute | solution.py:335
  120.8 5.1 %collective-permute-start.39 = (bf16[24,1280]{1,0:T(8,128)(2,1)S(1)}, bf16[24,1280]{1,0:T(8,128)(2,1)S(1)}, u32[]{:S(2)}, u32[]{:S(2)}) collective-permute-start(bf16[24,1280]{1,0:T(8,128)(2,1)S(1)} %get-tuple-element.121), channel_id=1, source_target_pairs={{0,6},{1,7},{2,4},{3,5},{4,2},{5,3},{6,0},{7,1},{8,14},{9,15},{10,... | collective-permute-start | bytes 184328 | tf_op jit(solution)/shard_map/ppermute | solution.py:335
  128.8 4.3 %collective-permute-start.42 = (f32[8,1024]{1,0:T(8,128)S(1)}, f32[8,1024]{1,0:T(8,128)S(1)}, u32[]{:S(2)}, u32[]{:S(2)}) collective-permute-start(f32[8,1024]{1,0:T(8,128)S(1)} %shard_map.215.refs_0_), channel_id=1, source_target_pairs={{0,4},{1,5},{2,6},{3,7},{4,0},{5,1},{6,2},{7,3},{8,12},{9,13},{10,... | collective-permute-start | bytes 98312 | tf_op jit(solution)/shard_map/ppermute | solution.py:335
  129.3 4.8 %collective-permute-start.43 = (f32[8,1024]{1,0:T(8,128)S(1)}, f32[8,1024]{1,0:T(8,128)S(1)}, u32[]{:S(2)}, u32[]{:S(2)}) collective-permute-start(f32[8,1024]{1,0:T(8,128)S(1)} %shard_map.215.refs_0_), channel_id=1, source_target_pairs={{0,6},{1,7},{2,4},{3,5},{4,2},{5,3},{6,0},{7,1},{8,14},{9,15},{10,... | collective-permute-start | bytes 98312 | tf_op jit(solution)/shard_map/ppermute | solution.py:335
  (37 other events, 388.0 us)

commit v6 on v5

--- a/solution.py
+++ b/solution.py
@@ -92,8 +92,10 @@
     return lax.axis_index("scen"), lax.div(line, 2), lax.rem(line, 2)
 
 
-def place(sz, gens, select, block):
-    return unstacked(dot_t(stacked(gens), select[block]), sz.rows)
+def place(sz, gens, select):
+    pile = stacked(gens)
+    blocks = [dot_t(pile[:, block * LANES : (block + 1) * LANES], select[block]) for block in range(sz.gens // LANES)]
+    return [unstacked(product, sz.rows) for product in blocks]
 
 
 def blocks_of(sz):
@@ -108,10 +110,11 @@
     bus = lax.broadcasted_iota(jnp.int32, (sz.width, LANES), 0)
     for block, rows, cols in blocks_of(sz):
         lanes = slice(block * LANES, (block + 1) * LANES)
-        buses = slice(block * sz.width, (block + 1) * sz.width)
         local = gen_bus[:, lanes] - (first + block * sz.width)
         select[block] = (bus == local).astype(F32).astype(BF)
-        inject[rows, cols] = (place(sz, dispatch[:, lanes], select, block) + net[:, buses]).astype(BF)
+    placed = place(sz, dispatch[...], select)
+    for block, rows, cols in blocks_of(sz):
+        inject[rows, cols] = (placed[block] + net[:, block * sz.width : (block + 1) * sz.width]).astype(BF)
 
 
 def forward_kernel(sz, chunk, *refs):
@@ -291,25 +294,30 @@
     else:
         gens_out, shed_out, lam_out, inject = rest
     lam_out[...] = jnp.broadcast_to(lam_now + balance, lam_out.shape)
+    piles = [stacked(grad[fold * sz.rows : (fold + 1) * sz.rows]) for fold in range(sz.fold)]
+    picked = [
+        unstacked(jnp.dot(piles[rows.start // sz.rows][:, cols], select[block], preferred_element_type=F32), sz.rows)
+        for block, rows, cols in blocks_of(sz)
+    ]
+    picked = jnp.concatenate(picked, 1)
+    now = gens[...]
+    gen_grad = costs[:1] + costs[1:] * now + dual[...] + (now - previous[...]) + picked
+    now = jnp.minimum(jnp.maximum(now - 0.4 * gen_grad, 0.0), capacity)
+    gens_out[...] = now
+    if last:
+        dual_out[...] = dual[...] + now
+        weighted_out[:1] = jnp.sum(weights[:, :1] * now, axis=0, keepdims=True)
+        all_weights = jnp.sum(weights[:, :1], axis=0, keepdims=True)
+        weighted_out[1:] = jnp.broadcast_to(all_weights, (7, sz.gens))
+    else:
+        placed = place(sz, now, select)
     for block, rows, cols in blocks_of(sz):
-        lanes = slice(block * LANES, (block + 1) * LANES)
         buses = slice(block * sz.width, (block + 1) * sz.width)
         load = loads[:, buses]
         shed_next = jnp.minimum(jnp.maximum(shed[:, buses] - 0.4 * (1.5 + grad[rows, cols]), 0.0), load)
         shed_out[:, buses] = shed_next
-        picked = jnp.dot(stacked(grad[rows, cols]), select[block], preferred_element_type=F32)
-        picked = unstacked(picked, sz.rows)
-        now = gens[:, lanes]
-        gen_grad = costs[:1, lanes] + costs[1:, lanes] * now + dual[:, lanes] + (now - previous[:, lanes]) + picked
-        now = jnp.minimum(jnp.maximum(now - 0.4 * gen_grad, 0.0), capacity[:, lanes])
-        gens_out[:, lanes] = now
-        if last:
-            dual_out[:, lanes] = dual[:, lanes] + now
-            weighted_out[:1, lanes] = jnp.sum(weights[:, :1] * now, axis=0, keepdims=True)
-            all_weights = jnp.sum(weights[:, :1], axis=0, keepdims=True)
-            weighted_out[1:, lanes] = jnp.broadcast_to(all_weights, (7, LANES))
-        else:
-            inject[rows, cols] = (place(sz, now, select, block) + shed_next - load).astype(BF)
+        if not last:
+            inject[rows, cols] = (placed[block] + shed_next - load).astype(BF)
 
 
 def add_kernel(first, second, out):

time: 135 us -> 134 us (level)
  no operation moved by 1% of the time
where the time goes in v6:
time: 134 us
  starting transfers between devices  46.8 us (35%)
  Pallas kernels  44 us (33%)
  waiting for transfers between devices  37.3 us (28%)
  local copies, waits for them, and re-layouts  2.71 us (2%)
  other arithmetic  1.99 us (1%)
    pallas_call x19, Pallas kernels, call(): pl.pallas_call(kernel, in_specs=[WHOLE] * len(args), out_specs=[WHOLE] *...  44 us
    ppermute x18, starting transfers between devices, to_scen(): return lax.ppermute(value, 'scen', [(i, i ^ away) for i in range(n)])  27.9 us
    ppermute x15, waiting for transfers between devices, to_chip(): return lax.ppermute(value, 'line', [(i, i ^ 2 * away) for i in range(n)])  18.8 us
    ppermute x15, starting transfers between devices, to_chip(): return lax.ppermute(value, 'line', [(i, i ^ 2 * away) for i in range(n)])  18.7 us
    ppermute x18, waiting for transfers between devices, to_scen(): return lax.ppermute(value, 'scen', [(i, i ^ away) for i in range(n)])  12.7 us
    ppermute x11, waiting for transfers between devices, to_core(): return lax.ppermute(value, 'line', [(i, i ^ 1) for i in range(n)])  5.84 us
  transfers between devices with their start and end apart: 44, of which 25 were waited for; matrix products, arithmetic and copies ran while one was open for 1% of the time, Pallas kernels for 13%

profile of v6, /device:TPU:0, one launch (start us, length us, event | category | flops | bytes accessed | tf_op | source)
XLA Modules:
  0.0 134.0 jit_solution(6762667964899959044)
XLA Ops:
  4.2 3.0 %collective-permute-start = (bf16[24,1280]{1,0:T(8,128)(2,1)S(1)}, bf16[24,1280]{1,0:T(8,128)(2,1)S(1)}, u32[]{:S(2)}, u32[]{:S(2)}) collective-permute-start(bf16[24,1280]{1,0:T(8,128)(2,1)S(1)} %get-tuple-element.72.refs_0_), channel_id=1, source_target_pairs={{0,2},{1,3},{2,0},{3,1},{4,6},{5,7},{6,4},{7,5},{8,10},{9,11},{10,... | collective-permute-start | bytes 184328 | tf_op jit(solution)/shard_map/ppermute | solution.py:343
  7.2 1.5 %collective-permute-start.1 = (bf16[24,1280]{1,0:T(8,128)(2,1)S(1)}, bf16[24,1280]{1,0:T(8,128)(2,1)S(1)}, u32[]{:S(2)}, u32[]{:S(2)}) collective-permute-start(bf16[24,1280]{1,0:T(8,128)(2,1)S(1)} %get-tuple-element.72.refs_0_), channel_id=1, source_target_pairs={{0,4},{1,5},{2,6},{3,7},{4,0},{5,1},{6,2},{7,3},{8,12},{9,13},{10,... | collective-permute-start | bytes 184328 | tf_op jit(solution)/shard_map/ppermute | solution.py:343
  9.5 1.9 %collective-permute-done.1.refs_2_ = bf16[24,1280]{1,0:T(8,128)(2,1)S(1)} collective-permute-done((bf16[24,1280]{1,0:T(8,128)(2,1)S(1)}, bf16[24,1280]{1,0:T(8,128)(2,1)S(1)}, u32[]{:S(2)}, u32[]{:S(2)}) %collective-permute-start.1) | collective-permute-done | bytes 61472 | tf_op jit(solution)/shard_map/ppermute | solution.py:343
  11.4 2.4 %collective-permute-done.2.refs_3_ = bf16[24,1280]{1,0:T(8,128)(2,1)S(1)} collective-permute-done((bf16[24,1280]{1,0:T(8,128)(2,1)S(1)}, bf16[24,1280]{1,0:T(8,128)(2,1)S(1)}, u32[]{:S(2)}, u32[]{:S(2)}) %collective-permute-start.2) | collective-permute-done | bytes 61472 | tf_op jit(solution)/shard_map/ppermute | solution.py:343
  15.3 6.5 %shard_map.200 = (f32[24,1280]{1,0:T(8,128)S(1)}, bf16[24,1280]{1,0:T(8,128)(2,1)S(1)}, bf16[24,1280]{1,0:T(8,128)(2,1)S(1)}, bf16[24,1280]{1,0:T(8,128)(2,1)S(1)}) custom-call(bf16[24,1280]{1,0:T(8,128)(2,1)S(1)} %get-tuple-element.72.refs_0_, bf16[24,1280]{1,0:T(8,128)(2,1)S(1)} %collective-permute-done.refs_1_, ...), custom_call_target="tpu_custom_call" | custom-call | flops 1132462080 | bytes 42434560 | tf_op jit(solution)/shard_map/pallas_call | solution.py:28
  21.8 3.1 %collective-permute-start.7 = (bf16[24,1280]{1,0:T(8,128)(2,1)S(1)}, bf16[24,1280]{1,0:T(8,128)(2,1)S(1)}, u32[]{:S(2)}, u32[]{:S(2)}) collective-permute-start(bf16[24,1280]{1,0:T(8,128)(2,1)S(1)} %get-tuple-element.75), channel_id=1, source_target_pairs={{0,8},{8,0},{16,24},{24,16},{1,9},{9,1},{17,25},{25,17},{2,10},{10... | collective-permute-start | bytes 184328 | tf_op jit(solution)/shard_map/ppermute | solution.py:339
  24.9 2.6 %collective-permute-start.8 = (bf16[24,1280]{1,0:T(8,128)(2,1)S(1)}, bf16[24,1280]{1,0:T(8,128)(2,1)S(1)}, u32[]{:S(2)}, u32[]{:S(2)}) collective-permute-start(bf16[24,1280]{1,0:T(8,128)(2,1)S(1)} %get-tuple-element.76), channel_id=1, source_target_pairs={{0,16},{8,24},{16,0},{24,8},{1,17},{9,25},{17,1},{25,9},{2,18},{10... | collective-permute-start | bytes 184328 | tf_op jit(solution)/shard_map/ppermute | solution.py:339
  27.5 5.1 %shard_map.199 = (f32[24,896]{1,0:T(8,128)S(1)}, bf16[24,896]{1,0:T(8,128)(2,1)S(1)}, bf16[24,896]{1,0:T(8,128)(2,1)S(1)}, bf16[24,896]{1,0:T(8,128)(2,1)S(1)}) custom-call(bf16[24,1280]{1,0:T(8,128)(2,1)S(1)} %get-tuple-element.72.refs_0_, bf16[24,1280]{1,0:T(8,128)(2,1)S(1)} %collective-permute-done.refs_1_, ...), custom_call_target="tpu_custom_call" | custom-call | flops 880803840 | bytes 42434560 | tf_op jit(solution)/shard_map/pallas_call | solution.py:28
  33.7 3.5 %collective-permute-start.11 = (bf16[24,1920]{1,0:T(8,128)(2,1)S(1)}, bf16[24,1920]{1,0:T(8,128)(2,1)S(1)}, u32[]{:S(2)}, u32[]{:S(2)}) collective-permute-start(bf16[24,1920]{1,0:T(8,128)(2,1)S(1)} %get-tuple-element.82), channel_id=1, source_target_pairs={{0,16},{8,24},{16,0},{24,8},{1,17},{9,25},{17,1},{25,9},{2,18},{10... | collective-permute-start | bytes 276488 | tf_op jit(solution)/shard_map/ppermute | solution.py:339
  38.7 5.0 %collective-permute-done.11.refs_2_ = bf16[24,1920]{1,0:T(8,128)(2,1)S(1)} collective-permute-done((bf16[24,1920]{1,0:T(8,128)(2,1)S(1)}, bf16[24,1920]{1,0:T(8,128)(2,1)S(1)}, u32[]{:S(2)}, u32[]{:S(2)}) %collective-permute-start.11) | collective-permute-done | bytes 92192 | tf_op jit(solution)/shard_map/ppermute | solution.py:339
  43.8 1.6 %collective-permute-start.13 = (bf16[24,1152]{1,0:T(8,128)(2,1)S(1)}, bf16[24,1152]{1,0:T(8,128)(2,1)S(1)}, u32[]{:S(2)}, u32[]{:S(2)}) collective-permute-start(bf16[24,1152]{1,0:T(8,128)(2,1)S(1)} %get-tuple-element.85.refs_0_), channel_id=1, source_target_pairs={{0,8},{8,0},{16,24},{24,16},{1,9},{9,1},{17,25},{25,17},{2,10},{10... | collective-permute-start | bytes 165896 | tf_op jit(solution)/shard_map/ppermute | solution.py:339
  48.2 3.9 %shard_map.203 = (f32[48,5120]{1,0:T(8,128)S(1)}, f32[12,128]{1,0:T(8,128)S(1)}) custom-call(bf16[24,1024]{1,0:T(8,128)(2,1)S(1)} %get-tuple-element.86.refs_0_, bf16[24,1920]{1,0:T(8,128)(2,1)S(1)} %collective-permute-done.10.refs_1_, bf16[24,1920]{1,0:T(8,128)(2,1)S(1)} %collective-permute-done.11.refs_2_, ...), custom_call_target="tpu_custom_call" | custom-call | flops 1006632960 | bytes 42268672 | tf_op jit(solution)/shard_map/pallas_call | solution.py:28
  52.9 4.7 %shard_map.204 = (f32[24,5120]{1,0:T(8,128)S(1)}, bf16[24,5120]{1,0:T(8,128)(2,1)S(1)}) custom-call(bf16[24,1152]{1,0:T(8,128)(2,1)S(1)} %get-tuple-element.85.refs_0_, bf16[24,1152]{1,0:T(8,128)(2,1)S(1)} %collective-permute-done.13.refs_1_, bf16[24,1152]{1,0:T(8,128)(2,1)S(1)} %collective-permute-done.14.refs_2_, ...), custom_call_target="tpu_custom_call" | custom-call | flops 1006632960 | bytes 43147264 | tf_op jit(solution)/shard_map/pallas_call | solution.py:28
  59.3 1.6 %collective-permute-start.17 = (bf16[24,1280]{1,0:T(8,128)(2,1)S(1)}, bf16[24,1280]{1,0:T(8,128)(2,1)S(1)}, u32[]{:S(2)}, u32[]{:S(2)}) collective-permute-start(bf16[24,1280]{1,0:T(8,128)(2,1)S(1)} %get-tuple-element.91), channel_id=1, source_target_pairs={{0,2},{1,3},{2,0},{3,1},{4,6},{5,7},{6,4},{7,5},{8,10},{9,11},{10,... | collective-permute-start | bytes 184328 | tf_op jit(solution)/shard_map/ppermute | solution.py:343
  60.8 1.5 %collective-permute-start.18 = (bf16[24,1280]{1,0:T(8,128)(2,1)S(1)}, bf16[24,1280]{1,0:T(8,128)(2,1)S(1)}, u32[]{:S(2)}, u32[]{:S(2)}) collective-permute-start(bf16[24,1280]{1,0:T(8,128)(2,1)S(1)} %get-tuple-element.92), channel_id=1, source_target_pairs={{0,4},{1,5},{2,6},{3,7},{4,0},{5,1},{6,2},{7,3},{8,12},{9,13},{10,... | collective-permute-start | bytes 184328 | tf_op jit(solution)/shard_map/ppermute | solution.py:343
  65.1 2.4 %collective-permute-done.19.refs_3_ = bf16[24,1280]{1,0:T(8,128)(2,1)S(1)} collective-permute-done((bf16[24,1280]{1,0:T(8,128)(2,1)S(1)}, bf16[24,1280]{1,0:T(8,128)(2,1)S(1)}, u32[]{:S(2)}, u32[]{:S(2)}) %collective-permute-start.19) | collective-permute-done | bytes 61472 | tf_op jit(solution)/shard_map/ppermute | solution.py:343
  69.6 2.5 %collective-permute-start.22 = (bf16[24,1280]{1,0:T(8,128)(2,1)S(1)}, bf16[24,1280]{1,0:T(8,128)(2,1)S(1)}, u32[]{:S(2)}, u32[]{:S(2)}) collective-permute-start(bf16[24,1280]{1,0:T(8,128)(2,1)S(1)} %get-tuple-element.96.refs_0_), channel_id=1, source_target_pairs={{0,6},{1,7},{2,4},{3,5},{4,2},{5,3},{6,0},{7,1},{8,14},{9,15},{10,... | collective-permute-start | bytes 184328 | tf_op jit(solution)/shard_map/ppermute | solution.py:343
  75.9 6.5 %shard_map.208 = (f32[24,1280]{1,0:T(8,128)S(1)}, bf16[24,1280]{1,0:T(8,128)(2,1)S(1)}, bf16[24,1280]{1,0:T(8,128)(2,1)S(1)}, bf16[24,1280]{1,0:T(8,128)(2,1)S(1)}) custom-call(bf16[24,1280]{1,0:T(8,128)(2,1)S(1)} %get-tuple-element.96.refs_0_, bf16[24,1280]{1,0:T(8,128)(2,1)S(1)} %collective-permute-done.20.refs_1_, ...), custom_call_target="tpu_custom_call" | custom-call | flops 1132462080 | bytes 42434560 | tf_op jit(solution)/shard_map/pallas_call | solution.py:28
  82.5 2.4 %collective-permute-start.28 = (bf16[24,1280]{1,0:T(8,128)(2,1)S(1)}, bf16[24,1280]{1,0:T(8,128)(2,1)S(1)}, u32[]{:S(2)}, u32[]{:S(2)}) collective-permute-start(bf16[24,1280]{1,0:T(8,128)(2,1)S(1)} %get-tuple-element.100), channel_id=1, source_target_pairs={{0,16},{8,24},{16,0},{24,8},{1,17},{9,25},{17,1},{25,9},{2,18},{10... | collective-permute-start | bytes 184328 | tf_op jit(solution)/shard_map/ppermute | solution.py:339
  84.9 2.0 %collective-permute-start.29 = (bf16[24,1280]{1,0:T(8,128)(2,1)S(1)}, bf16[24,1280]{1,0:T(8,128)(2,1)S(1)}, u32[]{:S(2)}, u32[]{:S(2)}) collective-permute-start(bf16[24,1280]{1,0:T(8,128)(2,1)S(1)} %get-tuple-element.101), channel_id=1, source_target_pairs={{0,24},{8,16},{16,8},{24,0},{1,25},{9,17},{17,9},{25,1},{2,26},{10... | collective-permute-start | bytes 184328 | tf_op jit(solution)/shard_map/ppermute | solution.py:339
  86.9 5.1 %shard_map.207 = (f32[24,896]{1,0:T(8,128)S(1)}, bf16[24,896]{1,0:T(8,128)(2,1)S(1)}, bf16[24,896]{1,0:T(8,128)(2,1)S(1)}, bf16[24,896]{1,0:T(8,128)(2,1)S(1)}) custom-call(bf16[24,1280]{1,0:T(8,128)(2,1)S(1)} %get-tuple-element.96.refs_0_, bf16[24,1280]{1,0:T(8,128)(2,1)S(1)} %collective-permute-done.20.refs_1_, ...), custom_call_target="tpu_custom_call" | custom-call | flops 880803840 | bytes 42434560 | tf_op jit(solution)/shard_map/pallas_call | solution.py:28
  92.4 2.2 %collective-permute-start.31 = (bf16[24,1920]{1,0:T(8,128)(2,1)S(1)}, bf16[24,1920]{1,0:T(8,128)(2,1)S(1)}, u32[]{:S(2)}, u32[]{:S(2)}) collective-permute-start(bf16[24,1920]{1,0:T(8,128)(2,1)S(1)} %get-tuple-element.108), channel_id=1, source_target_pairs={{0,16},{8,24},{16,0},{24,8},{1,17},{9,25},{17,1},{25,9},{2,18},{10... | collective-permute-start | bytes 276488 | tf_op jit(solution)/shard_map/ppermute | solution.py:339
  94.6 2.0 %collective-permute-start.32 = (bf16[24,1920]{1,0:T(8,128)(2,1)S(1)}, bf16[24,1920]{1,0:T(8,128)(2,1)S(1)}, u32[]{:S(2)}, u32[]{:S(2)}) collective-permute-start(bf16[24,1920]{1,0:T(8,128)(2,1)S(1)} %get-tuple-element.109), channel_id=1, source_target_pairs={{0,24},{8,16},{16,8},{24,0},{1,25},{9,17},{17,9},{25,1},{2,26},{10... | collective-permute-start | bytes 276488 | tf_op jit(solution)/shard_map/ppermute | solution.py:339
  97.2 4.9 %collective-permute-done.31.refs_2_ = bf16[24,1920]{1,0:T(8,128)(2,1)S(1)} collective-permute-done((bf16[24,1920]{1,0:T(8,128)(2,1)S(1)}, bf16[24,1920]{1,0:T(8,128)(2,1)S(1)}, u32[]{:S(2)}, u32[]{:S(2)}) %collective-permute-start.31) | collective-permute-done | bytes 92192 | tf_op jit(solution)/shard_map/ppermute | solution.py:339
  102.2 1.6 %collective-permute-start.33 = (bf16[24,1152]{1,0:T(8,128)(2,1)S(1)}, bf16[24,1152]{1,0:T(8,128)(2,1)S(1)}, u32[]{:S(2)}, u32[]{:S(2)}) collective-permute-start(bf16[24,1152]{1,0:T(8,128)(2,1)S(1)} %get-tuple-element.113.refs_0_), channel_id=1, source_target_pairs={{0,8},{8,0},{16,24},{24,16},{1,9},{9,1},{17,25},{25,17},{2,10},{10... | collective-permute-start | bytes 165896 | tf_op jit(solution)/shard_map/ppermute | solution.py:339
  104.5 2.1 %collective-permute-start.35 = (bf16[24,1152]{1,0:T(8,128)(2,1)S(1)}, bf16[24,1152]{1,0:T(8,128)(2,1)S(1)}, u32[]{:S(2)}, u32[]{:S(2)}) collective-permute-start(bf16[24,1152]{1,0:T(8,128)(2,1)S(1)} %get-tuple-element.113.refs_0_), channel_id=1, source_target_pairs={{0,24},{8,16},{16,8},{24,0},{1,25},{9,17},{17,9},{25,1},{2,26},{10... | collective-permute-start | bytes 165896 | tf_op jit(solution)/shard_map/ppermute | solution.py:339
  106.6 3.9 %shard_map.211 = (f32[48,5120]{1,0:T(8,128)S(1)}, f32[12,128]{1,0:T(8,128)S(1)}) custom-call(bf16[24,1024]{1,0:T(8,128)(2,1)S(1)} %get-tuple-element.114.refs_0_, bf16[24,1920]{1,0:T(8,128)(2,1)S(1)} %collective-permute-done.30.refs_1_, bf16[24,1920]{1,0:T(8,128)(2,1)S(1)} %collective-permute-done.31.refs_2_, ...), custom_call_target="tpu_custom_call" | custom-call | flops 1006632960 | bytes 42268672 | tf_op jit(solution)/shard_map/pallas_call | solution.py:28
  110.5 4.7 %shard_map.212 = (f32[24,5120]{1,0:T(8,128)S(1)}, bf16[24,5120]{1,0:T(8,128)(2,1)S(1)}) custom-call(bf16[24,1152]{1,0:T(8,128)(2,1)S(1)} %get-tuple-element.113.refs_0_, bf16[24,1152]{1,0:T(8,128)(2,1)S(1)} %collective-permute-done.33.refs_1_, bf16[24,1152]{1,0:T(8,128)(2,1)S(1)} %collective-permute-done.34.refs_2_, ...), custom_call_target="tpu_custom_call" | custom-call | flops 1006632960 | bytes 43147264 | tf_op jit(solution)/shard_map/pallas_call | solution.py:28
  116.9 1.6 %collective-permute-start.37 = (bf16[24,1280]{1,0:T(8,128)(2,1)S(1)}, bf16[24,1280]{1,0:T(8,128)(2,1)S(1)}, u32[]{:S(2)}, u32[]{:S(2)}) collective-permute-start(bf16[24,1280]{1,0:T(8,128)(2,1)S(1)} %get-tuple-element.119), channel_id=1, source_target_pairs={{0,2},{1,3},{2,0},{3,1},{4,6},{5,7},{6,4},{7,5},{8,10},{9,11},{10,... | collective-permute-start | bytes 184328 | tf_op jit(solution)/shard_map/ppermute | solution.py:343
  118.5 1.5 %collective-permute-start.38 = (bf16[24,1280]{1,0:T(8,128)(2,1)S(1)}, bf16[24,1280]{1,0:T(8,128)(2,1)S(1)}, u32[]{:S(2)}, u32[]{:S(2)}) collective-permute-start(bf16[24,1280]{1,0:T(8,128)(2,1)S(1)} %get-tuple-element.120), channel_id=1, source_target_pairs={{0,4},{1,5},{2,6},{3,7},{4,0},{5,1},{6,2},{7,3},{8,12},{9,13},{10,... | collective-permute-start | bytes 184328 | tf_op jit(solution)/shard_map/ppermute | solution.py:343
  122.7 2.4 %collective-permute-done.39.refs_3_ = bf16[24,1280]{1,0:T(8,128)(2,1)S(1)} collective-permute-done((bf16[24,1280]{1,0:T(8,128)(2,1)S(1)}, bf16[24,1280]{1,0:T(8,128)(2,1)S(1)}, u32[]{:S(2)}, u32[]{:S(2)}) %collective-permute-start.39) | collective-permute-done | bytes 61472 | tf_op jit(solution)/shard_map/ppermute | solution.py:343
  128.5 2.4 %collective-permute-start.43 = (f32[8,1024]{1,0:T(8,128)S(1)}, f32[8,1024]{1,0:T(8,128)S(1)}, u32[]{:S(2)}, u32[]{:S(2)}) collective-permute-start(f32[8,1024]{1,0:T(8,128)S(1)} %shard_map.215.refs_0_), channel_id=1, source_target_pairs={{0,6},{1,7},{2,4},{3,5},{4,2},{5,3},{6,0},{7,1},{8,14},{9,15},{10,... | collective-permute-start | bytes 98312 | tf_op jit(solution)/shard_map/ppermute | solution.py:343
  (131 shorter events, 34.9 us)
Async XLA Ops:
  4.2 5.3 %collective-permute-start = (bf16[24,1280]{1,0:T(8,128)(2,1)S(1)}, bf16[24,1280]{1,0:T(8,128)(2,1)S(1)}, u32[]{:S(2)}, u32[]{:S(2)}) collective-permute-start(bf16[24,1280]{1,0:T(8,128)(2,1)S(1)} %get-tuple-element.72.refs_0_), channel_id=1, source_target_pairs={{0,2},{1,3},{2,0},{3,1},{4,6},{5,7},{6,4},{7,5},{8,10},{9,11},{10,... | collective-permute-start | bytes 184328 | tf_op jit(solution)/shard_map/ppermute | solution.py:343
  7.2 4.2 %collective-permute-start.1 = (bf16[24,1280]{1,0:T(8,128)(2,1)S(1)}, bf16[24,1280]{1,0:T(8,128)(2,1)S(1)}, u32[]{:S(2)}, u32[]{:S(2)}) collective-permute-start(bf16[24,1280]{1,0:T(8,128)(2,1)S(1)} %get-tuple-element.72.refs_0_), channel_id=1, source_target_pairs={{0,4},{1,5},{2,6},{3,7},{4,0},{5,1},{6,2},{7,3},{8,12},{9,13},{10,... | collective-permute-start | bytes 184328 | tf_op jit(solution)/shard_map/ppermute | solution.py:343
  8.7 5.1 %collective-permute-start.2 = (bf16[24,1280]{1,0:T(8,128)(2,1)S(1)}, bf16[24,1280]{1,0:T(8,128)(2,1)S(1)}, u32[]{:S(2)}, u32[]{:S(2)}) collective-permute-start(bf16[24,1280]{1,0:T(8,128)(2,1)S(1)} %get-tuple-element.72.refs_0_), channel_id=1, source_target_pairs={{0,6},{1,7},{2,4},{3,5},{4,2},{5,3},{6,0},{7,1},{8,14},{9,15},{10,... | collective-permute-start | bytes 184328 | tf_op jit(solution)/shard_map/ppermute | solution.py:343
  8.8 5.1 %collective-permute-start.3 = (bf16[24,1280]{1,0:T(8,128)(2,1)S(1)}, bf16[24,1280]{1,0:T(8,128)(2,1)S(1)}, u32[]{:S(2)}, u32[]{:S(2)}) collective-permute-start(bf16[24,1280]{1,0:T(8,128)(2,1)S(1)} %get-tuple-element.72.refs_0_), channel_id=1, source_target_pairs={{0,1},{1,0},{2,3},{3,2},{4,5},{5,4},{6,7},{7,6},{8,9},{9,8},{10,11... | collective-permute-start | bytes 184328 | tf_op jit(solution)/shard_map/ppermute | solution.py:352
  9.5 4.4 %collective-permute-start.4 = (bf16[24,1280]{1,0:T(8,128)(2,1)S(1)}, bf16[24,1280]{1,0:T(8,128)(2,1)S(1)}, u32[]{:S(2)}, u32[]{:S(2)}) collective-permute-start(bf16[24,1280]{1,0:T(8,128)(2,1)S(1)} %collective-permute-done.refs_1_), channel_id=1, source_target_pairs={{0,1},{1,0},{2,3},{3,2},{4,5},{5,4},{6,7},{7,6},{8,9},{9,8},{10,11... | collective-permute-start | bytes 184328 | tf_op jit(solution)/shard_map/ppermute | solution.py:352
  21.8 10.8 %collective-permute-start.7 = (bf16[24,1280]{1,0:T(8,128)(2,1)S(1)}, bf16[24,1280]{1,0:T(8,128)(2,1)S(1)}, u32[]{:S(2)}, u32[]{:S(2)}) collective-permute-start(bf16[24,1280]{1,0:T(8,128)(2,1)S(1)} %get-tuple-element.75), channel_id=1, source_target_pairs={{0,8},{8,0},{16,24},{24,16},{1,9},{9,1},{17,25},{25,17},{2,10},{10... | collective-permute-start | bytes 184328 | tf_op jit(solution)/shard_map/ppermute | solution.py:339
  24.9 7.7 %collective-permute-start.8 = (bf16[24,1280]{1,0:T(8,128)(2,1)S(1)}, bf16[24,1280]{1,0:T(8,128)(2,1)S(1)}, u32[]{:S(2)}, u32[]{:S(2)}) collective-permute-start(bf16[24,1280]{1,0:T(8,128)(2,1)S(1)} %get-tuple-element.76), channel_id=1, source_target_pairs={{0,16},{8,24},{16,0},{24,8},{1,17},{9,25},{17,1},{25,9},{2,18},{10... | collective-permute-start | bytes 184328 | tf_op jit(solution)/shard_map/ppermute | solution.py:339
  27.5 6.0 %collective-permute-start.9 = (bf16[24,1280]{1,0:T(8,128)(2,1)S(1)}, bf16[24,1280]{1,0:T(8,128)(2,1)S(1)}, u32[]{:S(2)}, u32[]{:S(2)}) collective-permute-start(bf16[24,1280]{1,0:T(8,128)(2,1)S(1)} %get-tuple-element.77), channel_id=1, source_target_pairs={{0,24},{8,16},{16,8},{24,0},{1,25},{9,17},{17,9},{25,1},{2,26},{10... | collective-permute-start | bytes 184328 | tf_op jit(solution)/shard_map/ppermute | solution.py:339
  33.6 5.0 %collective-permute-start.10 = (bf16[24,1920]{1,0:T(8,128)(2,1)S(1)}, bf16[24,1920]{1,0:T(8,128)(2,1)S(1)}, u32[]{:S(2)}, u32[]{:S(2)}) collective-permute-start(bf16[24,1920]{1,0:T(8,128)(2,1)S(1)} %get-tuple-element.81), channel_id=1, source_target_pairs={{0,8},{8,0},{16,24},{24,16},{1,9},{9,1},{17,25},{25,17},{2,10},{10... | collective-permute-start | bytes 276488 | tf_op jit(solution)/shard_map/ppermute | solution.py:339
  33.7 10.0 %collective-permute-start.11 = (bf16[24,1920]{1,0:T(8,128)(2,1)S(1)}, bf16[24,1920]{1,0:T(8,128)(2,1)S(1)}, u32[]{:S(2)}, u32[]{:S(2)}) collective-permute-start(bf16[24,1920]{1,0:T(8,128)(2,1)S(1)} %get-tuple-element.82), channel_id=1, source_target_pairs={{0,16},{8,24},{16,0},{24,8},{1,17},{9,25},{17,1},{25,9},{2,18},{10... | collective-permute-start | bytes 276488 | tf_op jit(solution)/shard_map/ppermute | solution.py:339
  37.2 6.5 %collective-permute-start.12 = (bf16[24,1920]{1,0:T(8,128)(2,1)S(1)}, bf16[24,1920]{1,0:T(8,128)(2,1)S(1)}, u32[]{:S(2)}, u32[]{:S(2)}) collective-permute-start(bf16[24,1920]{1,0:T(8,128)(2,1)S(1)} %get-tuple-element.83), channel_id=1, source_target_pairs={{0,24},{8,16},{16,8},{24,0},{1,25},{9,17},{17,9},{25,1},{2,26},{10... | collective-permute-start | bytes 276488 | tf_op jit(solution)/shard_map/ppermute | solution.py:339
  43.8 8.3 %collective-permute-start.13 = (bf16[24,1152]{1,0:T(8,128)(2,1)S(1)}, bf16[24,1152]{1,0:T(8,128)(2,1)S(1)}, u32[]{:S(2)}, u32[]{:S(2)}) collective-permute-start(bf16[24,1152]{1,0:T(8,128)(2,1)S(1)} %get-tuple-element.85.refs_0_), channel_id=1, source_target_pairs={{0,8},{8,0},{16,24},{24,16},{1,9},{9,1},{17,25},{25,17},{2,10},{10... | collective-permute-start | bytes 165896 | tf_op jit(solution)/shard_map/ppermute | solution.py:339
  45.4 6.7 %collective-permute-start.14 = (bf16[24,1152]{1,0:T(8,128)(2,1)S(1)}, bf16[24,1152]{1,0:T(8,128)(2,1)S(1)}, u32[]{:S(2)}, u32[]{:S(2)}) collective-permute-start(bf16[24,1152]{1,0:T(8,128)(2,1)S(1)} %get-tuple-element.85.refs_0_), channel_id=1, source_target_pairs={{0,16},{8,24},{16,0},{24,8},{1,17},{9,25},{17,1},{25,9},{2,18},{10... | collective-permute-start | bytes 165896 | tf_op jit(solution)/shard_map/ppermute | solution.py:339
  46.8 6.0 %collective-permute-start.15 = (bf16[24,1152]{1,0:T(8,128)(2,1)S(1)}, bf16[24,1152]{1,0:T(8,128)(2,1)S(1)}, u32[]{:S(2)}, u32[]{:S(2)}) collective-permute-start(bf16[24,1152]{1,0:T(8,128)(2,1)S(1)} %get-tuple-element.85.refs_0_), channel_id=1, source_target_pairs={{0,24},{8,16},{16,8},{24,0},{1,25},{9,17},{17,9},{25,1},{2,26},{10... | collective-permute-start | bytes 165896 | tf_op jit(solution)/shard_map/ppermute | solution.py:339
  59.3 4.3 %collective-permute-start.17 = (bf16[24,1280]{1,0:T(8,128)(2,1)S(1)}, bf16[24,1280]{1,0:T(8,128)(2,1)S(1)}, u32[]{:S(2)}, u32[]{:S(2)}) collective-permute-start(bf16[24,1280]{1,0:T(8,128)(2,1)S(1)} %get-tuple-element.91), channel_id=1, source_target_pairs={{0,2},{1,3},{2,0},{3,1},{4,6},{5,7},{6,4},{7,5},{8,10},{9,11},{10,... | collective-permute-start | bytes 184328 | tf_op jit(solution)/shard_map/ppermute | solution.py:343
  60.8 4.2 %collective-permute-start.18 = (bf16[24,1280]{1,0:T(8,128)(2,1)S(1)}, bf16[24,1280]{1,0:T(8,128)(2,1)S(1)}, u32[]{:S(2)}, u32[]{:S(2)}) collective-permute-start(bf16[24,1280]{1,0:T(8,128)(2,1)S(1)} %get-tuple-element.92), channel_id=1, source_target_pairs={{0,4},{1,5},{2,6},{3,7},{4,0},{5,1},{6,2},{7,3},{8,12},{9,13},{10,... | collective-permute-start | bytes 184328 | tf_op jit(solution)/shard_map/ppermute | solution.py:343
  62.4 5.1 %collective-permute-start.19 = (bf16[24,1280]{1,0:T(8,128)(2,1)S(1)}, bf16[24,1280]{1,0:T(8,128)(2,1)S(1)}, u32[]{:S(2)}, u32[]{:S(2)}) collective-permute-start(bf16[24,1280]{1,0:T(8,128)(2,1)S(1)} %get-tuple-element.93), channel_id=1, source_target_pairs={{0,6},{1,7},{2,4},{3,5},{4,2},{5,3},{6,0},{7,1},{8,14},{9,15},{10,... | collective-permute-start | bytes 184328 | tf_op jit(solution)/shard_map/ppermute | solution.py:343
  68.5 4.3 %collective-permute-start.20 = (bf16[24,1280]{1,0:T(8,128)(2,1)S(1)}, bf16[24,1280]{1,0:T(8,128)(2,1)S(1)}, u32[]{:S(2)}, u32[]{:S(2)}) collective-permute-start(bf16[24,1280]{1,0:T(8,128)(2,1)S(1)} %get-tuple-element.96.refs_0_), channel_id=1, source_target_pairs={{0,2},{1,3},{2,0},{3,1},{4,6},{5,7},{6,4},{7,5},{8,10},{9,11},{10,... | collective-permute-start | bytes 184328 | tf_op jit(solution)/shard_map/ppermute | solution.py:343
  69.6 5.1 %collective-permute-start.22 = (bf16[24,1280]{1,0:T(8,128)(2,1)S(1)}, bf16[24,1280]{1,0:T(8,128)(2,1)S(1)}, u32[]{:S(2)}, u32[]{:S(2)}) collective-permute-start(bf16[24,1280]{1,0:T(8,128)(2,1)S(1)} %get-tuple-element.96.refs_0_), channel_id=1, source_target_pairs={{0,6},{1,7},{2,4},{3,5},{4,2},{5,3},{6,0},{7,1},{8,14},{9,15},{10,... | collective-permute-start | bytes 184328 | tf_op jit(solution)/shard_map/ppermute | solution.py:343
  82.4 9.5 %collective-permute-start.27 = (bf16[24,1280]{1,0:T(8,128)(2,1)S(1)}, bf16[24,1280]{1,0:T(8,128)(2,1)S(1)}, u32[]{:S(2)}, u32[]{:S(2)}) collective-permute-start(bf16[24,1280]{1,0:T(8,128)(2,1)S(1)} %get-tuple-element.99), channel_id=1, source_target_pairs={{0,8},{8,0},{16,24},{24,16},{1,9},{9,1},{17,25},{25,17},{2,10},{10... | collective-permute-start | bytes 184328 | tf_op jit(solution)/shard_map/ppermute | solution.py:339
  82.5 9.5 %collective-permute-start.28 = (bf16[24,1280]{1,0:T(8,128)(2,1)S(1)}, bf16[24,1280]{1,0:T(8,128)(2,1)S(1)}, u32[]{:S(2)}, u32[]{:S(2)}) collective-permute-start(bf16[24,1280]{1,0:T(8,128)(2,1)S(1)} %get-tuple-element.100), channel_id=1, source_target_pairs={{0,16},{8,24},{16,0},{24,8},{1,17},{9,25},{17,1},{25,9},{2,18},{10... | collective-permute-start | bytes 184328 | tf_op jit(solution)/shard_map/ppermute | solution.py:339
  84.9 7.1 %collective-permute-start.29 = (bf16[24,1280]{1,0:T(8,128)(2,1)S(1)}, bf16[24,1280]{1,0:T(8,128)(2,1)S(1)}, u32[]{:S(2)}, u32[]{:S(2)}) collective-permute-start(bf16[24,1280]{1,0:T(8,128)(2,1)S(1)} %get-tuple-element.101), channel_id=1, source_target_pairs={{0,24},{8,16},{16,8},{24,0},{1,25},{9,17},{17,9},{25,1},{2,26},{10... | collective-permute-start | bytes 184328 | tf_op jit(solution)/shard_map/ppermute | solution.py:339
  92.1 5.1 %collective-permute-start.30 = (bf16[24,1920]{1,0:T(8,128)(2,1)S(1)}, bf16[24,1920]{1,0:T(8,128)(2,1)S(1)}, u32[]{:S(2)}, u32[]{:S(2)}) collective-permute-start(bf16[24,1920]{1,0:T(8,128)(2,1)S(1)} %get-tuple-element.107), channel_id=1, source_target_pairs={{0,8},{8,0},{16,24},{24,16},{1,9},{9,1},{17,25},{25,17},{2,10},{10... | collective-permute-start | bytes 276488 | tf_op jit(solution)/shard_map/ppermute | solution.py:339
  92.4 9.7 %collective-permute-start.31 = (bf16[24,1920]{1,0:T(8,128)(2,1)S(1)}, bf16[24,1920]{1,0:T(8,128)(2,1)S(1)}, u32[]{:S(2)}, u32[]{:S(2)}) collective-permute-start(bf16[24,1920]{1,0:T(8,128)(2,1)S(1)} %get-tuple-element.108), channel_id=1, source_target_pairs={{0,16},{8,24},{16,0},{24,8},{1,17},{9,25},{17,1},{25,9},{2,18},{10... | collective-permute-start | bytes 276488 | tf_op jit(solution)/shard_map/ppermute | solution.py:339
  94.6 7.5 %collective-permute-start.32 = (bf16[24,1920]{1,0:T(8,128)(2,1)S(1)}, bf16[24,1920]{1,0:T(8,128)(2,1)S(1)}, u32[]{:S(2)}, u32[]{:S(2)}) collective-permute-start(bf16[24,1920]{1,0:T(8,128)(2,1)S(1)} %get-tuple-element.109), channel_id=1, source_target_pairs={{0,24},{8,16},{16,8},{24,0},{1,25},{9,17},{17,9},{25,1},{2,26},{10... | collective-permute-start | bytes 276488 | tf_op jit(solution)/shard_map/ppermute | solution.py:339
  102.2 8.3 %collective-permute-start.33 = (bf16[24,1152]{1,0:T(8,128)(2,1)S(1)}, bf16[24,1152]{1,0:T(8,128)(2,1)S(1)}, u32[]{:S(2)}, u32[]{:S(2)}) collective-permute-start(bf16[24,1152]{1,0:T(8,128)(2,1)S(1)} %get-tuple-element.113.refs_0_), channel_id=1, source_target_pairs={{0,8},{8,0},{16,24},{24,16},{1,9},{9,1},{17,25},{25,17},{2,10},{10... | collective-permute-start | bytes 165896 | tf_op jit(solution)/shard_map/ppermute | solution.py:339
  103.8 6.7 %collective-permute-start.34 = (bf16[24,1152]{1,0:T(8,128)(2,1)S(1)}, bf16[24,1152]{1,0:T(8,128)(2,1)S(1)}, u32[]{:S(2)}, u32[]{:S(2)}) collective-permute-start(bf16[24,1152]{1,0:T(8,128)(2,1)S(1)} %get-tuple-element.113.refs_0_), channel_id=1, source_target_pairs={{0,16},{8,24},{16,0},{24,8},{1,17},{9,25},{17,1},{25,9},{2,18},{10... | collective-permute-start | bytes 165896 | tf_op jit(solution)/shard_map/ppermute | solution.py:339
  104.5 6.0 %collective-permute-start.35 = (bf16[24,1152]{1,0:T(8,128)(2,1)S(1)}, bf16[24,1152]{1,0:T(8,128)(2,1)S(1)}, u32[]{:S(2)}, u32[]{:S(2)}) collective-permute-start(bf16[24,1152]{1,0:T(8,128)(2,1)S(1)} %get-tuple-element.113.refs_0_), channel_id=1, source_target_pairs={{0,24},{8,16},{16,8},{24,0},{1,25},{9,17},{17,9},{25,1},{2,26},{10... | collective-permute-start | bytes 165896 | tf_op jit(solution)/shard_map/ppermute | solution.py:339
  116.9 4.3 %collective-permute-start.37 = (bf16[24,1280]{1,0:T(8,128)(2,1)S(1)}, bf16[24,1280]{1,0:T(8,128)(2,1)S(1)}, u32[]{:S(2)}, u32[]{:S(2)}) collective-permute-start(bf16[24,1280]{1,0:T(8,128)(2,1)S(1)} %get-tuple-element.119), channel_id=1, source_target_pairs={{0,2},{1,3},{2,0},{3,1},{4,6},{5,7},{6,4},{7,5},{8,10},{9,11},{10,... | collective-permute-start | bytes 184328 | tf_op jit(solution)/shard_map/ppermute | solution.py:343
  120.0 5.1 %collective-permute-start.39 = (bf16[24,1280]{1,0:T(8,128)(2,1)S(1)}, bf16[24,1280]{1,0:T(8,128)(2,1)S(1)}, u32[]{:S(2)}, u32[]{:S(2)}) collective-permute-start(bf16[24,1280]{1,0:T(8,128)(2,1)S(1)} %get-tuple-element.121), channel_id=1, source_target_pairs={{0,6},{1,7},{2,4},{3,5},{4,2},{5,3},{6,0},{7,1},{8,14},{9,15},{10,... | collective-permute-start | bytes 184328 | tf_op jit(solution)/shard_map/ppermute | solution.py:343
  128.0 4.3 %collective-permute-start.42 = (f32[8,1024]{1,0:T(8,128)S(1)}, f32[8,1024]{1,0:T(8,128)S(1)}, u32[]{:S(2)}, u32[]{:S(2)}) collective-permute-start(f32[8,1024]{1,0:T(8,128)S(1)} %shard_map.215.refs_0_), channel_id=1, source_target_pairs={{0,4},{1,5},{2,6},{3,7},{4,0},{5,1},{6,2},{7,3},{8,12},{9,13},{10,... | collective-permute-start | bytes 98312 | tf_op jit(solution)/shard_map/ppermute | solution.py:343
  128.5 4.8 %collective-permute-start.43 = (f32[8,1024]{1,0:T(8,128)S(1)}, f32[8,1024]{1,0:T(8,128)S(1)}, u32[]{:S(2)}, u32[]{:S(2)}) collective-permute-start(f32[8,1024]{1,0:T(8,128)S(1)} %shard_map.215.refs_0_), channel_id=1, source_target_pairs={{0,6},{1,7},{2,4},{3,5},{4,2},{5,3},{6,0},{7,1},{8,14},{9,15},{10,... | collective-permute-start | bytes 98312 | tf_op jit(solution)/shard_map/ppermute | solution.py:343
  (37 other events, 388.0 us)

commit v7 on v6

--- a/solution.py
+++ b/solution.py
@@ -11,7 +11,7 @@
 BUSES = 20480
 ITERS = 2
 CHUNKS = 2
-FIRST_SHARE = 0.5625
+FIRST_SHARE = 0.5
 EARLY_SHARE = 0.4375
 LANES = 128
 GRANT = 11 << 20
@@ -167,18 +167,14 @@
     parts = refs[:scen]
     copies, duals, limits = refs[scen : scen + 3]
     if chunk == 0:
-        flows = refs[scen + 3 : 2 * scen + 2]
-        residual, rest, copy_out, dual_out = refs[2 * scen + 2 : 2 * scen + 6]
-        messages = refs[2 * scen + 6 :]
-        skip = 0
+        residual, rest, copy_out, dual_out = refs[scen + 4 :]
     else:
         rest, residual, copy_out, dual_out = refs[scen + 3 :]
         before = rest.shape[1]
         residual[:, :before] = rest[...]
-        skip = early + LANES
     total = parts[0][...]
     for part in parts[1:]:
-        total = total + part[:, skip:].astype(F32)
+        total = total + part[...].astype(F32)
     for side in range(2):
         rows = slice(side * sz.pair, (side + 1) * sz.pair)
         base = start if copies.shape[1] == sz.lines else 0
@@ -201,9 +197,6 @@
         lane = lax.broadcasted_iota(jnp.int32, (2 * sz.pair, LANES), 1)
         tile = jnp.where(lane == 0, high, jnp.where(lane == 1, middle, jnp.where(lane == 2, low, 0.0)))
         residual[:, early:] = tile.astype(BF)
-        for message, flow in zip(messages, flows):
-            message[:, : early + LANES] = residual[...]
-            message[:, early + LANES :] = flow[...]
 
 
 def backward_kernel(sz, chunk, step, *refs):
@@ -416,18 +409,17 @@
                 parts = [flows[0][0]] + spread(to_scen, n_scen, flows[0][1:])
         state = lambda width: [((sz.pair, width), F32)] * 2
         old = (flow_copy, flow_dual) if iteration == 0 else None
-        first_res, rest, first_copy, first_dual, *messages = call(
+        first_res, rest, first_copy, first_dual = call(
             functools.partial(residual_kernel, sz, 0),
-            (*parts, *(old or (copies[0], duals[0])), limits, *flows[1][1:]),
+            (*parts, *(old or (copies[0], duals[0])), limits, flows[1][0]),
             [
                 ((tall, sz.early + LANES), BF),
                 ((tall, sz.halves[0] - sz.early), BF),
                 *state(2 * sz.halves[0]),
-                *[((tall, sz.early + LANES + sz.halves[1]), BF)] * (n_scen - 1),
             ],
             keep=shift_factors,
         )
-        got = spread(to_scen, n_scen, messages)
+        got = spread(to_scen, n_scen, flows[1][1:])
         second_res, second_copy, second_dual = call(
             functools.partial(residual_kernel, sz, 1),
             (
@@ -441,7 +433,7 @@
             keep=shift_factors,
         )
         residuals = [
-            [first_res, *got],
+            [first_res] + spread(to_scen, n_scen, [first_res] * (n_scen - 1)),
             [second_res] + spread(to_scen, n_scen, [second_res] * (n_scen - 1)),
         ]
         new_copies, new_duals = [first_copy, second_copy], [first_dual, second_dual]

time: 134 us -> 133 us (level)
  waiting for transfers between devices: 37.3 us -> 26.7 us
  starting transfers between devices: 46.8 us -> 55.7 us
    ppermute x18 -> x24, waiting for transfers between devices: 12.7 us -> 2.11 us  [to_scen(): return lax.ppermute(value, 'scen', [(i, i ^ away) for i in range(n)])]
    ppermute x18 -> x24, starting transfers between devices: 27.9 us -> 36.8 us  [to_scen(): return lax.ppermute(value, 'scen', [(i, i ^ away) for i in range(n)])]
  transfers between devices with their start and end apart: 44 -> 50, of which waited for: 25 -> 22; matrix products, arithmetic and copies ran while one was open for 1% -> 1% of each run, Pallas kernels for 13% -> 15%
where the time goes in v7:
time: 133 us; the launch traced here: 132 us
  starting transfers between devices  55.7 us (42%)
  Pallas kernels  44.2 us (33%)
  waiting for transfers between devices  26.7 us (20%)
  local copies, waits for them, and re-layouts  2.71 us (2%)
  other arithmetic  1.99 us (1%)
    pallas_call x19, Pallas kernels, call(): pl.pallas_call(kernel, in_specs=[WHOLE] * len(args), out_specs=[WHOLE] *...  44.2 us
    ppermute x24, starting transfers between devices, to_scen(): return lax.ppermute(value, 'scen', [(i, i ^ away) for i in range(n)])  36.8 us
    ppermute x15, waiting for transfers between devices, to_chip(): return lax.ppermute(value, 'line', [(i, i ^ 2 * away) for i in range(n)])  18.8 us
    ppermute x15, starting transfers between devices, to_chip(): return lax.ppermute(value, 'line', [(i, i ^ 2 * away) for i in range(n)])  18.7 us
    ppermute x11, waiting for transfers between devices, to_core(): return lax.ppermute(value, 'line', [(i, i ^ 1) for i in range(n)])  5.84 us
  transfers between devices with their start and end apart: 50, of which 22 were waited for; matrix products, arithmetic and copies ran while one was open for 1% of the time, Pallas kernels for 15%

profile of v7, /device:TPU:0, one launch (start us, length us, event | category | flops | bytes accessed | tf_op | source)
XLA Modules:
  0.0 132.4 jit_solution(4988087853668224382)
XLA Ops:
  4.2 3.0 %collective-permute-start = (bf16[24,1280]{1,0:T(8,128)(2,1)S(1)}, bf16[24,1280]{1,0:T(8,128)(2,1)S(1)}, u32[]{:S(2)}, u32[]{:S(2)}) collective-permute-start(bf16[24,1280]{1,0:T(8,128)(2,1)S(1)} %get-tuple-element.66.refs_0_), channel_id=1, source_target_pairs={{0,2},{1,3},{2,0},{3,1},{4,6},{5,7},{6,4},{7,5},{8,10},{9,11},{10,... | collective-permute-start | bytes 184328 | tf_op jit(solution)/shard_map/ppermute | solution.py:336
  7.2 1.5 %collective-permute-start.1 = (bf16[24,1280]{1,0:T(8,128)(2,1)S(1)}, bf16[24,1280]{1,0:T(8,128)(2,1)S(1)}, u32[]{:S(2)}, u32[]{:S(2)}) collective-permute-start(bf16[24,1280]{1,0:T(8,128)(2,1)S(1)} %get-tuple-element.66.refs_0_), channel_id=1, source_target_pairs={{0,4},{1,5},{2,6},{3,7},{4,0},{5,1},{6,2},{7,3},{8,12},{9,13},{10,... | collective-permute-start | bytes 184328 | tf_op jit(solution)/shard_map/ppermute | solution.py:336
  9.5 1.9 %collective-permute-done.1.refs_2_ = bf16[24,1280]{1,0:T(8,128)(2,1)S(1)} collective-permute-done((bf16[24,1280]{1,0:T(8,128)(2,1)S(1)}, bf16[24,1280]{1,0:T(8,128)(2,1)S(1)}, u32[]{:S(2)}, u32[]{:S(2)}) %collective-permute-start.1) | collective-permute-done | bytes 61472 | tf_op jit(solution)/shard_map/ppermute | solution.py:336
  11.4 2.4 %collective-permute-done.2.refs_3_ = bf16[24,1280]{1,0:T(8,128)(2,1)S(1)} collective-permute-done((bf16[24,1280]{1,0:T(8,128)(2,1)S(1)}, bf16[24,1280]{1,0:T(8,128)(2,1)S(1)}, u32[]{:S(2)}, u32[]{:S(2)}) %collective-permute-start.2) | collective-permute-done | bytes 61472 | tf_op jit(solution)/shard_map/ppermute | solution.py:336
  15.3 5.8 %shard_map.200 = (f32[24,1152]{1,0:T(8,128)S(1)}, bf16[24,1152]{1,0:T(8,128)(2,1)S(1)}, bf16[24,1152]{1,0:T(8,128)(2,1)S(1)}, bf16[24,1152]{1,0:T(8,128)(2,1)S(1)}) custom-call(bf16[24,1280]{1,0:T(8,128)(2,1)S(1)} %get-tuple-element.66.refs_0_, bf16[24,1280]{1,0:T(8,128)(2,1)S(1)} %collective-permute-done.refs_1_, ...), custom_call_target="tpu_custom_call" | custom-call | flops 1006632960 | bytes 42434560 | tf_op jit(solution)/shard_map/pallas_call | solution.py:28
  21.1 3.1 %collective-permute-start.10 = (bf16[24,1152]{1,0:T(8,128)(2,1)S(1)}, bf16[24,1152]{1,0:T(8,128)(2,1)S(1)}, u32[]{:S(2)}, u32[]{:S(2)}) collective-permute-start(bf16[24,1152]{1,0:T(8,128)(2,1)S(1)} %get-tuple-element.72), channel_id=1, source_target_pairs={{0,8},{8,0},{16,24},{24,16},{1,9},{9,1},{17,25},{25,17},{2,10},{10... | collective-permute-start | bytes 165896 | tf_op jit(solution)/shard_map/ppermute | solution.py:332
  24.2 2.6 %collective-permute-start.11 = (bf16[24,1152]{1,0:T(8,128)(2,1)S(1)}, bf16[24,1152]{1,0:T(8,128)(2,1)S(1)}, u32[]{:S(2)}, u32[]{:S(2)}) collective-permute-start(bf16[24,1152]{1,0:T(8,128)(2,1)S(1)} %get-tuple-element.73), channel_id=1, source_target_pairs={{0,16},{8,24},{16,0},{24,8},{1,17},{9,25},{17,1},{25,9},{2,18},{10... | collective-permute-start | bytes 165896 | tf_op jit(solution)/shard_map/ppermute | solution.py:332
  26.8 5.8 %shard_map.199 = (f32[24,1024]{1,0:T(8,128)S(1)}, bf16[24,1024]{1,0:T(8,128)(2,1)S(1)}, bf16[24,1024]{1,0:T(8,128)(2,1)S(1)}, bf16[24,1024]{1,0:T(8,128)(2,1)S(1)}) custom-call(bf16[24,1280]{1,0:T(8,128)(2,1)S(1)} %get-tuple-element.66.refs_0_, bf16[24,1280]{1,0:T(8,128)(2,1)S(1)} %collective-permute-done.refs_1_, ...), custom_call_target="tpu_custom_call" | custom-call | flops 1006632960 | bytes 42434560 | tf_op jit(solution)/shard_map/pallas_call | solution.py:28
  33.5 3.5 %collective-permute-start.8 = (bf16[24,1024]{1,0:T(8,128)(2,1)S(1)}, bf16[24,1024]{1,0:T(8,128)(2,1)S(1)}, u32[]{:S(2)}, u32[]{:S(2)}) collective-permute-start(bf16[24,1024]{1,0:T(8,128)(2,1)S(1)} %get-tuple-element.69), channel_id=1, source_target_pairs={{0,16},{8,24},{16,0},{24,8},{1,17},{9,25},{17,1},{25,9},{2,18},{10... | collective-permute-start | bytes 147464 | tf_op jit(solution)/shard_map/ppermute | solution.py:332
  37.8 3.8 %collective-permute-start.17 = (bf16[24,1024]{1,0:T(8,128)(2,1)S(1)}, bf16[24,1024]{1,0:T(8,128)(2,1)S(1)}, u32[]{:S(2)}, u32[]{:S(2)}) collective-permute-start(bf16[24,1024]{1,0:T(8,128)(2,1)S(1)} %get-tuple-element.77.refs_0_), channel_id=1, source_target_pairs={{0,16},{8,24},{16,0},{24,8},{1,17},{9,25},{17,1},{25,9},{2,18},{10... | collective-permute-start | bytes 147464 | tf_op jit(solution)/shard_map/ppermute | solution.py:332
  43.1 3.0 %collective-permute-start.14 = (bf16[24,1152]{1,0:T(8,128)(2,1)S(1)}, bf16[24,1152]{1,0:T(8,128)(2,1)S(1)}, u32[]{:S(2)}, u32[]{:S(2)}) collective-permute-start(bf16[24,1152]{1,0:T(8,128)(2,1)S(1)} %get-tuple-element.76.refs_0_), channel_id=1, source_target_pairs={{0,16},{8,24},{16,0},{24,8},{1,17},{9,25},{17,1},{25,9},{2,18},{10... | collective-permute-start | bytes 165896 | tf_op jit(solution)/shard_map/ppermute | solution.py:332
  47.8 3.9 %shard_map.203 = (f32[48,5120]{1,0:T(8,128)S(1)}, f32[12,128]{1,0:T(8,128)S(1)}) custom-call(bf16[24,1024]{1,0:T(8,128)(2,1)S(1)} %get-tuple-element.77.refs_0_, bf16[24,1024]{1,0:T(8,128)(2,1)S(1)} %collective-permute-done.16.refs_1_, bf16[24,1024]{1,0:T(8,128)(2,1)S(1)} %collective-permute-done.17.refs_2_, ...), custom_call_target="tpu_custom_call" | custom-call | flops 1006632960 | bytes 42139648 | tf_op jit(solution)/shard_map/pallas_call | solution.py:28
  52.2 4.7 %shard_map.204 = (f32[24,5120]{1,0:T(8,128)S(1)}, bf16[24,5120]{1,0:T(8,128)(2,1)S(1)}) custom-call(bf16[24,1152]{1,0:T(8,128)(2,1)S(1)} %get-tuple-element.76.refs_0_, bf16[24,1152]{1,0:T(8,128)(2,1)S(1)} %collective-permute-done.13.refs_1_, bf16[24,1152]{1,0:T(8,128)(2,1)S(1)} %collective-permute-done.14.refs_2_, ...), custom_call_target="tpu_custom_call" | custom-call | flops 1006632960 | bytes 43147264 | tf_op jit(solution)/shard_map/pallas_call | solution.py:28
  58.6 1.6 %collective-permute-start.20 = (bf16[24,1280]{1,0:T(8,128)(2,1)S(1)}, bf16[24,1280]{1,0:T(8,128)(2,1)S(1)}, u32[]{:S(2)}, u32[]{:S(2)}) collective-permute-start(bf16[24,1280]{1,0:T(8,128)(2,1)S(1)} %get-tuple-element.82), channel_id=1, source_target_pairs={{0,2},{1,3},{2,0},{3,1},{4,6},{5,7},{6,4},{7,5},{8,10},{9,11},{10,... | collective-permute-start | bytes 184328 | tf_op jit(solution)/shard_map/ppermute | solution.py:336
  64.4 2.4 %collective-permute-done.22.refs_3_ = bf16[24,1280]{1,0:T(8,128)(2,1)S(1)} collective-permute-done((bf16[24,1280]{1,0:T(8,128)(2,1)S(1)}, bf16[24,1280]{1,0:T(8,128)(2,1)S(1)}, u32[]{:S(2)}, u32[]{:S(2)}) %collective-permute-start.22) | collective-permute-done | bytes 61472 | tf_op jit(solution)/shard_map/ppermute | solution.py:336
  68.9 2.4 %collective-permute-start.25 = (bf16[24,1280]{1,0:T(8,128)(2,1)S(1)}, bf16[24,1280]{1,0:T(8,128)(2,1)S(1)}, u32[]{:S(2)}, u32[]{:S(2)}) collective-permute-start(bf16[24,1280]{1,0:T(8,128)(2,1)S(1)} %get-tuple-element.87.refs_0_), channel_id=1, source_target_pairs={{0,6},{1,7},{2,4},{3,5},{4,2},{5,3},{6,0},{7,1},{8,14},{9,15},{10,... | collective-permute-start | bytes 184328 | tf_op jit(solution)/shard_map/ppermute | solution.py:336
  75.3 5.8 %shard_map.208 = (f32[24,1152]{1,0:T(8,128)S(1)}, bf16[24,1152]{1,0:T(8,128)(2,1)S(1)}, bf16[24,1152]{1,0:T(8,128)(2,1)S(1)}, bf16[24,1152]{1,0:T(8,128)(2,1)S(1)}) custom-call(bf16[24,1280]{1,0:T(8,128)(2,1)S(1)} %get-tuple-element.87.refs_0_, bf16[24,1280]{1,0:T(8,128)(2,1)S(1)} %collective-permute-done.23.refs_1_, ...), custom_call_target="tpu_custom_call" | custom-call | flops 1006632960 | bytes 42434560 | tf_op jit(solution)/shard_map/pallas_call | solution.py:28
  81.2 2.5 %collective-permute-start.34 = (bf16[24,1152]{1,0:T(8,128)(2,1)S(1)}, bf16[24,1152]{1,0:T(8,128)(2,1)S(1)}, u32[]{:S(2)}, u32[]{:S(2)}) collective-permute-start(bf16[24,1152]{1,0:T(8,128)(2,1)S(1)} %get-tuple-element.96), channel_id=1, source_target_pairs={{0,16},{8,24},{16,0},{24,8},{1,17},{9,25},{17,1},{25,9},{2,18},{10... | collective-permute-start | bytes 165896 | tf_op jit(solution)/shard_map/ppermute | solution.py:332
  83.6 1.9 %collective-permute-start.35 = (bf16[24,1152]{1,0:T(8,128)(2,1)S(1)}, bf16[24,1152]{1,0:T(8,128)(2,1)S(1)}, u32[]{:S(2)}, u32[]{:S(2)}) collective-permute-start(bf16[24,1152]{1,0:T(8,128)(2,1)S(1)} %get-tuple-element.97), channel_id=1, source_target_pairs={{0,24},{8,16},{16,8},{24,0},{1,25},{9,17},{17,9},{25,1},{2,26},{10... | collective-permute-start | bytes 165896 | tf_op jit(solution)/shard_map/ppermute | solution.py:332
  85.5 5.8 %shard_map.207 = (f32[24,1024]{1,0:T(8,128)S(1)}, bf16[24,1024]{1,0:T(8,128)(2,1)S(1)}, bf16[24,1024]{1,0:T(8,128)(2,1)S(1)}, bf16[24,1024]{1,0:T(8,128)(2,1)S(1)}) custom-call(bf16[24,1280]{1,0:T(8,128)(2,1)S(1)} %get-tuple-element.87.refs_0_, bf16[24,1280]{1,0:T(8,128)(2,1)S(1)} %collective-permute-done.23.refs_1_, ...), custom_call_target="tpu_custom_call" | custom-call | flops 1006632960 | bytes 42434560 | tf_op jit(solution)/shard_map/pallas_call | solution.py:28
  91.4 2.5 %collective-permute-start.31 = (bf16[24,1024]{1,0:T(8,128)(2,1)S(1)}, bf16[24,1024]{1,0:T(8,128)(2,1)S(1)}, u32[]{:S(2)}, u32[]{:S(2)}) collective-permute-start(bf16[24,1024]{1,0:T(8,128)(2,1)S(1)} %get-tuple-element.90), channel_id=1, source_target_pairs={{0,16},{8,24},{16,0},{24,8},{1,17},{9,25},{17,1},{25,9},{2,18},{10... | collective-permute-start | bytes 147464 | tf_op jit(solution)/shard_map/ppermute | solution.py:332
  93.8 1.9 %collective-permute-start.32 = (bf16[24,1024]{1,0:T(8,128)(2,1)S(1)}, bf16[24,1024]{1,0:T(8,128)(2,1)S(1)}, u32[]{:S(2)}, u32[]{:S(2)}) collective-permute-start(bf16[24,1024]{1,0:T(8,128)(2,1)S(1)} %get-tuple-element.91), channel_id=1, source_target_pairs={{0,24},{8,16},{16,8},{24,0},{1,25},{9,17},{17,9},{25,1},{2,26},{10... | collective-permute-start | bytes 147464 | tf_op jit(solution)/shard_map/ppermute | solution.py:332
  95.9 2.5 %collective-permute-start.40 = (bf16[24,1024]{1,0:T(8,128)(2,1)S(1)}, bf16[24,1024]{1,0:T(8,128)(2,1)S(1)}, u32[]{:S(2)}, u32[]{:S(2)}) collective-permute-start(bf16[24,1024]{1,0:T(8,128)(2,1)S(1)} %get-tuple-element.102.refs_0_), channel_id=1, source_target_pairs={{0,16},{8,24},{16,0},{24,8},{1,17},{9,25},{17,1},{25,9},{2,18},{10... | collective-permute-start | bytes 147464 | tf_op jit(solution)/shard_map/ppermute | solution.py:332
  98.4 1.9 %collective-permute-start.41 = (bf16[24,1024]{1,0:T(8,128)(2,1)S(1)}, bf16[24,1024]{1,0:T(8,128)(2,1)S(1)}, u32[]{:S(2)}, u32[]{:S(2)}) collective-permute-start(bf16[24,1024]{1,0:T(8,128)(2,1)S(1)} %get-tuple-element.102.refs_0_), channel_id=1, source_target_pairs={{0,24},{8,16},{16,8},{24,0},{1,25},{9,17},{17,9},{25,1},{2,26},{10... | collective-permute-start | bytes 147464 | tf_op jit(solution)/shard_map/ppermute | solution.py:332
  100.5 2.5 %collective-permute-start.37 = (bf16[24,1152]{1,0:T(8,128)(2,1)S(1)}, bf16[24,1152]{1,0:T(8,128)(2,1)S(1)}, u32[]{:S(2)}, u32[]{:S(2)}) collective-permute-start(bf16[24,1152]{1,0:T(8,128)(2,1)S(1)} %get-tuple-element.101.refs_0_), channel_id=1, source_target_pairs={{0,16},{8,24},{16,0},{24,8},{1,17},{9,25},{17,1},{25,9},{2,18},{10... | collective-permute-start | bytes 165896 | tf_op jit(solution)/shard_map/ppermute | solution.py:332
  103.0 1.9 %collective-permute-start.38 = (bf16[24,1152]{1,0:T(8,128)(2,1)S(1)}, bf16[24,1152]{1,0:T(8,128)(2,1)S(1)}, u32[]{:S(2)}, u32[]{:S(2)}) collective-permute-start(bf16[24,1152]{1,0:T(8,128)(2,1)S(1)} %get-tuple-element.101.refs_0_), channel_id=1, source_target_pairs={{0,24},{8,16},{16,8},{24,0},{1,25},{9,17},{17,9},{25,1},{2,26},{10... | collective-permute-start | bytes 165896 | tf_op jit(solution)/shard_map/ppermute | solution.py:332
  104.9 4.0 %shard_map.211 = (f32[48,5120]{1,0:T(8,128)S(1)}, f32[12,128]{1,0:T(8,128)S(1)}) custom-call(bf16[24,1024]{1,0:T(8,128)(2,1)S(1)} %get-tuple-element.102.refs_0_, bf16[24,1024]{1,0:T(8,128)(2,1)S(1)} %collective-permute-done.39.refs_1_, bf16[24,1024]{1,0:T(8,128)(2,1)S(1)} %collective-permute-done.40.refs_2_, ...), custom_call_target="tpu_custom_call" | custom-call | flops 1006632960 | bytes 42139648 | tf_op jit(solution)/shard_map/pallas_call | solution.py:28
  108.9 4.7 %shard_map.212 = (f32[24,5120]{1,0:T(8,128)S(1)}, bf16[24,5120]{1,0:T(8,128)(2,1)S(1)}) custom-call(bf16[24,1152]{1,0:T(8,128)(2,1)S(1)} %get-tuple-element.101.refs_0_, bf16[24,1152]{1,0:T(8,128)(2,1)S(1)} %collective-permute-done.36.refs_1_, bf16[24,1152]{1,0:T(8,128)(2,1)S(1)} %collective-permute-done.37.refs_2_, ...), custom_call_target="tpu_custom_call" | custom-call | flops 1006632960 | bytes 43147264 | tf_op jit(solution)/shard_map/pallas_call | solution.py:28
  115.4 1.5 %collective-permute-start.43 = (bf16[24,1280]{1,0:T(8,128)(2,1)S(1)}, bf16[24,1280]{1,0:T(8,128)(2,1)S(1)}, u32[]{:S(2)}, u32[]{:S(2)}) collective-permute-start(bf16[24,1280]{1,0:T(8,128)(2,1)S(1)} %get-tuple-element.107), channel_id=1, source_target_pairs={{0,2},{1,3},{2,0},{3,1},{4,6},{5,7},{6,4},{7,5},{8,10},{9,11},{10,... | collective-permute-start | bytes 184328 | tf_op jit(solution)/shard_map/ppermute | solution.py:336
  117.0 1.5 %collective-permute-start.44 = (bf16[24,1280]{1,0:T(8,128)(2,1)S(1)}, bf16[24,1280]{1,0:T(8,128)(2,1)S(1)}, u32[]{:S(2)}, u32[]{:S(2)}) collective-permute-start(bf16[24,1280]{1,0:T(8,128)(2,1)S(1)} %get-tuple-element.108), channel_id=1, source_target_pairs={{0,4},{1,5},{2,6},{3,7},{4,0},{5,1},{6,2},{7,3},{8,12},{9,13},{10,... | collective-permute-start | bytes 184328 | tf_op jit(solution)/shard_map/ppermute | solution.py:336
  121.2 2.4 %collective-permute-done.45.refs_3_ = bf16[24,1280]{1,0:T(8,128)(2,1)S(1)} collective-permute-done((bf16[24,1280]{1,0:T(8,128)(2,1)S(1)}, bf16[24,1280]{1,0:T(8,128)(2,1)S(1)}, u32[]{:S(2)}, u32[]{:S(2)}) %collective-permute-start.45) | collective-permute-done | bytes 61472 | tf_op jit(solution)/shard_map/ppermute | solution.py:336
  127.0 2.4 %collective-permute-start.49 = (f32[8,1024]{1,0:T(8,128)S(1)}, f32[8,1024]{1,0:T(8,128)S(1)}, u32[]{:S(2)}, u32[]{:S(2)}) collective-permute-start(f32[8,1024]{1,0:T(8,128)S(1)} %shard_map.215.refs_0_), channel_id=1, source_target_pairs={{0,6},{1,7},{2,4},{3,5},{4,2},{5,3},{6,0},{7,1},{8,14},{9,15},{10,... | collective-permute-start | bytes 98312 | tf_op jit(solution)/shard_map/ppermute | solution.py:336
  (143 shorter events, 34.2 us)
Async XLA Ops:
  4.2 5.3 %collective-permute-start = (bf16[24,1280]{1,0:T(8,128)(2,1)S(1)}, bf16[24,1280]{1,0:T(8,128)(2,1)S(1)}, u32[]{:S(2)}, u32[]{:S(2)}) collective-permute-start(bf16[24,1280]{1,0:T(8,128)(2,1)S(1)} %get-tuple-element.66.refs_0_), channel_id=1, source_target_pairs={{0,2},{1,3},{2,0},{3,1},{4,6},{5,7},{6,4},{7,5},{8,10},{9,11},{10,... | collective-permute-start | bytes 184328 | tf_op jit(solution)/shard_map/ppermute | solution.py:336
  8.7 5.1 %collective-permute-start.2 = (bf16[24,1280]{1,0:T(8,128)(2,1)S(1)}, bf16[24,1280]{1,0:T(8,128)(2,1)S(1)}, u32[]{:S(2)}, u32[]{:S(2)}) collective-permute-start(bf16[24,1280]{1,0:T(8,128)(2,1)S(1)} %get-tuple-element.66.refs_0_), channel_id=1, source_target_pairs={{0,6},{1,7},{2,4},{3,5},{4,2},{5,3},{6,0},{7,1},{8,14},{9,15},{10,... | collective-permute-start | bytes 184328 | tf_op jit(solution)/shard_map/ppermute | solution.py:336
  8.8 5.1 %collective-permute-start.3 = (bf16[24,1280]{1,0:T(8,128)(2,1)S(1)}, bf16[24,1280]{1,0:T(8,128)(2,1)S(1)}, u32[]{:S(2)}, u32[]{:S(2)}) collective-permute-start(bf16[24,1280]{1,0:T(8,128)(2,1)S(1)} %get-tuple-element.66.refs_0_), channel_id=1, source_target_pairs={{0,1},{1,0},{2,3},{3,2},{4,5},{5,4},{6,7},{7,6},{8,9},{9,8},{10,11... | collective-permute-start | bytes 184328 | tf_op jit(solution)/shard_map/ppermute | solution.py:345
  9.5 4.4 %collective-permute-start.4 = (bf16[24,1280]{1,0:T(8,128)(2,1)S(1)}, bf16[24,1280]{1,0:T(8,128)(2,1)S(1)}, u32[]{:S(2)}, u32[]{:S(2)}) collective-permute-start(bf16[24,1280]{1,0:T(8,128)(2,1)S(1)} %collective-permute-done.refs_1_), channel_id=1, source_target_pairs={{0,1},{1,0},{2,3},{3,2},{4,5},{5,4},{6,7},{7,6},{8,9},{9,8},{10,11... | collective-permute-start | bytes 184328 | tf_op jit(solution)/shard_map/ppermute | solution.py:345
  21.1 15.9 %collective-permute-start.10 = (bf16[24,1152]{1,0:T(8,128)(2,1)S(1)}, bf16[24,1152]{1,0:T(8,128)(2,1)S(1)}, u32[]{:S(2)}, u32[]{:S(2)}) collective-permute-start(bf16[24,1152]{1,0:T(8,128)(2,1)S(1)} %get-tuple-element.72), channel_id=1, source_target_pairs={{0,8},{8,0},{16,24},{24,16},{1,9},{9,1},{17,25},{25,17},{2,10},{10... | collective-permute-start | bytes 165896 | tf_op jit(solution)/shard_map/ppermute | solution.py:332
  24.2 12.8 %collective-permute-start.11 = (bf16[24,1152]{1,0:T(8,128)(2,1)S(1)}, bf16[24,1152]{1,0:T(8,128)(2,1)S(1)}, u32[]{:S(2)}, u32[]{:S(2)}) collective-permute-start(bf16[24,1152]{1,0:T(8,128)(2,1)S(1)} %get-tuple-element.73), channel_id=1, source_target_pairs={{0,16},{8,24},{16,0},{24,8},{1,17},{9,25},{17,1},{25,9},{2,18},{10... | collective-permute-start | bytes 165896 | tf_op jit(solution)/shard_map/ppermute | solution.py:332
  26.8 10.2 %collective-permute-start.12 = (bf16[24,1152]{1,0:T(8,128)(2,1)S(1)}, bf16[24,1152]{1,0:T(8,128)(2,1)S(1)}, u32[]{:S(2)}, u32[]{:S(2)}) collective-permute-start(bf16[24,1152]{1,0:T(8,128)(2,1)S(1)} %get-tuple-element.74), channel_id=1, source_target_pairs={{0,24},{8,16},{16,8},{24,0},{1,25},{9,17},{17,9},{25,1},{2,26},{10... | collective-permute-start | bytes 165896 | tf_op jit(solution)/shard_map/ppermute | solution.py:332
  32.5 9.0 %collective-permute-start.7 = (bf16[24,1024]{1,0:T(8,128)(2,1)S(1)}, bf16[24,1024]{1,0:T(8,128)(2,1)S(1)}, u32[]{:S(2)}, u32[]{:S(2)}) collective-permute-start(bf16[24,1024]{1,0:T(8,128)(2,1)S(1)} %get-tuple-element.68), channel_id=1, source_target_pairs={{0,8},{8,0},{16,24},{24,16},{1,9},{9,1},{17,25},{25,17},{2,10},{10... | collective-permute-start | bytes 147464 | tf_op jit(solution)/shard_map/ppermute | solution.py:332
  33.5 8.1 %collective-permute-start.8 = (bf16[24,1024]{1,0:T(8,128)(2,1)S(1)}, bf16[24,1024]{1,0:T(8,128)(2,1)S(1)}, u32[]{:S(2)}, u32[]{:S(2)}) collective-permute-start(bf16[24,1024]{1,0:T(8,128)(2,1)S(1)} %get-tuple-element.69), channel_id=1, source_target_pairs={{0,16},{8,24},{16,0},{24,8},{1,17},{9,25},{17,1},{25,9},{2,18},{10... | collective-permute-start | bytes 147464 | tf_op jit(solution)/shard_map/ppermute | solution.py:332
  37.0 6.0 %collective-permute-start.9 = (bf16[24,1024]{1,0:T(8,128)(2,1)S(1)}, bf16[24,1024]{1,0:T(8,128)(2,1)S(1)}, u32[]{:S(2)}, u32[]{:S(2)}) collective-permute-start(bf16[24,1024]{1,0:T(8,128)(2,1)S(1)} %get-tuple-element.70), channel_id=1, source_target_pairs={{0,24},{8,16},{16,8},{24,0},{1,25},{9,17},{17,9},{25,1},{2,26},{10... | collective-permute-start | bytes 147464 | tf_op jit(solution)/shard_map/ppermute | solution.py:332
  37.2 9.0 %collective-permute-start.16 = (bf16[24,1024]{1,0:T(8,128)(2,1)S(1)}, bf16[24,1024]{1,0:T(8,128)(2,1)S(1)}, u32[]{:S(2)}, u32[]{:S(2)}) collective-permute-start(bf16[24,1024]{1,0:T(8,128)(2,1)S(1)} %get-tuple-element.77.refs_0_), channel_id=1, source_target_pairs={{0,8},{8,0},{16,24},{24,16},{1,9},{9,1},{17,25},{25,17},{2,10},{10... | collective-permute-start | bytes 147464 | tf_op jit(solution)/shard_map/ppermute | solution.py:332
  37.8 9.8 %collective-permute-start.17 = (bf16[24,1024]{1,0:T(8,128)(2,1)S(1)}, bf16[24,1024]{1,0:T(8,128)(2,1)S(1)}, u32[]{:S(2)}, u32[]{:S(2)}) collective-permute-start(bf16[24,1024]{1,0:T(8,128)(2,1)S(1)} %get-tuple-element.77.refs_0_), channel_id=1, source_target_pairs={{0,16},{8,24},{16,0},{24,8},{1,17},{9,25},{17,1},{25,9},{2,18},{10... | collective-permute-start | bytes 147464 | tf_op jit(solution)/shard_map/ppermute | solution.py:332
  41.6 6.2 %collective-permute-start.18 = (bf16[24,1024]{1,0:T(8,128)(2,1)S(1)}, bf16[24,1024]{1,0:T(8,128)(2,1)S(1)}, u32[]{:S(2)}, u32[]{:S(2)}) collective-permute-start(bf16[24,1024]{1,0:T(8,128)(2,1)S(1)} %get-tuple-element.77.refs_0_), channel_id=1, source_target_pairs={{0,24},{8,16},{16,8},{24,0},{1,25},{9,17},{17,9},{25,1},{2,26},{10... | collective-permute-start | bytes 147464 | tf_op jit(solution)/shard_map/ppermute | solution.py:332
  43.1 8.6 %collective-permute-start.13 = (bf16[24,1152]{1,0:T(8,128)(2,1)S(1)}, bf16[24,1152]{1,0:T(8,128)(2,1)S(1)}, u32[]{:S(2)}, u32[]{:S(2)}) collective-permute-start(bf16[24,1152]{1,0:T(8,128)(2,1)S(1)} %get-tuple-element.76.refs_0_), channel_id=1, source_target_pairs={{0,8},{8,0},{16,24},{24,16},{1,9},{9,1},{17,25},{25,17},{2,10},{10... | collective-permute-start | bytes 165896 | tf_op jit(solution)/shard_map/ppermute | solution.py:332
  43.1 8.5 %collective-permute-start.14 = (bf16[24,1152]{1,0:T(8,128)(2,1)S(1)}, bf16[24,1152]{1,0:T(8,128)(2,1)S(1)}, u32[]{:S(2)}, u32[]{:S(2)}) collective-permute-start(bf16[24,1152]{1,0:T(8,128)(2,1)S(1)} %get-tuple-element.76.refs_0_), channel_id=1, source_target_pairs={{0,16},{8,24},{16,0},{24,8},{1,17},{9,25},{17,1},{25,9},{2,18},{10... | collective-permute-start | bytes 165896 | tf_op jit(solution)/shard_map/ppermute | solution.py:332
  46.1 6.0 %collective-permute-start.15 = (bf16[24,1152]{1,0:T(8,128)(2,1)S(1)}, bf16[24,1152]{1,0:T(8,128)(2,1)S(1)}, u32[]{:S(2)}, u32[]{:S(2)}) collective-permute-start(bf16[24,1152]{1,0:T(8,128)(2,1)S(1)} %get-tuple-element.76.refs_0_), channel_id=1, source_target_pairs={{0,24},{8,16},{16,8},{24,0},{1,25},{9,17},{17,9},{25,1},{2,26},{10... | collective-permute-start | bytes 165896 | tf_op jit(solution)/shard_map/ppermute | solution.py:332
  61.7 5.1 %collective-permute-start.22 = (bf16[24,1280]{1,0:T(8,128)(2,1)S(1)}, bf16[24,1280]{1,0:T(8,128)(2,1)S(1)}, u32[]{:S(2)}, u32[]{:S(2)}) collective-permute-start(bf16[24,1280]{1,0:T(8,128)(2,1)S(1)} %get-tuple-element.84), channel_id=1, source_target_pairs={{0,6},{1,7},{2,4},{3,5},{4,2},{5,3},{6,0},{7,1},{8,14},{9,15},{10,... | collective-permute-start | bytes 184328 | tf_op jit(solution)/shard_map/ppermute | solution.py:336
  68.9 5.1 %collective-permute-start.25 = (bf16[24,1280]{1,0:T(8,128)(2,1)S(1)}, bf16[24,1280]{1,0:T(8,128)(2,1)S(1)}, u32[]{:S(2)}, u32[]{:S(2)}) collective-permute-start(bf16[24,1280]{1,0:T(8,128)(2,1)S(1)} %get-tuple-element.87.refs_0_), channel_id=1, source_target_pairs={{0,6},{1,7},{2,4},{3,5},{4,2},{5,3},{6,0},{7,1},{8,14},{9,15},{10,... | collective-permute-start | bytes 184328 | tf_op jit(solution)/shard_map/ppermute | solution.py:336
  81.1 12.8 %collective-permute-start.33 = (bf16[24,1152]{1,0:T(8,128)(2,1)S(1)}, bf16[24,1152]{1,0:T(8,128)(2,1)S(1)}, u32[]{:S(2)}, u32[]{:S(2)}) collective-permute-start(bf16[24,1152]{1,0:T(8,128)(2,1)S(1)} %get-tuple-element.95), channel_id=1, source_target_pairs={{0,8},{8,0},{16,24},{24,16},{1,9},{9,1},{17,25},{25,17},{2,10},{10... | collective-permute-start | bytes 165896 | tf_op jit(solution)/shard_map/ppermute | solution.py:332
  81.2 14.6 %collective-permute-start.34 = (bf16[24,1152]{1,0:T(8,128)(2,1)S(1)}, bf16[24,1152]{1,0:T(8,128)(2,1)S(1)}, u32[]{:S(2)}, u32[]{:S(2)}) collective-permute-start(bf16[24,1152]{1,0:T(8,128)(2,1)S(1)} %get-tuple-element.96), channel_id=1, source_target_pairs={{0,16},{8,24},{16,0},{24,8},{1,17},{9,25},{17,1},{25,9},{2,18},{10... | collective-permute-start | bytes 165896 | tf_op jit(solution)/shard_map/ppermute | solution.py:332
  83.6 12.1 %collective-permute-start.35 = (bf16[24,1152]{1,0:T(8,128)(2,1)S(1)}, bf16[24,1152]{1,0:T(8,128)(2,1)S(1)}, u32[]{:S(2)}, u32[]{:S(2)}) collective-permute-start(bf16[24,1152]{1,0:T(8,128)(2,1)S(1)} %get-tuple-element.97), channel_id=1, source_target_pairs={{0,24},{8,16},{16,8},{24,0},{1,25},{9,17},{17,9},{25,1},{2,26},{10... | collective-permute-start | bytes 165896 | tf_op jit(solution)/shard_map/ppermute | solution.py:332
  91.3 7.1 %collective-permute-start.30 = (bf16[24,1024]{1,0:T(8,128)(2,1)S(1)}, bf16[24,1024]{1,0:T(8,128)(2,1)S(1)}, u32[]{:S(2)}, u32[]{:S(2)}) collective-permute-start(bf16[24,1024]{1,0:T(8,128)(2,1)S(1)} %get-tuple-element.89), channel_id=1, source_target_pairs={{0,8},{8,0},{16,24},{24,16},{1,9},{9,1},{17,25},{25,17},{2,10},{10... | collective-permute-start | bytes 147464 | tf_op jit(solution)/shard_map/ppermute | solution.py:332
  91.4 8.9 %collective-permute-start.31 = (bf16[24,1024]{1,0:T(8,128)(2,1)S(1)}, bf16[24,1024]{1,0:T(8,128)(2,1)S(1)}, u32[]{:S(2)}, u32[]{:S(2)}) collective-permute-start(bf16[24,1024]{1,0:T(8,128)(2,1)S(1)} %get-tuple-element.90), channel_id=1, source_target_pairs={{0,16},{8,24},{16,0},{24,8},{1,17},{9,25},{17,1},{25,9},{2,18},{10... | collective-permute-start | bytes 147464 | tf_op jit(solution)/shard_map/ppermute | solution.py:332
  93.8 6.5 %collective-permute-start.32 = (bf16[24,1024]{1,0:T(8,128)(2,1)S(1)}, bf16[24,1024]{1,0:T(8,128)(2,1)S(1)}, u32[]{:S(2)}, u32[]{:S(2)}) collective-permute-start(bf16[24,1024]{1,0:T(8,128)(2,1)S(1)} %get-tuple-element.91), channel_id=1, source_target_pairs={{0,24},{8,16},{16,8},{24,0},{1,25},{9,17},{17,9},{25,1},{2,26},{10... | collective-permute-start | bytes 147464 | tf_op jit(solution)/shard_map/ppermute | solution.py:332
  95.9 7.1 %collective-permute-start.39 = (bf16[24,1024]{1,0:T(8,128)(2,1)S(1)}, bf16[24,1024]{1,0:T(8,128)(2,1)S(1)}, u32[]{:S(2)}, u32[]{:S(2)}) collective-permute-start(bf16[24,1024]{1,0:T(8,128)(2,1)S(1)} %get-tuple-element.102.refs_0_), channel_id=1, source_target_pairs={{0,8},{8,0},{16,24},{24,16},{1,9},{9,1},{17,25},{25,17},{2,10},{10... | collective-permute-start | bytes 147464 | tf_op jit(solution)/shard_map/ppermute | solution.py:332
  95.9 8.9 %collective-permute-start.40 = (bf16[24,1024]{1,0:T(8,128)(2,1)S(1)}, bf16[24,1024]{1,0:T(8,128)(2,1)S(1)}, u32[]{:S(2)}, u32[]{:S(2)}) collective-permute-start(bf16[24,1024]{1,0:T(8,128)(2,1)S(1)} %get-tuple-element.102.refs_0_), channel_id=1, source_target_pairs={{0,16},{8,24},{16,0},{24,8},{1,17},{9,25},{17,1},{25,9},{2,18},{10... | collective-permute-start | bytes 147464 | tf_op jit(solution)/shard_map/ppermute | solution.py:332
  98.4 6.5 %collective-permute-start.41 = (bf16[24,1024]{1,0:T(8,128)(2,1)S(1)}, bf16[24,1024]{1,0:T(8,128)(2,1)S(1)}, u32[]{:S(2)}, u32[]{:S(2)}) collective-permute-start(bf16[24,1024]{1,0:T(8,128)(2,1)S(1)} %get-tuple-element.102.refs_0_), channel_id=1, source_target_pairs={{0,24},{8,16},{16,8},{24,0},{1,25},{9,17},{17,9},{25,1},{2,26},{10... | collective-permute-start | bytes 147464 | tf_op jit(solution)/shard_map/ppermute | solution.py:332
  100.4 8.5 %collective-permute-start.36 = (bf16[24,1152]{1,0:T(8,128)(2,1)S(1)}, bf16[24,1152]{1,0:T(8,128)(2,1)S(1)}, u32[]{:S(2)}, u32[]{:S(2)}) collective-permute-start(bf16[24,1152]{1,0:T(8,128)(2,1)S(1)} %get-tuple-element.101.refs_0_), channel_id=1, source_target_pairs={{0,8},{8,0},{16,24},{24,16},{1,9},{9,1},{17,25},{25,17},{2,10},{10... | collective-permute-start | bytes 165896 | tf_op jit(solution)/shard_map/ppermute | solution.py:332
  100.5 8.4 %collective-permute-start.37 = (bf16[24,1152]{1,0:T(8,128)(2,1)S(1)}, bf16[24,1152]{1,0:T(8,128)(2,1)S(1)}, u32[]{:S(2)}, u32[]{:S(2)}) collective-permute-start(bf16[24,1152]{1,0:T(8,128)(2,1)S(1)} %get-tuple-element.101.refs_0_), channel_id=1, source_target_pairs={{0,16},{8,24},{16,0},{24,8},{1,17},{9,25},{17,1},{25,9},{2,18},{10... | collective-permute-start | bytes 165896 | tf_op jit(solution)/shard_map/ppermute | solution.py:332
  103.0 6.0 %collective-permute-start.38 = (bf16[24,1152]{1,0:T(8,128)(2,1)S(1)}, bf16[24,1152]{1,0:T(8,128)(2,1)S(1)}, u32[]{:S(2)}, u32[]{:S(2)}) collective-permute-start(bf16[24,1152]{1,0:T(8,128)(2,1)S(1)} %get-tuple-element.101.refs_0_), channel_id=1, source_target_pairs={{0,24},{8,16},{16,8},{24,0},{1,25},{9,17},{17,9},{25,1},{2,26},{10... | collective-permute-start | bytes 165896 | tf_op jit(solution)/shard_map/ppermute | solution.py:332
  118.5 5.1 %collective-permute-start.45 = (bf16[24,1280]{1,0:T(8,128)(2,1)S(1)}, bf16[24,1280]{1,0:T(8,128)(2,1)S(1)}, u32[]{:S(2)}, u32[]{:S(2)}) collective-permute-start(bf16[24,1280]{1,0:T(8,128)(2,1)S(1)} %get-tuple-element.109), channel_id=1, source_target_pairs={{0,6},{1,7},{2,4},{3,5},{4,2},{5,3},{6,0},{7,1},{8,14},{9,15},{10,... | collective-permute-start | bytes 184328 | tf_op jit(solution)/shard_map/ppermute | solution.py:336
  127.0 4.8 %collective-permute-start.49 = (f32[8,1024]{1,0:T(8,128)S(1)}, f32[8,1024]{1,0:T(8,128)S(1)}, u32[]{:S(2)}, u32[]{:S(2)}) collective-permute-start(f32[8,1024]{1,0:T(8,128)S(1)} %shard_map.215.refs_0_), channel_id=1, source_target_pairs={{0,6},{1,7},{2,4},{3,5},{4,2},{5,3},{6,0},{7,1},{8,14},{9,15},{10,... | collective-permute-start | bytes 98312 | tf_op jit(solution)/shard_map/ppermute | solution.py:336
  (43 other events, 429.3 us)

commit v8 on v7

--- a/solution.py
+++ b/solution.py
@@ -79,6 +79,7 @@
         self.width = self.stretch * LANES
         self.fold = next(f for f in (4, 2, 1) if buses % (f * self.width) == 0)
         self.part = buses // self.fold
+        self.pack = next(p for p in (4, 2, 1) if gens % (p * LANES) == 0)
         tiles = lambda share, least, most: min(max(round(share * lines / 2 / LANES), least), most) * LANES
         first = tiles(FIRST_SHARE, 2, lines // 2 // LANES - 1)
         self.halves = (first, lines // 2 - first)
@@ -299,9 +300,11 @@
     gens_out[...] = now
     if last:
         dual_out[...] = dual[...] + now
-        weighted_out[:1] = jnp.sum(weights[:, :1] * now, axis=0, keepdims=True)
+        weighted = jnp.sum(weights[:, :1] * now, axis=0, keepdims=True)
         all_weights = jnp.sum(weights[:, :1], axis=0, keepdims=True)
-        weighted_out[1:] = jnp.broadcast_to(all_weights, (7, sz.gens))
+        weighted_out[sz.pack :] = jnp.broadcast_to(all_weights, (8 - sz.pack, sz.gens // sz.pack))
+        for i in range(sz.pack):
+            weighted_out[i : i + 1] = weighted[:, i * sz.gens // sz.pack : (i + 1) * sz.gens // sz.pack]
     else:
         placed = place(sz, now, select)
     for block, rows, cols in blocks_of(sz):
@@ -323,7 +326,7 @@
     total = parts[0][...]
     for part in parts[1:]:
         total = total + part[...]
-    mean = total[:1] / total[1:2]
+    mean = jnp.concatenate([total[i : i + 1] / total[sz.pack : sz.pack + 1] for i in range(sz.pack)], 1)
     consensus[...] = mean
     dual_out[...] = dual[...] - mean
 
@@ -477,9 +480,9 @@
             generation, shed, lam, weighted, dual_sum = call(
                 functools.partial(update_kernel, sz, True),
                 (*args, weights),
-                [((rows, gens), F32), ((rows, buses), F32), ((rows, LANES), F32), ((8, gens), F32), ((rows, gens), F32)],
+                [((rows, gens), F32), ((rows, buses), F32), ((rows, LANES), F32), ((8, gens // sz.pack), F32), ((rows, gens), F32)],
             )
-    (weighted,) = call(add_kernel, (weighted, to_core(n_line, weighted)), [((8, gens), F32)])
+    (weighted,) = call(add_kernel, (weighted, to_core(n_line, weighted)), [((8, gens // sz.pack), F32)])
     parts = [weighted] + spread(to_chip, n_line, [weighted] * (chips - 1))
     consensus, dual_out = call(
         functools.partial(finish_kernel, sz),

time: 133 us -> 132 us (level)
  no operation moved by 1% of the time
where the time goes in v8:
time: 132 us
  starting transfers between devices  55.7 us (42%)
  Pallas kernels  44.2 us (33%)
  waiting for transfers between devices  26.4 us (20%)
  local copies, waits for them, and re-layouts  2.71 us (2%)
  other arithmetic  1.99 us (2%)
    pallas_call x19, Pallas kernels, call(): pl.pallas_call(kernel, in_specs=[WHOLE] * len(args), out_specs=[WHOLE] *...  44.2 us
    ppermute x24, starting transfers between devices, to_scen(): return lax.ppermute(value, 'scen', [(i, i ^ away) for i in range(n)])  36.8 us
    ppermute x15, starting transfers between devices, to_chip(): return lax.ppermute(value, 'line', [(i, i ^ 2 * away) for i in range(n)])  18.7 us
    ppermute x15, waiting for transfers between devices, to_chip(): return lax.ppermute(value, 'line', [(i, i ^ 2 * away) for i in range(n)])  18.5 us
    ppermute x11, waiting for transfers between devices, to_core(): return lax.ppermute(value, 'line', [(i, i ^ 1) for i in range(n)])  5.81 us
  transfers between devices with their start and end apart: 50, of which 22 were waited for; matrix products, arithmetic and copies ran while one was open for 1% of the time, Pallas kernels for 15%

profile of v8, /device:TPU:0, one launch (start us, length us, event | category | flops | bytes accessed | tf_op | source)
XLA Modules:
  0.0 132.1 jit_solution(10446956573679270273)
XLA Ops:
  4.2 3.0 %collective-permute-start = (bf16[24,1280]{1,0:T(8,128)(2,1)S(1)}, bf16[24,1280]{1,0:T(8,128)(2,1)S(1)}, u32[]{:S(2)}, u32[]{:S(2)}) collective-permute-start(bf16[24,1280]{1,0:T(8,128)(2,1)S(1)} %get-tuple-element.66.refs_0_), channel_id=1, source_target_pairs={{0,2},{1,3},{2,0},{3,1},{4,6},{5,7},{6,4},{7,5},{8,10},{9,11},{10,... | collective-permute-start | bytes 184328 | tf_op jit(solution)/shard_map/ppermute | solution.py:339
  7.2 1.5 %collective-permute-start.1 = (bf16[24,1280]{1,0:T(8,128)(2,1)S(1)}, bf16[24,1280]{1,0:T(8,128)(2,1)S(1)}, u32[]{:S(2)}, u32[]{:S(2)}) collective-permute-start(bf16[24,1280]{1,0:T(8,128)(2,1)S(1)} %get-tuple-element.66.refs_0_), channel_id=1, source_target_pairs={{0,4},{1,5},{2,6},{3,7},{4,0},{5,1},{6,2},{7,3},{8,12},{9,13},{10,... | collective-permute-start | bytes 184328 | tf_op jit(solution)/shard_map/ppermute | solution.py:339
  9.5 1.9 %collective-permute-done.1.refs_2_ = bf16[24,1280]{1,0:T(8,128)(2,1)S(1)} collective-permute-done((bf16[24,1280]{1,0:T(8,128)(2,1)S(1)}, bf16[24,1280]{1,0:T(8,128)(2,1)S(1)}, u32[]{:S(2)}, u32[]{:S(2)}) %collective-permute-start.1) | collective-permute-done | bytes 61472 | tf_op jit(solution)/shard_map/ppermute | solution.py:339
  11.4 2.4 %collective-permute-done.2.refs_3_ = bf16[24,1280]{1,0:T(8,128)(2,1)S(1)} collective-permute-done((bf16[24,1280]{1,0:T(8,128)(2,1)S(1)}, bf16[24,1280]{1,0:T(8,128)(2,1)S(1)}, u32[]{:S(2)}, u32[]{:S(2)}) %collective-permute-start.2) | collective-permute-done | bytes 61472 | tf_op jit(solution)/shard_map/ppermute | solution.py:339
  15.3 5.8 %shard_map.200 = (f32[24,1152]{1,0:T(8,128)S(1)}, bf16[24,1152]{1,0:T(8,128)(2,1)S(1)}, bf16[24,1152]{1,0:T(8,128)(2,1)S(1)}, bf16[24,1152]{1,0:T(8,128)(2,1)S(1)}) custom-call(bf16[24,1280]{1,0:T(8,128)(2,1)S(1)} %get-tuple-element.66.refs_0_, bf16[24,1280]{1,0:T(8,128)(2,1)S(1)} %collective-permute-done.refs_1_, ...), custom_call_target="tpu_custom_call" | custom-call | flops 1006632960 | bytes 42434560 | tf_op jit(solution)/shard_map/pallas_call | solution.py:28
  21.1 3.1 %collective-permute-start.10 = (bf16[24,1152]{1,0:T(8,128)(2,1)S(1)}, bf16[24,1152]{1,0:T(8,128)(2,1)S(1)}, u32[]{:S(2)}, u32[]{:S(2)}) collective-permute-start(bf16[24,1152]{1,0:T(8,128)(2,1)S(1)} %get-tuple-element.72), channel_id=1, source_target_pairs={{0,8},{8,0},{16,24},{24,16},{1,9},{9,1},{17,25},{25,17},{2,10},{10... | collective-permute-start | bytes 165896 | tf_op jit(solution)/shard_map/ppermute | solution.py:335
  24.2 2.6 %collective-permute-start.11 = (bf16[24,1152]{1,0:T(8,128)(2,1)S(1)}, bf16[24,1152]{1,0:T(8,128)(2,1)S(1)}, u32[]{:S(2)}, u32[]{:S(2)}) collective-permute-start(bf16[24,1152]{1,0:T(8,128)(2,1)S(1)} %get-tuple-element.73), channel_id=1, source_target_pairs={{0,16},{8,24},{16,0},{24,8},{1,17},{9,25},{17,1},{25,9},{2,18},{10... | collective-permute-start | bytes 165896 | tf_op jit(solution)/shard_map/ppermute | solution.py:335
  26.8 5.8 %shard_map.199 = (f32[24,1024]{1,0:T(8,128)S(1)}, bf16[24,1024]{1,0:T(8,128)(2,1)S(1)}, bf16[24,1024]{1,0:T(8,128)(2,1)S(1)}, bf16[24,1024]{1,0:T(8,128)(2,1)S(1)}) custom-call(bf16[24,1280]{1,0:T(8,128)(2,1)S(1)} %get-tuple-element.66.refs_0_, bf16[24,1280]{1,0:T(8,128)(2,1)S(1)} %collective-permute-done.refs_1_, ...), custom_call_target="tpu_custom_call" | custom-call | flops 1006632960 | bytes 42434560 | tf_op jit(solution)/shard_map/pallas_call | solution.py:28
  33.5 3.5 %collective-permute-start.8 = (bf16[24,1024]{1,0:T(8,128)(2,1)S(1)}, bf16[24,1024]{1,0:T(8,128)(2,1)S(1)}, u32[]{:S(2)}, u32[]{:S(2)}) collective-permute-start(bf16[24,1024]{1,0:T(8,128)(2,1)S(1)} %get-tuple-element.69), channel_id=1, source_target_pairs={{0,16},{8,24},{16,0},{24,8},{1,17},{9,25},{17,1},{25,9},{2,18},{10... | collective-permute-start | bytes 147464 | tf_op jit(solution)/shard_map/ppermute | solution.py:335
  37.8 3.8 %collective-permute-start.17 = (bf16[24,1024]{1,0:T(8,128)(2,1)S(1)}, bf16[24,1024]{1,0:T(8,128)(2,1)S(1)}, u32[]{:S(2)}, u32[]{:S(2)}) collective-permute-start(bf16[24,1024]{1,0:T(8,128)(2,1)S(1)} %get-tuple-element.77.refs_0_), channel_id=1, source_target_pairs={{0,16},{8,24},{16,0},{24,8},{1,17},{9,25},{17,1},{25,9},{2,18},{10... | collective-permute-start | bytes 147464 | tf_op jit(solution)/shard_map/ppermute | solution.py:335
  43.1 3.0 %collective-permute-start.14 = (bf16[24,1152]{1,0:T(8,128)(2,1)S(1)}, bf16[24,1152]{1,0:T(8,128)(2,1)S(1)}, u32[]{:S(2)}, u32[]{:S(2)}) collective-permute-start(bf16[24,1152]{1,0:T(8,128)(2,1)S(1)} %get-tuple-element.76.refs_0_), channel_id=1, source_target_pairs={{0,16},{8,24},{16,0},{24,8},{1,17},{9,25},{17,1},{25,9},{2,18},{10... | collective-permute-start | bytes 165896 | tf_op jit(solution)/shard_map/ppermute | solution.py:335
  47.8 3.9 %shard_map.203 = (f32[48,5120]{1,0:T(8,128)S(1)}, f32[12,128]{1,0:T(8,128)S(1)}) custom-call(bf16[24,1024]{1,0:T(8,128)(2,1)S(1)} %get-tuple-element.77.refs_0_, bf16[24,1024]{1,0:T(8,128)(2,1)S(1)} %collective-permute-done.16.refs_1_, bf16[24,1024]{1,0:T(8,128)(2,1)S(1)} %collective-permute-done.17.refs_2_, ...), custom_call_target="tpu_custom_call" | custom-call | flops 1006632960 | bytes 42139648 | tf_op jit(solution)/shard_map/pallas_call | solution.py:28
  52.2 4.7 %shard_map.204 = (f32[24,5120]{1,0:T(8,128)S(1)}, bf16[24,5120]{1,0:T(8,128)(2,1)S(1)}) custom-call(bf16[24,1152]{1,0:T(8,128)(2,1)S(1)} %get-tuple-element.76.refs_0_, bf16[24,1152]{1,0:T(8,128)(2,1)S(1)} %collective-permute-done.13.refs_1_, bf16[24,1152]{1,0:T(8,128)(2,1)S(1)} %collective-permute-done.14.refs_2_, ...), custom_call_target="tpu_custom_call" | custom-call | flops 1006632960 | bytes 43147264 | tf_op jit(solution)/shard_map/pallas_call | solution.py:28
  58.6 1.6 %collective-permute-start.20 = (bf16[24,1280]{1,0:T(8,128)(2,1)S(1)}, bf16[24,1280]{1,0:T(8,128)(2,1)S(1)}, u32[]{:S(2)}, u32[]{:S(2)}) collective-permute-start(bf16[24,1280]{1,0:T(8,128)(2,1)S(1)} %get-tuple-element.82), channel_id=1, source_target_pairs={{0,2},{1,3},{2,0},{3,1},{4,6},{5,7},{6,4},{7,5},{8,10},{9,11},{10,... | collective-permute-start | bytes 184328 | tf_op jit(solution)/shard_map/ppermute | solution.py:339
  64.4 2.4 %collective-permute-done.22.refs_3_ = bf16[24,1280]{1,0:T(8,128)(2,1)S(1)} collective-permute-done((bf16[24,1280]{1,0:T(8,128)(2,1)S(1)}, bf16[24,1280]{1,0:T(8,128)(2,1)S(1)}, u32[]{:S(2)}, u32[]{:S(2)}) %collective-permute-start.22) | collective-permute-done | bytes 61472 | tf_op jit(solution)/shard_map/ppermute | solution.py:339
  68.9 2.4 %collective-permute-start.25 = (bf16[24,1280]{1,0:T(8,128)(2,1)S(1)}, bf16[24,1280]{1,0:T(8,128)(2,1)S(1)}, u32[]{:S(2)}, u32[]{:S(2)}) collective-permute-start(bf16[24,1280]{1,0:T(8,128)(2,1)S(1)} %get-tuple-element.87.refs_0_), channel_id=1, source_target_pairs={{0,6},{1,7},{2,4},{3,5},{4,2},{5,3},{6,0},{7,1},{8,14},{9,15},{10,... | collective-permute-start | bytes 184328 | tf_op jit(solution)/shard_map/ppermute | solution.py:339
  75.3 5.8 %shard_map.208 = (f32[24,1152]{1,0:T(8,128)S(1)}, bf16[24,1152]{1,0:T(8,128)(2,1)S(1)}, bf16[24,1152]{1,0:T(8,128)(2,1)S(1)}, bf16[24,1152]{1,0:T(8,128)(2,1)S(1)}) custom-call(bf16[24,1280]{1,0:T(8,128)(2,1)S(1)} %get-tuple-element.87.refs_0_, bf16[24,1280]{1,0:T(8,128)(2,1)S(1)} %collective-permute-done.23.refs_1_, ...), custom_call_target="tpu_custom_call" | custom-call | flops 1006632960 | bytes 42434560 | tf_op jit(solution)/shard_map/pallas_call | solution.py:28
  81.2 2.5 %collective-permute-start.34 = (bf16[24,1152]{1,0:T(8,128)(2,1)S(1)}, bf16[24,1152]{1,0:T(8,128)(2,1)S(1)}, u32[]{:S(2)}, u32[]{:S(2)}) collective-permute-start(bf16[24,1152]{1,0:T(8,128)(2,1)S(1)} %get-tuple-element.96), channel_id=1, source_target_pairs={{0,16},{8,24},{16,0},{24,8},{1,17},{9,25},{17,1},{25,9},{2,18},{10... | collective-permute-start | bytes 165896 | tf_op jit(solution)/shard_map/ppermute | solution.py:335
  83.6 1.9 %collective-permute-start.35 = (bf16[24,1152]{1,0:T(8,128)(2,1)S(1)}, bf16[24,1152]{1,0:T(8,128)(2,1)S(1)}, u32[]{:S(2)}, u32[]{:S(2)}) collective-permute-start(bf16[24,1152]{1,0:T(8,128)(2,1)S(1)} %get-tuple-element.97), channel_id=1, source_target_pairs={{0,24},{8,16},{16,8},{24,0},{1,25},{9,17},{17,9},{25,1},{2,26},{10... | collective-permute-start | bytes 165896 | tf_op jit(solution)/shard_map/ppermute | solution.py:335
  85.5 5.8 %shard_map.207 = (f32[24,1024]{1,0:T(8,128)S(1)}, bf16[24,1024]{1,0:T(8,128)(2,1)S(1)}, bf16[24,1024]{1,0:T(8,128)(2,1)S(1)}, bf16[24,1024]{1,0:T(8,128)(2,1)S(1)}) custom-call(bf16[24,1280]{1,0:T(8,128)(2,1)S(1)} %get-tuple-element.87.refs_0_, bf16[24,1280]{1,0:T(8,128)(2,1)S(1)} %collective-permute-done.23.refs_1_, ...), custom_call_target="tpu_custom_call" | custom-call | flops 1006632960 | bytes 42434560 | tf_op jit(solution)/shard_map/pallas_call | solution.py:28
  91.4 2.5 %collective-permute-start.31 = (bf16[24,1024]{1,0:T(8,128)(2,1)S(1)}, bf16[24,1024]{1,0:T(8,128)(2,1)S(1)}, u32[]{:S(2)}, u32[]{:S(2)}) collective-permute-start(bf16[24,1024]{1,0:T(8,128)(2,1)S(1)} %get-tuple-element.90), channel_id=1, source_target_pairs={{0,16},{8,24},{16,0},{24,8},{1,17},{9,25},{17,1},{25,9},{2,18},{10... | collective-permute-start | bytes 147464 | tf_op jit(solution)/shard_map/ppermute | solution.py:335
  93.8 1.9 %collective-permute-start.32 = (bf16[24,1024]{1,0:T(8,128)(2,1)S(1)}, bf16[24,1024]{1,0:T(8,128)(2,1)S(1)}, u32[]{:S(2)}, u32[]{:S(2)}) collective-permute-start(bf16[24,1024]{1,0:T(8,128)(2,1)S(1)} %get-tuple-element.91), channel_id=1, source_target_pairs={{0,24},{8,16},{16,8},{24,0},{1,25},{9,17},{17,9},{25,1},{2,26},{10... | collective-permute-start | bytes 147464 | tf_op jit(solution)/shard_map/ppermute | solution.py:335
  95.9 2.5 %collective-permute-start.40 = (bf16[24,1024]{1,0:T(8,128)(2,1)S(1)}, bf16[24,1024]{1,0:T(8,128)(2,1)S(1)}, u32[]{:S(2)}, u32[]{:S(2)}) collective-permute-start(bf16[24,1024]{1,0:T(8,128)(2,1)S(1)} %get-tuple-element.102.refs_0_), channel_id=1, source_target_pairs={{0,16},{8,24},{16,0},{24,8},{1,17},{9,25},{17,1},{25,9},{2,18},{10... | collective-permute-start | bytes 147464 | tf_op jit(solution)/shard_map/ppermute | solution.py:335
  98.4 1.9 %collective-permute-start.41 = (bf16[24,1024]{1,0:T(8,128)(2,1)S(1)}, bf16[24,1024]{1,0:T(8,128)(2,1)S(1)}, u32[]{:S(2)}, u32[]{:S(2)}) collective-permute-start(bf16[24,1024]{1,0:T(8,128)(2,1)S(1)} %get-tuple-element.102.refs_0_), channel_id=1, source_target_pairs={{0,24},{8,16},{16,8},{24,0},{1,25},{9,17},{17,9},{25,1},{2,26},{10... | collective-permute-start | bytes 147464 | tf_op jit(solution)/shard_map/ppermute | solution.py:335
  100.5 2.5 %collective-permute-start.37 = (bf16[24,1152]{1,0:T(8,128)(2,1)S(1)}, bf16[24,1152]{1,0:T(8,128)(2,1)S(1)}, u32[]{:S(2)}, u32[]{:S(2)}) collective-permute-start(bf16[24,1152]{1,0:T(8,128)(2,1)S(1)} %get-tuple-element.101.refs_0_), channel_id=1, source_target_pairs={{0,16},{8,24},{16,0},{24,8},{1,17},{9,25},{17,1},{25,9},{2,18},{10... | collective-permute-start | bytes 165896 | tf_op jit(solution)/shard_map/ppermute | solution.py:335
  103.0 1.9 %collective-permute-start.38 = (bf16[24,1152]{1,0:T(8,128)(2,1)S(1)}, bf16[24,1152]{1,0:T(8,128)(2,1)S(1)}, u32[]{:S(2)}, u32[]{:S(2)}) collective-permute-start(bf16[24,1152]{1,0:T(8,128)(2,1)S(1)} %get-tuple-element.101.refs_0_), channel_id=1, source_target_pairs={{0,24},{8,16},{16,8},{24,0},{1,25},{9,17},{17,9},{25,1},{2,26},{10... | collective-permute-start | bytes 165896 | tf_op jit(solution)/shard_map/ppermute | solution.py:335
  104.9 4.0 %shard_map.211 = (f32[48,5120]{1,0:T(8,128)S(1)}, f32[12,128]{1,0:T(8,128)S(1)}) custom-call(bf16[24,1024]{1,0:T(8,128)(2,1)S(1)} %get-tuple-element.102.refs_0_, bf16[24,1024]{1,0:T(8,128)(2,1)S(1)} %collective-permute-done.39.refs_1_, bf16[24,1024]{1,0:T(8,128)(2,1)S(1)} %collective-permute-done.40.refs_2_, ...), custom_call_target="tpu_custom_call" | custom-call | flops 1006632960 | bytes 42139648 | tf_op jit(solution)/shard_map/pallas_call | solution.py:28
  108.9 4.7 %shard_map.212 = (f32[24,5120]{1,0:T(8,128)S(1)}, bf16[24,5120]{1,0:T(8,128)(2,1)S(1)}) custom-call(bf16[24,1152]{1,0:T(8,128)(2,1)S(1)} %get-tuple-element.101.refs_0_, bf16[24,1152]{1,0:T(8,128)(2,1)S(1)} %collective-permute-done.36.refs_1_, bf16[24,1152]{1,0:T(8,128)(2,1)S(1)} %collective-permute-done.37.refs_2_, ...), custom_call_target="tpu_custom_call" | custom-call | flops 1006632960 | bytes 43147264 | tf_op jit(solution)/shard_map/pallas_call | solution.py:28
  115.4 1.5 %collective-permute-start.43 = (bf16[24,1280]{1,0:T(8,128)(2,1)S(1)}, bf16[24,1280]{1,0:T(8,128)(2,1)S(1)}, u32[]{:S(2)}, u32[]{:S(2)}) collective-permute-start(bf16[24,1280]{1,0:T(8,128)(2,1)S(1)} %get-tuple-element.107), channel_id=1, source_target_pairs={{0,2},{1,3},{2,0},{3,1},{4,6},{5,7},{6,4},{7,5},{8,10},{9,11},{10,... | collective-permute-start | bytes 184328 | tf_op jit(solution)/shard_map/ppermute | solution.py:339
  117.0 1.5 %collective-permute-start.44 = (bf16[24,1280]{1,0:T(8,128)(2,1)S(1)}, bf16[24,1280]{1,0:T(8,128)(2,1)S(1)}, u32[]{:S(2)}, u32[]{:S(2)}) collective-permute-start(bf16[24,1280]{1,0:T(8,128)(2,1)S(1)} %get-tuple-element.108), channel_id=1, source_target_pairs={{0,4},{1,5},{2,6},{3,7},{4,0},{5,1},{6,2},{7,3},{8,12},{9,13},{10,... | collective-permute-start | bytes 184328 | tf_op jit(solution)/shard_map/ppermute | solution.py:339
  121.2 2.4 %collective-permute-done.45.refs_3_ = bf16[24,1280]{1,0:T(8,128)(2,1)S(1)} collective-permute-done((bf16[24,1280]{1,0:T(8,128)(2,1)S(1)}, bf16[24,1280]{1,0:T(8,128)(2,1)S(1)}, u32[]{:S(2)}, u32[]{:S(2)}) %collective-permute-start.45) | collective-permute-done | bytes 61472 | tf_op jit(solution)/shard_map/ppermute | solution.py:339
  127.0 2.4 %collective-permute-start.49 = (f32[8,256]{1,0:T(8,128)S(1)}, f32[8,256]{1,0:T(8,128)S(1)}, u32[]{:S(2)}, u32[]{:S(2)}) collective-permute-start(f32[8,256]{1,0:T(8,128)S(1)} %shard_map.215.refs_0_), channel_id=1, source_target_pairs={{0,6},{1,7},{2,4},{3,5},{4,2},{5,3},{6,0},{7,1},{8,14},{9,15},{10,... | collective-permute-start | bytes 24584 | tf_op jit(solution)/shard_map/ppermute | solution.py:339
  (143 shorter events, 33.9 us)
Async XLA Ops:
  4.2 5.3 %collective-permute-start = (bf16[24,1280]{1,0:T(8,128)(2,1)S(1)}, bf16[24,1280]{1,0:T(8,128)(2,1)S(1)}, u32[]{:S(2)}, u32[]{:S(2)}) collective-permute-start(bf16[24,1280]{1,0:T(8,128)(2,1)S(1)} %get-tuple-element.66.refs_0_), channel_id=1, source_target_pairs={{0,2},{1,3},{2,0},{3,1},{4,6},{5,7},{6,4},{7,5},{8,10},{9,11},{10,... | collective-permute-start | bytes 184328 | tf_op jit(solution)/shard_map/ppermute | solution.py:339
  8.7 5.1 %collective-permute-start.2 = (bf16[24,1280]{1,0:T(8,128)(2,1)S(1)}, bf16[24,1280]{1,0:T(8,128)(2,1)S(1)}, u32[]{:S(2)}, u32[]{:S(2)}) collective-permute-start(bf16[24,1280]{1,0:T(8,128)(2,1)S(1)} %get-tuple-element.66.refs_0_), channel_id=1, source_target_pairs={{0,6},{1,7},{2,4},{3,5},{4,2},{5,3},{6,0},{7,1},{8,14},{9,15},{10,... | collective-permute-start | bytes 184328 | tf_op jit(solution)/shard_map/ppermute | solution.py:339
  8.8 5.1 %collective-permute-start.3 = (bf16[24,1280]{1,0:T(8,128)(2,1)S(1)}, bf16[24,1280]{1,0:T(8,128)(2,1)S(1)}, u32[]{:S(2)}, u32[]{:S(2)}) collective-permute-start(bf16[24,1280]{1,0:T(8,128)(2,1)S(1)} %get-tuple-element.66.refs_0_), channel_id=1, source_target_pairs={{0,1},{1,0},{2,3},{3,2},{4,5},{5,4},{6,7},{7,6},{8,9},{9,8},{10,11... | collective-permute-start | bytes 184328 | tf_op jit(solution)/shard_map/ppermute | solution.py:348
  9.5 4.4 %collective-permute-start.4 = (bf16[24,1280]{1,0:T(8,128)(2,1)S(1)}, bf16[24,1280]{1,0:T(8,128)(2,1)S(1)}, u32[]{:S(2)}, u32[]{:S(2)}) collective-permute-start(bf16[24,1280]{1,0:T(8,128)(2,1)S(1)} %collective-permute-done.refs_1_), channel_id=1, source_target_pairs={{0,1},{1,0},{2,3},{3,2},{4,5},{5,4},{6,7},{7,6},{8,9},{9,8},{10,11... | collective-permute-start | bytes 184328 | tf_op jit(solution)/shard_map/ppermute | solution.py:348
  21.1 15.9 %collective-permute-start.10 = (bf16[24,1152]{1,0:T(8,128)(2,1)S(1)}, bf16[24,1152]{1,0:T(8,128)(2,1)S(1)}, u32[]{:S(2)}, u32[]{:S(2)}) collective-permute-start(bf16[24,1152]{1,0:T(8,128)(2,1)S(1)} %get-tuple-element.72), channel_id=1, source_target_pairs={{0,8},{8,0},{16,24},{24,16},{1,9},{9,1},{17,25},{25,17},{2,10},{10... | collective-permute-start | bytes 165896 | tf_op jit(solution)/shard_map/ppermute | solution.py:335
  24.2 12.8 %collective-permute-start.11 = (bf16[24,1152]{1,0:T(8,128)(2,1)S(1)}, bf16[24,1152]{1,0:T(8,128)(2,1)S(1)}, u32[]{:S(2)}, u32[]{:S(2)}) collective-permute-start(bf16[24,1152]{1,0:T(8,128)(2,1)S(1)} %get-tuple-element.73), channel_id=1, source_target_pairs={{0,16},{8,24},{16,0},{24,8},{1,17},{9,25},{17,1},{25,9},{2,18},{10... | collective-permute-start | bytes 165896 | tf_op jit(solution)/shard_map/ppermute | solution.py:335
  26.8 10.2 %collective-permute-start.12 = (bf16[24,1152]{1,0:T(8,128)(2,1)S(1)}, bf16[24,1152]{1,0:T(8,128)(2,1)S(1)}, u32[]{:S(2)}, u32[]{:S(2)}) collective-permute-start(bf16[24,1152]{1,0:T(8,128)(2,1)S(1)} %get-tuple-element.74), channel_id=1, source_target_pairs={{0,24},{8,16},{16,8},{24,0},{1,25},{9,17},{17,9},{25,1},{2,26},{10... | collective-permute-start | bytes 165896 | tf_op jit(solution)/shard_map/ppermute | solution.py:335
  32.5 9.0 %collective-permute-start.7 = (bf16[24,1024]{1,0:T(8,128)(2,1)S(1)}, bf16[24,1024]{1,0:T(8,128)(2,1)S(1)}, u32[]{:S(2)}, u32[]{:S(2)}) collective-permute-start(bf16[24,1024]{1,0:T(8,128)(2,1)S(1)} %get-tuple-element.68), channel_id=1, source_target_pairs={{0,8},{8,0},{16,24},{24,16},{1,9},{9,1},{17,25},{25,17},{2,10},{10... | collective-permute-start | bytes 147464 | tf_op jit(solution)/shard_map/ppermute | solution.py:335
  33.5 8.1 %collective-permute-start.8 = (bf16[24,1024]{1,0:T(8,128)(2,1)S(1)}, bf16[24,1024]{1,0:T(8,128)(2,1)S(1)}, u32[]{:S(2)}, u32[]{:S(2)}) collective-permute-start(bf16[24,1024]{1,0:T(8,128)(2,1)S(1)} %get-tuple-element.69), channel_id=1, source_target_pairs={{0,16},{8,24},{16,0},{24,8},{1,17},{9,25},{17,1},{25,9},{2,18},{10... | collective-permute-start | bytes 147464 | tf_op jit(solution)/shard_map/ppermute | solution.py:335
  37.0 6.0 %collective-permute-start.9 = (bf16[24,1024]{1,0:T(8,128)(2,1)S(1)}, bf16[24,1024]{1,0:T(8,128)(2,1)S(1)}, u32[]{:S(2)}, u32[]{:S(2)}) collective-permute-start(bf16[24,1024]{1,0:T(8,128)(2,1)S(1)} %get-tuple-element.70), channel_id=1, source_target_pairs={{0,24},{8,16},{16,8},{24,0},{1,25},{9,17},{17,9},{25,1},{2,26},{10... | collective-permute-start | bytes 147464 | tf_op jit(solution)/shard_map/ppermute | solution.py:335
  37.2 9.0 %collective-permute-start.16 = (bf16[24,1024]{1,0:T(8,128)(2,1)S(1)}, bf16[24,1024]{1,0:T(8,128)(2,1)S(1)}, u32[]{:S(2)}, u32[]{:S(2)}) collective-permute-start(bf16[24,1024]{1,0:T(8,128)(2,1)S(1)} %get-tuple-element.77.refs_0_), channel_id=1, source_target_pairs={{0,8},{8,0},{16,24},{24,16},{1,9},{9,1},{17,25},{25,17},{2,10},{10... | collective-permute-start | bytes 147464 | tf_op jit(solution)/shard_map/ppermute | solution.py:335
  37.8 9.8 %collective-permute-start.17 = (bf16[24,1024]{1,0:T(8,128)(2,1)S(1)}, bf16[24,1024]{1,0:T(8,128)(2,1)S(1)}, u32[]{:S(2)}, u32[]{:S(2)}) collective-permute-start(bf16[24,1024]{1,0:T(8,128)(2,1)S(1)} %get-tuple-element.77.refs_0_), channel_id=1, source_target_pairs={{0,16},{8,24},{16,0},{24,8},{1,17},{9,25},{17,1},{25,9},{2,18},{10... | collective-permute-start | bytes 147464 | tf_op jit(solution)/shard_map/ppermute | solution.py:335
  41.6 6.2 %collective-permute-start.18 = (bf16[24,1024]{1,0:T(8,128)(2,1)S(1)}, bf16[24,1024]{1,0:T(8,128)(2,1)S(1)}, u32[]{:S(2)}, u32[]{:S(2)}) collective-permute-start(bf16[24,1024]{1,0:T(8,128)(2,1)S(1)} %get-tuple-element.77.refs_0_), channel_id=1, source_target_pairs={{0,24},{8,16},{16,8},{24,0},{1,25},{9,17},{17,9},{25,1},{2,26},{10... | collective-permute-start | bytes 147464 | tf_op jit(solution)/shard_map/ppermute | solution.py:335
  43.1 8.6 %collective-permute-start.13 = (bf16[24,1152]{1,0:T(8,128)(2,1)S(1)}, bf16[24,1152]{1,0:T(8,128)(2,1)S(1)}, u32[]{:S(2)}, u32[]{:S(2)}) collective-permute-start(bf16[24,1152]{1,0:T(8,128)(2,1)S(1)} %get-tuple-element.76.refs_0_), channel_id=1, source_target_pairs={{0,8},{8,0},{16,24},{24,16},{1,9},{9,1},{17,25},{25,17},{2,10},{10... | collective-permute-start | bytes 165896 | tf_op jit(solution)/shard_map/ppermute | solution.py:335
  43.1 8.5 %collective-permute-start.14 = (bf16[24,1152]{1,0:T(8,128)(2,1)S(1)}, bf16[24,1152]{1,0:T(8,128)(2,1)S(1)}, u32[]{:S(2)}, u32[]{:S(2)}) collective-permute-start(bf16[24,1152]{1,0:T(8,128)(2,1)S(1)} %get-tuple-element.76.refs_0_), channel_id=1, source_target_pairs={{0,16},{8,24},{16,0},{24,8},{1,17},{9,25},{17,1},{25,9},{2,18},{10... | collective-permute-start | bytes 165896 | tf_op jit(solution)/shard_map/ppermute | solution.py:335
  46.1 6.0 %collective-permute-start.15 = (bf16[24,1152]{1,0:T(8,128)(2,1)S(1)}, bf16[24,1152]{1,0:T(8,128)(2,1)S(1)}, u32[]{:S(2)}, u32[]{:S(2)}) collective-permute-start(bf16[24,1152]{1,0:T(8,128)(2,1)S(1)} %get-tuple-element.76.refs_0_), channel_id=1, source_target_pairs={{0,24},{8,16},{16,8},{24,0},{1,25},{9,17},{17,9},{25,1},{2,26},{10... | collective-permute-start | bytes 165896 | tf_op jit(solution)/shard_map/ppermute | solution.py:335
  61.7 5.1 %collective-permute-start.22 = (bf16[24,1280]{1,0:T(8,128)(2,1)S(1)}, bf16[24,1280]{1,0:T(8,128)(2,1)S(1)}, u32[]{:S(2)}, u32[]{:S(2)}) collective-permute-start(bf16[24,1280]{1,0:T(8,128)(2,1)S(1)} %get-tuple-element.84), channel_id=1, source_target_pairs={{0,6},{1,7},{2,4},{3,5},{4,2},{5,3},{6,0},{7,1},{8,14},{9,15},{10,... | collective-permute-start | bytes 184328 | tf_op jit(solution)/shard_map/ppermute | solution.py:339
  68.9 5.1 %collective-permute-start.25 = (bf16[24,1280]{1,0:T(8,128)(2,1)S(1)}, bf16[24,1280]{1,0:T(8,128)(2,1)S(1)}, u32[]{:S(2)}, u32[]{:S(2)}) collective-permute-start(bf16[24,1280]{1,0:T(8,128)(2,1)S(1)} %get-tuple-element.87.refs_0_), channel_id=1, source_target_pairs={{0,6},{1,7},{2,4},{3,5},{4,2},{5,3},{6,0},{7,1},{8,14},{9,15},{10,... | collective-permute-start | bytes 184328 | tf_op jit(solution)/shard_map/ppermute | solution.py:339
  81.1 12.8 %collective-permute-start.33 = (bf16[24,1152]{1,0:T(8,128)(2,1)S(1)}, bf16[24,1152]{1,0:T(8,128)(2,1)S(1)}, u32[]{:S(2)}, u32[]{:S(2)}) collective-permute-start(bf16[24,1152]{1,0:T(8,128)(2,1)S(1)} %get-tuple-element.95), channel_id=1, source_target_pairs={{0,8},{8,0},{16,24},{24,16},{1,9},{9,1},{17,25},{25,17},{2,10},{10... | collective-permute-start | bytes 165896 | tf_op jit(solution)/shard_map/ppermute | solution.py:335
  81.2 14.6 %collective-permute-start.34 = (bf16[24,1152]{1,0:T(8,128)(2,1)S(1)}, bf16[24,1152]{1,0:T(8,128)(2,1)S(1)}, u32[]{:S(2)}, u32[]{:S(2)}) collective-permute-start(bf16[24,1152]{1,0:T(8,128)(2,1)S(1)} %get-tuple-element.96), channel_id=1, source_target_pairs={{0,16},{8,24},{16,0},{24,8},{1,17},{9,25},{17,1},{25,9},{2,18},{10... | collective-permute-start | bytes 165896 | tf_op jit(solution)/shard_map/ppermute | solution.py:335
  83.6 12.1 %collective-permute-start.35 = (bf16[24,1152]{1,0:T(8,128)(2,1)S(1)}, bf16[24,1152]{1,0:T(8,128)(2,1)S(1)}, u32[]{:S(2)}, u32[]{:S(2)}) collective-permute-start(bf16[24,1152]{1,0:T(8,128)(2,1)S(1)} %get-tuple-element.97), channel_id=1, source_target_pairs={{0,24},{8,16},{16,8},{24,0},{1,25},{9,17},{17,9},{25,1},{2,26},{10... | collective-permute-start | bytes 165896 | tf_op jit(solution)/shard_map/ppermute | solution.py:335
  91.3 7.1 %collective-permute-start.30 = (bf16[24,1024]{1,0:T(8,128)(2,1)S(1)}, bf16[24,1024]{1,0:T(8,128)(2,1)S(1)}, u32[]{:S(2)}, u32[]{:S(2)}) collective-permute-start(bf16[24,1024]{1,0:T(8,128)(2,1)S(1)} %get-tuple-element.89), channel_id=1, source_target_pairs={{0,8},{8,0},{16,24},{24,16},{1,9},{9,1},{17,25},{25,17},{2,10},{10... | collective-permute-start | bytes 147464 | tf_op jit(solution)/shard_map/ppermute | solution.py:335
  91.4 8.9 %collective-permute-start.31 = (bf16[24,1024]{1,0:T(8,128)(2,1)S(1)}, bf16[24,1024]{1,0:T(8,128)(2,1)S(1)}, u32[]{:S(2)}, u32[]{:S(2)}) collective-permute-start(bf16[24,1024]{1,0:T(8,128)(2,1)S(1)} %get-tuple-element.90), channel_id=1, source_target_pairs={{0,16},{8,24},{16,0},{24,8},{1,17},{9,25},{17,1},{25,9},{2,18},{10... | collective-permute-start | bytes 147464 | tf_op jit(solution)/shard_map/ppermute | solution.py:335
  93.8 6.5 %collective-permute-start.32 = (bf16[24,1024]{1,0:T(8,128)(2,1)S(1)}, bf16[24,1024]{1,0:T(8,128)(2,1)S(1)}, u32[]{:S(2)}, u32[]{:S(2)}) collective-permute-start(bf16[24,1024]{1,0:T(8,128)(2,1)S(1)} %get-tuple-element.91), channel_id=1, source_target_pairs={{0,24},{8,16},{16,8},{24,0},{1,25},{9,17},{17,9},{25,1},{2,26},{10... | collective-permute-start | bytes 147464 | tf_op jit(solution)/shard_map/ppermute | solution.py:335
  95.9 7.1 %collective-permute-start.39 = (bf16[24,1024]{1,0:T(8,128)(2,1)S(1)}, bf16[24,1024]{1,0:T(8,128)(2,1)S(1)}, u32[]{:S(2)}, u32[]{:S(2)}) collective-permute-start(bf16[24,1024]{1,0:T(8,128)(2,1)S(1)} %get-tuple-element.102.refs_0_), channel_id=1, source_target_pairs={{0,8},{8,0},{16,24},{24,16},{1,9},{9,1},{17,25},{25,17},{2,10},{10... | collective-permute-start | bytes 147464 | tf_op jit(solution)/shard_map/ppermute | solution.py:335
  95.9 8.9 %collective-permute-start.40 = (bf16[24,1024]{1,0:T(8,128)(2,1)S(1)}, bf16[24,1024]{1,0:T(8,128)(2,1)S(1)}, u32[]{:S(2)}, u32[]{:S(2)}) collective-permute-start(bf16[24,1024]{1,0:T(8,128)(2,1)S(1)} %get-tuple-element.102.refs_0_), channel_id=1, source_target_pairs={{0,16},{8,24},{16,0},{24,8},{1,17},{9,25},{17,1},{25,9},{2,18},{10... | collective-permute-start | bytes 147464 | tf_op jit(solution)/shard_map/ppermute | solution.py:335
  98.4 6.5 %collective-permute-start.41 = (bf16[24,1024]{1,0:T(8,128)(2,1)S(1)}, bf16[24,1024]{1,0:T(8,128)(2,1)S(1)}, u32[]{:S(2)}, u32[]{:S(2)}) collective-permute-start(bf16[24,1024]{1,0:T(8,128)(2,1)S(1)} %get-tuple-element.102.refs_0_), channel_id=1, source_target_pairs={{0,24},{8,16},{16,8},{24,0},{1,25},{9,17},{17,9},{25,1},{2,26},{10... | collective-permute-start | bytes 147464 | tf_op jit(solution)/shard_map/ppermute | solution.py:335
  100.4 8.5 %collective-permute-start.36 = (bf16[24,1152]{1,0:T(8,128)(2,1)S(1)}, bf16[24,1152]{1,0:T(8,128)(2,1)S(1)}, u32[]{:S(2)}, u32[]{:S(2)}) collective-permute-start(bf16[24,1152]{1,0:T(8,128)(2,1)S(1)} %get-tuple-element.101.refs_0_), channel_id=1, source_target_pairs={{0,8},{8,0},{16,24},{24,16},{1,9},{9,1},{17,25},{25,17},{2,10},{10... | collective-permute-start | bytes 165896 | tf_op jit(solution)/shard_map/ppermute | solution.py:335
  100.5 8.4 %collective-permute-start.37 = (bf16[24,1152]{1,0:T(8,128)(2,1)S(1)}, bf16[24,1152]{1,0:T(8,128)(2,1)S(1)}, u32[]{:S(2)}, u32[]{:S(2)}) collective-permute-start(bf16[24,1152]{1,0:T(8,128)(2,1)S(1)} %get-tuple-element.101.refs_0_), channel_id=1, source_target_pairs={{0,16},{8,24},{16,0},{24,8},{1,17},{9,25},{17,1},{25,9},{2,18},{10... | collective-permute-start | bytes 165896 | tf_op jit(solution)/shard_map/ppermute | solution.py:335
  103.0 6.0 %collective-permute-start.38 = (bf16[24,1152]{1,0:T(8,128)(2,1)S(1)}, bf16[24,1152]{1,0:T(8,128)(2,1)S(1)}, u32[]{:S(2)}, u32[]{:S(2)}) collective-permute-start(bf16[24,1152]{1,0:T(8,128)(2,1)S(1)} %get-tuple-element.101.refs_0_), channel_id=1, source_target_pairs={{0,24},{8,16},{16,8},{24,0},{1,25},{9,17},{17,9},{25,1},{2,26},{10... | collective-permute-start | bytes 165896 | tf_op jit(solution)/shard_map/ppermute | solution.py:335
  118.5 5.1 %collective-permute-start.45 = (bf16[24,1280]{1,0:T(8,128)(2,1)S(1)}, bf16[24,1280]{1,0:T(8,128)(2,1)S(1)}, u32[]{:S(2)}, u32[]{:S(2)}) collective-permute-start(bf16[24,1280]{1,0:T(8,128)(2,1)S(1)} %get-tuple-element.109), channel_id=1, source_target_pairs={{0,6},{1,7},{2,4},{3,5},{4,2},{5,3},{6,0},{7,1},{8,14},{9,15},{10,... | collective-permute-start | bytes 184328 | tf_op jit(solution)/shard_map/ppermute | solution.py:339
  127.0 4.5 %collective-permute-start.49 = (f32[8,256]{1,0:T(8,128)S(1)}, f32[8,256]{1,0:T(8,128)S(1)}, u32[]{:S(2)}, u32[]{:S(2)}) collective-permute-start(f32[8,256]{1,0:T(8,128)S(1)} %shard_map.215.refs_0_), channel_id=1, source_target_pairs={{0,6},{1,7},{2,4},{3,5},{4,2},{5,3},{6,0},{7,1},{8,14},{9,15},{10,... | collective-permute-start | bytes 24584 | tf_op jit(solution)/shard_map/ppermute | solution.py:339
  (43 other events, 428.6 us)
